TPU v7x, 256 devices: a whole 4x4x8 slice. The times are simulated.
256 devices in a mesh: lat: 4 (over y_lo, core), lon: 64 (over x, z, y_hi).
Axes of the slice: x: 4, y: 4 (y_hi: 2, y_lo: 2; y = y_hi * 2 + y_lo), z: 8, core: 2. Of those that a mesh axis runs over, the one named last changes fastest.
Arguments:
- activation: float32 [64, 768, 640], P('lat', 'lon'), may hold values from -6 to 6
- cotangent: float32 [64, 768, 640], P('lat', 'lon'), may hold values from -6 to 6
- weight_in: float32 [1280, 640], replicated, may hold values from -0.25 to 0.25
- weight_out: float32 [1280, 640], replicated, may hold values from -0.15625 to 0.15625
- kernels: float32 [3, 64, 7, 768], P(None, 'lat'), may hold values from -0.21875 to 0.21875
- mixing: float32 [640, 3], P('lon'), may hold values from -3.5 to 3.5
Outputs:
- field_grad: float32 [64, 768, 640], P('lat', 'lon')
- grad_in: float32 [1280, 640], P('lon', 'lat')
- grad_out: float32 [1280, 640], P('lon', 'lat')
All inputs are finite; a program needn't handle non-finite values.
Results may differ from a plain program's by a relative error of at most 0.0001.
Values sent between devices are 32-bit elements; how exact they have to be, the bound alone decides.
No kernel may reach another device: no remote copies, remote signals or barrier semaphores. Data moves between devices by JAX's collectives and lax.ppermute only.
A program may use at most 128 MiB of HBM per device.

v0:
```python
import math

import jax
import jax.numpy as jnp
from jax import lax
from jax.sharding import PartitionSpec as P


def with_halo(block, sides, width):
    for axis, dim in sides:
        count = lax.axis_size(axis)
        forward = [(i, i + 1) for i in range(count - 1)]
        backward = [(target, source) for source, target in forward]
        low = lax.ppermute(
            lax.slice_in_dim(block, block.shape[dim] - width, None, axis=dim), axis, forward
        )
        high = lax.ppermute(lax.slice_in_dim(block, 0, width, axis=dim), axis, backward)
        block = jnp.concatenate([low, block, high], axis=dim)
    return block


def gelu_parts(preact):
    normal_cdf = 0.5 * (1.0 + jax.scipy.special.erf(preact / math.sqrt(2.0)))
    density = jnp.exp(-0.5 * preact * preact) / math.sqrt(2.0 * math.pi)
    return (preact * normal_cdf, normal_cdf + preact * density)


def tables(circle):
    half = circle // 2 + 1
    index = jnp.arange(circle, dtype=jnp.int32)
    freqs = jnp.arange(half, dtype=jnp.int32)
    product = index[:, None] * freqs[None, :] % circle
    angle = product.astype(jnp.float32) * (2.0 * math.pi / circle)
    cosine = jnp.cos(angle)
    sine = jnp.sin(angle)
    weights = (
        jnp.where((freqs == 0) | (freqs == circle // 2), 1.0, 2.0).astype(jnp.float32) / circle
    )
    return (cosine, sine, (cosine * weights[None, :]).T, (sine * weights[None, :]).T)


def per_device(activation, cotangent, weight_in, weight_out, kernels, mixing):
    high = lax.Precision.HIGHEST
    lat_rows, lon_cols, width = activation.shape
    flat_act = activation.reshape(lat_rows * lon_cols, width)
    flat_cot = cotangent.reshape(lat_rows * lon_cols, width)
    preact = jnp.einsum(
        "rd,hd->rh", flat_act, weight_in, precision=high, preferred_element_type=jnp.float32
    )
    hidden, slope = gelu_parts(preact)
    hidden_grad = (
        jnp.einsum(
            "rd,hd->rh", flat_cot, weight_out, precision=high, preferred_element_type=jnp.float32
        )
        * slope
    )
    unit_grad = flat_cot + jnp.dot(
        hidden_grad, weight_in, precision=high, preferred_element_type=jnp.float32
    )
    part_in = jnp.einsum(
        "rh,rd->hd", hidden_grad, flat_act, precision=high, preferred_element_type=jnp.float32
    )
    part_out = jnp.einsum(
        "rh,rd->hd", hidden, flat_cot, precision=high, preferred_element_type=jnp.float32
    )
    first_in, first_out = (
        lax.psum_scatter(part_in, "lon", scatter_dimension=0, tiled=True),
        lax.psum_scatter(part_out, "lon", scatter_dimension=0, tiled=True),
    )
    grad_in, grad_out = (
        lax.psum_scatter(first_in, "lat", scatter_dimension=1, tiled=True),
        lax.psum_scatter(first_out, "lat", scatter_dimension=1, tiled=True),
    )
    unit_field = unit_grad.reshape(lat_rows, lon_cols, width)
    bordered = with_halo(unit_field, (("lat", 0),), 3)
    spread = lax.all_to_all(bordered, "lon", split_axis=2, concat_axis=1, tiled=True)
    circle = spread.shape[1]
    cosine_table, sine_table, back_cosine, back_sine = tables(circle)
    data_real = jnp.einsum("jlc,lf->cjf", spread, cosine_table, precision=high)
    data_imag = -jnp.einsum("jlc,lf->cjf", spread, sine_table, precision=high)
    kernel_real = jnp.einsum("bjkl,lf->bjkf", kernels, cosine_table, precision=high)
    kernel_imag = -jnp.einsum("bjkl,lf->bjkf", kernels, sine_table, precision=high)
    filter_real = jnp.einsum("cb,bjkf->cjkf", mixing, kernel_real, precision=high)
    filter_imag = jnp.einsum("cb,bjkf->cjkf", mixing, kernel_imag, precision=high)
    half = cosine_table.shape[1]
    total_real = jnp.zeros((spread.shape[2], lat_rows, half), jnp.float32)
    total_imag = jnp.zeros((spread.shape[2], lat_rows, half), jnp.float32)
    for offset in range(kernels.shape[2]):
        shifted_real = data_real[:, 6 - offset : 6 - offset + lat_rows]
        shifted_imag = data_imag[:, 6 - offset : 6 - offset + lat_rows]
        part_real = filter_real[:, :, offset]
        part_imag = filter_imag[:, :, offset]
        total_real = total_real + part_real * shifted_real + part_imag * shifted_imag
        total_imag = total_imag + part_real * shifted_imag - part_imag * shifted_real
    inverse = jnp.einsum("cjf,fl->jlc", total_real, back_cosine, precision=high)
    inverse = inverse - jnp.einsum("cjf,fl->jlc", total_imag, back_sine, precision=high)
    field_grad = lax.all_to_all(inverse, "lon", split_axis=1, concat_axis=2, tiled=True)
    return (field_grad, grad_in, grad_out)


def solution(mesh):
    placed = (
        P("lat", "lon", None),
        P("lat", "lon", None),
        P(),
        P(),
        P(None, "lat", None, None),
        P("lon", None),
    )
    return jax.shard_map(
        per_device,
        mesh=mesh,
        in_specs=placed,
        out_specs=(P("lat", "lon", None), P("lon", "lat"), P("lon", "lat")),
        check_vma=False,
    )
```

profile of v0, /device:TPU:1, one launch (start us, length us, event | category | flops | bytes accessed | tf_op | source)
XLA Modules:
  0.0 813.3 jit_solution(17169375615728162185)
XLA Ops:
  7.2 0.0 copy-start
  7.2 0.0 all-reduce.5.cloned.1.call-start
  7.2 2.2 copy.84
  9.4 1.9 reshape.27
  11.4 2.0 copy.83
  13.4 1.9 reshape.26
  15.3 0.0 copy-done
  15.3 4.7 fusion.159
  20.0 0.0 copy-start.5
  20.0 5.1 fusion.29
  25.1 0.0 copy-done.5
  25.1 3.7 convolution_multiply_fusion
  28.8 0.9 copy-done.2
  29.8 5.4 fusion.160
  35.2 0.0 all-reduce.5.cloned.1.call-update
  35.2 4.0 convolution_add_fusion
  39.2 0.0 copy-start.6
  39.2 0.8 copy-done.6
  40.0 4.6 collective-permute-start
  44.6 1.9 collective-permute-start.1
  46.6 1.1 reshape.28
  47.7 7.6 fusion
  55.3 0.0 collective-permute-done
  55.3 0.0 collective-permute-done.1
  55.3 0.1 pad_maximum_fusion
  55.4 3.3 copy.85
  58.7 5.6 reshape.42
  64.3 14.4 %all-to-all-start = ((f32[64,1,2640]{2,1,0:T(1,128)}), f32[64,1,2640]{2,1,0:T(1,128)S(1)}, u32[]{:S(2)}, u32[]{:S(2)}) async-start(f32[64,1,2640]{2,1,0:T(1,128)} %reshape.42), calls=%async_computation | async-start | bytes 1376256 | tf_op jit(solution)/shard_map/all_to_all | solution.py:76
  78.7 0.0 copy-start.7
  78.7 7.6 convolution_bitcast_fusion
  86.3 3.6 fusion.31
  89.9 3.8 fusion.33
  93.7 5.6 copy_bitcast_fusion
  99.3 4.3 all-to-all-done
  103.6 0.5 broadcast.25
  104.1 2.3 reduce
  106.4 4.5 reshape.43
  110.8 9.6 %copy.87 = f32[22,64,12,10]{2,1,0,3:T(8,128)} copy(f32[22,64,12,10]{0,2,3,1:T(8,128)} %bitcast.196) | data formatting | bytes 1351680 | tf_op jit(solution)/shard_map/all_to_all | solution.py:76
  120.4 7.4 all_to_all.29
  127.8 6.0 convolution_bitcast_fusion.1
  133.8 6.4 fusion.2
  140.3 8.4 %fusion.10 = f32[768,10,16]{0,2,1:T(8,128)S(1)} fusion(f32[385]{0:T(512)S(1)} %select_multiply_fusion, f32[10,16,7,385]{3,1,0,2:T(8,128)} %get-tuple-element.8, f32[10,16,7,385]{3,1,0,2:T(8,128)} %get-tuple-element.7, f32[10,22,385]{2,1,0:T(8,128)S(1)} %fusion.2, f32[10,22,385]{2,1,0:T(8,128)S(1)} %convolution_bitcast_fusion.1), kind=kOutput, calls=%fused_computation.21 | convolution fusion | flops 572325632 | bytes 8530688 | tf_op jit(solution)/shard_map/cjf,fl->jlc/dot_general | solution.py:95
  148.7 8.6 %fusion.1 = f32[16,768,10]{1,0,2:T(8,128)S(1)} fusion(f32[768,10,16]{0,2,1:T(8,128)S(1)} %fusion.10, f32[385]{0:T(512)S(1)} %select_multiply_fusion, f32[10,16,7,385]{3,1,0,2:T(8,128)} %get-tuple-element.8, f32[10,16,7,385]{3,1,0,2:T(8,128)} %get-tuple-element.7, f32[10,22,385]{2,1,0:T(8,128)S(1)} %fusion.2, f32[10,22,385]{2,1,0:T(8,128)S(1)} %convolution_bitcast_fusion.1), kind=kOutput, calls=%fused_computation.9 | convolution fusion | flops 572448512 | bytes 9022208 | tf_op jit(solution)/shard_map/cjf,fl->jlc/dot_general | solution.py:96
  157.3 5.0 copy.90
  162.2 5.1 reshape.44
  167.4 7.9 all-to-all-start.1
  175.3 0.0 reduce-scatter.7.cloned.1.call-start
  175.4 0.6 dynamic-slice
  176.6 545.5 %all-reduce.5.cloned.1.call-done = (f32[1280,640]{1,0:T(8,128)}, f32[1280,640]{1,0:T(8,128)}) async-done(((f32[1280,640]{1,0:T(8,128)}, f32[1280,640]{1,0:T(8,128)}), (f32[1280,640]{1,0:T(8,128)}, f32[1280,640]{1,0:T(8,128)})) %all-reduce.5.cloned.1.call-update) | async-done | bytes 6553616
  722.1 0.9 constant_dynamic-slice_fusion
  723.0 0.9 copy.100
  724.0 0.0 reduce-scatter.7.cloned.1.call-update
  724.0 0.0 reduce-scatter.9.cloned.1.call-start
  724.0 0.9 copy.102
  725.0 0.0 reduce-scatter.9.cloned.1.call-update
  725.0 0.0 all-to-all-done.1
  725.0 1.8 reduce.1
  726.8 3.9 reshape.45
  730.7 9.1 %copy.92 = f32[16,12,64,10]{3,2,0,1:T(8,128)} copy(f32[16,12,64,10]{0,3,1,2:T(8,128)} %bitcast.194) | data formatting | bytes 983040 | tf_op jit(solution)/shard_map/all_to_all | solution.py:97
  739.8 6.3 all_to_all.33
  746.1 35.1 %reduce-scatter.7.cloned.1.call-done = f32[160,20]{1,0:T(8,128)} async-done(((f32[640,20]{1,0:T(8,128)}), f32[160,20]{1,0:T(8,128)}) %reduce-scatter.7.cloned.1.call-update) | async-done | bytes 12816
  781.3 1.6 copy.101
  782.8 22.2 %reduce-scatter.9.cloned.1.call-done = f32[160,20]{1,0:T(8,128)} async-done(((f32[640,20]{1,0:T(8,128)}), f32[160,20]{1,0:T(8,128)}) %reduce-scatter.9.cloned.1.call-update) | async-done | bytes 12816
  805.0 1.6 copy.103
  (14 shorter events, 0.1 us)
Async XLA Ops:
  7.2 8.2 %copy-start = (f32[1280,640]{1,0:T(8,128)S(1)}, f32[1280,640]{1,0:T(8,128)}, u32[]{:S(2)}) copy-start(f32[1280,640]{1,0:T(8,128)} %param.8) | copy-start | bytes 9830404
  7.2 714.9 %all-reduce.5.cloned.1.call-start = ((), (), s32[]{:S(2)}) async-start(), calls=%async_computation.6 | async-start | bytes 13107200
  15.3 4.7 copy-start.3
  20.0 5.1 copy-start.5
  25.1 4.6 copy-start.4
  28.8 1.0 copy-start.2
  39.2 0.8 copy-start.6
  40.0 15.3 %collective-permute-start = (f32[3,12,640]{2,1,0:T(8,128)S(1)}, f32[3,12,640]{2,1,0:T(8,128)S(1)}, u32[]{:S(2)}, u32[]{:S(2)}) collective-permute-start(f32[3,12,640]{2,1,0:T(8,128)S(1)} %slice.98), channel_id=1, source_target_pairs={{0,64},{64,128},{128,192},{1,65},{65,129},{129,193},{2,66},{66,130... | collective-permute-start | bytes 276488 | tf_op jit(solution)/shard_map/ppermute | solution.py:14
  44.6 10.7 %collective-permute-start.1 = (f32[3,12,640]{2,1,0:T(8,128)S(1)}, f32[3,12,640]{2,1,0:T(8,128)S(1)}, u32[]{:S(2)}, u32[]{:S(2)}) collective-permute-start(f32[3,12,640]{2,1,0:T(8,128)S(1)} %slice.100), channel_id=1, source_target_pairs={{64,0},{128,64},{192,128},{65,1},{129,65},{193,129},{66,2},{130,66... | collective-permute-start | bytes 276488 | tf_op jit(solution)/shard_map/ppermute | solution.py:17
  64.3 39.3 %all-to-all-start = ((f32[64,1,2640]{2,1,0:T(1,128)}), f32[64,1,2640]{2,1,0:T(1,128)S(1)}, u32[]{:S(2)}, u32[]{:S(2)}) async-start(f32[64,1,2640]{2,1,0:T(1,128)} %reshape.42), calls=%async_computation | async-start | bytes 1376256 | tf_op jit(solution)/shard_map/all_to_all | solution.py:76
  78.7 7.6 copy-start.7
  162.2 13.1 %copy-start.8 = (u32[256]{0:T(256)S(1)}, u32[256]{0:T(256)}, u32[]{:S(2)}) copy-start(u32[256]{0:T(256)} %constant.40) | copy-start | bytes 3076
  167.4 557.6 %all-to-all-start.1 = ((f32[64,1,1920]{2,1,0:T(1,128)}), f32[64,1,1920]{2,1,0:T(1,128)S(1)}, u32[]{:S(2)}, u32[]{:S(2)}) async-start(f32[64,1,1920]{2,1,0:T(1,128)} %reshape.44), calls=%async_computation.1 | async-start | bytes 983040 | tf_op jit(solution)/shard_map/all_to_all | solution.py:97
  175.3 605.9 %reduce-scatter.7.cloned.1.call-start = ((), (), s32[]{:S(2)}) async-start(), calls=%async_computation.4 | async-start | bytes 409600
  724.0 81.1 %reduce-scatter.9.cloned.1.call-start = ((), (), s32[]{:S(2)}) async-start(), calls=%async_computation.5 | async-start | bytes 409600
  739.8 66.8 %copy-start.1 = (f32[1280,640]{1,0:T(8,128)S(1)}, f32[1280,640]{1,0:T(8,128)}, u32[]{:S(2)}) copy-start(f32[1280,640]{1,0:T(8,128)} %param.8) | copy-start | bytes 9830404
Sparse Core Ops, SparseCore 0:
  35.3 686.7 all-reduce.4
  724.8 56.4 reduce-scatter.6
  784.0 21.0 reduce-scatter.8
where the time goes:
time: 823 us; the launch traced here: 813 us
  waiting for transfers between devices  607 us (74%)
  local copies, waits for them, and re-layouts  83.4 us (10%)
  matrix products  74.8 us (9%)
  starting transfers between devices  28.9 us (4%)
  between operations  14.9 us (2%)
    unnamed x6, waiting for transfers between devices  603 us
    unnamed x30, local copies, waits for them, and re-layouts  31.6 us
    all_to_all x3, local copies, waits for them, and re-layouts, per_device(): lax.all_to_all(bordered, 'lon', split_axis=2, concat_axis=1, tiled=True)  17.5 us
  transfers between devices with their start and end apart: 7, of which 4 were waited for; matrix products, arithmetic and copies ran while one was open for 15% of the time, Pallas kernels for 0%

commit v1 on v0

v1 whole, which is shorter than its diff:
```python
import functools
import math

import jax
import jax.numpy as jnp
import ml_dtypes
import numpy as np
from jax import lax
from jax.experimental import pallas as pl
from jax.experimental.pallas import tpu as pltpu
from jax.sharding import Mesh
from jax.sharding import PartitionSpec as P

AXES = ("yl", "co", "x", "z", "yh")
LAT = ("yl", "co")
LON = ("x", "z", "yh")
F32 = jnp.float32
BF16 = jnp.bfloat16
SHARDS = 64
COLS = 12
ROWS = 16
OWN = 10
CIRCLE = 768
HALF = 384
TAPS = 7
BASIS = 3
MIB = 1 << 20


def split(value):
    top = value.astype(BF16)
    return top, (value - top.astype(F32)).astype(BF16)


def dot3(left, right, dims):
    (a, b), (c, d) = left, right
    numbers = (dims, ((), ()))
    one = functools.partial(lax.dot_general, dimension_numbers=numbers, preferred_element_type=F32)
    return one(a, c) + (one(a, d) + one(b, c))


def whole(n):
    return [pl.BlockSpec(memory_space=pltpu.VMEM)] * n


def params(mib):
    return pltpu.CompilerParams(vmem_limit_bytes=mib * MIB)


def cost(flops, moved):
    return pl.CostEstimate(flops=flops, bytes_accessed=moved, transcendentals=0)


def table(order):
    angle = 2.0 * np.pi / CIRCLE * (order[:, None] * np.arange(HALF)[None, :] % CIRCLE)
    nyquist = np.where(order % 2 == 0, 1.0, -1.0)
    real, imag = np.cos(angle), -np.sin(angle)
    imag[:, 0] = nyquist
    return np.concatenate([real, imag], axis=1)


def parts(matrix):
    exact = matrix.astype(np.float32)
    top = exact.astype(ml_dtypes.bfloat16)
    return top, (exact - top.astype(np.float32)).astype(ml_dtypes.bfloat16)


def forward_table(order):
    return parts(table(order))


def backward_table(order):
    weight = np.full((2, HALF), 2.0 / CIRCLE)
    weight[:, 0] = 1.0 / CIRCLE
    return parts(table(order) * weight.reshape(1, -1))


def shard_order():
    return (np.arange(COLS)[:, None] + COLS * np.arange(SHARDS)[None, :]).reshape(-1)


def pack(unit, out_ref):
    def piece(l, r):
        return unit[ROWS * l : ROWS * (l + 1), SHARDS * r : SHARDS * (r + 1)]

    for l in range(COLS):
        out_ref[:, l, :] = jnp.concatenate([piece(l, r) for r in range(8)], axis=0).T
    for q in range(3):
        chunk = [piece(3 * g + q, r) for g in range(4) for r in (8, 9)]
        out_ref[:, 12 + q, :] = jnp.concatenate(chunk, axis=0).T
    out_ref[:, 15, :] = jnp.zeros((SHARDS, 128), F32)


def mlp_kernel(act_ref, cot_ref, in_ref, out_ref, block_ref, hidden_ref, grad_ref, unit_ref):
    step = pl.program_id(0)
    act, cot = split(act_ref[...]), split(cot_ref[...])
    w_in, w_out = split(in_ref[...]), split(out_ref[...])
    preact = dot3(act, w_in, ((1,), (1,)))
    cdf = 0.5 * (1.0 + lax.erf(preact * (1.0 / math.sqrt(2.0))))
    density = jnp.exp(-0.5 * preact * preact) * (1.0 / math.sqrt(2.0 * math.pi))
    hidden_ref[...] = preact * cdf
    grad = dot3(cot, w_out, ((1,), (1,))) * (cdf + preact * density)
    grad_ref[...] = grad
    term = dot3(split(grad), w_in, ((1,), (0,)))

    @pl.when(step == 0)
    def _():
        unit_ref[...] = cot_ref[...] + term

    @pl.when(step > 0)
    def _():
        unit_ref[...] += term

    @pl.when(step == pl.num_programs(0) - 1)
    def _():
        pack(unit_ref[...], block_ref)


def mlp(act, cot, weight_in, weight_out):
    points, width = act.shape
    units = weight_in.shape[0]
    tile = 256
    full = lambda shape: pl.BlockSpec(shape, lambda i: (0,) * len(shape))
    return pl.pallas_call(
        mlp_kernel,
        grid=(units // tile,),
        in_specs=[
            full((points, width)),
            full((points, width)),
            pl.BlockSpec((tile, width), lambda i: (i, 0)),
            pl.BlockSpec((tile, width), lambda i: (i, 0)),
        ],
        out_specs=[
            full((SHARDS, 16, 128)),
            pl.BlockSpec((points, tile), lambda i: (0, i)),
            pl.BlockSpec((points, tile), lambda i: (0, i)),
        ],
        out_shape=[
            jax.ShapeDtypeStruct((SHARDS, 16, 128), F32),
            jax.ShapeDtypeStruct((points, units), F32),
            jax.ShapeDtypeStruct((points, units), F32),
        ],
        scratch_shapes=[pltpu.VMEM((points, width), F32)],
        compiler_params=params(32),
        cost_estimate=cost(18 * points * width * units, 10_000_000),
        name="mlp",
    )(act, cot, weight_in, weight_out)


def pick(field, core):
    even = jnp.concatenate([field[:, 0:160], field[:, 320:480]], axis=1)
    odd = jnp.concatenate([field[:, 160:320], field[:, 480:640]], axis=1)
    return split(jnp.where(core == 0, even, odd))


def weight_kernel(core_ref, grad_ref, hidden_ref, act_ref, cot_ref, *rest):
    out_ref = rest[-1]
    core = core_ref[0]
    act, cot = pick(act_ref[...], core), pick(cot_ref[...], core)
    contract = ((0,), (0,))
    first = dot3(split(grad_ref[...]), act, contract)
    second = dot3(split(hidden_ref[...]), cot, contract)
    total = jnp.concatenate([first, second], axis=1)
    if len(rest) == 2:
        total += rest[0][...]
    out_ref[...] = total


def weight_part(core, grad, hidden, act, cot, arrived):
    points, units = grad.shape
    width = act.shape[1]
    tile = 256
    tall = pl.BlockSpec((points, tile), lambda i: (0, i))
    flat = pl.BlockSpec((points, width), lambda i: (0, 0))
    wide = pl.BlockSpec((tile, width), lambda i: (i, 0))
    return pl.pallas_call(
        weight_kernel,
        grid=(units // tile,),
        in_specs=[pl.BlockSpec(memory_space=pltpu.SMEM), tall, tall, flat, flat]
        + [wide] * len(arrived),
        out_specs=wide,
        out_shape=jax.ShapeDtypeStruct((units, width), F32),
        compiler_params=params(24),
        cost_estimate=cost(6 * points * width * units, 10_000_000),
        name="weights",
    )(core, grad, hidden, act, cot, *arrived)


def last_kernel(place_ref, total_ref, first_ref, second_ref):
    total = total_ref[...]
    upper, right = place_ref[0], place_ref[1]
    kept = jnp.where(right == 1, total[20:40], total[0:20])
    first_ref[...] = jnp.where(upper == 1, kept[:, 160:320], kept[:, 0:160])
    second_ref[...] = jnp.where(upper == 1, kept[:, 480:640], kept[:, 320:480])


def weight_gradients(grad, hidden, act, cot):
    core = lax.axis_index("co")
    other = weight_part((1 - core).reshape(1), grad, hidden, act, cot, ())
    arrived = lax.ppermute(other, "co", [(0, 1), (1, 0)])
    total = weight_part(core.reshape(1), grad, hidden, act, cot, (arrived,))
    total = lax.psum_scatter(total, ("x", "z"), scatter_dimension=0, tiled=True)
    total = lax.psum(total, ("yl", "yh"))
    place = jnp.stack([lax.axis_index("yl"), lax.axis_index("yh")])
    return pl.pallas_call(
        last_kernel,
        in_specs=[pl.BlockSpec(memory_space=pltpu.SMEM)] + whole(1),
        out_specs=whole(2),
        out_shape=[jax.ShapeDtypeStruct((20, 160), F32)] * 2,
        name="last",
    )(place, total)


def spectrum_kernel(block_ref, top_ref, low_ref, out_ref, first_ref, final_ref, flat_ref):
    for p in range(COLS // 2):
        pair = jnp.concatenate([block_ref[:, 2 * p, :], block_ref[:, 2 * p + 1, :]], axis=0)
        flat_ref[0:128, 128 * p : 128 * (p + 1)] = pair.T
    rest = [block_ref[:, 12 + q, :].T for q in range(3)]
    pieces = [rest[q][32 * g : 32 * (g + 1), :] for g in range(4) for q in range(3)]
    flat_ref[128:160, :] = jnp.concatenate(pieces, axis=1)
    result = dot3(split(flat_ref[...]), (top_ref[...], low_ref[...]), ((1,), (0,)))
    out_ref[...] = result
    for r in range(OWN):
        first_ref[3 * r : 3 * r + 3, :] = result[ROWS * r : ROWS * r + 3, :]
        final_ref[3 * r : 3 * r + 3, :] = result[ROWS * r + 13 : ROWS * r + 16, :]


def spectrum(block):
    top, low = forward_table(shard_order())
    rows = OWN * ROWS
    return pl.pallas_call(
        spectrum_kernel,
        in_specs=whole(3),
        out_specs=whole(3),
        out_shape=[
            jax.ShapeDtypeStruct((rows, CIRCLE), F32),
            jax.ShapeDtypeStruct((3 * OWN, CIRCLE), F32),
            jax.ShapeDtypeStruct((3 * OWN, CIRCLE), F32),
        ],
        scratch_shapes=[pltpu.VMEM((rows, CIRCLE), F32)],
        compiler_params=params(24),
        cost_estimate=cost(6 * rows * CIRCLE * CIRCLE, 4_000_000),
        name="spectrum",
    )(block, jnp.asarray(top), jnp.asarray(low))


def kernel_spectrum_kernel(kernel_ref, top_ref, low_ref, out_ref):
    out_ref[...] = dot3(split(kernel_ref[...]), (top_ref[...], low_ref[...]), ((1,), (0,)))


def kernel_spectrum(kernels):
    top, low = forward_table(np.arange(CIRCLE))
    rows = BASIS * TAPS * ROWS
    flat = kernels.transpose(0, 2, 1, 3).reshape(rows, CIRCLE)
    return pl.pallas_call(
        kernel_spectrum_kernel,
        in_specs=whole(3),
        out_specs=whole(1)[0],
        out_shape=jax.ShapeDtypeStruct((rows, CIRCLE), F32),
        compiler_params=params(24),
        cost_estimate=cost(6 * rows * CIRCLE * CIRCLE, 5_000_000),
        name="kernel_spectrum",
    )(flat, jnp.asarray(top), jnp.asarray(low))


def filter_kernel(
    mixing_ref, data_ref, before_ref, after_ref, kernel_ref, top_ref, low_ref, out_ref, rows_ref, sum_ref
):
    for r in range(OWN):
        rows_ref[r, 0:3, :] = before_ref[3 * r : 3 * r + 3, :]
        rows_ref[r, 3 : 3 + ROWS, :] = data_ref[ROWS * r : ROWS * (r + 1), :]
        rows_ref[r, 3 + ROWS : 6 + ROWS, :] = after_ref[3 * r : 3 * r + 3, :]
    lane = lax.broadcasted_iota(jnp.int32, (ROWS, HALF), 1)
    ends = lane == 0

    def channel(r, carry):
        real = jnp.zeros((ROWS, HALF), F32)
        imag = jnp.zeros((ROWS, HALF), F32)
        for k in range(TAPS):
            mixed_real = jnp.zeros((ROWS, HALF), F32)
            mixed_imag = jnp.zeros((ROWS, HALF), F32)
            for b in range(BASIS):
                weight = mixing_ref[r, b]
                at = ROWS * (TAPS * b + k)
                mixed_real += weight * kernel_ref[at : at + ROWS, 0:HALF]
                mixed_imag += weight * kernel_ref[at : at + ROWS, HALF:CIRCLE]
            own = jnp.where(ends, mixed_imag, mixed_real)
            cross = jnp.where(ends, 0.0, mixed_imag)
            data_real = rows_ref[r, 6 - k : 6 - k + ROWS, 0:HALF]
            data_imag = rows_ref[r, 6 - k : 6 - k + ROWS, HALF:CIRCLE]
            real += mixed_real * data_real + cross * data_imag
            imag += own * data_imag - cross * data_real
        sum_ref[r, :, 0:HALF] = real
        sum_ref[r, :, HALF:CIRCLE] = imag
        return carry

    lax.fori_loop(0, OWN, channel, 0)
    total = split(sum_ref[...].reshape(OWN * ROWS, CIRCLE))
    field = dot3((top_ref[...], low_ref[...]), total, ((1,), (1,)))
    for l in range(COLS):
        out_ref[:, l, :] = field[SHARDS * l : SHARDS * (l + 1), 0:128]
    for q in range(3):
        pieces = [
            field[SHARDS * (3 * g + q) : SHARDS * (3 * g + q + 1), 128:160] for g in range(4)
        ]
        out_ref[:, 12 + q, :] = jnp.concatenate(pieces, axis=1)
    out_ref[:, 15, :] = jnp.zeros((SHARDS, 128), F32)


def filtered(mixing, data, before, after, kernel):
    top, low = backward_table(shard_order())
    return pl.pallas_call(
        filter_kernel,
        in_specs=[pl.BlockSpec(memory_space=pltpu.SMEM)] + whole(6),
        out_specs=whole(1)[0],
        out_shape=jax.ShapeDtypeStruct((SHARDS, 16, 128), F32),
        scratch_shapes=[
            pltpu.VMEM((OWN, 24, CIRCLE), F32),
            pltpu.VMEM((OWN, ROWS, CIRCLE), F32),
        ],
        compiler_params=params(32),
        cost_estimate=cost(6 * OWN * ROWS * CIRCLE * CIRCLE, 5_000_000),
        name="filter",
    )(mixing, data, before, after, kernel, jnp.asarray(top), jnp.asarray(low))


def unpack_kernel(block_ref, out_ref):
    def put(l, r, pair):
        out_ref[ROWS * l : ROWS * (l + 1), SHARDS * r : SHARDS * (r + 2)] = jnp.concatenate(
            pair, axis=1
        )

    for l in range(COLS):
        turned = block_ref[:, l, :].T
        for r in range(0, 8, 2):
            put(l, r, [turned[ROWS * r : ROWS * (r + 1)], turned[ROWS * (r + 1) : ROWS * (r + 2)]])
    for q in range(3):
        turned = block_ref[:, 12 + q, :].T
        for g in range(4):
            at = 32 * g
            put(3 * g + q, 8, [turned[at : at + ROWS], turned[at + ROWS : at + 2 * ROWS]])


def unpack(block):
    return pl.pallas_call(
        unpack_kernel,
        in_specs=whole(1),
        out_specs=whole(1)[0],
        out_shape=jax.ShapeDtypeStruct((ROWS * COLS, SHARDS * OWN), F32),
        name="unpack",
    )(block)


def across(block):
    return lax.all_to_all(block, LON, split_axis=0, concat_axis=0, tiled=True)


def per_device(activation, cotangent, weight_in, weight_out, kernels, mixing):
    points = ROWS * COLS
    width = activation.shape[2]
    act = activation.transpose(1, 0, 2).reshape(points, width)
    cot = cotangent.transpose(1, 0, 2).reshape(points, width)
    every = lax.all_gather(mixing, LON, axis=0, tiled=True).reshape(OWN, SHARDS, BASIS)
    shard = lax.axis_index(LON)
    own_mixing = lax.dynamic_slice_in_dim(every, shard, 1, 1).reshape(OWN, BASIS)
    block, hidden, grad = mlp(act, cot, weight_in, weight_out)
    spread = across(block)
    grad_in, grad_out = weight_gradients(grad, hidden, act, cot)
    kernel = kernel_spectrum(kernels)
    data, first, final = spectrum(spread)
    forward = [(i, i + 1) for i in range(3)]
    backward = [(target, source) for source, target in forward]
    before = lax.ppermute(final, LAT, forward)
    after = lax.ppermute(first, LAT, backward)
    result = across(filtered(own_mixing, data, before, after, kernel))
    field = unpack(result).reshape(COLS, ROWS, width).transpose(1, 0, 2)
    return (field, grad_in, grad_out)


def solution(mesh):
    fine = Mesh(mesh.devices.reshape(2, 2, 4, 8, 2), AXES)
    placed = (
        P(LAT, LON, None),
        P(LAT, LON, None),
        P(),
        P(),
        P(None, LAT, None, None),
        P(LON, None),
    )
    return jax.shard_map(
        per_device,
        mesh=fine,
        in_specs=placed,
        out_specs=(P(LAT, LON, None), P(LON, LAT), P(LON, LAT)),
        check_vma=False,
    )
```

time: 823 us -> 315 us (0.38); the launches traced: 813 us -> 314 us
  waiting for transfers between devices: 607 us -> 50 us
  blocking collectives: 0 us -> 156 us
  local copies, waits for them, and re-layouts: 83.4 us -> 8.36 us
  matrix products: 74.8 us -> 0 us
  Pallas kernels: 0 us -> 28.8 us
  starting transfers between devices: 28.9 us -> 56.1 us
    unnamed x6 -> x3, waiting for transfers between devices: 603 us -> 0.7 us
    all_gather x0 -> x1, blocking collectives: none -> 156 us  [per_device(): lax.all_gather(mixing, LON, axis=0, tiled=True).reshape(OWN, SHARDS, BASIS)]
    dot_general x13 -> x0, matrix products: 74.8 us -> none  [the longest x1 8.59 us: per_device(): jnp.einsum('cjf,fl->jlc', total_imag, back_sine, precision=high)]
    all_to_all x5 -> x0, local copies, waits for them, and re-layouts: 32.9 us -> none  [the longest x3 17.5 us: per_device(): lax.all_to_all(bordered, 'lon', split_axis=2, concat_axis=1, tiled=True)]
    ppermute x2 -> x3, starting transfers between devices: 6.51 us -> 36.9 us  [the longest x1 31.7 us: per_device(): before = lax.ppermute(final, LAT, forward)]
    pallas_call x0 -> x8, Pallas kernels: none -> 28.8 us  [the longest x2 10.2 us: weight_part(): pl.pallas_call(weight_kernel, grid=(units // tile,), in_specs=[pl.BlockSp...]
    psum x0 -> x1, waiting for transfers between devices: none -> 26.2 us  [weight_gradients(): total = lax.psum(total, ('yl', 'yh'))]
    unnamed x30, local copies, waits for them, and re-layouts: 31.6 us -> 7.97 us
  transfers between devices with their start and end apart: 7 -> 7, of which waited for: 4 -> 4; matrix products, arithmetic and copies ran while one was open for 15% -> 0% of each run, Pallas kernels for 0% -> 3%
where the time goes in v1:
time: 315 us; the launch traced here: 314 us
  blocking collectives  156 us (50%)
  starting transfers between devices  56.1 us (18%)
  waiting for transfers between devices  50 us (16%)
  Pallas kernels  28.8 us (9%)
  between operations  14.2 us (5%)
  local copies, waits for them, and re-layouts  8.36 us (3%)
    all_gather x1, blocking collectives, per_device(): lax.all_gather(mixing, LON, axis=0, tiled=True).reshape(OWN, SHARDS, BASIS)  156 us
    ppermute x1, starting transfers between devices, per_device(): before = lax.ppermute(final, LAT, forward)  31.7 us
    psum x1, waiting for transfers between devices, weight_gradients(): total = lax.psum(total, ('yl', 'yh'))  26.2 us
    all_to_all x2, starting transfers between devices, across(): return lax.all_to_all(block, LON, split_axis=0, concat_axis=0, tiled=True)  19.1 us
    all_to_all x2, waiting for transfers between devices, across(): return lax.all_to_all(block, LON, split_axis=0, concat_axis=0, tiled=True)  16.2 us
    pallas_call x2, Pallas kernels, weight_part(): pl.pallas_call(weight_kernel, grid=(units // tile,), in_specs=[pl.BlockSp...  10.2 us
    unnamed x30, local copies, waits for them, and re-layouts  7.97 us
    pallas_call x1, Pallas kernels, mlp(): pl.pallas_call(mlp_kernel, grid=(units // tile,), in_specs=[full((points,...  7.87 us
  transfers between devices with their start and end apart: 7, of which 4 were waited for; matrix products, arithmetic and copies ran while one was open for 0% of the time, Pallas kernels for 3%

profile of v1, /device:TPU:1, one launch (start us, length us, event | category | flops | bytes accessed | tf_op | source)
XLA Modules:
  0.0 313.8 jit_solution(6603858660418120801)
XLA Ops:
  7.2 0.0 reduce-scatter.4.cloned.1.call-start
  7.2 0.0 copy-start
  7.2 1.0 copy-done
  8.2 0.0 copy-start.2
  8.3 1.0 copy-done.2
  9.3 0.0 copy-start.11
  9.3 1.9 copy-done.11
  11.2 0.0 copy-start.12
  11.2 1.9 copy-done.12
  13.1 7.9 %mlp.1 = (f32[64,16,128]{2,1,0:T(8,128)}, f32[192,1280]{1,0:T(8,128)S(1)}, f32[192,1280]{1,0:T(8,128)S(1)}) custom-call(f32[192,640]{1,0:T(8,128)S(1)} %bitcast.21, f32[192,640]{1,0:T(8,128)S(1)} %bitcast.24, f32[1280,640]{1,0:T(8,128)S(1)} %copy-done.11, f32[1280,640]{1,0:T(8,128)S(1)} %copy-done.12), custom_call_target="tpu_custom_call" | custom-call | flops 2831155200 | bytes 10000000 | tf_op jit(solution)/shard_map/mlp/pallas_call | solution.py:124
  21.0 0.0 copy-start.1
  21.0 0.0 copy-start.3
  21.0 4.7 %weights.2 = f32[1280,640]{1,0:T(8,128)S(1)} custom-call(s32[1]{0:T(128)} %bitcast.15.core_ref, f32[192,1280]{1,0:T(8,128)S(1)} %get-tuple-element.15.grad_ref, f32[192,1280]{1,0:T(8,128)S(1)} %get-tuple-element.16.hidden_ref, f32[192,640]{1,0:T(8,128)S(1)} %bitcast.22, f32[192,640]{1,0:T(8,128)S(1)} %bitcast.25), custom_call_target="tpu_custom_call" | custom-call | flops 943718400 | bytes 10000000 | tf_op jit(solution)/shard_map/weights/pallas_call | solution.py:176
  25.7 3.3 %collective-permute-start.2 = (f32[1280,640]{1,0:T(8,128)S(1)}, f32[1280,640]{1,0:T(8,128)S(1)}, u32[]{:S(2)}, u32[]{:S(2)}) collective-permute-start(f32[1280,640]{1,0:T(8,128)S(1)} %weights.2), channel_id=1, source_target_pairs={{0,64},{64,0},{1,65},{65,1},{2,66},{66,2},{3,67},{67,3},{4,68},{68... | collective-permute-start | bytes 9830408 | tf_op jit(solution)/shard_map/ppermute | solution.py:200
  29.0 5.5 %collective-permute-done.2.rest_0_ = f32[1280,640]{1,0:T(8,128)S(1)} collective-permute-done((f32[1280,640]{1,0:T(8,128)S(1)}, f32[1280,640]{1,0:T(8,128)S(1)}, u32[]{:S(2)}, u32[]{:S(2)}) %collective-permute-start.2) | collective-permute-done | bytes 3276832 | tf_op jit(solution)/shard_map/ppermute | solution.py:200
  34.5 0.0 copy-done.1
  34.5 0.0 copy-done.3
  34.5 5.5 %weights.3 = f32[1280,640]{1,0:T(8,128)} custom-call(s32[1]{0:T(128)} %bitcast.12.core_ref, f32[192,1280]{1,0:T(8,128)S(1)} %get-tuple-element.15.grad_ref, f32[192,1280]{1,0:T(8,128)S(1)} %get-tuple-element.16.hidden_ref, f32[192,640]{1,0:T(8,128)S(1)} %bitcast.23, f32[192,640]{1,0:T(8,128)S(1)} %bitcast.26, f32[1280,640]{1,0:T(8,128)S(1)} %collective-permute-done.2.rest_0_), custom_call_target="tpu_custom_call" | custom-call | flops 943718400 | bytes 10000000 | tf_op jit(solution)/shard_map/weights/pallas_call | solution.py:176
  40.1 0.0 copy-start.14
  40.1 0.0 copy-start.7
  40.1 0.0 reduce-scatter.4.cloned.1.call-update
  40.1 0.0 copy-start.6
  40.1 12.7 %all-to-all-start = ((f32[64,16,128]{2,1,0:T(8,128)}), f32[64,16,128]{2,1,0:T(8,128)S(1)}, u32[]{:S(2)}, u32[]{:S(2)}) async-start(f32[64,16,128]{2,1,0:T(8,128)} %get-tuple-element.11), calls=%async_computation | async-start | bytes 1048576 | tf_op jit(solution)/shard_map/all_to_all | solution.py:355
  52.8 0.0 copy-done.14
  52.8 155.8 %all-gather = f32[64,10,3]{1,2,0:T(4,128)S(1)} all-gather(f32[1,10,3]{1,2,0:T(4,128)S(1)} %bitcast.30), channel_id=1, replica_groups=mesh['yl'=2,'co'=2,'x'=4,'z'=8,'yh'=2] {'x','z','yh'}, dimensions={0}, use_global_device_ids=true | all-gather | bytes 7800 | tf_op jit(solution)/shard_map/all_gather | solution.py:363
  208.6 0.1 reshape.30
  208.8 0.1 constant_dynamic-slice_fusion
  208.8 0.2 copy.22
  209.0 0.0 all-to-all-done.block_ref
  209.0 0.0 copy-done.7
  209.0 0.0 copy-done.6
  209.0 0.0 copy-start.8
  209.1 0.0 copy-start.9
  209.1 1.0 spectrum.1
  210.1 31.7 %collective-permute-start = (f32[30,768]{1,0:T(8,128)S(1)}, f32[30,768]{1,0:T(8,128)S(1)}, u32[]{:S(2)}, u32[]{:S(2)}) collective-permute-start(f32[30,768]{1,0:T(8,128)S(1)} %get-tuple-element.13), channel_id=1, source_target_pairs={{0,64},{64,128},{128,192},{1,65},{65,129},{129,193},{2,66},{66,130... | collective-permute-start | bytes 276488 | tf_op jit(solution)/shard_map/ppermute | solution.py:373
  241.8 1.9 collective-permute-start.1
  243.7 0.0 copy-done.8
  243.7 0.0 copy-done.9
  243.7 0.0 copy-start.10
  243.7 1.2 copy-done.10
  244.9 0.0 copy-start.4
  244.9 0.0 copy-start.5
  244.9 1.4 kernel_spectrum.1.kernel_ref
  246.3 0.0 collective-permute-done.before_ref
  246.3 1.4 collective-permute-done.1.after_ref
  247.7 0.0 copy-done.4
  247.7 0.0 copy-done.5
  247.7 4.3 %filter.1 = f32[64,16,128]{2,1,0:T(8,128)} custom-call(f32[10,3]{1,0:T(8,128)S(1)} %bitcast.28, f32[160,768]{1,0:T(8,128)S(1)} %get-tuple-element.12.data_ref, f32[30,768]{1,0:T(8,128)S(1)} %collective-permute-done.before_ref, f32[30,768]{1,0:T(8,128)S(1)} %collective-permute-done.1.after_ref, f32[336,768]{1,0:T(8,128)S(1)} %kernel_spectrum.1.kernel_ref, ...), custom_call_target="tpu_custom_call" | custom-call | flops 566231040 | bytes 5000000 | tf_op jit(solution)/shard_map/filter/pallas_call | solution.py:312
  252.0 6.4 %all-to-all-start.1 = ((f32[64,16,128]{2,1,0:T(8,128)}), f32[64,16,128]{2,1,0:T(8,128)S(1)}, u32[]{:S(2)}, u32[]{:S(2)}) async-start(f32[64,16,128]{2,1,0:T(8,128)} %filter.1), calls=%async_computation.1 | async-start | bytes 1048576 | tf_op jit(solution)/shard_map/all_to_all | solution.py:355
  258.4 0.0 all-reduce.3.cloned.1.call-start
  258.5 0.0 reduce-scatter.4.cloned.1.call-done
  258.5 0.7 all-reduce.3.cloned.1.call-update
  259.2 0.6 pad_add_fusion.place_ref
  259.7 16.2 %all-to-all-done.1.block_ref = f32[64,16,128]{2,1,0:T(8,128)S(1)} async-done(((f32[64,16,128]{2,1,0:T(8,128)}), f32[64,16,128]{2,1,0:T(8,128)S(1)}, u32[]{:S(2)}, u32[]{:S(2)}) %all-to-all-start.1) | async-done | bytes 524320 | tf_op jit(solution)/shard_map/all_to_all | solution.py:355
  276.0 0.0 copy-start.13
  276.0 0.8 copy-done.13
  276.8 2.3 unpack.1
  279.1 26.2 %all-reduce.3.cloned.1.call-done.total_ref = f32[40,640]{1,0:T(8,128)} async-done(((f32[40,640]{1,0:T(8,128)}), f32[40,640]{1,0:T(8,128)}) %all-reduce.3.cloned.1.call-update) | async-done | bytes 102416 | tf_op jit(solution)/shard_map/psum | solution.py:203
  305.3 1.7 last.1
  (1 shorter events, 0.0 us)
Async XLA Ops:
  7.2 251.3 %reduce-scatter.4.cloned.1.call-start = ((), (), s32[]{:S(2)}) async-start(), calls=%async_computation.4 | async-start | bytes 3379200
  7.2 1.0 copy-start
  8.2 1.0 copy-start.2
  9.3 1.9 copy-start.11
  11.2 1.9 copy-start.12
  21.0 13.5 %copy-start.1 = (f32[16,12,640]{2,0,1:T(8,128)S(1)}, f32[16,12,640]{2,0,1:T(8,128)}, u32[]{:S(2)}) copy-start(f32[16,12,640]{2,0,1:T(8,128)} %param.12) | copy-start | bytes 1474564
  21.0 13.5 %copy-start.3 = (f32[16,12,640]{2,0,1:T(8,128)S(1)}, f32[16,12,640]{2,0,1:T(8,128)}, u32[]{:S(2)}) copy-start(f32[16,12,640]{2,0,1:T(8,128)} %param.13) | copy-start | bytes 1474564
  25.7 8.8 %collective-permute-start.2 = (f32[1280,640]{1,0:T(8,128)S(1)}, f32[1280,640]{1,0:T(8,128)S(1)}, u32[]{:S(2)}, u32[]{:S(2)}) collective-permute-start(f32[1280,640]{1,0:T(8,128)S(1)} %weights.2), channel_id=1, source_target_pairs={{0,64},{64,0},{1,65},{65,1},{2,66},{66,2},{3,67},{67,3},{4,68},{68... | collective-permute-start | bytes 9830408 | tf_op jit(solution)/shard_map/ppermute | solution.py:200
  40.1 12.8 %copy-start.14 = (f32[10,3]{0,1:T(4,128)S(1)}, f32[10,3]{0,1:T(4,128)}, u32[]{:S(2)}) copy-start(f32[10,3]{0,1:T(4,128)} %param.17) | copy-start | bytes 364
  40.1 169.0 %copy-start.7 = (bf16[768,768]{1,0:T(8,128)(2,1)S(1)}, bf16[768,768]{1,0:T(8,128)(2,1)}, u32[]{:S(2)}) copy-start(bf16[768,768]{1,0:T(8,128)(2,1)} %constant.45.clone.top_ref) | copy-start | bytes 3538948
  40.1 168.9 %copy-start.6 = (bf16[768,768]{1,0:T(8,128)(2,1)S(1)}, bf16[768,768]{1,0:T(8,128)(2,1)}, u32[]{:S(2)}) copy-start(bf16[768,768]{1,0:T(8,128)(2,1)} %constant.46.clone.low_ref) | copy-start | bytes 3538948
  40.1 168.9 %all-to-all-start = ((f32[64,16,128]{2,1,0:T(8,128)}), f32[64,16,128]{2,1,0:T(8,128)S(1)}, u32[]{:S(2)}, u32[]{:S(2)}) async-start(f32[64,16,128]{2,1,0:T(8,128)} %get-tuple-element.11), calls=%async_computation | async-start | bytes 1048576 | tf_op jit(solution)/shard_map/all_to_all | solution.py:355
  209.0 34.6 %copy-start.8 = (bf16[768,768]{1,0:T(8,128)(2,1)S(1)}, bf16[768,768]{1,0:T(8,128)(2,1)}, u32[]{:S(2)}) copy-start(bf16[768,768]{1,0:T(8,128)(2,1)} %constant.44.clone.low_ref) | copy-start | bytes 3538948
  209.1 34.6 %copy-start.9 = (bf16[768,768]{1,0:T(8,128)(2,1)S(1)}, bf16[768,768]{1,0:T(8,128)(2,1)}, u32[]{:S(2)}) copy-start(bf16[768,768]{1,0:T(8,128)(2,1)} %constant.43.clone.top_ref) | copy-start | bytes 3538948
  210.1 36.2 %collective-permute-start = (f32[30,768]{1,0:T(8,128)S(1)}, f32[30,768]{1,0:T(8,128)S(1)}, u32[]{:S(2)}, u32[]{:S(2)}) collective-permute-start(f32[30,768]{1,0:T(8,128)S(1)} %get-tuple-element.13), channel_id=1, source_target_pairs={{0,64},{64,128},{128,192},{1,65},{65,129},{129,193},{2,66},{66,130... | collective-permute-start | bytes 276488 | tf_op jit(solution)/shard_map/ppermute | solution.py:373
  241.8 5.9 %collective-permute-start.1 = (f32[30,768]{1,0:T(8,128)S(1)}, f32[30,768]{1,0:T(8,128)S(1)}, u32[]{:S(2)}, u32[]{:S(2)}) collective-permute-start(f32[30,768]{1,0:T(8,128)S(1)} %get-tuple-element.14), channel_id=1, source_target_pairs={{64,0},{128,64},{192,128},{65,1},{129,65},{193,129},{66,2},{130,66... | collective-permute-start | bytes 276488 | tf_op jit(solution)/shard_map/ppermute | solution.py:374
  243.7 1.2 copy-start.10
  244.9 2.8 copy-start.4
  244.9 2.8 copy-start.5
  252.0 24.0 %all-to-all-start.1 = ((f32[64,16,128]{2,1,0:T(8,128)}), f32[64,16,128]{2,1,0:T(8,128)S(1)}, u32[]{:S(2)}, u32[]{:S(2)}) async-start(f32[64,16,128]{2,1,0:T(8,128)} %filter.1), calls=%async_computation.1 | async-start | bytes 1048576 | tf_op jit(solution)/shard_map/all_to_all | solution.py:355
  258.4 46.9 %all-reduce.3.cloned.1.call-start = ((), (), s32[]{:S(2)}) async-start(), calls=%async_computation.3 | async-start | bytes 204800 | tf_op jit(solution)/shard_map/psum | solution.py:203
  276.0 0.8 copy-start.13
Sparse Core Ops, SparseCore 0:
  40.2 202.7 reduce-scatter.3
  261.7 43.5 all-reduce.2

commit v2 on v1

--- a/solution.py
+++ b/solution.py
@@ -79,7 +79,7 @@
     return (np.arange(COLS)[:, None] + COLS * np.arange(SHARDS)[None, :]).reshape(-1)
 
 
-def pack(unit, out_ref):
+def pack(unit, mixing_ref, shard, out_ref):
     def piece(l, r):
         return unit[ROWS * l : ROWS * (l + 1), SHARDS * r : SHARDS * (r + 1)]
 
@@ -88,10 +88,21 @@
     for q in range(3):
         chunk = [piece(3 * g + q, r) for g in range(4) for r in (8, 9)]
         out_ref[:, 12 + q, :] = jnp.concatenate(chunk, axis=0).T
-    out_ref[:, 15, :] = jnp.zeros((SHARDS, 128), F32)
-
-
-def mlp_kernel(act_ref, cot_ref, in_ref, out_ref, block_ref, hidden_ref, grad_ref, unit_ref):
+    target = lax.broadcasted_iota(jnp.int32, (SHARDS, 128), 0)
+    lane = lax.broadcasted_iota(jnp.int32, (SHARDS, 128), 1)
+    weights = jnp.zeros((SHARDS, 128), F32)
+    for i in range(OWN):
+        channel = OWN * shard + i
+        here = target == lax.rem(channel, SHARDS)
+        first = BASIS * lax.div(channel, SHARDS)
+        for b in range(BASIS):
+            weights = jnp.where(here & (lane == first + b), mixing_ref[i, b], weights)
+    out_ref[:, 15, :] = weights
+
+
+def mlp_kernel(
+    shard_ref, mixing_ref, act_ref, cot_ref, in_ref, out_ref, block_ref, hidden_ref, grad_ref, unit_ref
+):
     step = pl.program_id(0)
     act, cot = split(act_ref[...]), split(cot_ref[...])
     w_in, w_out = split(in_ref[...]), split(out_ref[...])
@@ -113,10 +124,10 @@
 
     @pl.when(step == pl.num_programs(0) - 1)
     def _():
-        pack(unit_ref[...], block_ref)
-
-
-def mlp(act, cot, weight_in, weight_out):
+        pack(unit_ref[...], mixing_ref, shard_ref[0], block_ref)
+
+
+def mlp(shard, mixing, act, cot, weight_in, weight_out):
     points, width = act.shape
     units = weight_in.shape[0]
     tile = 256
@@ -125,6 +136,8 @@
         mlp_kernel,
         grid=(units // tile,),
         in_specs=[
+            pl.BlockSpec(memory_space=pltpu.SMEM),
+            pl.BlockSpec(memory_space=pltpu.SMEM),
             full((points, width)),
             full((points, width)),
             pl.BlockSpec((tile, width), lambda i: (i, 0)),
@@ -141,10 +154,10 @@
             jax.ShapeDtypeStruct((points, units), F32),
         ],
         scratch_shapes=[pltpu.VMEM((points, width), F32)],
-        compiler_params=params(32),
+        compiler_params=params(60),
         cost_estimate=cost(18 * points * width * units, 10_000_000),
         name="mlp",
-    )(act, cot, weight_in, weight_out)
+    )(shard, mixing, act, cot, weight_in, weight_out)
 
 
 def pick(field, core):
@@ -186,32 +199,63 @@
     )(core, grad, hidden, act, cot, *arrived)
 
 
-def last_kernel(place_ref, total_ref, first_ref, second_ref):
+def quarter(total, upper, right):
+    kept = jnp.where(right == 1, total[20:40], total[0:20])
+    first = jnp.where(upper == 1, kept[:, 160:320], kept[:, 0:160])
+    second = jnp.where(upper == 1, kept[:, 480:640], kept[:, 320:480])
+    return first, second
+
+
+def cut_kernel(place_ref, total_ref, *out_refs):
     total = total_ref[...]
-    upper, right = place_ref[0], place_ref[1]
-    kept = jnp.where(right == 1, total[20:40], total[0:20])
-    first_ref[...] = jnp.where(upper == 1, kept[:, 160:320], kept[:, 0:160])
-    second_ref[...] = jnp.where(upper == 1, kept[:, 480:640], kept[:, 320:480])
-
-
-def weight_gradients(grad, hidden, act, cot):
+    for m, out_ref in enumerate(out_refs):
+        upper, right = place_ref[0], place_ref[1]
+        upper = 1 - upper if m & 2 else upper
+        right = 1 - right if m & 1 else right
+        first, second = quarter(total, upper, right)
+        out_ref[0:20, :] = first
+        out_ref[24:44, :] = second
+
+
+def sum_kernel(*refs):
+    first_ref, second_ref = refs[4:]
+    first_ref[...] = (refs[0][0:20] + refs[1][0:20]) + (refs[2][0:20] + refs[3][0:20])
+    second_ref[...] = (refs[0][24:44] + refs[1][24:44]) + (refs[2][24:44] + refs[3][24:44])
+
+
+def weight_sums(grad, hidden, act, cot):
     core = lax.axis_index("co")
     other = weight_part((1 - core).reshape(1), grad, hidden, act, cot, ())
     arrived = lax.ppermute(other, "co", [(0, 1), (1, 0)])
     total = weight_part(core.reshape(1), grad, hidden, act, cot, (arrived,))
-    total = lax.psum_scatter(total, ("x", "z"), scatter_dimension=0, tiled=True)
-    total = lax.psum(total, ("yl", "yh"))
+    return lax.psum_scatter(total, "x", scatter_dimension=0, tiled=True)
+
+
+def finish(total):
+    total = lax.psum_scatter(total, "z", scatter_dimension=0, tiled=True)
     place = jnp.stack([lax.axis_index("yl"), lax.axis_index("yh")])
-    return pl.pallas_call(
-        last_kernel,
+    pieces = pl.pallas_call(
+        cut_kernel,
         in_specs=[pl.BlockSpec(memory_space=pltpu.SMEM)] + whole(1),
+        out_specs=whole(4),
+        out_shape=[jax.ShapeDtypeStruct((48, 160), F32)] * 4,
+        name="cut",
+    )(place, total)
+    moved = [pieces[0]] + [
+        lax.ppermute(pieces[m], ("yl", "yh"), [(i, i ^ m) for i in range(4)]) for m in (1, 2, 3)
+    ]
+    return pl.pallas_call(
+        sum_kernel,
+        in_specs=whole(4),
         out_specs=whole(2),
         out_shape=[jax.ShapeDtypeStruct((20, 160), F32)] * 2,
         name="last",
-    )(place, total)
-
-
-def spectrum_kernel(block_ref, top_ref, low_ref, out_ref, first_ref, final_ref, flat_ref):
+    )(*moved)
+
+
+def spectrum_kernel(
+    block_ref, top_ref, low_ref, out_ref, first_ref, final_ref, mixing_ref, flat_ref
+):
     for p in range(COLS // 2):
         pair = jnp.concatenate([block_ref[:, 2 * p, :], block_ref[:, 2 * p + 1, :]], axis=0)
         flat_ref[0:128, 128 * p : 128 * (p + 1)] = pair.T
@@ -220,6 +264,7 @@
     flat_ref[128:160, :] = jnp.concatenate(pieces, axis=1)
     result = dot3(split(flat_ref[...]), (top_ref[...], low_ref[...]), ((1,), (0,)))
     out_ref[...] = result
+    mixing_ref[...] = jnp.sum(block_ref[:, 15, :], axis=0, keepdims=True)
     for r in range(OWN):
         first_ref[3 * r : 3 * r + 3, :] = result[ROWS * r : ROWS * r + 3, :]
         final_ref[3 * r : 3 * r + 3, :] = result[ROWS * r + 13 : ROWS * r + 16, :]
@@ -231,11 +276,12 @@
     return pl.pallas_call(
         spectrum_kernel,
         in_specs=whole(3),
-        out_specs=whole(3),
+        out_specs=whole(4),
         out_shape=[
             jax.ShapeDtypeStruct((rows, CIRCLE), F32),
             jax.ShapeDtypeStruct((3 * OWN, CIRCLE), F32),
             jax.ShapeDtypeStruct((3 * OWN, CIRCLE), F32),
+            jax.ShapeDtypeStruct((1, 128), F32),
         ],
         scratch_shapes=[pltpu.VMEM((rows, CIRCLE), F32)],
         compiler_params=params(24),
@@ -280,7 +326,7 @@
             mixed_real = jnp.zeros((ROWS, HALF), F32)
             mixed_imag = jnp.zeros((ROWS, HALF), F32)
             for b in range(BASIS):
-                weight = mixing_ref[r, b]
+                weight = mixing_ref[0, BASIS * r + b]
                 at = ROWS * (TAPS * b + k)
                 mixed_real += weight * kernel_ref[at : at + ROWS, 0:HALF]
                 mixed_imag += weight * kernel_ref[at : at + ROWS, HALF:CIRCLE]
@@ -360,19 +406,20 @@
     width = activation.shape[2]
     act = activation.transpose(1, 0, 2).reshape(points, width)
     cot = cotangent.transpose(1, 0, 2).reshape(points, width)
-    every = lax.all_gather(mixing, LON, axis=0, tiled=True).reshape(OWN, SHARDS, BASIS)
-    shard = lax.axis_index(LON)
-    own_mixing = lax.dynamic_slice_in_dim(every, shard, 1, 1).reshape(OWN, BASIS)
-    block, hidden, grad = mlp(act, cot, weight_in, weight_out)
+    shard = lax.axis_index(LON).reshape(1)
+    block, hidden, grad = mlp(shard, mixing, act, cot, weight_in, weight_out)
     spread = across(block)
-    grad_in, grad_out = weight_gradients(grad, hidden, act, cot)
+    total = weight_sums(grad, hidden, act, cot)
     kernel = kernel_spectrum(kernels)
-    data, first, final = spectrum(spread)
+    data, first, final, own_mixing = spectrum(spread)
     forward = [(i, i + 1) for i in range(3)]
     backward = [(target, source) for source, target in forward]
     before = lax.ppermute(final, LAT, forward)
     after = lax.ppermute(first, LAT, backward)
-    result = across(filtered(own_mixing, data, before, after, kernel))
+    sent = filtered(own_mixing, data, before, after, kernel)
+    result = across(sent)
+    total, _ = lax.optimization_barrier((total, sent))
+    grad_in, grad_out = finish(total)
     field = unpack(result).reshape(COLS, ROWS, width).transpose(1, 0, 2)
     return (field, grad_in, grad_out)
 

time: 315 us -> 152 us (0.48)
  the two profiles are of different devices: /device:TPU:1 before, /device:TPU:6 now
where the time goes in v2:
time: 152 us; the launch traced here: 151 us
  waiting for transfers between devices  44.6 us (29%)
  blocking collectives  32.9 us (22%)
  Pallas kernels  32.4 us (21%)
  starting transfers between devices  20.4 us (13%)
  between operations  14.2 us (9%)
  local copies, waits for them, and re-layouts  6.19 us (4%)
    all_to_all x1, blocking collectives, across(): return lax.all_to_all(block, LON, split_axis=0, concat_axis=0, tiled=True)  32.9 us
    unnamed x3, waiting for transfers between devices  31.1 us
    all_to_all x1, starting transfers between devices, across(): return lax.all_to_all(block, LON, split_axis=0, concat_axis=0, tiled=True)  13.5 us
    pallas_call x2, Pallas kernels, weight_part(): pl.pallas_call(weight_kernel, grid=(units // tile,), in_specs=[pl.BlockSp...  10.2 us
    pallas_call x1, Pallas kernels, mlp(): pl.pallas_call(mlp_kernel, grid=(units // tile,), in_specs=[pl.BlockSpec(...  10 us
    unnamed x33, local copies, waits for them, and re-layouts  6.19 us
    ppermute x1, waiting for transfers between devices, weight_sums(): arrived = lax.ppermute(other, 'co', [(0, 1), (1, 0)])  5.83 us
    pallas_call x1, Pallas kernels, filtered(): pl.pallas_call(filter_kernel, in_specs=[pl.BlockSpec(memory_space=pltpu.S...  4.21 us
  transfers between devices with their start and end apart: 9, of which 6 were waited for; matrix products, arithmetic and copies ran while one was open for 0% of the time, Pallas kernels for 7%

profile of v2, /device:TPU:6, one launch (start us, length us, event | category | flops | bytes accessed | tf_op | source)
XLA Modules:
  0.0 151.2 jit_solution(17414927744034016874)
XLA Ops:
  7.2 0.0 reduce-scatter.5.cloned.1.call-start
  7.2 1.4 copy.16.mixing_ref
  8.6 0.0 copy-start.2
  8.6 0.0 copy-start.3
  8.6 10.0 %mlp.1 = (f32[64,16,128]{2,1,0:T(8,128)}, f32[192,1280]{1,0:T(8,128)}, f32[192,1280]{1,0:T(8,128)}) custom-call(s32[1]{0:T(128)} %bitcast.shard_ref, f32[10,3]{1,0:T(8,128)} %copy.16.mixing_ref, f32[192,640]{1,0:T(8,128)} %bitcast.18, f32[192,640]{1,0:T(8,128)} %bitcast.21, f32[1280,640]{1,0:T(8,128)} %in_ref.1, f32[1280,640]{1,0:T(8,128)} %out_ref.1), custom_call_target="tpu_custom_call" | custom-call | flops 2831155200 | bytes 10000000 | tf_op jit(solution)/shard_map/mlp/pallas_call | solution.py:135
  18.6 0.0 copy-done.2
  18.6 0.0 copy-done.3
  18.6 0.0 copy-start
  18.6 1.2 copy-done
  19.8 0.0 copy-start.1
  19.8 1.2 copy-done.1
  21.0 4.7 %weights.2 = f32[1280,640]{1,0:T(8,128)S(1)} custom-call(s32[1]{0:T(128)} %bitcast.14.core_ref, f32[192,1280]{1,0:T(8,128)S(1)} %copy-done.1, f32[192,1280]{1,0:T(8,128)S(1)} %copy-done, f32[192,640]{1,0:T(8,128)S(1)} %bitcast.19, f32[192,640]{1,0:T(8,128)S(1)} %bitcast.22), custom_call_target="tpu_custom_call" | custom-call | flops 943718400 | bytes 10000000 | tf_op jit(solution)/shard_map/weights/pallas_call | solution.py:189
  25.7 0.1 collective-permute-start.2
  25.8 5.8 %collective-permute-done.2.rest_0_ = f32[1280,640]{1,0:T(8,128)S(1)} collective-permute-done((f32[1280,640]{1,0:T(8,128)S(1)}, f32[1280,640]{1,0:T(8,128)S(1)}, u32[]{:S(2)}, u32[]{:S(2)}) %collective-permute-start.2) | collective-permute-done | bytes 3276832 | tf_op jit(solution)/shard_map/ppermute | solution.py:229
  31.6 5.6 %weights.3 = f32[1280,640]{1,0:T(8,128)} custom-call(s32[1]{0:T(128)} %bitcast.11.core_ref, f32[192,1280]{1,0:T(8,128)S(1)} %copy-done.1, f32[192,1280]{1,0:T(8,128)S(1)} %copy-done, f32[192,640]{1,0:T(8,128)S(1)} %bitcast.20, f32[192,640]{1,0:T(8,128)S(1)} %bitcast.23, f32[1280,640]{1,0:T(8,128)S(1)} %collective-permute-done.2.rest_0_), custom_call_target="tpu_custom_call" | custom-call | flops 943718400 | bytes 10000000 | tf_op jit(solution)/shard_map/weights/pallas_call | solution.py:189
  37.2 0.0 copy-start.12
  37.2 0.0 copy-start.6
  37.2 0.0 copy-start.7
  37.2 0.0 reduce-scatter.5.cloned.1.call-update
  37.2 0.0 reduce-scatter.7.cloned.1.call-start
  37.3 1.0 copy-done.12
  38.2 0.0 copy-start.10
  38.2 32.9 %all_to_all.10.block_ref = f32[64,16,128]{2,1,0:T(8,128)S(1)} all-to-all(f32[64,16,128]{2,1,0:T(8,128)S(1)} %copy-done.12), channel_id=1, replica_groups=mesh['yl'=2,'co'=2,'x'=4,'z'=8,'yh'=2] {'x','z','yh'}, dimensions={0} | all-to-all | bytes 1048576 | tf_op jit(solution)/shard_map/all_to_all | solution.py:401
  71.1 0.0 copy-done.6
  71.1 0.0 copy-done.7
  71.1 0.0 copy-start.8
  71.1 0.0 copy-start.9
  71.1 1.0 spectrum.1
  72.1 1.3 collective-permute-start
  73.4 1.3 collective-permute-start.1
  74.7 0.0 copy-done.10
  74.8 0.0 copy-done.8
  74.8 0.0 copy-done.9
  74.8 0.0 copy-start.4
  74.8 0.0 copy-start.5
  74.8 1.4 kernel_spectrum.1.kernel_ref
  76.2 0.0 collective-permute-done.before_ref
  76.2 1.3 collective-permute-done.1.after_ref
  77.5 0.0 copy-done.4
  77.6 0.0 copy-done.5
  77.6 4.2 %filter.1 = f32[64,16,128]{2,1,0:T(8,128)} custom-call(f32[1,128]{1,0:T(1,128)S(1)} %get-tuple-element.18.mixing_ref, f32[160,768]{1,0:T(8,128)S(1)} %get-tuple-element.19.data_ref, f32[30,768]{1,0:T(8,128)S(1)} %collective-permute-done.before_ref, f32[30,768]{1,0:T(8,128)S(1)} %collective-permute-done.1.after_ref, ...), custom_call_target="tpu_custom_call" | custom-call | flops 566231040 | bytes 5000000 | tf_op jit(solution)/shard_map/filter/pallas_call | solution.py:358
  81.8 4.1 %reduce-scatter.5.cloned.1.call-done = f32[320,640]{1,0:T(8,128)} async-done(((f32[1280,640]{1,0:T(8,128)}), f32[320,640]{1,0:T(8,128)}) %reduce-scatter.5.cloned.1.call-update) | async-done | bytes 819216 | tf_op jit(solution)/shard_map/reduce_scatter | solution.py:231
  85.9 0.0 reduce-scatter.7.cloned.1.call-update
  85.9 13.5 %all-to-all-start.1 = ((f32[64,16,128]{2,1,0:T(8,128)}), f32[64,16,128]{2,1,0:T(8,128)S(1)}, u32[]{:S(2)}, u32[]{:S(2)}) async-start(f32[64,16,128]{2,1,0:T(8,128)} %filter.1), calls=%async_computation.1 | async-start | bytes 1048576 | tf_op jit(solution)/shard_map/all_to_all | solution.py:401
  99.4 0.6 pad_add_fusion.place_ref
  100.0 31.0 %reduce-scatter.7.cloned.1.call-done.total_ref = f32[40,640]{1,0:T(8,128)} async-done(((f32[320,640]{1,0:T(8,128)}), f32[40,640]{1,0:T(8,128)}) %reduce-scatter.7.cloned.1.call-update) | async-done | bytes 102416
  131.1 1.8 %cut.1 = (f32[48,160]{1,0:T(8,128)}, f32[48,160]{1,0:T(8,128)}, f32[48,160]{1,0:T(8,128)}, f32[48,160]{1,0:T(8,128)}) custom-call(s32[2]{0:T(128)} %pad_add_fusion.place_ref, f32[40,640]{1,0:T(8,128)} %reduce-scatter.7.cloned.1.call-done.total_ref), custom_call_target="tpu_custom_call" | custom-call | tf_op jit(solution)/shard_map/cut/pallas_call | solution.py:237
  132.8 3.2 %collective-permute-start.3 = (f32[48,160]{1,0:T(8,128)}, f32[48,160]{1,0:T(8,128)S(1)}, u32[]{:S(2)}, u32[]{:S(2)}) collective-permute-start(f32[48,160]{1,0:T(8,128)} %get-tuple-element.26), channel_id=1, source_target_pairs={{0,1},{1,0},{128,129},{129,128},{2,3},{3,2},{130,131},{131,130},{4... | collective-permute-start | bytes 92168 | tf_op jit(solution)/shard_map/ppermute | solution.py:245
  136.0 0.7 collective-permute-start.4
  136.8 0.1 collective-permute-start.5
  136.9 0.0 all-to-all-done.1.block_ref
  136.9 0.0 copy-start.11
  136.9 0.8 copy-done.11
  137.7 2.3 %unpack.1 = f32[192,640]{1,0:T(8,128)} custom-call(f32[64,16,128]{2,1,0:T(8,128)} %copy-done.11), custom_call_target="tpu_custom_call" | custom-call | tf_op jit(solution)/shard_map/unpack/pallas_call | solution.py:391
  140.1 0.0 collective-permute-done.3.refs_1_
  140.1 0.0 copy-start.13
  140.1 0.3 collective-permute-done.4.refs_2_
  140.3 0.0 copy-start.14
  140.3 1.9 %collective-permute-done.5.refs_3_ = f32[48,160]{1,0:T(8,128)S(1)} collective-permute-done((f32[48,160]{1,0:T(8,128)}, f32[48,160]{1,0:T(8,128)S(1)}, u32[]{:S(2)}, u32[]{:S(2)}) %collective-permute-start.5) | collective-permute-done | bytes 30752 | tf_op jit(solution)/shard_map/ppermute | solution.py:245
  142.3 0.0 copy-start.15
  142.3 0.0 copy-done.13
  142.3 0.0 copy-done.14
  142.3 0.6 copy-done.15
  142.9 1.5 last.1
Async XLA Ops:
  7.2 78.7 %reduce-scatter.5.cloned.1.call-start = ((), (), s32[]{:S(2)}) async-start(), calls=%async_computation.4 | async-start | bytes 4096000 | tf_op jit(solution)/shard_map/reduce_scatter | solution.py:231
  8.6 10.0 %copy-start.2 = (f32[16,12,640]{2,0,1:T(8,128)S(1)}, f32[16,12,640]{2,0,1:T(8,128)}, u32[]{:S(2)}) copy-start(f32[16,12,640]{2,0,1:T(8,128)} %param.12) | copy-start | bytes 1474564
  8.6 10.0 %copy-start.3 = (f32[16,12,640]{2,0,1:T(8,128)S(1)}, f32[16,12,640]{2,0,1:T(8,128)}, u32[]{:S(2)}) copy-start(f32[16,12,640]{2,0,1:T(8,128)} %param.13) | copy-start | bytes 1474564
  18.6 1.2 copy-start
  19.8 1.2 copy-start.1
  25.7 5.9 %collective-permute-start.2 = (f32[1280,640]{1,0:T(8,128)S(1)}, f32[1280,640]{1,0:T(8,128)S(1)}, u32[]{:S(2)}, u32[]{:S(2)}) collective-permute-start(f32[1280,640]{1,0:T(8,128)S(1)} %weights.2), channel_id=1, source_target_pairs={{0,64},{64,0},{1,65},{65,1},{2,66},{66,2},{3,67},{67,3},{4,68},{68... | collective-permute-start | bytes 9830408 | tf_op jit(solution)/shard_map/ppermute | solution.py:229
  37.2 1.0 copy-start.12
  37.2 33.9 %copy-start.6 = (bf16[768,768]{1,0:T(8,128)(2,1)S(1)}, bf16[768,768]{1,0:T(8,128)(2,1)}, u32[]{:S(2)}) copy-start(bf16[768,768]{1,0:T(8,128)(2,1)} %constant.41.clone.top_ref) | copy-start | bytes 3538948
  37.2 33.9 %copy-start.7 = (bf16[768,768]{1,0:T(8,128)(2,1)S(1)}, bf16[768,768]{1,0:T(8,128)(2,1)}, u32[]{:S(2)}) copy-start(bf16[768,768]{1,0:T(8,128)(2,1)} %constant.42.clone.low_ref) | copy-start | bytes 3538948
  37.2 93.8 %reduce-scatter.7.cloned.1.call-start = ((), (), s32[]{:S(2)}) async-start(), calls=%async_computation.5 | async-start | bytes 921600
  38.2 36.5 %copy-start.10 = (f32[3,16,7,768]{3,1,2,0:T(8,128)S(1)}, f32[3,16,7,768]{3,1,2,0:T(8,128)}, u32[]{:S(2)}) copy-start(f32[3,16,7,768]{3,1,2,0:T(8,128)} %param.16) | copy-start | bytes 3096580
  71.1 3.6 %copy-start.8 = (bf16[768,768]{1,0:T(8,128)(2,1)S(1)}, bf16[768,768]{1,0:T(8,128)(2,1)}, u32[]{:S(2)}) copy-start(bf16[768,768]{1,0:T(8,128)(2,1)} %constant.39.clone.top_ref) | copy-start | bytes 3538948
  71.1 3.6 %copy-start.9 = (bf16[768,768]{1,0:T(8,128)(2,1)S(1)}, bf16[768,768]{1,0:T(8,128)(2,1)}, u32[]{:S(2)}) copy-start(bf16[768,768]{1,0:T(8,128)(2,1)} %constant.40.clone.low_ref) | copy-start | bytes 3538948
  72.1 4.1 %collective-permute-start = (f32[30,768]{1,0:T(8,128)S(1)}, f32[30,768]{1,0:T(8,128)S(1)}, u32[]{:S(2)}, u32[]{:S(2)}) collective-permute-start(f32[30,768]{1,0:T(8,128)S(1)} %get-tuple-element.20), channel_id=1, source_target_pairs={{0,64},{64,128},{128,192},{1,65},{65,129},{129,193},{2,66},{66,130... | collective-permute-start | bytes 276488 | tf_op jit(solution)/shard_map/ppermute | solution.py:417
  73.4 4.1 %collective-permute-start.1 = (f32[30,768]{1,0:T(8,128)S(1)}, f32[30,768]{1,0:T(8,128)S(1)}, u32[]{:S(2)}, u32[]{:S(2)}) collective-permute-start(f32[30,768]{1,0:T(8,128)S(1)} %get-tuple-element.21), channel_id=1, source_target_pairs={{64,0},{128,64},{192,128},{65,1},{129,65},{193,129},{66,2},{130,66... | collective-permute-start | bytes 276488 | tf_op jit(solution)/shard_map/ppermute | solution.py:418
  74.8 2.8 %copy-start.4 = (bf16[768,768]{1,0:T(8,128)(2,1)S(1)}, bf16[768,768]{1,0:T(8,128)(2,1)}, u32[]{:S(2)}) copy-start(bf16[768,768]{1,0:T(8,128)(2,1)} %constant.43.clone.top_ref) | copy-start | bytes 3538948
  74.8 2.8 %copy-start.5 = (bf16[768,768]{1,0:T(8,128)(2,1)S(1)}, bf16[768,768]{1,0:T(8,128)(2,1)}, u32[]{:S(2)}) copy-start(bf16[768,768]{1,0:T(8,128)(2,1)} %constant.44.clone.low_ref) | copy-start | bytes 3538948
  85.9 51.0 %all-to-all-start.1 = ((f32[64,16,128]{2,1,0:T(8,128)}), f32[64,16,128]{2,1,0:T(8,128)S(1)}, u32[]{:S(2)}, u32[]{:S(2)}) async-start(f32[64,16,128]{2,1,0:T(8,128)} %filter.1), calls=%async_computation.1 | async-start | bytes 1048576 | tf_op jit(solution)/shard_map/all_to_all | solution.py:401
  132.8 7.2 %collective-permute-start.3 = (f32[48,160]{1,0:T(8,128)}, f32[48,160]{1,0:T(8,128)S(1)}, u32[]{:S(2)}, u32[]{:S(2)}) collective-permute-start(f32[48,160]{1,0:T(8,128)} %get-tuple-element.26), channel_id=1, source_target_pairs={{0,1},{1,0},{128,129},{129,128},{2,3},{3,2},{130,131},{131,130},{4... | collective-permute-start | bytes 92168 | tf_op jit(solution)/shard_map/ppermute | solution.py:245
  136.0 4.3 %collective-permute-start.4 = (f32[48,160]{1,0:T(8,128)}, f32[48,160]{1,0:T(8,128)S(1)}, u32[]{:S(2)}, u32[]{:S(2)}) collective-permute-start(f32[48,160]{1,0:T(8,128)} %get-tuple-element.27), channel_id=1, source_target_pairs={{0,128},{1,129},{128,0},{129,1},{2,130},{3,131},{130,2},{131,3},{4... | collective-permute-start | bytes 92168 | tf_op jit(solution)/shard_map/ppermute | solution.py:245
  136.8 5.5 %collective-permute-start.5 = (f32[48,160]{1,0:T(8,128)}, f32[48,160]{1,0:T(8,128)S(1)}, u32[]{:S(2)}, u32[]{:S(2)}) collective-permute-start(f32[48,160]{1,0:T(8,128)} %get-tuple-element.28), channel_id=1, source_target_pairs={{0,129},{1,128},{128,1},{129,0},{2,131},{3,130},{130,3},{131,2},{4... | collective-permute-start | bytes 92168 | tf_op jit(solution)/shard_map/ppermute | solution.py:245
  136.9 0.8 copy-start.11
  140.1 2.2 %copy-start.13 = (f32[48,160]{1,0:T(8,128)}, f32[48,160]{1,0:T(8,128)S(1)}, u32[]{:S(2)}) copy-start(f32[48,160]{1,0:T(8,128)S(1)} %collective-permute-done.3.refs_1_) | copy-start | bytes 92164
  140.3 2.0 %copy-start.14 = (f32[48,160]{1,0:T(8,128)}, f32[48,160]{1,0:T(8,128)S(1)}, u32[]{:S(2)}) copy-start(f32[48,160]{1,0:T(8,128)S(1)} %collective-permute-done.4.refs_2_) | copy-start | bytes 92164
  142.3 0.6 copy-start.15
Sparse Core Ops, SparseCore 0:
  37.3 48.5 reduce-scatter.4
  88.4 42.5 reduce-scatter.6

commit v3 on v2

--- a/solution.py
+++ b/solution.py
@@ -101,18 +101,47 @@
 
 
 def mlp_kernel(
-    shard_ref, mixing_ref, act_ref, cot_ref, in_ref, out_ref, block_ref, hidden_ref, grad_ref, unit_ref
+    place_ref,
+    mixing_ref,
+    act_ref,
+    cot_ref,
+    in_ref,
+    out_ref,
+    block_ref,
+    own_ref,
+    other_ref,
+    unit_ref,
+    act_top,
+    act_low,
+    cot_top,
+    cot_low,
+    act_cols_top,
+    act_cols_low,
+    cot_cols_top,
+    cot_cols_low,
 ):
     step = pl.program_id(0)
-    act, cot = split(act_ref[...]), split(cot_ref[...])
+
+    @pl.when(step == 0)
+    def _():
+        act, cot = act_ref[...], cot_ref[...]
+        act_top[...], act_low[...] = split(act)
+        cot_top[...], cot_low[...] = split(cot)
+        even = [act[:, 0:160], act[:, 320:480]]
+        odd = [act[:, 160:320], act[:, 480:640]]
+        act_cols_top[...], act_cols_low[...] = split(jnp.concatenate(even + odd, axis=1))
+        even = [cot[:, 0:160], cot[:, 320:480]]
+        odd = [cot[:, 160:320], cot[:, 480:640]]
+        cot_cols_top[...], cot_cols_low[...] = split(jnp.concatenate(odd + even, axis=1))
+
     w_in, w_out = split(in_ref[...]), split(out_ref[...])
-    preact = dot3(act, w_in, ((1,), (1,)))
+    preact = dot3((act_top[...], act_low[...]), w_in, ((1,), (1,)))
     cdf = 0.5 * (1.0 + lax.erf(preact * (1.0 / math.sqrt(2.0))))
     density = jnp.exp(-0.5 * preact * preact) * (1.0 / math.sqrt(2.0 * math.pi))
-    hidden_ref[...] = preact * cdf
-    grad = dot3(cot, w_out, ((1,), (1,))) * (cdf + preact * density)
-    grad_ref[...] = grad
-    term = dot3(split(grad), w_in, ((1,), (0,)))
+    hidden = split(preact * cdf)
+    slope = cdf + preact * density
+    grad = split(dot3((cot_top[...], cot_low[...]), w_out, ((1,), (1,))) * slope)
+    term = dot3(grad, w_in, ((1,), (0,)))
 
     @pl.when(step == 0)
     def _():
@@ -122,135 +151,139 @@
     def _():
         unit_ref[...] += term
 
+    contract = ((0,), (0,))
+    first = dot3(grad, (act_cols_top[...], act_cols_low[...]), contract)
+    second = dot3(hidden, (cot_cols_top[...], cot_cols_low[...]), contract)
+    left = lax.broadcasted_iota(jnp.int32, first.shape, 1) < 320
+    mine = left == (place_ref[1] == 0)
+    own_ref[...] = jnp.where(mine, first, second)
+    other_ref[...] = jnp.where(mine, second, first)
+
     @pl.when(step == pl.num_programs(0) - 1)
     def _():
-        pack(unit_ref[...], mixing_ref, shard_ref[0], block_ref)
-
-
-def mlp(shard, mixing, act, cot, weight_in, weight_out):
+        pack(unit_ref[...], mixing_ref, place_ref[0], block_ref)
+
+
+def mlp(place, mixing, act, cot, weight_in, weight_out):
     points, width = act.shape
     units = weight_in.shape[0]
     tile = 256
     full = lambda shape: pl.BlockSpec(shape, lambda i: (0,) * len(shape))
+    rows = pl.BlockSpec((tile, width), lambda i: (i, 0))
+    scalars = pl.BlockSpec(memory_space=pltpu.SMEM)
     return pl.pallas_call(
         mlp_kernel,
         grid=(units // tile,),
-        in_specs=[
-            pl.BlockSpec(memory_space=pltpu.SMEM),
-            pl.BlockSpec(memory_space=pltpu.SMEM),
-            full((points, width)),
-            full((points, width)),
-            pl.BlockSpec((tile, width), lambda i: (i, 0)),
-            pl.BlockSpec((tile, width), lambda i: (i, 0)),
-        ],
-        out_specs=[
-            full((SHARDS, 16, 128)),
-            pl.BlockSpec((points, tile), lambda i: (0, i)),
-            pl.BlockSpec((points, tile), lambda i: (0, i)),
-        ],
+        in_specs=[scalars, scalars, full((points, width)), full((points, width)), rows, rows],
+        out_specs=[full((SHARDS, 16, 128)), rows, rows],
         out_shape=[
             jax.ShapeDtypeStruct((SHARDS, 16, 128), F32),
-            jax.ShapeDtypeStruct((points, units), F32),
-            jax.ShapeDtypeStruct((points, units), F32),
+            jax.ShapeDtypeStruct((units, width), F32),
+            jax.ShapeDtypeStruct((units, width), F32),
         ],
-        scratch_shapes=[pltpu.VMEM((points, width), F32)],
+        scratch_shapes=[pltpu.VMEM((points, width), F32)]
+        + [pltpu.VMEM((points, width), BF16)] * 8,
         compiler_params=params(60),
-        cost_estimate=cost(18 * points * width * units, 10_000_000),
+        cost_estimate=cost(30 * points * width * units, 15_000_000),
         name="mlp",
-    )(shard, mixing, act, cot, weight_in, weight_out)
-
-
-def pick(field, core):
-    even = jnp.concatenate([field[:, 0:160], field[:, 320:480]], axis=1)
-    odd = jnp.concatenate([field[:, 160:320], field[:, 480:640]], axis=1)
-    return split(jnp.where(core == 0, even, odd))
-
-
-def weight_kernel(core_ref, grad_ref, hidden_ref, act_ref, cot_ref, *rest):
-    out_ref = rest[-1]
-    core = core_ref[0]
-    act, cot = pick(act_ref[...], core), pick(cot_ref[...], core)
-    contract = ((0,), (0,))
-    first = dot3(split(grad_ref[...]), act, contract)
-    second = dot3(split(hidden_ref[...]), cot, contract)
-    total = jnp.concatenate([first, second], axis=1)
-    if len(rest) == 2:
-        total += rest[0][...]
-    out_ref[...] = total
-
-
-def weight_part(core, grad, hidden, act, cot, arrived):
-    points, units = grad.shape
-    width = act.shape[1]
-    tile = 256
-    tall = pl.BlockSpec((points, tile), lambda i: (0, i))
-    flat = pl.BlockSpec((points, width), lambda i: (0, 0))
-    wide = pl.BlockSpec((tile, width), lambda i: (i, 0))
-    return pl.pallas_call(
-        weight_kernel,
-        grid=(units // tile,),
-        in_specs=[pl.BlockSpec(memory_space=pltpu.SMEM), tall, tall, flat, flat]
-        + [wide] * len(arrived),
-        out_specs=wide,
-        out_shape=jax.ShapeDtypeStruct((units, width), F32),
-        compiler_params=params(24),
-        cost_estimate=cost(6 * points * width * units, 10_000_000),
-        name="weights",
-    )(core, grad, hidden, act, cot, *arrived)
-
-
-def quarter(total, upper, right):
-    kept = jnp.where(right == 1, total[20:40], total[0:20])
+    )(place, mixing, act, cot, weight_in, weight_out)
+
+
+def choose(upper, right, rows, low, high):
+    kept = jnp.where(right == 1, rows[high], rows[low])
     first = jnp.where(upper == 1, kept[:, 160:320], kept[:, 0:160])
     second = jnp.where(upper == 1, kept[:, 480:640], kept[:, 320:480])
-    return first, second
-
-
-def cut_kernel(place_ref, total_ref, *out_refs):
-    total = total_ref[...]
-    for m, out_ref in enumerate(out_refs):
-        upper, right = place_ref[0], place_ref[1]
-        upper = 1 - upper if m & 2 else upper
-        right = 1 - right if m & 1 else right
-        first, second = quarter(total, upper, right)
-        out_ref[0:20, :] = first
-        out_ref[24:44, :] = second
-
-
-def sum_kernel(*refs):
-    first_ref, second_ref = refs[4:]
-    first_ref[...] = (refs[0][0:20] + refs[1][0:20]) + (refs[2][0:20] + refs[3][0:20])
-    second_ref[...] = (refs[0][24:44] + refs[1][24:44]) + (refs[2][24:44] + refs[3][24:44])
-
-
-def weight_sums(grad, hidden, act, cot):
-    core = lax.axis_index("co")
-    other = weight_part((1 - core).reshape(1), grad, hidden, act, cot, ())
-    arrived = lax.ppermute(other, "co", [(0, 1), (1, 0)])
-    total = weight_part(core.reshape(1), grad, hidden, act, cot, (arrived,))
-    return lax.psum_scatter(total, "x", scatter_dimension=0, tiled=True)
-
-
-def finish(total):
-    total = lax.psum_scatter(total, "z", scatter_dimension=0, tiled=True)
-    place = jnp.stack([lax.axis_index("yl"), lax.axis_index("yh")])
-    pieces = pl.pallas_call(
-        cut_kernel,
-        in_specs=[pl.BlockSpec(memory_space=pltpu.SMEM)] + whole(1),
-        out_specs=whole(4),
-        out_shape=[jax.ShapeDtypeStruct((48, 160), F32)] * 4,
-        name="cut",
-    )(place, total)
-    moved = [pieces[0]] + [
+    return [first, second]
+
+
+def partner(place_ref, m):
+    upper, right = place_ref[2], place_ref[3]
+    return (1 - upper if m & 2 else upper), (1 - right if m & 1 else right)
+
+
+def cut_kernel(place_ref, own_ref, arrived_ref, *out_refs):
+    for m in range(4):
+        start = pl.multiple_of(320 * lax.rem(place_ref[4] + m, 4), 8)
+        rows = pl.ds(start, 160)
+        out_refs[m][...] = own_ref[rows, :] + arrived_ref[rows, :]
+    for x in range(4):
+        at = 320 * x + 160
+        total = own_ref[at : at + 160, :] + arrived_ref[at : at + 160, :]
+        for m in range(4):
+            upper, right = partner(place_ref, m)
+            for z in range(4):
+                low = slice(40 * z, 40 * z + 20)
+                high = slice(40 * z + 20, 40 * z + 40)
+                piece = jnp.concatenate(choose(upper, right, total, low, high), axis=1)
+                row, col = 80 * (x % 2) + 20 * z, 320 * (x // 2)
+                out_refs[4 + m][row : row + 20, col : col + 320] = piece
+
+
+def swap_kernel(place_ref, *refs):
+    ins, outs, kept_ref = refs[:8], refs[8:16], refs[16]
+    along_x = (ins[0][...] + ins[1][...]) + (ins[2][...] + ins[3][...])
+    along_y = (ins[4][...] + ins[5][...]) + (ins[6][...] + ins[7][...])
+    for m in range(4):
+        upper, right = partner(place_ref, m)
+        for z in range(4):
+            low = slice(40 * z, 40 * z + 20)
+            high = slice(40 * z + 20, 40 * z + 40)
+            piece = jnp.concatenate(choose(upper, right, along_x, low, high), axis=1)
+            row, col = 20 * (z % 2), 320 * (z // 2)
+            outs[m][row : row + 20, col : col + 320] = piece
+    for x in range(4):
+        row, col = 80 * (x % 2), 320 * (x // 2)
+        part = along_y[row : row + 80, col : col + 320]
+        kept_ref[x] = jnp.concatenate([part[0:40], part[40:80]], axis=1)
+    for m in range(4):
+        outs[4 + m][...] = kept_ref[lax.rem(place_ref[4] + m, 4)]
+
+
+def stack_kernel(*refs):
+    out_ref = refs[8]
+    out_ref[...] = jnp.zeros(out_ref.shape, F32)
+    for half in range(2):
+        ins = refs[4 * half : 4 * half + 4]
+        total = (ins[0][...] + ins[1][...]) + (ins[2][...] + ins[3][...])
+        for z in range(4):
+            row, col, at = 20 * (z % 2), 320 * (z // 2), 24 * (4 * half + z)
+            out_ref[at : at + 20, 0:320] = total[row : row + 20, col : col + 320]
+
+
+def last_kernel(place_ref, total_ref, first_ref, second_ref):
+    total = total_ref[0:20, 0:320]
+    even = place_ref[1] == 0
+    first_ref[...] = jnp.where(even, total[:, 0:160], total[:, 160:320])
+    second_ref[...] = jnp.where(even, total[:, 160:320], total[:, 0:160])
+
+
+def small(kernel, operands, shapes, scalars=0, scratch=(), name=None):
+    return pl.pallas_call(
+        kernel,
+        in_specs=[pl.BlockSpec(memory_space=pltpu.SMEM)] * scalars
+        + whole(len(operands) - scalars),
+        out_specs=whole(len(shapes)),
+        out_shape=[jax.ShapeDtypeStruct(shape, F32) for shape in shapes],
+        scratch_shapes=scratch,
+        compiler_params=params(32),
+        name=name,
+    )(*operands)
+
+
+def exchange_x(pieces):
+    return [pieces[0]] + [
+        lax.ppermute(pieces[m], "x", [(i, (i + m) % 4) for i in range(4)]) for m in (1, 2, 3)
+    ]
+
+
+def exchange_y(pieces):
+    return [pieces[0]] + [
         lax.ppermute(pieces[m], ("yl", "yh"), [(i, i ^ m) for i in range(4)]) for m in (1, 2, 3)
     ]
-    return pl.pallas_call(
-        sum_kernel,
-        in_specs=whole(4),
-        out_specs=whole(2),
-        out_shape=[jax.ShapeDtypeStruct((20, 160), F32)] * 2,
-        name="last",
-    )(*moved)
+
+
+def after(value, earlier):
+    return lax.optimization_barrier((value, earlier))[0]
 
 
 def spectrum_kernel(
@@ -406,20 +439,27 @@
     width = activation.shape[2]
     act = activation.transpose(1, 0, 2).reshape(points, width)
     cot = cotangent.transpose(1, 0, 2).reshape(points, width)
-    shard = lax.axis_index(LON).reshape(1)
-    block, hidden, grad = mlp(shard, mixing, act, cot, weight_in, weight_out)
-    spread = across(block)
-    total = weight_sums(grad, hidden, act, cot)
+    place = jnp.stack([lax.axis_index(axis) for axis in (LON, "co", "yl", "yh", "x")])
+    block, own, other = mlp(place, mixing, act, cot, weight_in, weight_out)
+    arrived = lax.ppermute(other, "co", [(0, 1), (1, 0)])
+    cut = small(cut_kernel, (place, own, arrived), [(160, 640)] * 8, 1, name="cut")
+    spread = across(after(block, cut[0]))
+    moved = exchange_x(cut[:4]) + exchange_y(cut[4:])
+    swapped = small(
+        swap_kernel, (place, *moved), [(40, 640)] * 8, 1, (pltpu.VMEM((4, 40, 640), F32),), "swap"
+    )
+    moved = exchange_y(swapped[:4]) + exchange_x(swapped[4:])
     kernel = kernel_spectrum(kernels)
-    data, first, final, own_mixing = spectrum(spread)
+    data, first, final, own_mixing = spectrum(after(spread, swapped[0]))
     forward = [(i, i + 1) for i in range(3)]
     backward = [(target, source) for source, target in forward]
     before = lax.ppermute(final, LAT, forward)
-    after = lax.ppermute(first, LAT, backward)
-    sent = filtered(own_mixing, data, before, after, kernel)
-    result = across(sent)
-    total, _ = lax.optimization_barrier((total, sent))
-    grad_in, grad_out = finish(total)
+    after_rows = lax.ppermute(first, LAT, backward)
+    sent = filtered(own_mixing, data, before, after_rows, kernel)
+    (blocks,) = small(stack_kernel, moved, [(192, 384)], name="stack")
+    result = across(after(sent, blocks))
+    total = lax.psum_scatter(blocks, "z", scatter_dimension=0, tiled=True)
+    grad_in, grad_out = small(last_kernel, (place, total), [(20, 160)] * 2, 1, name="last")
     field = unpack(result).reshape(COLS, ROWS, width).transpose(1, 0, 2)
     return (field, grad_in, grad_out)
 

time: 152 us -> 189 us (1.24)
  the two profiles are of different devices: /device:TPU:6 before, /device:TPU:4 now
where the time goes in v3:
time: 189 us; the launch traced here: 188 us
  waiting for transfers between devices  67.2 us (36%)
  starting transfers between devices  52.3 us (28%)
  Pallas kernels  39.9 us (21%)
  local copies, waits for them, and re-layouts  14.3 us (8%)
  between operations  14.3 us (8%)
    unnamed x2, waiting for transfers between devices  44.5 us
    all_to_all x2, starting transfers between devices, across(): return lax.all_to_all(block, LON, split_axis=0, concat_axis=0, tiled=True)  25.9 us
    ppermute x6, starting transfers between devices, exchange_y(): lax.ppermute(pieces[m], ('yl', 'yh'), [(i, i ^ m) for i in range(4)])  18 us
    pallas_call x1, Pallas kernels, mlp(): pl.pallas_call(mlp_kernel, grid=(units // tile,), in_specs=[scalars, scal...  16 us
    pallas_call x4, Pallas kernels, small(): pl.pallas_call(kernel, in_specs=[pl.BlockSpec(memory_space=pltpu.SMEM)] *...  14 us
    unnamed x53, local copies, waits for them, and re-layouts  13.6 us
    ppermute x6, waiting for transfers between devices, exchange_x(): lax.ppermute(pieces[m], 'x', [(i, (i + m) % 4) for i in range(4)])  10.7 us
    ppermute x1, waiting for transfers between devices, per_device(): arrived = lax.ppermute(other, 'co', [(0, 1), (1, 0)])  6.05 us
  transfers between devices with their start and end apart: 18, of which 4 were waited for; matrix products, arithmetic and copies ran while one was open for 0% of the time, Pallas kernels for 5%

profile of v3, /device:TPU:4, one launch (start us, length us, event | category | flops | bytes accessed | tf_op | source)
XLA Modules:
  0.0 188.0 jit_solution(6887098270707307245)
XLA Ops:
  7.2 1.4 copy.16.mixing_ref
  8.5 0.7 stack.24.place_ref
  9.2 16.0 %mlp.1 = (f32[64,16,128]{2,1,0:T(8,128)}, f32[1280,640]{1,0:T(8,128)}, f32[1280,640]{1,0:T(8,128)}) custom-call(s32[5]{0:T(128)} %stack.24.place_ref, f32[10,3]{1,0:T(8,128)} %copy.16.mixing_ref, f32[192,640]{1,0:T(8,128)} %bitcast.20, f32[192,640]{1,0:T(8,128)} %bitcast.21, f32[1280,640]{1,0:T(8,128)} %in_ref.1, f32[1280,640]{1,0:T(8,128)} %out_ref.1), custom_call_target="tpu_custom_call" | custom-call | flops 4718592000 | bytes 15000000 | tf_op jit(solution)/shard_map/mlp/pallas_call | solution.py:174
  25.2 0.0 collective-permute-start
  25.2 6.0 %collective-permute-done.arrived_ref = f32[1280,640]{1,0:T(8,128)S(1)} collective-permute-done((f32[1280,640]{1,0:T(8,128)}, f32[1280,640]{1,0:T(8,128)S(1)}, u32[]{:S(2)}, u32[]{:S(2)}) %collective-permute-start) | collective-permute-done | bytes 3276832 | tf_op jit(solution)/shard_map/ppermute | solution.py:444
  31.2 1.9 %copy-done = f32[1280,640]{1,0:T(8,128)S(1)} copy-done((f32[1280,640]{1,0:T(8,128)S(1)}, f32[1280,640]{1,0:T(8,128)}, u32[]{:S(2)}) %copy-start) | copy-done | bytes 3276824
  33.2 7.8 %cut.1 = (f32[160,640]{1,0:T(8,128)S(1)}, f32[160,640]{1,0:T(8,128)S(1)}, f32[160,640]{1,0:T(8,128)S(1)}, f32[160,640]{1,0:T(8,128)S(1)}, f32[160,640]{1,0:T(8,1...) custom-call(s32[5]{0:T(128)S(1)} %copy-done.21, f32[1280,640]{1,0:T(8,128)S(1)} %copy-done, ...), custom_call_target="tpu_custom_call" | custom-call | tf_op jit(solution)/shard_map/cut/pallas_call | solution.py:261
  41.0 0.7 copy-done.10
  41.7 0.7 copy-done.22
  42.5 14.7 %all-to-all-start = ((f32[64,16,128]{2,1,0:T(8,128)}), f32[64,16,128]{2,1,0:T(8,128)S(1)}, u32[]{:S(2)}, u32[]{:S(2)}) async-start(f32[64,16,128]{2,1,0:T(8,128)} %get-tuple-element.35), calls=%async_computation | async-start | bytes 1048576 | tf_op jit(solution)/shard_map/all_to_all | solution.py:434
  57.2 1.4 collective-permute-start.1
  58.6 0.7 collective-permute-start.2
  59.2 1.1 collective-permute-start.3
  60.3 3.1 %collective-permute-start.4 = (f32[160,640]{1,0:T(8,128)S(1)}, f32[160,640]{1,0:T(8,128)S(1)}, u32[]{:S(2)}, u32[]{:S(2)}) collective-permute-start(f32[160,640]{1,0:T(8,128)S(1)} %get-tuple-element.40), channel_id=1, source_target_pairs={{0,1},{1,0},{128,129},{129,128},{2,3},{3,2},{130,131},{131,130},{4... | collective-permute-start | bytes 1228808 | tf_op jit(solution)/shard_map/ppermute | solution.py:281
  63.3 0.7 collective-permute-start.5
  64.0 10.7 %collective-permute-done.1.refs_1_ = f32[160,640]{1,0:T(8,128)S(1)} collective-permute-done((f32[160,640]{1,0:T(8,128)}, f32[160,640]{1,0:T(8,128)S(1)}, u32[]{:S(2)}, u32[]{:S(2)}) %collective-permute-start.1) | collective-permute-done | bytes 409632 | tf_op jit(solution)/shard_map/ppermute | solution.py:275
  74.7 10.2 %collective-permute-start.6 = (f32[160,640]{1,0:T(8,128)S(1)}, f32[160,640]{1,0:T(8,128)S(1)}, u32[]{:S(2)}, u32[]{:S(2)}) collective-permute-start(f32[160,640]{1,0:T(8,128)S(1)} %get-tuple-element.42), channel_id=1, source_target_pairs={{0,129},{1,128},{128,1},{129,0},{2,131},{3,130},{130,3},{131,2},{4... | collective-permute-start | bytes 1228808 | tf_op jit(solution)/shard_map/ppermute | solution.py:281
  84.9 0.0 collective-permute-done.2.refs_2_
  84.9 0.0 collective-permute-done.3.refs_3_
  84.9 0.0 collective-permute-done.4.refs_5_
  84.9 0.0 collective-permute-done.5.refs_6_
  84.9 5.9 %collective-permute-done.6.refs_7_ = f32[160,640]{1,0:T(8,128)S(1)} collective-permute-done((f32[160,640]{1,0:T(8,128)S(1)}, f32[160,640]{1,0:T(8,128)S(1)}, u32[]{:S(2)}, u32[]{:S(2)}) %collective-permute-start.6) | collective-permute-done | bytes 409632 | tf_op jit(solution)/shard_map/ppermute | solution.py:281
  90.9 1.0 copy-done.11
  91.9 3.1 %swap.1 = (f32[40,640]{1,0:T(8,128)S(1)}, f32[40,640]{1,0:T(8,128)}, f32[40,640]{1,0:T(8,128)}, f32[40,640]{1,0:T(8,128)}, f32[40,640]{1,0:T(8,128)S(1)}, /*inde...) custom-call(s32[5]{0:T(128)S(1)} %copy-done.21, f32[160,640]{1,0:T(8,128)S(1)} %get-tuple-element.34.refs_0_, ...), custom_call_target="tpu_custom_call" | custom-call | tf_op jit(solution)/shard_map/swap/pallas_call | solution.py:261
  94.9 0.6 copy-done.12
  95.6 0.6 copy-done.23
  96.2 2.2 %collective-permute-start.9 = (f32[40,640]{1,0:T(8,128)}, f32[40,640]{1,0:T(8,128)S(1)}, u32[]{:S(2)}, u32[]{:S(2)}) collective-permute-start(f32[40,640]{1,0:T(8,128)} %get-tuple-element.49), channel_id=1, source_target_pairs={{0,1},{1,0},{128,129},{129,128},{2,3},{3,2},{130,131},{131,130},{4... | collective-permute-start | bytes 307208 | tf_op jit(solution)/shard_map/ppermute | solution.py:281
  98.4 1.9 %collective-permute-start.10 = (f32[40,640]{1,0:T(8,128)}, f32[40,640]{1,0:T(8,128)S(1)}, u32[]{:S(2)}, u32[]{:S(2)}) collective-permute-start(f32[40,640]{1,0:T(8,128)} %get-tuple-element.50), channel_id=1, source_target_pairs={{0,128},{1,129},{128,0},{129,1},{2,130},{3,131},{130,2},{131,3},{4... | collective-permute-start | bytes 307208 | tf_op jit(solution)/shard_map/ppermute | solution.py:281
  100.3 0.0 collective-permute-start.11
  100.3 0.0 collective-permute-start.12
  100.3 0.0 collective-permute-start.13
  100.3 0.0 all-to-all-done.block_ref
  100.4 0.0 copy-start.5
  100.4 0.0 copy-start.6
  100.4 1.7 spectrum.1
  102.1 0.8 copy-done.8
  102.8 0.0 collective-permute-done.9.refs_1_
  102.8 0.6 copy-done.14
  103.5 2.0 %collective-permute-start.14 = (f32[40,640]{1,0:T(8,128)S(1)}, f32[40,640]{1,0:T(8,128)S(1)}, u32[]{:S(2)}, u32[]{:S(2)}) collective-permute-start(f32[40,640]{1,0:T(8,128)S(1)} %copy-done.24), channel_id=1, source_target_pairs={{0,48},{16,0},{32,16},{48,32},{1,49},{17,1},{33,17},{49,33},{2,50}... | collective-permute-start | bytes 307208 | tf_op jit(solution)/shard_map/ppermute | solution.py:275
  105.5 0.6 copy-done.16
  106.1 1.9 %collective-permute-start.7 = (f32[30,768]{1,0:T(8,128)}, f32[30,768]{1,0:T(8,128)}, u32[]{:S(2)}, u32[]{:S(2)}) collective-permute-start(f32[30,768]{1,0:T(8,128)} %get-tuple-element.47), channel_id=1, source_target_pairs={{0,64},{64,128},{128,192},{1,65},{65,129},{129,193},{2,66},{66,130... | collective-permute-start | bytes 276488 | tf_op jit(solution)/shard_map/ppermute | solution.py:456
  108.1 0.6 copy-done.18
  108.7 1.3 collective-permute-start.8
  110.0 0.0 copy-start.7
  110.0 1.2 copy-done.7
  111.2 0.0 copy-start.1
  111.3 0.0 copy-start.2
  111.3 1.4 kernel_spectrum.1.kernel_ref
  112.7 0.0 collective-permute-done.14.refs_7_
  112.7 1.8 stack.25
  114.5 0.0 collective-permute-done.7.before_ref
  114.5 0.0 collective-permute-done.8.after_ref
  114.6 0.0 copy-start.9
  114.6 1.0 copy-done.9
  115.6 4.6 %filter.1 = f32[64,16,128]{2,1,0:T(8,128)} custom-call(f32[1,128]{1,0:T(1,128)S(1)} %get-tuple-element.45.mixing_ref, f32[160,768]{1,0:T(8,128)S(1)} %copy-done.9, f32[30,768]{1,0:T(8,128)} %collective-permute-done.7.before_ref, f32[30,768]{1,0:T(8,128)} %collective-permute-done.8.after_ref, f32[336,768]{1,0:T(8,128)S(1)} %kernel_spectrum.1.kernel_ref, ...), custom_call_target="tpu_custom_call" | custom-call | flops 566231040 | bytes 5000000 | tf_op jit(solution)/shard_map/filter/pallas_call | solution.py:391
  120.2 11.2 %all-to-all-start.1 = ((f32[64,16,128]{2,1,0:T(8,128)}), f32[64,16,128]{2,1,0:T(8,128)S(1)}, u32[]{:S(2)}, u32[]{:S(2)}) async-start(f32[64,16,128]{2,1,0:T(8,128)} %filter.1), calls=%async_computation.1 | async-start | bytes 1048576 | tf_op jit(solution)/shard_map/all_to_all | solution.py:434
  131.3 0.0 reduce-scatter.4.cloned.1.call-start
  131.4 0.7 reduce-scatter.4.cloned.1.call-update
  132.1 43.8 %reduce-scatter.4.cloned.1.call-done.total_ref = f32[24,384]{1,0:T(8,128)} async-done(((f32[192,384]{1,0:T(8,128)}), f32[24,384]{1,0:T(8,128)}) %reduce-scatter.4.cloned.1.call-update) | async-done | bytes 36880
  175.9 0.8 copy-done.20
  176.7 1.3 last.1
  178.0 0.0 all-to-all-done.1.block_ref
  178.0 0.8 copy-done.25
  178.8 2.3 %unpack.1 = f32[192,640]{1,0:T(8,128)} custom-call(f32[64,16,128]{2,1,0:T(8,128)} %copy-done.25), custom_call_target="tpu_custom_call" | custom-call | tf_op jit(solution)/shard_map/unpack/pallas_call | solution.py:424
  (36 shorter events, 0.1 us)
Async XLA Ops:
  9.2 22.0 %copy-start.21 = (s32[5]{0:T(128)S(1)}, s32[5]{0:T(128)}, u32[]{:S(2)}) copy-start(s32[5]{0:T(128)} %stack.24.place_ref) | copy-start | bytes 64
  25.2 6.1 %collective-permute-start = (f32[1280,640]{1,0:T(8,128)}, f32[1280,640]{1,0:T(8,128)S(1)}, u32[]{:S(2)}, u32[]{:S(2)}) collective-permute-start(f32[1280,640]{1,0:T(8,128)} %get-tuple-element.33), channel_id=1, source_target_pairs={{0,64},{64,0},{1,65},{65,1},{2,66},{66,2},{3,67},{67,3},{4,68},{68... | collective-permute-start | bytes 9830408 | tf_op jit(solution)/shard_map/ppermute | solution.py:444
  31.2 1.9 %copy-start = (f32[1280,640]{1,0:T(8,128)S(1)}, f32[1280,640]{1,0:T(8,128)}, u32[]{:S(2)}) copy-start(f32[1280,640]{1,0:T(8,128)} %get-tuple-element.32.own_ref) | copy-start | bytes 9830404
  41.0 0.7 copy-start.10
  41.7 0.8 copy-start.22
  42.5 57.8 %all-to-all-start = ((f32[64,16,128]{2,1,0:T(8,128)}), f32[64,16,128]{2,1,0:T(8,128)S(1)}, u32[]{:S(2)}, u32[]{:S(2)}) async-start(f32[64,16,128]{2,1,0:T(8,128)} %get-tuple-element.35), calls=%async_computation | async-start | bytes 1048576 | tf_op jit(solution)/shard_map/all_to_all | solution.py:434
  57.2 17.5 %collective-permute-start.1 = (f32[160,640]{1,0:T(8,128)}, f32[160,640]{1,0:T(8,128)S(1)}, u32[]{:S(2)}, u32[]{:S(2)}) collective-permute-start(f32[160,640]{1,0:T(8,128)} %copy-done.22), channel_id=1, source_target_pairs={{0,16},{16,32},{32,48},{48,0},{1,17},{17,33},{33,49},{49,1},{2,18}... | collective-permute-start | bytes 1228808 | tf_op jit(solution)/shard_map/ppermute | solution.py:275
  58.6 26.4 %collective-permute-start.2 = (f32[160,640]{1,0:T(8,128)S(1)}, f32[160,640]{1,0:T(8,128)S(1)}, u32[]{:S(2)}, u32[]{:S(2)}) collective-permute-start(f32[160,640]{1,0:T(8,128)S(1)} %get-tuple-element.37), channel_id=1, source_target_pairs={{0,32},{16,48},{32,0},{48,16},{1,33},{17,49},{33,1},{49,17},{2,34}... | collective-permute-start | bytes 1228808 | tf_op jit(solution)/shard_map/ppermute | solution.py:275
  59.2 25.7 %collective-permute-start.3 = (f32[160,640]{1,0:T(8,128)S(1)}, f32[160,640]{1,0:T(8,128)S(1)}, u32[]{:S(2)}, u32[]{:S(2)}) collective-permute-start(f32[160,640]{1,0:T(8,128)S(1)} %get-tuple-element.38), channel_id=1, source_target_pairs={{0,48},{16,0},{32,16},{48,32},{1,49},{17,1},{33,17},{49,33},{2,50}... | collective-permute-start | bytes 1228808 | tf_op jit(solution)/shard_map/ppermute | solution.py:275
  60.3 24.7 %collective-permute-start.4 = (f32[160,640]{1,0:T(8,128)S(1)}, f32[160,640]{1,0:T(8,128)S(1)}, u32[]{:S(2)}, u32[]{:S(2)}) collective-permute-start(f32[160,640]{1,0:T(8,128)S(1)} %get-tuple-element.40), channel_id=1, source_target_pairs={{0,1},{1,0},{128,129},{129,128},{2,3},{3,2},{130,131},{131,130},{4... | collective-permute-start | bytes 1228808 | tf_op jit(solution)/shard_map/ppermute | solution.py:281
  63.3 21.6 %collective-permute-start.5 = (f32[160,640]{1,0:T(8,128)S(1)}, f32[160,640]{1,0:T(8,128)S(1)}, u32[]{:S(2)}, u32[]{:S(2)}) collective-permute-start(f32[160,640]{1,0:T(8,128)S(1)} %get-tuple-element.41), channel_id=1, source_target_pairs={{0,128},{1,129},{128,0},{129,1},{2,130},{3,131},{130,2},{131,3},{4... | collective-permute-start | bytes 1228808 | tf_op jit(solution)/shard_map/ppermute | solution.py:281
  74.7 16.1 %collective-permute-start.6 = (f32[160,640]{1,0:T(8,128)S(1)}, f32[160,640]{1,0:T(8,128)S(1)}, u32[]{:S(2)}, u32[]{:S(2)}) collective-permute-start(f32[160,640]{1,0:T(8,128)S(1)} %get-tuple-element.42), channel_id=1, source_target_pairs={{0,129},{1,128},{128,1},{129,0},{2,131},{3,130},{130,3},{131,2},{4... | collective-permute-start | bytes 1228808 | tf_op jit(solution)/shard_map/ppermute | solution.py:281
  90.9 1.0 copy-start.11
  91.9 8.5 %copy-start.3 = (bf16[768,768]{1,0:T(8,128)(2,1)S(1)}, bf16[768,768]{1,0:T(8,128)(2,1)}, u32[]{:S(2)}) copy-start(bf16[768,768]{1,0:T(8,128)(2,1)} %constant.39.clone.top_ref) | copy-start | bytes 3538948
  91.9 8.5 %copy-start.4 = (bf16[768,768]{1,0:T(8,128)(2,1)S(1)}, bf16[768,768]{1,0:T(8,128)(2,1)}, u32[]{:S(2)}) copy-start(bf16[768,768]{1,0:T(8,128)(2,1)} %constant.40.clone.low_ref) | copy-start | bytes 3538948
  94.9 0.6 copy-start.12
  95.6 0.7 copy-start.23
  96.2 6.6 %collective-permute-start.9 = (f32[40,640]{1,0:T(8,128)}, f32[40,640]{1,0:T(8,128)S(1)}, u32[]{:S(2)}, u32[]{:S(2)}) collective-permute-start(f32[40,640]{1,0:T(8,128)} %get-tuple-element.49), channel_id=1, source_target_pairs={{0,1},{1,0},{128,129},{129,128},{2,3},{3,2},{130,131},{131,130},{4... | collective-permute-start | bytes 307208 | tf_op jit(solution)/shard_map/ppermute | solution.py:281
  98.4 7.1 %collective-permute-start.10 = (f32[40,640]{1,0:T(8,128)}, f32[40,640]{1,0:T(8,128)S(1)}, u32[]{:S(2)}, u32[]{:S(2)}) collective-permute-start(f32[40,640]{1,0:T(8,128)} %get-tuple-element.50), channel_id=1, source_target_pairs={{0,128},{1,129},{128,0},{129,1},{2,130},{3,131},{130,2},{131,3},{4... | collective-permute-start | bytes 307208 | tf_op jit(solution)/shard_map/ppermute | solution.py:281
  100.3 7.8 %collective-permute-start.11 = (f32[40,640]{1,0:T(8,128)}, f32[40,640]{1,0:T(8,128)S(1)}, u32[]{:S(2)}, u32[]{:S(2)}) collective-permute-start(f32[40,640]{1,0:T(8,128)} %get-tuple-element.51), channel_id=1, source_target_pairs={{0,129},{1,128},{128,1},{129,0},{2,131},{3,130},{130,3},{131,2},{4... | collective-permute-start | bytes 307208 | tf_op jit(solution)/shard_map/ppermute | solution.py:281
  100.3 12.4 %collective-permute-start.12 = (f32[40,640]{1,0:T(8,128)}, f32[40,640]{1,0:T(8,128)}, u32[]{:S(2)}, u32[]{:S(2)}) collective-permute-start(f32[40,640]{1,0:T(8,128)} %get-tuple-element.53), channel_id=1, source_target_pairs={{0,16},{16,32},{32,48},{48,0},{1,17},{17,33},{33,49},{49,1},{2,18}... | collective-permute-start | bytes 307208 | tf_op jit(solution)/shard_map/ppermute | solution.py:275
  100.3 12.4 %collective-permute-start.13 = (f32[40,640]{1,0:T(8,128)}, f32[40,640]{1,0:T(8,128)}, u32[]{:S(2)}, u32[]{:S(2)}) collective-permute-start(f32[40,640]{1,0:T(8,128)} %get-tuple-element.54), channel_id=1, source_target_pairs={{0,32},{16,48},{32,0},{48,16},{1,33},{17,49},{33,1},{49,17},{2,34}... | collective-permute-start | bytes 307208 | tf_op jit(solution)/shard_map/ppermute | solution.py:275
  100.3 3.1 %copy-start.24 = (f32[40,640]{1,0:T(8,128)S(1)}, f32[40,640]{1,0:T(8,128)}, u32[]{:S(2)}) copy-start(f32[40,640]{1,0:T(8,128)} %copy-done.23) | copy-start | bytes 307204
  100.4 9.6 %copy-start.5 = (bf16[768,768]{1,0:T(8,128)(2,1)S(1)}, bf16[768,768]{1,0:T(8,128)(2,1)}, u32[]{:S(2)}) copy-start(bf16[768,768]{1,0:T(8,128)(2,1)} %constant.37.clone.top_ref) | copy-start | bytes 3538948
  100.4 9.6 %copy-start.6 = (bf16[768,768]{1,0:T(8,128)(2,1)S(1)}, bf16[768,768]{1,0:T(8,128)(2,1)}, u32[]{:S(2)}) copy-start(bf16[768,768]{1,0:T(8,128)(2,1)} %constant.38.clone.low_ref) | copy-start | bytes 3538948
  102.1 0.8 copy-start.8
  102.8 0.6 copy-start.14
  103.5 9.2 %collective-permute-start.14 = (f32[40,640]{1,0:T(8,128)S(1)}, f32[40,640]{1,0:T(8,128)S(1)}, u32[]{:S(2)}, u32[]{:S(2)}) collective-permute-start(f32[40,640]{1,0:T(8,128)S(1)} %copy-done.24), channel_id=1, source_target_pairs={{0,48},{16,0},{32,16},{48,32},{1,49},{17,1},{33,17},{49,33},{2,50}... | collective-permute-start | bytes 307208 | tf_op jit(solution)/shard_map/ppermute | solution.py:275
  105.5 0.6 copy-start.16
  106.1 8.4 %collective-permute-start.7 = (f32[30,768]{1,0:T(8,128)}, f32[30,768]{1,0:T(8,128)}, u32[]{:S(2)}, u32[]{:S(2)}) collective-permute-start(f32[30,768]{1,0:T(8,128)} %get-tuple-element.47), channel_id=1, source_target_pairs={{0,64},{64,128},{128,192},{1,65},{65,129},{129,193},{2,66},{66,130... | collective-permute-start | bytes 276488 | tf_op jit(solution)/shard_map/ppermute | solution.py:456
  108.1 0.6 copy-start.18
  108.7 5.8 %collective-permute-start.8 = (f32[30,768]{1,0:T(8,128)}, f32[30,768]{1,0:T(8,128)}, u32[]{:S(2)}, u32[]{:S(2)}) collective-permute-start(f32[30,768]{1,0:T(8,128)} %get-tuple-element.48), channel_id=1, source_target_pairs={{64,0},{128,64},{192,128},{65,1},{129,65},{193,129},{66,2},{130,66... | collective-permute-start | bytes 276488 | tf_op jit(solution)/shard_map/ppermute | solution.py:457
  110.0 1.2 copy-start.7
  111.2 1.5 copy-start.13
  111.2 1.5 copy-start.15
  111.2 1.5 copy-start.17
  111.2 1.5 copy-start.19
  111.2 3.3 %copy-start.1 = (bf16[768,768]{1,0:T(8,128)(2,1)S(1)}, bf16[768,768]{1,0:T(8,128)(2,1)}, u32[]{:S(2)}) copy-start(bf16[768,768]{1,0:T(8,128)(2,1)} %constant.41.clone.top_ref) | copy-start | bytes 3538948
  111.3 3.3 %copy-start.2 = (bf16[768,768]{1,0:T(8,128)(2,1)S(1)}, bf16[768,768]{1,0:T(8,128)(2,1)}, u32[]{:S(2)}) copy-start(bf16[768,768]{1,0:T(8,128)(2,1)} %constant.42.clone.low_ref) | copy-start | bytes 3538948
  114.6 1.0 copy-start.9
  120.2 57.8 %all-to-all-start.1 = ((f32[64,16,128]{2,1,0:T(8,128)}), f32[64,16,128]{2,1,0:T(8,128)S(1)}, u32[]{:S(2)}, u32[]{:S(2)}) async-start(f32[64,16,128]{2,1,0:T(8,128)} %filter.1), calls=%async_computation.1 | async-start | bytes 1048576 | tf_op jit(solution)/shard_map/all_to_all | solution.py:434
  131.3 44.6 %reduce-scatter.4.cloned.1.call-start = ((), (), s32[]{:S(2)}) async-start(), calls=%async_computation.3 | async-start | bytes 331776
  175.9 0.8 copy-start.20
  178.0 0.8 copy-start.25
Sparse Core Ops, SparseCore 0:
  134.7 41.1 reduce-scatter.3

commit v4 on v3

--- a/solution.py
+++ b/solution.py
@@ -96,7 +96,7 @@
         here = target == lax.rem(channel, SHARDS)
         first = BASIS * lax.div(channel, SHARDS)
         for b in range(BASIS):
-            weights = jnp.where(here & (lane == first + b), mixing_ref[i, b], weights)
+            weights = jnp.where(here & (lane == first + b), mixing_ref[b, i], weights)
     out_ref[:, 15, :] = weights
 
 
@@ -115,8 +115,6 @@
     act_low,
     cot_top,
     cot_low,
-    act_cols_top,
-    act_cols_low,
     cot_cols_top,
     cot_cols_low,
 ):
@@ -127,12 +125,8 @@
         act, cot = act_ref[...], cot_ref[...]
         act_top[...], act_low[...] = split(act)
         cot_top[...], cot_low[...] = split(cot)
-        even = [act[:, 0:160], act[:, 320:480]]
-        odd = [act[:, 160:320], act[:, 480:640]]
-        act_cols_top[...], act_cols_low[...] = split(jnp.concatenate(even + odd, axis=1))
-        even = [cot[:, 0:160], cot[:, 320:480]]
-        odd = [cot[:, 160:320], cot[:, 480:640]]
-        cot_cols_top[...], cot_cols_low[...] = split(jnp.concatenate(odd + even, axis=1))
+        pairs = [cot[:, 160:320], cot[:, 0:160], cot[:, 480:640], cot[:, 320:480]]
+        cot_cols_top[...], cot_cols_low[...] = split(jnp.concatenate(pairs, axis=1))
 
     w_in, w_out = split(in_ref[...]), split(out_ref[...])
     preact = dot3((act_top[...], act_low[...]), w_in, ((1,), (1,)))
@@ -152,10 +146,11 @@
         unit_ref[...] += term
 
     contract = ((0,), (0,))
-    first = dot3(grad, (act_cols_top[...], act_cols_low[...]), contract)
+    first = dot3(grad, (act_top[...], act_low[...]), contract)
     second = dot3(hidden, (cot_cols_top[...], cot_cols_low[...]), contract)
-    left = lax.broadcasted_iota(jnp.int32, first.shape, 1) < 320
-    mine = left == (place_ref[1] == 0)
+    lane = lax.broadcasted_iota(jnp.int32, first.shape, 1)
+    even = (lane < 160) | ((lane >= 320) & (lane < 480))
+    mine = even == (place_ref[1] == 0)
     own_ref[...] = jnp.where(mine, first, second)
     other_ref[...] = jnp.where(mine, second, first)
 
@@ -182,61 +177,72 @@
             jax.ShapeDtypeStruct((units, width), F32),
         ],
         scratch_shapes=[pltpu.VMEM((points, width), F32)]
-        + [pltpu.VMEM((points, width), BF16)] * 8,
+        + [pltpu.VMEM((points, width), BF16)] * 6,
         compiler_params=params(60),
         cost_estimate=cost(30 * points * width * units, 15_000_000),
         name="mlp",
     )(place, mixing, act, cot, weight_in, weight_out)
 
 
-def choose(upper, right, rows, low, high):
-    kept = jnp.where(right == 1, rows[high], rows[low])
-    first = jnp.where(upper == 1, kept[:, 160:320], kept[:, 0:160])
-    second = jnp.where(upper == 1, kept[:, 480:640], kept[:, 320:480])
-    return [first, second]
-
-
 def partner(place_ref, m):
     upper, right = place_ref[2], place_ref[3]
-    return (1 - upper if m & 2 else upper), (1 - right if m & 1 else right)
-
-
-def cut_kernel(place_ref, own_ref, arrived_ref, *out_refs):
-    for m in range(4):
-        start = pl.multiple_of(320 * lax.rem(place_ref[4] + m, 4), 8)
-        rows = pl.ds(start, 160)
-        out_refs[m][...] = own_ref[rows, :] + arrived_ref[rows, :]
-    for x in range(4):
-        at = 320 * x + 160
-        total = own_ref[at : at + 160, :] + arrived_ref[at : at + 160, :]
+    return 2 * (1 - upper if m & 2 else upper) + (1 - right if m & 1 else right)
+
+
+def by_chip(rows):
+    low = jnp.concatenate([rows[40 * z : 40 * z + 20] for z in range(4)], axis=0)
+    high = jnp.concatenate([rows[40 * z + 20 : 40 * z + 40] for z in range(4)], axis=0)
+    return [low[:, 0:320], high[:, 0:320], low[:, 320:640], high[:, 320:640]]
+
+
+def cut_kernel(place_ref, own_ref, arrived_ref, half_ref, *refs):
+    outs, kept_ref = refs[:4], refs[4]
+    x = pl.program_id(0)
+    half_ref[...] = own_ref[0:160, :] + arrived_ref[0:160, :]
+    pieces = by_chip(own_ref[160:320, :] + arrived_ref[160:320, :])
+    for at in range(4):
+
+        @pl.when(x == at)
+        def _():
+            row, col = 80 * (at % 2), 320 * (at // 2)
+            for chip in range(4):
+                kept_ref[chip, row : row + 80, col : col + 320] = pieces[chip]
+
+    @pl.when(x == 3)
+    def _():
         for m in range(4):
-            upper, right = partner(place_ref, m)
-            for z in range(4):
-                low = slice(40 * z, 40 * z + 20)
-                high = slice(40 * z + 20, 40 * z + 40)
-                piece = jnp.concatenate(choose(upper, right, total, low, high), axis=1)
-                row, col = 80 * (x % 2) + 20 * z, 320 * (x // 2)
-                out_refs[4 + m][row : row + 20, col : col + 320] = piece
-
-
-def swap_kernel(place_ref, *refs):
-    ins, outs, kept_ref = refs[:8], refs[8:16], refs[16]
-    along_x = (ins[0][...] + ins[1][...]) + (ins[2][...] + ins[3][...])
-    along_y = (ins[4][...] + ins[5][...]) + (ins[6][...] + ins[7][...])
-    for m in range(4):
-        upper, right = partner(place_ref, m)
-        for z in range(4):
-            low = slice(40 * z, 40 * z + 20)
-            high = slice(40 * z + 20, 40 * z + 40)
-            piece = jnp.concatenate(choose(upper, right, along_x, low, high), axis=1)
-            row, col = 20 * (z % 2), 320 * (z // 2)
-            outs[m][row : row + 20, col : col + 320] = piece
+            outs[m][...] = kept_ref[partner(place_ref, m)]
+
+
+def cut(place, own, arrived):
+    rows = pl.BlockSpec((320, 640), lambda i: (i, 0))
+    return pl.pallas_call(
+        cut_kernel,
+        grid=(4,),
+        in_specs=[pl.BlockSpec(memory_space=pltpu.SMEM), rows, rows],
+        out_specs=[pl.BlockSpec((160, 640), lambda i: (i, 0))]
+        + [pl.BlockSpec((160, 640), lambda i: (0, 0))] * 4,
+        out_shape=[jax.ShapeDtypeStruct((640, 640), F32)]
+        + [jax.ShapeDtypeStruct((160, 640), F32)] * 4,
+        scratch_shapes=[pltpu.VMEM((4, 160, 640), F32)],
+        compiler_params=params(60),
+        cost_estimate=cost(2_000_000, 10_000_000),
+        name="cut",
+    )(place, own, arrived)
+
+
+def swap_kernel(place_ref, half_ref, *refs):
+    ins, outs, kept_ref = refs[:4], refs[4:12], refs[12]
+    along_y = (ins[0][...] + ins[1][...]) + (ins[2][...] + ins[3][...])
+    for chip, piece in enumerate(by_chip(half_ref[...])):
+        kept_ref[chip] = jnp.concatenate([piece[0:40], piece[40:80]], axis=1)
     for x in range(4):
         row, col = 80 * (x % 2), 320 * (x // 2)
         part = along_y[row : row + 80, col : col + 320]
-        kept_ref[x] = jnp.concatenate([part[0:40], part[40:80]], axis=1)
+        kept_ref[4 + x] = jnp.concatenate([part[0:40], part[40:80]], axis=1)
     for m in range(4):
-        outs[4 + m][...] = kept_ref[lax.rem(place_ref[4] + m, 4)]
+        outs[m][...] = kept_ref[partner(place_ref, m)]
+        outs[4 + m][...] = kept_ref[4 + lax.rem(place_ref[4] + m, 4)]
 
 
 def stack_kernel(*refs):
@@ -246,12 +252,14 @@
         ins = refs[4 * half : 4 * half + 4]
         total = (ins[0][...] + ins[1][...]) + (ins[2][...] + ins[3][...])
         for z in range(4):
-            row, col, at = 20 * (z % 2), 320 * (z // 2), 24 * (4 * half + z)
-            out_ref[at : at + 20, 0:320] = total[row : row + 20, col : col + 320]
-
-
-def last_kernel(place_ref, total_ref, first_ref, second_ref):
-    total = total_ref[0:20, 0:320]
+            row, col = 20 * (z % 2), 320 * (z // 2)
+            out_ref[4 * half + z, 0:20, 0:320] = total[row : row + 20, col : col + 320]
+
+
+def last_kernel(place_ref, blocks_ref, first_ref, second_ref):
+    total = blocks_ref[0, 0:20, 0:320]
+    for z in range(1, 8):
+        total += blocks_ref[z, 0:20, 0:320]
     even = place_ref[1] == 0
     first_ref[...] = jnp.where(even, total[:, 0:160], total[:, 160:320])
     second_ref[...] = jnp.where(even, total[:, 160:320], total[:, 0:160])
@@ -440,26 +448,26 @@
     act = activation.transpose(1, 0, 2).reshape(points, width)
     cot = cotangent.transpose(1, 0, 2).reshape(points, width)
     place = jnp.stack([lax.axis_index(axis) for axis in (LON, "co", "yl", "yh", "x")])
-    block, own, other = mlp(place, mixing, act, cot, weight_in, weight_out)
+    block, own, other = mlp(place, mixing.T, act, cot, weight_in, weight_out)
     arrived = lax.ppermute(other, "co", [(0, 1), (1, 0)])
-    cut = small(cut_kernel, (place, own, arrived), [(160, 640)] * 8, 1, name="cut")
-    spread = across(after(block, cut[0]))
-    moved = exchange_x(cut[:4]) + exchange_y(cut[4:])
-    swapped = small(
-        swap_kernel, (place, *moved), [(40, 640)] * 8, 1, (pltpu.VMEM((4, 40, 640), F32),), "swap"
-    )
-    moved = exchange_y(swapped[:4]) + exchange_x(swapped[4:])
+    half, *pieces = cut(place, own, arrived)
+    half = lax.psum_scatter(half, "x", scatter_dimension=0, tiled=True)
+    moved = exchange_y(pieces)
+    spread = across(block)
     kernel = kernel_spectrum(kernels)
-    data, first, final, own_mixing = spectrum(after(spread, swapped[0]))
+    data, first, final, own_mixing = spectrum(after(spread, moved))
     forward = [(i, i + 1) for i in range(3)]
     backward = [(target, source) for source, target in forward]
     before = lax.ppermute(final, LAT, forward)
-    after_rows = lax.ppermute(first, LAT, backward)
-    sent = filtered(own_mixing, data, before, after_rows, kernel)
-    (blocks,) = small(stack_kernel, moved, [(192, 384)], name="stack")
-    result = across(after(sent, blocks))
-    total = lax.psum_scatter(blocks, "z", scatter_dimension=0, tiled=True)
-    grad_in, grad_out = small(last_kernel, (place, total), [(20, 160)] * 2, 1, name="last")
+    beyond = lax.ppermute(first, LAT, backward)
+    result = across(filtered(own_mixing, data, before, beyond, kernel))
+    swapped = small(
+        swap_kernel, (place, half, *moved), [(40, 640)] * 8, 1, (pltpu.VMEM((8, 40, 640), F32),), "swap"
+    )
+    moved = exchange_y(swapped[:4]) + exchange_x(swapped[4:])
+    (blocks,) = small(stack_kernel, moved, [(8, 24, 384)], name="stack")
+    blocks = lax.all_to_all(blocks, "z", split_axis=0, concat_axis=0, tiled=True)
+    grad_in, grad_out = small(last_kernel, (place, blocks), [(20, 160)] * 2, 1, name="last")
     field = unpack(result).reshape(COLS, ROWS, width).transpose(1, 0, 2)
     return (field, grad_in, grad_out)
 

time: 189 us -> 149 us (0.79)
  the two profiles are of different devices: /device:TPU:4 before, /device:TPU:1 now
where the time goes in v4:
time: 149 us; the launch traced here: 146 us
  starting transfers between devices  47.7 us (32%)
  waiting for transfers between devices  45.5 us (31%)
  Pallas kernels  34 us (23%)
  between operations  14.2 us (10%)
  local copies, waits for them, and re-layouts  4.6 us (3%)
    all_to_all x2, starting transfers between devices, across(): return lax.all_to_all(block, LON, split_axis=0, concat_axis=0, tiled=True)  23.5 us
    pallas_call x1, Pallas kernels, mlp(): pl.pallas_call(mlp_kernel, grid=(units // tile,), in_specs=[scalars, scal...  15.9 us
    all_to_all x2, waiting for transfers between devices, across(): return lax.all_to_all(block, LON, split_axis=0, concat_axis=0, tiled=True)  14.2 us
    ppermute x6, waiting for transfers between devices, exchange_y(): lax.ppermute(pieces[m], ('yl', 'yh'), [(i, i ^ m) for i in range(4)])  10.8 us
    all_to_all x1, waiting for transfers between devices, per_device(): lax.all_to_all(blocks, 'z', split_axis=0, concat_axis=0, tiled=True)  8.29 us
    ppermute x6, starting transfers between devices, exchange_y(): lax.ppermute(pieces[m], ('yl', 'yh'), [(i, i ^ m) for i in range(4)])  6.68 us
    ppermute x1, waiting for transfers between devices, per_device(): arrived = lax.ppermute(other, 'co', [(0, 1), (1, 0)])  5.68 us
    pallas_call x1, Pallas kernels, cut(): pl.pallas_call(cut_kernel, grid=(4,), in_specs=[pl.BlockSpec(memory_space...  5.58 us
  transfers between devices with their start and end apart: 16, of which 9 were waited for; matrix products, arithmetic and copies ran while one was open for 0% of the time, Pallas kernels for 8%

profile of v4, /device:TPU:1, one launch (start us, length us, event | category | flops | bytes accessed | tf_op | source)
XLA Modules:
  0.0 145.9 jit_solution(15992319215074299343)
XLA Ops:
  7.2 0.0 reduce-scatter.2.cloned.1.call-start
  7.2 0.6 stack.24.place_ref
  7.9 15.9 %mlp.1 = (f32[64,16,128]{2,1,0:T(8,128)}, f32[1280,640]{1,0:T(8,128)}, f32[1280,640]{1,0:T(8,128)}) custom-call(s32[5]{0:T(128)} %stack.24.place_ref, f32[3,10]{1,0:T(4,128)} %bitcast.22, f32[192,640]{1,0:T(8,128)} %bitcast.20, f32[192,640]{1,0:T(8,128)} %bitcast.21, f32[1280,640]{1,0:T(8,128)} %in_ref.1, f32[1280,640]{1,0:T(8,128)} %out_ref.1), custom_call_target="tpu_custom_call" | custom-call | flops 4718592000 | bytes 15000000 | tf_op jit(solution)/shard_map/mlp/pallas_call | solution.py:169
  23.8 3.2 %collective-permute-start = (f32[1280,640]{1,0:T(8,128)}, f32[1280,640]{1,0:T(8,128)S(1)}, u32[]{:S(2)}, u32[]{:S(2)}) collective-permute-start(f32[1280,640]{1,0:T(8,128)} %get-tuple-element.28), channel_id=1, source_target_pairs={{0,64},{64,0},{1,65},{65,1},{2,66},{66,2},{3,67},{67,3},{4,68},{68... | collective-permute-start | bytes 9830408 | tf_op jit(solution)/shard_map/ppermute | solution.py:452
  27.0 5.7 %collective-permute-done.arrived_ref = f32[1280,640]{1,0:T(8,128)S(1)} collective-permute-done((f32[1280,640]{1,0:T(8,128)}, f32[1280,640]{1,0:T(8,128)S(1)}, u32[]{:S(2)}, u32[]{:S(2)}) %collective-permute-start) | collective-permute-done | bytes 3276832 | tf_op jit(solution)/shard_map/ppermute | solution.py:452
  32.7 0.0 copy-start.10
  32.7 1.7 %copy-done.10 = f32[1280,640]{1,0:T(8,128)} copy-done((f32[1280,640]{1,0:T(8,128)}, f32[1280,640]{1,0:T(8,128)S(1)}, u32[]{:S(2)}) %copy-start.10) | copy-done | bytes 3276824
  34.4 5.6 %cut.1 = (f32[640,640]{1,0:T(8,128)}, f32[160,640]{1,0:T(8,128)}, f32[160,640]{1,0:T(8,128)}, f32[160,640]{1,0:T(8,128)}, f32[160,640]{1,0:T(8,128)}) custom-call(s32[5]{0:T(128)} %stack.24.place_ref, f32[1280,640]{1,0:T(8,128)} %get-tuple-element.27.own_ref, f32[1280,640]{1,0:T(8,128)} %copy-done.10), custom_call_target="tpu_custom_call" | custom-call | flops 2000000 | bytes 10000000 | tf_op jit(solution)/shard_map/cut/pallas_call | solution.py:219
  40.0 0.0 copy-start.3
  40.0 0.0 reduce-scatter.2.cloned.1.call-update
  40.1 12.7 %all-to-all-start = ((f32[64,16,128]{2,1,0:T(8,128)}), f32[64,16,128]{2,1,0:T(8,128)S(1)}, u32[]{:S(2)}, u32[]{:S(2)}) async-start(f32[64,16,128]{2,1,0:T(8,128)} %get-tuple-element.26), calls=%async_computation | async-start | bytes 1048576 | tf_op jit(solution)/shard_map/all_to_all | solution.py:442
  52.7 2.6 %collective-permute-start.1 = (f32[160,640]{1,0:T(8,128)}, f32[160,640]{1,0:T(8,128)S(1)}, u32[]{:S(2)}, u32[]{:S(2)}) collective-permute-start(f32[160,640]{1,0:T(8,128)} %get-tuple-element.30), channel_id=1, source_target_pairs={{0,1},{1,0},{128,129},{129,128},{2,3},{3,2},{130,131},{131,130},{4... | collective-permute-start | bytes 1228808 | tf_op jit(solution)/shard_map/ppermute | solution.py:289
  55.3 0.4 collective-permute-start.2
  55.7 0.3 collective-permute-start.3
  56.1 14.2 %all-to-all-done.block_ref = f32[64,16,128]{2,1,0:T(8,128)S(1)} async-done(((f32[64,16,128]{2,1,0:T(8,128)}), f32[64,16,128]{2,1,0:T(8,128)S(1)}, u32[]{:S(2)}, u32[]{:S(2)}) %all-to-all-start) | async-done | bytes 524320 | tf_op jit(solution)/shard_map/all_to_all | solution.py:442
  70.3 0.0 copy-start.4
  70.3 0.0 copy-start.5
  70.3 0.0 collective-permute-done.1.refs_1_
  70.3 8.4 %collective-permute-done.2.refs_2_ = f32[160,640]{1,0:T(8,128)} collective-permute-done((f32[160,640]{1,0:T(8,128)}, f32[160,640]{1,0:T(8,128)}, u32[]{:S(2)}, u32[]{:S(2)}) %collective-permute-start.2) | collective-permute-done | bytes 409632 | tf_op jit(solution)/shard_map/ppermute | solution.py:289
  78.7 1.7 %collective-permute-done.3.refs_3_ = f32[160,640]{1,0:T(8,128)} collective-permute-done((f32[160,640]{1,0:T(8,128)}, f32[160,640]{1,0:T(8,128)}, u32[]{:S(2)}, u32[]{:S(2)}) %collective-permute-start.3) | collective-permute-done | bytes 409632 | tf_op jit(solution)/shard_map/ppermute | solution.py:289
  80.3 0.0 copy-done.2
  80.3 0.0 copy-done.3
  80.3 1.0 spectrum.1
  81.4 2.7 %collective-permute-start.4 = (f32[30,768]{1,0:T(8,128)S(1)}, f32[30,768]{1,0:T(8,128)S(1)}, u32[]{:S(2)}, u32[]{:S(2)}) collective-permute-start(f32[30,768]{1,0:T(8,128)S(1)} %get-tuple-element.36), channel_id=1, source_target_pairs={{0,64},{64,128},{128,192},{1,65},{65,129},{129,193},{2,66},{66,130... | collective-permute-start | bytes 276488 | tf_op jit(solution)/shard_map/ppermute | solution.py:461
  84.1 1.9 %collective-permute-start.5 = (f32[30,768]{1,0:T(8,128)S(1)}, f32[30,768]{1,0:T(8,128)S(1)}, u32[]{:S(2)}, u32[]{:S(2)}) collective-permute-start(f32[30,768]{1,0:T(8,128)S(1)} %get-tuple-element.37), channel_id=1, source_target_pairs={{64,0},{128,64},{192,128},{65,1},{129,65},{193,129},{66,2},{130,66... | collective-permute-start | bytes 276488 | tf_op jit(solution)/shard_map/ppermute | solution.py:462
  86.0 0.0 copy-done.4
  86.0 0.0 copy-done.5
  86.0 0.0 copy-start.6
  86.0 1.2 copy-done.6
  87.2 0.0 copy-start
  87.2 0.0 copy-start.1
  87.2 1.4 kernel_spectrum.1.kernel_ref
  88.6 0.0 collective-permute-done.4.before_ref
  88.6 1.4 collective-permute-done.5.after_ref
  90.0 0.0 copy-done
  90.0 0.0 copy-done.1
  90.0 0.0 copy-start.7
  90.0 4.2 %filter.1 = f32[64,16,128]{2,1,0:T(8,128)} custom-call(f32[1,128]{1,0:T(1,128)S(1)} %get-tuple-element.34.mixing_ref, f32[160,768]{1,0:T(8,128)S(1)} %get-tuple-element.35.data_ref, f32[30,768]{1,0:T(8,128)S(1)} %collective-permute-done.4.before_ref, f32[30,768]{1,0:T(8,128)S(1)} %collective-permute-done.5.after_ref, ...), custom_call_target="tpu_custom_call" | custom-call | flops 566231040 | bytes 5000000 | tf_op jit(solution)/shard_map/filter/pallas_call | solution.py:399
  94.2 10.8 %all-to-all-start.1 = ((f32[64,16,128]{2,1,0:T(8,128)}), f32[64,16,128]{2,1,0:T(8,128)S(1)}, u32[]{:S(2)}, u32[]{:S(2)}) async-start(f32[64,16,128]{2,1,0:T(8,128)} %filter.1), calls=%async_computation.1 | async-start | bytes 1048576 | tf_op jit(solution)/shard_map/all_to_all | solution.py:442
  105.0 0.0 reduce-scatter.2.cloned.1.call-done.half_ref
  105.0 0.0 copy-done.7
  105.0 0.0 copy-done.9
  105.1 0.0 copy-start.8
  105.1 1.0 copy-done.8
  106.1 1.4 swap.1
  107.5 2.6 %collective-permute-start.6 = (f32[40,640]{1,0:T(8,128)S(1)}, f32[40,640]{1,0:T(8,128)S(1)}, u32[]{:S(2)}, u32[]{:S(2)}) collective-permute-start(f32[40,640]{1,0:T(8,128)S(1)} %get-tuple-element.40), channel_id=1, source_target_pairs={{0,1},{1,0},{128,129},{129,128},{2,3},{3,2},{130,131},{131,130},{4... | collective-permute-start | bytes 307208 | tf_op jit(solution)/shard_map/ppermute | solution.py:289
  110.1 0.0 collective-permute-start.7
  110.1 0.7 collective-permute-start.8
  110.8 1.0 collective-permute-start.9
  111.9 2.6 %collective-permute-start.10 = (f32[40,640]{1,0:T(8,128)S(1)}, f32[40,640]{1,0:T(8,128)S(1)}, u32[]{:S(2)}, u32[]{:S(2)}) collective-permute-start(f32[40,640]{1,0:T(8,128)S(1)} %get-tuple-element.45), channel_id=1, source_target_pairs={{0,32},{16,48},{32,0},{48,16},{1,33},{17,49},{33,1},{49,17},{2,34}... | collective-permute-start | bytes 307208 | tf_op jit(solution)/shard_map/ppermute | solution.py:283
  114.4 0.0 collective-permute-done.6.refs_1_
  114.5 1.6 %collective-permute-start.11 = (f32[40,640]{1,0:T(8,128)S(1)}, f32[40,640]{1,0:T(8,128)S(1)}, u32[]{:S(2)}, u32[]{:S(2)}) collective-permute-start(f32[40,640]{1,0:T(8,128)S(1)} %get-tuple-element.46), channel_id=1, source_target_pairs={{0,48},{16,0},{32,16},{48,32},{1,49},{17,1},{33,17},{49,33},{2,50}... | collective-permute-start | bytes 307208 | tf_op jit(solution)/shard_map/ppermute | solution.py:283
  116.1 0.7 collective-permute-done.7.refs_2_
  116.8 0.0 collective-permute-done.8.refs_3_
  116.8 1.7 %collective-permute-done.9.refs_5_ = f32[40,640]{1,0:T(8,128)S(1)} collective-permute-done((f32[40,640]{1,0:T(8,128)S(1)}, f32[40,640]{1,0:T(8,128)S(1)}, u32[]{:S(2)}, u32[]{:S(2)}) %collective-permute-start.9) | collective-permute-done | bytes 102432 | tf_op jit(solution)/shard_map/ppermute | solution.py:283
  118.4 3.5 %collective-permute-done.10.refs_6_ = f32[40,640]{1,0:T(8,128)S(1)} collective-permute-done((f32[40,640]{1,0:T(8,128)S(1)}, f32[40,640]{1,0:T(8,128)S(1)}, u32[]{:S(2)}, u32[]{:S(2)}) %collective-permute-start.10) | collective-permute-done | bytes 102432 | tf_op jit(solution)/shard_map/ppermute | solution.py:283
  121.9 0.0 collective-permute-done.11.refs_7_
  121.9 0.8 stack.25
  122.8 0.0 all-to-all-done.1.block_ref
  122.8 4.4 %all-to-all-start.2 = ((f32[8,24,384]{2,1,0:T(8,128)}), f32[8,24,384]{2,1,0:T(8,128)S(1)}, u32[]{:S(2)}, u32[]{:S(2)}) async-start(f32[8,24,384]{2,1,0:T(8,128)} %stack.25), calls=%async_computation.3 | async-start | bytes 589824 | tf_op jit(solution)/shard_map/all_to_all | solution.py:469
  127.2 0.0 copy-done.11
  127.2 2.3 %unpack.1 = f32[192,640]{1,0:T(8,128)} custom-call(f32[64,16,128]{2,1,0:T(8,128)} %copy-done.11), custom_call_target="tpu_custom_call" | custom-call | tf_op jit(solution)/shard_map/unpack/pallas_call | solution.py:432
  129.5 8.3 %all-to-all-done.2.blocks_ref = f32[8,24,384]{2,1,0:T(8,128)S(1)} async-done(((f32[8,24,384]{2,1,0:T(8,128)}), f32[8,24,384]{2,1,0:T(8,128)S(1)}, u32[]{:S(2)}, u32[]{:S(2)}) %all-to-all-start.2) | async-done | bytes 294944 | tf_op jit(solution)/shard_map/all_to_all | solution.py:469
  137.8 1.3 last.1
  (3 shorter events, 0.0 us)
Async XLA Ops:
  7.2 97.9 %reduce-scatter.2.cloned.1.call-start = ((), (), s32[]{:S(2)}) async-start(), calls=%async_computation.4 | async-start | bytes 2048000 | tf_op jit(solution)/shard_map/reduce_scatter | solution.py:454
  23.8 8.9 %collective-permute-start = (f32[1280,640]{1,0:T(8,128)}, f32[1280,640]{1,0:T(8,128)S(1)}, u32[]{:S(2)}, u32[]{:S(2)}) collective-permute-start(f32[1280,640]{1,0:T(8,128)} %get-tuple-element.28), channel_id=1, source_target_pairs={{0,64},{64,0},{1,65},{65,1},{2,66},{66,2},{3,67},{67,3},{4,68},{68... | collective-permute-start | bytes 9830408 | tf_op jit(solution)/shard_map/ppermute | solution.py:452
  32.7 1.7 %copy-start.10 = (f32[1280,640]{1,0:T(8,128)}, f32[1280,640]{1,0:T(8,128)S(1)}, u32[]{:S(2)}) copy-start(f32[1280,640]{1,0:T(8,128)S(1)} %collective-permute-done.arrived_ref) | copy-start | bytes 9830404
  40.0 40.3 %copy-start.2 = (bf16[768,768]{1,0:T(8,128)(2,1)S(1)}, bf16[768,768]{1,0:T(8,128)(2,1)}, u32[]{:S(2)}) copy-start(bf16[768,768]{1,0:T(8,128)(2,1)} %constant.39.clone.top_ref) | copy-start | bytes 3538948
  40.0 40.3 %copy-start.3 = (bf16[768,768]{1,0:T(8,128)(2,1)S(1)}, bf16[768,768]{1,0:T(8,128)(2,1)}, u32[]{:S(2)}) copy-start(bf16[768,768]{1,0:T(8,128)(2,1)} %constant.40.clone.low_ref) | copy-start | bytes 3538948
  40.1 30.2 %all-to-all-start = ((f32[64,16,128]{2,1,0:T(8,128)}), f32[64,16,128]{2,1,0:T(8,128)S(1)}, u32[]{:S(2)}, u32[]{:S(2)}) async-start(f32[64,16,128]{2,1,0:T(8,128)} %get-tuple-element.26), calls=%async_computation | async-start | bytes 1048576 | tf_op jit(solution)/shard_map/all_to_all | solution.py:442
  52.7 17.6 %collective-permute-start.1 = (f32[160,640]{1,0:T(8,128)}, f32[160,640]{1,0:T(8,128)S(1)}, u32[]{:S(2)}, u32[]{:S(2)}) collective-permute-start(f32[160,640]{1,0:T(8,128)} %get-tuple-element.30), channel_id=1, source_target_pairs={{0,1},{1,0},{128,129},{129,128},{2,3},{3,2},{130,131},{131,130},{4... | collective-permute-start | bytes 1228808 | tf_op jit(solution)/shard_map/ppermute | solution.py:289
  55.3 23.3 %collective-permute-start.2 = (f32[160,640]{1,0:T(8,128)}, f32[160,640]{1,0:T(8,128)}, u32[]{:S(2)}, u32[]{:S(2)}) collective-permute-start(f32[160,640]{1,0:T(8,128)} %get-tuple-element.31), channel_id=1, source_target_pairs={{0,128},{1,129},{128,0},{129,1},{2,130},{3,131},{130,2},{131,3},{4... | collective-permute-start | bytes 1228808 | tf_op jit(solution)/shard_map/ppermute | solution.py:289
  55.7 24.6 %collective-permute-start.3 = (f32[160,640]{1,0:T(8,128)}, f32[160,640]{1,0:T(8,128)}, u32[]{:S(2)}, u32[]{:S(2)}) collective-permute-start(f32[160,640]{1,0:T(8,128)} %get-tuple-element.32), channel_id=1, source_target_pairs={{0,129},{1,128},{128,1},{129,0},{2,131},{3,130},{130,3},{131,2},{4... | collective-permute-start | bytes 1228808 | tf_op jit(solution)/shard_map/ppermute | solution.py:289
  70.3 15.7 %copy-start.4 = (bf16[768,768]{1,0:T(8,128)(2,1)S(1)}, bf16[768,768]{1,0:T(8,128)(2,1)}, u32[]{:S(2)}) copy-start(bf16[768,768]{1,0:T(8,128)(2,1)} %constant.37.clone.top_ref) | copy-start | bytes 3538948
  70.3 15.7 %copy-start.5 = (bf16[768,768]{1,0:T(8,128)(2,1)S(1)}, bf16[768,768]{1,0:T(8,128)(2,1)}, u32[]{:S(2)}) copy-start(bf16[768,768]{1,0:T(8,128)(2,1)} %constant.38.clone.low_ref) | copy-start | bytes 3538948
  81.4 7.3 %collective-permute-start.4 = (f32[30,768]{1,0:T(8,128)S(1)}, f32[30,768]{1,0:T(8,128)S(1)}, u32[]{:S(2)}, u32[]{:S(2)}) collective-permute-start(f32[30,768]{1,0:T(8,128)S(1)} %get-tuple-element.36), channel_id=1, source_target_pairs={{0,64},{64,128},{128,192},{1,65},{65,129},{129,193},{2,66},{66,130... | collective-permute-start | bytes 276488 | tf_op jit(solution)/shard_map/ppermute | solution.py:461
  84.1 5.9 %collective-permute-start.5 = (f32[30,768]{1,0:T(8,128)S(1)}, f32[30,768]{1,0:T(8,128)S(1)}, u32[]{:S(2)}, u32[]{:S(2)}) collective-permute-start(f32[30,768]{1,0:T(8,128)S(1)} %get-tuple-element.37), channel_id=1, source_target_pairs={{64,0},{128,64},{192,128},{65,1},{129,65},{193,129},{66,2},{130,66... | collective-permute-start | bytes 276488 | tf_op jit(solution)/shard_map/ppermute | solution.py:462
  86.0 1.2 copy-start.6
  87.2 2.8 %copy-start = (bf16[768,768]{1,0:T(8,128)(2,1)S(1)}, bf16[768,768]{1,0:T(8,128)(2,1)}, u32[]{:S(2)}) copy-start(bf16[768,768]{1,0:T(8,128)(2,1)} %constant.41.clone.top_ref) | copy-start | bytes 3538948
  87.2 2.8 %copy-start.1 = (bf16[768,768]{1,0:T(8,128)(2,1)S(1)}, bf16[768,768]{1,0:T(8,128)(2,1)}, u32[]{:S(2)}) copy-start(bf16[768,768]{1,0:T(8,128)(2,1)} %constant.42.clone.low_ref) | copy-start | bytes 3538948
  90.0 15.0 %copy-start.7 = (f32[160,640]{1,0:T(8,128)S(1)}, f32[160,640]{1,0:T(8,128)}, u32[]{:S(2)}) copy-start(f32[160,640]{1,0:T(8,128)} %get-tuple-element.29.refs_0_) | copy-start | bytes 1228804
  90.0 15.0 %copy-start.9 = (s32[5]{0:T(128)S(1)}, s32[5]{0:T(128)}, u32[]{:S(2)}) copy-start(s32[5]{0:T(128)} %stack.24.place_ref) | copy-start | bytes 64
  94.2 28.6 %all-to-all-start.1 = ((f32[64,16,128]{2,1,0:T(8,128)}), f32[64,16,128]{2,1,0:T(8,128)S(1)}, u32[]{:S(2)}, u32[]{:S(2)}) async-start(f32[64,16,128]{2,1,0:T(8,128)} %filter.1), calls=%async_computation.1 | async-start | bytes 1048576 | tf_op jit(solution)/shard_map/all_to_all | solution.py:442
  105.1 1.0 copy-start.8
  107.5 7.0 %collective-permute-start.6 = (f32[40,640]{1,0:T(8,128)S(1)}, f32[40,640]{1,0:T(8,128)S(1)}, u32[]{:S(2)}, u32[]{:S(2)}) collective-permute-start(f32[40,640]{1,0:T(8,128)S(1)} %get-tuple-element.40), channel_id=1, source_target_pairs={{0,1},{1,0},{128,129},{129,128},{2,3},{3,2},{130,131},{131,130},{4... | collective-permute-start | bytes 307208 | tf_op jit(solution)/shard_map/ppermute | solution.py:289
  110.1 6.7 %collective-permute-start.7 = (f32[40,640]{1,0:T(8,128)S(1)}, f32[40,640]{1,0:T(8,128)S(1)}, u32[]{:S(2)}, u32[]{:S(2)}) collective-permute-start(f32[40,640]{1,0:T(8,128)S(1)} %get-tuple-element.41), channel_id=1, source_target_pairs={{0,128},{1,129},{128,0},{129,1},{2,130},{3,131},{130,2},{131,3},{4... | collective-permute-start | bytes 307208 | tf_op jit(solution)/shard_map/ppermute | solution.py:289
  110.1 6.7 %collective-permute-start.8 = (f32[40,640]{1,0:T(8,128)S(1)}, f32[40,640]{1,0:T(8,128)S(1)}, u32[]{:S(2)}, u32[]{:S(2)}) collective-permute-start(f32[40,640]{1,0:T(8,128)S(1)} %get-tuple-element.42), channel_id=1, source_target_pairs={{0,129},{1,128},{128,1},{129,0},{2,131},{3,130},{130,3},{131,2},{4... | collective-permute-start | bytes 307208 | tf_op jit(solution)/shard_map/ppermute | solution.py:289
  110.8 7.6 %collective-permute-start.9 = (f32[40,640]{1,0:T(8,128)S(1)}, f32[40,640]{1,0:T(8,128)S(1)}, u32[]{:S(2)}, u32[]{:S(2)}) collective-permute-start(f32[40,640]{1,0:T(8,128)S(1)} %get-tuple-element.44), channel_id=1, source_target_pairs={{0,16},{16,32},{32,48},{48,0},{1,17},{17,33},{33,49},{49,1},{2,18}... | collective-permute-start | bytes 307208 | tf_op jit(solution)/shard_map/ppermute | solution.py:283
  111.9 10.1 %collective-permute-start.10 = (f32[40,640]{1,0:T(8,128)S(1)}, f32[40,640]{1,0:T(8,128)S(1)}, u32[]{:S(2)}, u32[]{:S(2)}) collective-permute-start(f32[40,640]{1,0:T(8,128)S(1)} %get-tuple-element.45), channel_id=1, source_target_pairs={{0,32},{16,48},{32,0},{48,16},{1,33},{17,49},{33,1},{49,17},{2,34}... | collective-permute-start | bytes 307208 | tf_op jit(solution)/shard_map/ppermute | solution.py:283
  114.5 7.5 %collective-permute-start.11 = (f32[40,640]{1,0:T(8,128)S(1)}, f32[40,640]{1,0:T(8,128)S(1)}, u32[]{:S(2)}, u32[]{:S(2)}) collective-permute-start(f32[40,640]{1,0:T(8,128)S(1)} %get-tuple-element.46), channel_id=1, source_target_pairs={{0,48},{16,0},{32,16},{48,32},{1,49},{17,1},{33,17},{49,33},{2,50}... | collective-permute-start | bytes 307208 | tf_op jit(solution)/shard_map/ppermute | solution.py:283
  122.8 4.4 %copy-start.11 = (f32[64,16,128]{2,1,0:T(8,128)}, f32[64,16,128]{2,1,0:T(8,128)S(1)}, u32[]{:S(2)}) copy-start(f32[64,16,128]{2,1,0:T(8,128)S(1)} %all-to-all-done.1.block_ref) | copy-start | bytes 1572868
  122.8 15.0 %all-to-all-start.2 = ((f32[8,24,384]{2,1,0:T(8,128)}), f32[8,24,384]{2,1,0:T(8,128)S(1)}, u32[]{:S(2)}, u32[]{:S(2)}) async-start(f32[8,24,384]{2,1,0:T(8,128)} %stack.25), calls=%async_computation.3 | async-start | bytes 589824 | tf_op jit(solution)/shard_map/all_to_all | solution.py:469
Sparse Core Ops, SparseCore 0:
  40.2 35.0 reduce-scatter.1

commit v5 on v4

--- a/solution.py
+++ b/solution.py
@@ -100,169 +100,178 @@
     out_ref[:, 15, :] = weights
 
 
+def pack_kernel(place_ref, mixing_ref, unit_ref, arrived_ref, block_ref):
+    pack(unit_ref[...] + arrived_ref[...], mixing_ref, place_ref[0], block_ref)
+
+
+def along_x(place_ref, m):
+    return lax.rem(place_ref[4] + m, 4)
+
+
+def along_y(place_ref, m):
+    upper, right = place_ref[2], place_ref[3]
+    return 2 * (1 - upper if m & 2 else upper) + (1 - right if m & 1 else right)
+
+
+def low_high(rows):
+    low = jnp.concatenate([rows[40 * z : 40 * z + 20] for z in range(4)], axis=0)
+    high = jnp.concatenate([rows[40 * z + 20 : 40 * z + 40] for z in range(4)], axis=0)
+    return low, high
+
+
 def mlp_kernel(
     place_ref,
-    mixing_ref,
     act_ref,
+    act_other_ref,
     cot_ref,
+    cot_other_ref,
     in_ref,
     out_ref,
-    block_ref,
     own_ref,
     other_ref,
-    unit_ref,
-    act_top,
-    act_low,
-    cot_top,
-    cot_low,
-    cot_cols_top,
-    cot_cols_low,
+    *refs,
 ):
+    outs, (unit_ref, act_top, act_low, cot_top, cot_low, kept_ref) = refs[:4], refs[4:]
     step = pl.program_id(0)
+    core = place_ref[1]
+    points = act_ref.shape[0]
 
     @pl.when(step == 0)
     def _():
-        act, cot = act_ref[...], cot_ref[...]
-        act_top[...], act_low[...] = split(act)
-        cot_top[...], cot_low[...] = split(cot)
-        pairs = [cot[:, 160:320], cot[:, 0:160], cot[:, 480:640], cot[:, 320:480]]
-        cot_cols_top[...], cot_cols_low[...] = split(jnp.concatenate(pairs, axis=1))
-
-    w_in, w_out = split(in_ref[...]), split(out_ref[...])
-    preact = dot3((act_top[...], act_low[...]), w_in, ((1,), (1,)))
+        act_top[0:points, :], act_low[0:points, :] = split(act_ref[...])
+        act_top[points:, :], act_low[points:, :] = split(act_other_ref[...])
+        cot_top[0:points, :], cot_low[0:points, :] = split(cot_ref[...])
+        cot_top[points:, :], cot_low[points:, :] = split(cot_other_ref[...])
+
+    act, cot = (act_top[...], act_low[...]), (cot_top[...], cot_low[...])
+    w_in = split(in_ref[...].reshape(320, 640))
+    w_out = split(out_ref[...].reshape(320, 640))
+    preact = dot3(act, w_in, ((1,), (1,)))
     cdf = 0.5 * (1.0 + lax.erf(preact * (1.0 / math.sqrt(2.0))))
     density = jnp.exp(-0.5 * preact * preact) * (1.0 / math.sqrt(2.0 * math.pi))
     hidden = split(preact * cdf)
     slope = cdf + preact * density
-    grad = split(dot3((cot_top[...], cot_low[...]), w_out, ((1,), (1,))) * slope)
+    grad = split(dot3(cot, w_out, ((1,), (1,))) * slope)
     term = dot3(grad, w_in, ((1,), (0,)))
+    contract = ((0,), (0,))
+    first = dot3(grad, act, contract)
+    second = dot3(hidden, cot, contract)
 
     @pl.when(step == 0)
     def _():
-        unit_ref[...] = cot_ref[...] + term
-
-    @pl.when(step > 0)
-    def _():
-        unit_ref[...] += term
-
-    contract = ((0,), (0,))
-    first = dot3(grad, (act_top[...], act_low[...]), contract)
-    second = dot3(hidden, (cot_cols_top[...], cot_cols_low[...]), contract)
-    lane = lax.broadcasted_iota(jnp.int32, first.shape, 1)
-    even = (lane < 160) | ((lane >= 320) & (lane < 480))
-    mine = even == (place_ref[1] == 0)
-    own_ref[...] = jnp.where(mine, first, second)
-    other_ref[...] = jnp.where(mine, second, first)
-
-    @pl.when(step == pl.num_programs(0) - 1)
-    def _():
-        pack(unit_ref[...], mixing_ref, place_ref[0], block_ref)
-
-
-def mlp(place, mixing, act, cot, weight_in, weight_out):
+        unit_ref[...] = term
+
+    @pl.when(core == 0)
+    def _():
+        for x in range(2):
+            rows = slice(160 * x, 160 * x + 160)
+            kept_ref[2 * step + x, :, 0:640] = first[rows]
+            kept_ref[2 * step + x, :, 640:1280] = second[rows]
+
+    @pl.when(core == 1)
+    def _():
+        lanes = pl.ds(pl.multiple_of(640 * step, 128), 640)
+        for x in range(2):
+            rows = slice(160 * x, 160 * x + 160)
+            parts = zip(low_high(first[rows]), low_high(second[rows]))
+            for right, (a, b) in enumerate(parts):
+                for upper in range(2):
+                    cols = slice(320 * upper, 320 * upper + 320)
+                    piece = jnp.concatenate([a[:, cols], b[:, cols]], axis=1)
+                    kept_ref[2 * upper + right, 80 * x : 80 * x + 80, lanes] = piece
+
+    @pl.when(step == 1)
+    def _():
+        total = unit_ref[...] + term
+        own_ref[...] = cot_ref[...] + total[0:points]
+        other_ref[...] = total[points:]
+        for m in range(4):
+            index = jnp.where(core == 0, along_x(place_ref, m), along_y(place_ref, m))
+            outs[m][...] = kept_ref[index]
+
+
+def mlp(place, act, act_other, cot, cot_other, weight_in, weight_out):
     points, width = act.shape
     units = weight_in.shape[0]
-    tile = 256
-    full = lambda shape: pl.BlockSpec(shape, lambda i: (0,) * len(shape))
-    rows = pl.BlockSpec((tile, width), lambda i: (i, 0))
-    scalars = pl.BlockSpec(memory_space=pltpu.SMEM)
+    full = lambda shape: pl.BlockSpec(shape, lambda i, place: (0,) * len(shape))
+    rows = pl.BlockSpec((2, None, 160, width), lambda i, place: (i, place[1], 0, 0))
     return pl.pallas_call(
         mlp_kernel,
-        grid=(units // tile,),
-        in_specs=[scalars, scalars, full((points, width)), full((points, width)), rows, rows],
-        out_specs=[full((SHARDS, 16, 128)), rows, rows],
-        out_shape=[
-            jax.ShapeDtypeStruct((SHARDS, 16, 128), F32),
-            jax.ShapeDtypeStruct((units, width), F32),
-            jax.ShapeDtypeStruct((units, width), F32),
-        ],
-        scratch_shapes=[pltpu.VMEM((points, width), F32)]
-        + [pltpu.VMEM((points, width), BF16)] * 6,
+        grid_spec=pltpu.PrefetchScalarGridSpec(
+            num_scalar_prefetch=1,
+            grid=(2,),
+            in_specs=[full((points, width))] * 4 + [rows, rows],
+            out_specs=[full((points, width))] * 2 + [full((160, 1280))] * 4,
+            scratch_shapes=[pltpu.VMEM((2 * points, width), F32)]
+            + [pltpu.VMEM((2 * points, width), BF16)] * 4
+            + [pltpu.VMEM((4, 160, 1280), F32)],
+        ),
+        out_shape=[jax.ShapeDtypeStruct((points, width), F32)] * 2
+        + [jax.ShapeDtypeStruct((160, 1280), F32)] * 4,
         compiler_params=params(60),
-        cost_estimate=cost(30 * points * width * units, 15_000_000),
+        cost_estimate=cost(30 * points * width * units, 12_000_000),
         name="mlp",
-    )(place, mixing, act, cot, weight_in, weight_out)
-
-
-def partner(place_ref, m):
-    upper, right = place_ref[2], place_ref[3]
-    return 2 * (1 - upper if m & 2 else upper) + (1 - right if m & 1 else right)
-
-
-def by_chip(rows):
-    low = jnp.concatenate([rows[40 * z : 40 * z + 20] for z in range(4)], axis=0)
-    high = jnp.concatenate([rows[40 * z + 20 : 40 * z + 40] for z in range(4)], axis=0)
-    return [low[:, 0:320], high[:, 0:320], low[:, 320:640], high[:, 320:640]]
-
-
-def cut_kernel(place_ref, own_ref, arrived_ref, half_ref, *refs):
-    outs, kept_ref = refs[:4], refs[4]
-    x = pl.program_id(0)
-    half_ref[...] = own_ref[0:160, :] + arrived_ref[0:160, :]
-    pieces = by_chip(own_ref[160:320, :] + arrived_ref[160:320, :])
-    for at in range(4):
-
-        @pl.when(x == at)
-        def _():
-            row, col = 80 * (at % 2), 320 * (at // 2)
-            for chip in range(4):
-                kept_ref[chip, row : row + 80, col : col + 320] = pieces[chip]
-
-    @pl.when(x == 3)
-    def _():
-        for m in range(4):
-            outs[m][...] = kept_ref[partner(place_ref, m)]
-
-
-def cut(place, own, arrived):
-    rows = pl.BlockSpec((320, 640), lambda i: (i, 0))
-    return pl.pallas_call(
-        cut_kernel,
-        grid=(4,),
-        in_specs=[pl.BlockSpec(memory_space=pltpu.SMEM), rows, rows],
-        out_specs=[pl.BlockSpec((160, 640), lambda i: (i, 0))]
-        + [pl.BlockSpec((160, 640), lambda i: (0, 0))] * 4,
-        out_shape=[jax.ShapeDtypeStruct((640, 640), F32)]
-        + [jax.ShapeDtypeStruct((160, 640), F32)] * 4,
-        scratch_shapes=[pltpu.VMEM((4, 160, 640), F32)],
-        compiler_params=params(60),
-        cost_estimate=cost(2_000_000, 10_000_000),
-        name="cut",
-    )(place, own, arrived)
-
-
-def swap_kernel(place_ref, half_ref, *refs):
-    ins, outs, kept_ref = refs[:4], refs[4:12], refs[12]
-    along_y = (ins[0][...] + ins[1][...]) + (ins[2][...] + ins[3][...])
-    for chip, piece in enumerate(by_chip(half_ref[...])):
-        kept_ref[chip] = jnp.concatenate([piece[0:40], piece[40:80]], axis=1)
-    for x in range(4):
-        row, col = 80 * (x % 2), 320 * (x // 2)
-        part = along_y[row : row + 80, col : col + 320]
-        kept_ref[4 + x] = jnp.concatenate([part[0:40], part[40:80]], axis=1)
+    )(
+        place,
+        act,
+        act_other,
+        cot,
+        cot_other,
+        weight_in.reshape(4, 2, 160, width),
+        weight_out.reshape(4, 2, 160, width),
+    )
+
+
+def swap_kernel(place_ref, *refs):
+    ins, outs, kept_ref = refs[:4], refs[4:8], refs[8]
+    core = place_ref[1]
+    total = (ins[0][...] + ins[1][...]) + (ins[2][...] + ins[3][...])
+
+    @pl.when(core == 0)
+    def _():
+        for right, part in enumerate(low_high(total)):
+            for upper in range(2):
+                at = 320 * upper
+                pair = [part[:, at : at + 320], part[:, 640 + at : 960 + at]]
+                kept_ref[2 * upper + right] = jnp.concatenate(pair, axis=1)
+
+    @pl.when(core == 1)
+    def _():
+        for x in range(4):
+            row, col = 80 * (x % 2), 640 * (x // 2)
+            kept_ref[x] = total[row : row + 80, col : col + 640]
+
     for m in range(4):
-        outs[m][...] = kept_ref[partner(place_ref, m)]
-        outs[4 + m][...] = kept_ref[4 + lax.rem(place_ref[4] + m, 4)]
-
-
-def stack_kernel(*refs):
-    out_ref = refs[8]
+        index = jnp.where(core == 0, along_y(place_ref, m), along_x(place_ref, m))
+        outs[m][...] = kept_ref[index]
+
+
+def pair_kernel(place_ref, *refs):
+    ins, (mine_ref, send_ref) = refs[:4], refs[4:]
+    total = (ins[0][...] + ins[1][...]) + (ins[2][...] + ins[3][...])
+    even = jnp.concatenate([total[:, 0:160], total[:, 320:480]], axis=1)
+    odd = jnp.concatenate([total[:, 160:320], total[:, 480:640]], axis=1)
+    first = place_ref[1] == 0
+    mine_ref[...] = jnp.where(first, even, odd)
+    send_ref[...] = jnp.where(first, odd, even)
+
+
+def stack_kernel(place_ref, mine_ref, arrived_ref, out_ref):
     out_ref[...] = jnp.zeros(out_ref.shape, F32)
-    for half in range(2):
-        ins = refs[4 * half : 4 * half + 4]
-        total = (ins[0][...] + ins[1][...]) + (ins[2][...] + ins[3][...])
-        for z in range(4):
-            row, col = 20 * (z % 2), 320 * (z // 2)
-            out_ref[4 * half + z, 0:20, 0:320] = total[row : row + 20, col : col + 320]
-
-
-def last_kernel(place_ref, blocks_ref, first_ref, second_ref):
+    first = place_ref[1] == 0
+    mine, arrived = mine_ref[...], arrived_ref[...]
+    below, above = jnp.where(first, mine, arrived), jnp.where(first, arrived, mine)
+    for z in range(4):
+        out_ref[z, 0:20, 0:320] = below[20 * z : 20 * z + 20]
+        out_ref[4 + z, 0:20, 0:320] = above[20 * z : 20 * z + 20]
+
+
+def last_kernel(blocks_ref, first_ref, second_ref):
     total = blocks_ref[0, 0:20, 0:320]
     for z in range(1, 8):
         total += blocks_ref[z, 0:20, 0:320]
-    even = place_ref[1] == 0
-    first_ref[...] = jnp.where(even, total[:, 0:160], total[:, 160:320])
-    second_ref[...] = jnp.where(even, total[:, 160:320], total[:, 0:160])
+    first_ref[...] = total[:, 0:160]
+    second_ref[...] = total[:, 160:320]
 
 
 def small(kernel, operands, shapes, scalars=0, scratch=(), name=None):
@@ -278,16 +287,25 @@
     )(*operands)
 
 
-def exchange_x(pieces):
-    return [pieces[0]] + [
-        lax.ppermute(pieces[m], "x", [(i, (i + m) % 4) for i in range(4)]) for m in (1, 2, 3)
-    ]
-
-
-def exchange_y(pieces):
-    return [pieces[0]] + [
-        lax.ppermute(pieces[m], ("yl", "yh"), [(i, i ^ m) for i in range(4)]) for m in (1, 2, 3)
-    ]
+def exchange(pieces, cores):
+    def target(m, yl, co, x, z, yh):
+        if cores[co] == "x":
+            x = (x + m) % 4
+        else:
+            yl, yh = yl ^ (m >> 1), yh ^ (m & 1)
+        return yl, co, x, z, yh
+
+    sizes = (2, 2, 4, 8, 2)
+    order = lambda at: int(np.ravel_multi_index(at, sizes))
+    moved = [pieces[0]]
+    for m in (1, 2, 3):
+        pairs = [(order(at), order(target(m, *at))) for at in np.ndindex(*sizes)]
+        moved.append(lax.ppermute(pieces[m], AXES, pairs))
+    return moved
+
+
+def to_core(value):
+    return lax.ppermute(value, "co", [(0, 1), (1, 0)])
 
 
 def after(value, earlier):
@@ -448,26 +466,26 @@
     act = activation.transpose(1, 0, 2).reshape(points, width)
     cot = cotangent.transpose(1, 0, 2).reshape(points, width)
     place = jnp.stack([lax.axis_index(axis) for axis in (LON, "co", "yl", "yh", "x")])
-    block, own, other = mlp(place, mixing.T, act, cot, weight_in, weight_out)
-    arrived = lax.ppermute(other, "co", [(0, 1), (1, 0)])
-    half, *pieces = cut(place, own, arrived)
-    half = lax.psum_scatter(half, "x", scatter_dimension=0, tiled=True)
-    moved = exchange_y(pieces)
+    unit, other, *pieces = mlp(place, act, to_core(act), cot, to_core(cot), weight_in, weight_out)
+    (block,) = small(
+        pack_kernel, (place, mixing.T, unit, to_core(other)), [(SHARDS, 16, 128)], 2, name="pack"
+    )
+    moved = exchange(pieces, "xy")
     spread = across(block)
-    kernel = kernel_spectrum(kernels)
-    data, first, final, own_mixing = spectrum(after(spread, moved))
+    kernel = after(kernel_spectrum(kernels), moved)
+    data, first, final, own_mixing = spectrum(spread)
     forward = [(i, i + 1) for i in range(3)]
     backward = [(target, source) for source, target in forward]
     before = lax.ppermute(final, LAT, forward)
     beyond = lax.ppermute(first, LAT, backward)
     result = across(filtered(own_mixing, data, before, beyond, kernel))
-    swapped = small(
-        swap_kernel, (place, half, *moved), [(40, 640)] * 8, 1, (pltpu.VMEM((8, 40, 640), F32),), "swap"
-    )
-    moved = exchange_y(swapped[:4]) + exchange_x(swapped[4:])
-    (blocks,) = small(stack_kernel, moved, [(8, 24, 384)], name="stack")
+    kept = (pltpu.VMEM((4, 80, 640), F32),)
+    swapped = small(swap_kernel, (place, *moved), [(80, 640)] * 4, 1, kept, "swap")
+    moved = exchange(swapped, "yx")
+    mine, send = small(pair_kernel, (place, *moved), [(80, 320)] * 2, 1, name="pair")
+    (blocks,) = small(stack_kernel, (place, mine, to_core(send)), [(8, 24, 384)], 1, name="stack")
     blocks = lax.all_to_all(blocks, "z", split_axis=0, concat_axis=0, tiled=True)
-    grad_in, grad_out = small(last_kernel, (place, blocks), [(20, 160)] * 2, 1, name="last")
+    grad_in, grad_out = small(last_kernel, (blocks,), [(20, 160)] * 2, name="last")
     field = unpack(result).reshape(COLS, ROWS, width).transpose(1, 0, 2)
     return (field, grad_in, grad_out)
 

time: 149 us -> 121 us (0.81); the launches traced: 146 us -> 120 us
  waiting for transfers between devices: 45.5 us -> 30.3 us
  between operations: 14.2 us -> 0.82 us
  Pallas kernels: 34 us -> 30 us
  local copies, waits for them, and re-layouts: 4.6 us -> 8.58 us
  starting transfers between devices: 47.7 us -> 50.3 us
    ppermute x10, waiting for transfers between devices: 21.6 us -> 12 us  [the longest x6 9.4 us: exchange(): moved.append(lax.ppermute(pieces[m], AXES, pairs))]
    all_to_all x1, waiting for transfers between devices: 8.29 us -> 0.01 us  [per_device(): lax.all_to_all(blocks, 'z', split_axis=0, concat_axis=0, tiled=True)]
    pallas_call x2 -> x1, Pallas kernels: 21.5 us -> 14.8 us  [mlp(): pl.pallas_call(mlp_kernel, grid_spec=pltpu.PrefetchScalarGridSpec(num_sca...]
    unnamed x24 -> x36, local copies, waits for them, and re-layouts: 3.96 us -> 7.95 us
    all_to_all x1, starting transfers between devices: 4.37 us -> 7.96 us  [per_device(): lax.all_to_all(blocks, 'z', split_axis=0, concat_axis=0, tiled=True)]
    pallas_call x3 -> x5, Pallas kernels: 3.55 us -> 6.28 us  [small(): pl.pallas_call(kernel, in_specs=[pl.BlockSpec(memory_space=pltpu.SMEM)] *...]
    all_to_all x2, waiting for transfers between devices: 14.2 us -> 16.9 us  [across(): return lax.all_to_all(block, LON, split_axis=0, concat_axis=0, tiled=True)]
    ppermute x10, starting transfers between devices: 15.2 us -> 12.7 us  [the longest x6 7.35 us: exchange(): moved.append(lax.ppermute(pieces[m], AXES, pairs))]
  transfers between devices with their start and end apart: 16 -> 15, of which waited for: 9 -> 9; matrix products, arithmetic and copies ran while one was open for 0% -> 1% of each run, Pallas kernels for 8% -> 11%
where the time goes in v5:
time: 121 us; the launch traced here: 120 us
  starting transfers between devices  50.3 us (42%)
  waiting for transfers between devices  30.3 us (25%)
  Pallas kernels  30 us (25%)
  local copies, waits for them, and re-layouts  8.58 us (7%)
    all_to_all x2, starting transfers between devices, across(): return lax.all_to_all(block, LON, split_axis=0, concat_axis=0, tiled=True)  24.5 us
    all_to_all x2, waiting for transfers between devices, across(): return lax.all_to_all(block, LON, split_axis=0, concat_axis=0, tiled=True)  16.9 us
    pallas_call x1, Pallas kernels, mlp(): pl.pallas_call(mlp_kernel, grid_spec=pltpu.PrefetchScalarGridSpec(num_sca...  14.8 us
    ppermute x6, waiting for transfers between devices, exchange(): moved.append(lax.ppermute(pieces[m], AXES, pairs))  9.4 us
    all_to_all x1, starting transfers between devices, per_device(): lax.all_to_all(blocks, 'z', split_axis=0, concat_axis=0, tiled=True)  7.96 us
    unnamed x36, local copies, waits for them, and re-layouts  7.95 us
    ppermute x6, starting transfers between devices, exchange(): moved.append(lax.ppermute(pieces[m], AXES, pairs))  7.35 us
    pallas_call x5, Pallas kernels, small(): pl.pallas_call(kernel, in_specs=[pl.BlockSpec(memory_space=pltpu.SMEM)] *...  6.28 us
  transfers between devices with their start and end apart: 15, of which 9 were waited for; matrix products, arithmetic and copies ran while one was open for 1% of the time, Pallas kernels for 11%

profile of v5, /device:TPU:1, one launch (start us, length us, event | category | flops | bytes accessed | tf_op | source)
XLA Modules:
  0.0 120.0 jit_solution(7049861816476569081)
XLA Ops:
  0.6 3.3 %collective-permute-start = (f32[192,640]{1,0:T(8,128)}, f32[192,640]{1,0:T(8,128)S(1)}, u32[]{:S(2)}, u32[]{:S(2)}) collective-permute-start(f32[192,640]{1,0:T(8,128)} %bitcast.25), channel_id=1, source_target_pairs={{0,64},{64,0},{1,65},{65,1},{2,66},{66,2},{3,67},{67,3},{4,68},{68... | collective-permute-start | bytes 1474568 | tf_op jit(solution)/shard_map/ppermute | solution.py:308
  4.0 0.1 collective-permute-start.1
  4.1 0.6 stack.24.place_ref
  4.7 1.0 collective-permute-done.act_other_ref
  5.7 0.7 collective-permute-done.1.cot_other_ref
  6.4 0.1 copy-done.16
  6.4 0.7 copy-done.17
  7.2 14.8 %mlp.1 = (f32[192,640]{1,0:T(8,128)}, f32[192,640]{1,0:T(8,128)}, f32[160,1280]{1,0:T(8,128)}, f32[160,1280]{1,0:T(8,128)}, f32[160,1280]{1,0:T(8,128)}, /*index=5*/f32[160,1280]{1,0:T(8,128)}) custom-call(s32[5]{0:T(128)} %stack.24.place_ref, f32[192,640]{1,0:T(8,128)} %bitcast.26, f32[192,640]{1,0:T(8,128)} %copy-done.16, f32[192,640]{1,0:T(8,128)} %bitcast.28, ...), custom_call_target="tpu_custom_call" | custom-call | flops 4718592000 | bytes 12000000 | tf_op jit(solution)/shard_map/mlp/pallas_call | solution.py:198
  22.0 0.0 collective-permute-start.2
  22.0 1.2 %collective-permute-start.5 = (f32[160,1280]{1,0:T(8,128)}, f32[160,1280]{1,0:T(8,128)S(1)}, u32[]{:S(2)}, u32[]{:S(2)}) collective-permute-start(f32[160,1280]{1,0:T(8,128)} %get-tuple-element.29), channel_id=1, source_target_pairs={{0,16},{1,17},{2,18},{3,19},{4,20},{5,21},{6,22},{7,23},{8,24},{9,... | collective-permute-start | bytes 2457608 | tf_op jit(solution)/shard_map/ppermute | solution.py:303
  23.2 0.4 collective-permute-start.6
  23.6 1.7 %collective-permute-start.7 = (f32[160,1280]{1,0:T(8,128)}, f32[160,1280]{1,0:T(8,128)}, u32[]{:S(2)}, u32[]{:S(2)}) collective-permute-start(f32[160,1280]{1,0:T(8,128)} %get-tuple-element.31), channel_id=1, source_target_pairs={{0,48},{1,49},{2,50},{3,51},{4,52},{5,53},{6,54},{7,55},{8,56},{9,... | collective-permute-start | bytes 2457608 | tf_op jit(solution)/shard_map/ppermute | solution.py:303
  25.3 0.0 collective-permute-done.2.arrived_ref
  25.3 0.0 copy-done.13
  25.3 0.0 copy-done.14
  25.3 0.0 copy-start.12
  25.3 1.0 copy-done.12
  26.3 2.0 %pack.1 = f32[64,16,128]{2,1,0:T(8,128)} custom-call(s32[5]{0:T(128)S(1)} %copy-done.13, f32[3,10]{1,0:T(4,128)S(1)} %bitcast.21, f32[192,640]{1,0:T(8,128)S(1)} %copy-done.12, f32[192,640]{1,0:T(8,128)S(1)} %collective-permute-done.2.arrived_ref), custom_call_target="tpu_custom_call" | custom-call | tf_op jit(solution)/shard_map/pack/pallas_call | solution.py:278
  28.4 12.5 %all-to-all-start = ((f32[64,16,128]{2,1,0:T(8,128)}), f32[64,16,128]{2,1,0:T(8,128)S(1)}, u32[]{:S(2)}, u32[]{:S(2)}) async-start(f32[64,16,128]{2,1,0:T(8,128)} %pack.1), calls=%async_computation | async-start | bytes 1048576 | tf_op jit(solution)/shard_map/all_to_all | solution.py:460
  40.9 0.0 collective-permute-done.5.refs_1_
  40.9 0.0 copy-start.8
  41.0 0.9 copy-done.8
  41.8 0.9 collective-permute-done.6.refs_2_
  42.8 0.9 copy-done.10
  43.7 0.4 collective-permute-done.7.refs_3_
  44.0 0.0 copy-done.7
  44.0 1.1 copy-done.9
  45.2 1.1 copy-done.11
  46.3 1.6 %swap.1 = (f32[80,640]{1,0:T(8,128)S(1)}, f32[80,640]{1,0:T(8,128)S(1)}, f32[80,640]{1,0:T(8,128)S(1)}, f32[80,640]{1,0:T(8,128)S(1)}) custom-call(s32[5]{0:T(128)S(1)} %copy-done.13, f32[160,1280]{1,0:T(8,128)S(1)} %copy-done.7, f32[160,1280]{1,0:T(8,128)S(1)} %copy-done.9, f32[160,1280]{1,0:T(8,128)S(1)} %copy-done.11, ...), custom_call_target="tpu_custom_call" | custom-call | tf_op jit(solution)/shard_map/swap/pallas_call | solution.py:278
  47.9 0.0 copy-start.2
  47.9 2.3 %collective-permute-start.10 = (f32[80,640]{1,0:T(8,128)S(1)}, f32[80,640]{1,0:T(8,128)S(1)}, u32[]{:S(2)}, u32[]{:S(2)}) collective-permute-start(f32[80,640]{1,0:T(8,128)S(1)} %get-tuple-element.36), channel_id=1, source_target_pairs={{0,129},{1,128},{2,131},{3,130},{4,133},{5,132},{6,135},{7,134},{8... | collective-permute-start | bytes 614408 | tf_op jit(solution)/shard_map/ppermute | solution.py:303
  50.2 0.0 collective-permute-start.8
  50.2 1.7 %collective-permute-start.9 = (f32[80,640]{1,0:T(8,128)S(1)}, f32[80,640]{1,0:T(8,128)S(1)}, u32[]{:S(2)}, u32[]{:S(2)}) collective-permute-start(f32[80,640]{1,0:T(8,128)S(1)} %get-tuple-element.35), channel_id=1, source_target_pairs={{0,128},{1,129},{2,130},{3,131},{4,132},{5,133},{6,134},{7,135},{8... | collective-permute-start | bytes 614408 | tf_op jit(solution)/shard_map/ppermute | solution.py:303
  52.0 5.0 %collective-permute-done.10.refs_3_ = f32[80,640]{1,0:T(8,128)S(1)} collective-permute-done((f32[80,640]{1,0:T(8,128)S(1)}, f32[80,640]{1,0:T(8,128)S(1)}, u32[]{:S(2)}, u32[]{:S(2)}) %collective-permute-start.10) | collective-permute-done | bytes 204832 | tf_op jit(solution)/shard_map/ppermute | solution.py:303
  57.0 3.1 %collective-permute-done.8.refs_1_ = f32[80,640]{1,0:T(8,128)S(1)} collective-permute-done((f32[80,640]{1,0:T(8,128)S(1)}, f32[80,640]{1,0:T(8,128)S(1)}, u32[]{:S(2)}, u32[]{:S(2)}) %collective-permute-start.8) | collective-permute-done | bytes 204832 | tf_op jit(solution)/shard_map/ppermute | solution.py:303
  60.1 0.0 collective-permute-done.9.refs_2_
  60.1 0.7 pair.1
  60.8 1.9 %collective-permute-start.11 = (f32[80,320]{1,0:T(8,128)S(1)}, f32[80,320]{1,0:T(8,128)S(1)}, u32[]{:S(2)}, u32[]{:S(2)}) collective-permute-start(f32[80,320]{1,0:T(8,128)S(1)} %get-tuple-element.38), channel_id=1, source_target_pairs={{0,64},{64,0},{1,65},{65,1},{2,66},{66,2},{3,67},{67,3},{4,68},{68... | collective-permute-start | bytes 307208 | tf_op jit(solution)/shard_map/ppermute | solution.py:308
  62.6 1.0 collective-permute-done.11.arrived_ref
  63.6 1.3 %stack.25 = f32[8,24,384]{2,1,0:T(8,128)} custom-call(s32[5]{0:T(128)S(1)} %copy-done.13, f32[80,320]{1,0:T(8,128)S(1)} %get-tuple-element.37.mine_ref, f32[80,320]{1,0:T(8,128)S(1)} %collective-permute-done.11.arrived_ref), custom_call_target="tpu_custom_call" | custom-call | tf_op jit(solution)/shard_map/stack/pallas_call | solution.py:278
  64.9 0.0 all-to-all-done.block_ref
  64.9 8.0 %all-to-all-start.2 = ((f32[8,24,384]{2,1,0:T(8,128)}), f32[8,24,384]{2,1,0:T(8,128)S(1)}, u32[]{:S(2)}, u32[]{:S(2)}) async-start(f32[8,24,384]{2,1,0:T(8,128)} %stack.25), calls=%async_computation.2 | async-start | bytes 589824 | tf_op jit(solution)/shard_map/all_to_all | solution.py:487
  72.8 0.0 copy-done.3
  72.9 0.0 copy-done.2
  72.9 0.0 copy-start.4
  72.9 0.0 copy-start.5
  72.9 1.0 spectrum.1
  73.9 3.3 %collective-permute-start.3 = (f32[30,768]{1,0:T(8,128)S(1)}, f32[30,768]{1,0:T(8,128)S(1)}, u32[]{:S(2)}, u32[]{:S(2)}) collective-permute-start(f32[30,768]{1,0:T(8,128)S(1)} %get-tuple-element.26), channel_id=1, source_target_pairs={{0,64},{64,128},{128,192},{1,65},{65,129},{129,193},{2,66},{66,130... | collective-permute-start | bytes 276488 | tf_op jit(solution)/shard_map/ppermute | solution.py:479
  77.2 1.9 %collective-permute-start.4 = (f32[30,768]{1,0:T(8,128)S(1)}, f32[30,768]{1,0:T(8,128)S(1)}, u32[]{:S(2)}, u32[]{:S(2)}) collective-permute-start(f32[30,768]{1,0:T(8,128)S(1)} %get-tuple-element.27), channel_id=1, source_target_pairs={{64,0},{128,64},{192,128},{65,1},{129,65},{193,129},{66,2},{130,66... | collective-permute-start | bytes 276488 | tf_op jit(solution)/shard_map/ppermute | solution.py:480
  79.2 0.0 copy-done.4
  79.2 0.0 copy-done.5
  79.2 0.0 copy-start.6
  79.2 1.2 %copy-done.6 = f32[3,16,7,768]{3,1,2,0:T(8,128)S(1)} copy-done((f32[3,16,7,768]{3,1,2,0:T(8,128)S(1)}, f32[3,16,7,768]{3,1,2,0:T(8,128)}, u32[]{:S(2)}) %copy-start.6) | copy-done | bytes 1032216
  80.4 1.4 %kernel_spectrum.1.kernel_ref = f32[336,768]{1,0:T(8,128)S(1)} custom-call(f32[336,768]{1,0:T(8,128)S(1)} %bitcast.20, bf16[768,768]{1,0:T(8,128)(2,1)S(1)} %copy-done.4, bf16[768,768]{1,0:T(8,128)(2,1)S(1)} %copy-done.5), custom_call_target="tpu_custom_call" | custom-call | flops 1189085184 | bytes 5000000 | tf_op jit(solution)/shard_map/kernel_spectrum/pallas_call | solution.py:360
  81.8 0.0 collective-permute-done.3.before_ref
  81.8 1.4 %collective-permute-done.4.after_ref = f32[30,768]{1,0:T(8,128)S(1)} collective-permute-done((f32[30,768]{1,0:T(8,128)S(1)}, f32[30,768]{1,0:T(8,128)S(1)}, u32[]{:S(2)}, u32[]{:S(2)}) %collective-permute-start.4) | collective-permute-done | bytes 92192 | tf_op jit(solution)/shard_map/ppermute | solution.py:480
  83.2 0.0 copy-done
  83.2 4.2 %filter.1 = f32[64,16,128]{2,1,0:T(8,128)} custom-call(f32[1,128]{1,0:T(1,128)S(1)} %get-tuple-element.24.mixing_ref, f32[160,768]{1,0:T(8,128)S(1)} %get-tuple-element.25.data_ref, f32[30,768]{1,0:T(8,128)S(1)} %collective-permute-done.3.before_ref, f32[30,768]{1,0:T(8,128)S(1)} %collective-permute-done.4.after_ref, ...), custom_call_target="tpu_custom_call" | custom-call | flops 566231040 | bytes 5000000 | tf_op jit(solution)/shard_map/filter/pallas_call | solution.py:417
  87.4 0.0 all-to-all-done.2.blocks_ref
  87.4 11.9 %all-to-all-start.1 = ((f32[64,16,128]{2,1,0:T(8,128)}), f32[64,16,128]{2,1,0:T(8,128)S(1)}, u32[]{:S(2)}, u32[]{:S(2)}) async-start(f32[64,16,128]{2,1,0:T(8,128)} %filter.1), calls=%async_computation.1 | async-start | bytes 1048576 | tf_op jit(solution)/shard_map/all_to_all | solution.py:460
  99.3 0.7 last.1
  100.0 16.9 %all-to-all-done.1.block_ref = f32[64,16,128]{2,1,0:T(8,128)S(1)} async-done(((f32[64,16,128]{2,1,0:T(8,128)}), f32[64,16,128]{2,1,0:T(8,128)S(1)}, u32[]{:S(2)}, u32[]{:S(2)}) %all-to-all-start.1) | async-done | bytes 524320 | tf_op jit(solution)/shard_map/all_to_all | solution.py:460
  116.9 0.8 copy-done.15
  117.7 2.3 %unpack.1 = f32[192,640]{1,0:T(8,128)} custom-call(f32[64,16,128]{2,1,0:T(8,128)} %copy-done.15), custom_call_target="tpu_custom_call" | custom-call | tf_op jit(solution)/shard_map/unpack/pallas_call | solution.py:450
  (13 shorter events, 0.0 us)
Async XLA Ops:
  0.6 5.0 %collective-permute-start = (f32[192,640]{1,0:T(8,128)}, f32[192,640]{1,0:T(8,128)S(1)}, u32[]{:S(2)}, u32[]{:S(2)}) collective-permute-start(f32[192,640]{1,0:T(8,128)} %bitcast.25), channel_id=1, source_target_pairs={{0,64},{64,0},{1,65},{65,1},{2,66},{66,2},{3,67},{67,3},{4,68},{68... | collective-permute-start | bytes 1474568 | tf_op jit(solution)/shard_map/ppermute | solution.py:308
  4.0 2.4 %collective-permute-start.1 = (f32[192,640]{1,0:T(8,128)}, f32[192,640]{1,0:T(8,128)S(1)}, u32[]{:S(2)}, u32[]{:S(2)}) collective-permute-start(f32[192,640]{1,0:T(8,128)} %bitcast.27), channel_id=1, source_target_pairs={{0,64},{64,0},{1,65},{65,1},{2,66},{66,2},{3,67},{67,3},{4,68},{68... | collective-permute-start | bytes 1474568 | tf_op jit(solution)/shard_map/ppermute | solution.py:308
  5.7 0.8 copy-start.16
  6.4 0.8 copy-start.17
  7.1 18.2 %copy-start.13 = (s32[5]{0:T(128)S(1)}, s32[5]{0:T(128)}, u32[]{:S(2)}) copy-start(s32[5]{0:T(128)} %stack.24.place_ref) | copy-start | bytes 64
  7.2 18.2 %copy-start.14 = (f32[10,3]{0,1:T(4,128)S(1)}, f32[10,3]{0,1:T(4,128)}, u32[]{:S(2)}) copy-start(f32[10,3]{0,1:T(4,128)} %param.17) | copy-start | bytes 364
  22.0 3.3 %collective-permute-start.2 = (f32[192,640]{1,0:T(8,128)}, f32[192,640]{1,0:T(8,128)S(1)}, u32[]{:S(2)}, u32[]{:S(2)}) collective-permute-start(f32[192,640]{1,0:T(8,128)} %get-tuple-element.23), channel_id=1, source_target_pairs={{0,64},{64,0},{1,65},{65,1},{2,66},{66,2},{3,67},{67,3},{4,68},{68... | collective-permute-start | bytes 1474568 | tf_op jit(solution)/shard_map/ppermute | solution.py:308
  22.0 19.0 %collective-permute-start.5 = (f32[160,1280]{1,0:T(8,128)}, f32[160,1280]{1,0:T(8,128)S(1)}, u32[]{:S(2)}, u32[]{:S(2)}) collective-permute-start(f32[160,1280]{1,0:T(8,128)} %get-tuple-element.29), channel_id=1, source_target_pairs={{0,16},{1,17},{2,18},{3,19},{4,20},{5,21},{6,22},{7,23},{8,24},{9,... | collective-permute-start | bytes 2457608 | tf_op jit(solution)/shard_map/ppermute | solution.py:303
  23.2 19.6 %collective-permute-start.6 = (f32[160,1280]{1,0:T(8,128)}, f32[160,1280]{1,0:T(8,128)S(1)}, u32[]{:S(2)}, u32[]{:S(2)}) collective-permute-start(f32[160,1280]{1,0:T(8,128)} %get-tuple-element.30), channel_id=1, source_target_pairs={{0,32},{1,33},{2,34},{3,35},{4,36},{5,37},{6,38},{7,39},{8,40},{9,... | collective-permute-start | bytes 2457608 | tf_op jit(solution)/shard_map/ppermute | solution.py:303
  23.6 20.4 %collective-permute-start.7 = (f32[160,1280]{1,0:T(8,128)}, f32[160,1280]{1,0:T(8,128)}, u32[]{:S(2)}, u32[]{:S(2)}) collective-permute-start(f32[160,1280]{1,0:T(8,128)} %get-tuple-element.31), channel_id=1, source_target_pairs={{0,48},{1,49},{2,50},{3,51},{4,52},{5,53},{6,54},{7,55},{8,56},{9,... | collective-permute-start | bytes 2457608 | tf_op jit(solution)/shard_map/ppermute | solution.py:303
  25.3 1.0 copy-start.12
  26.3 17.7 %copy-start.7 = (f32[160,1280]{1,0:T(8,128)S(1)}, f32[160,1280]{1,0:T(8,128)}, u32[]{:S(2)}) copy-start(f32[160,1280]{1,0:T(8,128)} %get-tuple-element.28.refs_0_) | copy-start | bytes 2457604
  28.4 36.5 %all-to-all-start = ((f32[64,16,128]{2,1,0:T(8,128)}), f32[64,16,128]{2,1,0:T(8,128)S(1)}, u32[]{:S(2)}, u32[]{:S(2)}) async-start(f32[64,16,128]{2,1,0:T(8,128)} %pack.1), calls=%async_computation | async-start | bytes 1048576 | tf_op jit(solution)/shard_map/all_to_all | solution.py:460
  40.9 0.9 copy-start.8
  42.8 0.9 copy-start.10
  44.0 1.1 copy-start.9
  45.2 1.1 copy-start.11
  46.3 26.5 %copy-start.3 = (bf16[768,768]{1,0:T(8,128)(2,1)S(1)}, bf16[768,768]{1,0:T(8,128)(2,1)}, u32[]{:S(2)}) copy-start(bf16[768,768]{1,0:T(8,128)(2,1)} %constant.40.clone.low_ref) | copy-start | bytes 3538948
  47.9 24.9 %copy-start.2 = (bf16[768,768]{1,0:T(8,128)(2,1)S(1)}, bf16[768,768]{1,0:T(8,128)(2,1)}, u32[]{:S(2)}) copy-start(bf16[768,768]{1,0:T(8,128)(2,1)} %constant.39.clone.top_ref) | copy-start | bytes 3538948
  47.9 9.1 %collective-permute-start.10 = (f32[80,640]{1,0:T(8,128)S(1)}, f32[80,640]{1,0:T(8,128)S(1)}, u32[]{:S(2)}, u32[]{:S(2)}) collective-permute-start(f32[80,640]{1,0:T(8,128)S(1)} %get-tuple-element.36), channel_id=1, source_target_pairs={{0,129},{1,128},{2,131},{3,130},{4,133},{5,132},{6,135},{7,134},{8... | collective-permute-start | bytes 614408 | tf_op jit(solution)/shard_map/ppermute | solution.py:303
  50.2 9.8 %collective-permute-start.8 = (f32[80,640]{1,0:T(8,128)S(1)}, f32[80,640]{1,0:T(8,128)S(1)}, u32[]{:S(2)}, u32[]{:S(2)}) collective-permute-start(f32[80,640]{1,0:T(8,128)S(1)} %get-tuple-element.34), channel_id=1, source_target_pairs={{0,1},{1,0},{2,3},{3,2},{4,5},{5,4},{6,7},{7,6},{8,9},{9,8},{10,11... | collective-permute-start | bytes 614408 | tf_op jit(solution)/shard_map/ppermute | solution.py:303
  50.2 9.8 %collective-permute-start.9 = (f32[80,640]{1,0:T(8,128)S(1)}, f32[80,640]{1,0:T(8,128)S(1)}, u32[]{:S(2)}, u32[]{:S(2)}) collective-permute-start(f32[80,640]{1,0:T(8,128)S(1)} %get-tuple-element.35), channel_id=1, source_target_pairs={{0,128},{1,129},{2,130},{3,131},{4,132},{5,133},{6,134},{7,135},{8... | collective-permute-start | bytes 614408 | tf_op jit(solution)/shard_map/ppermute | solution.py:303
  60.8 2.8 %collective-permute-start.11 = (f32[80,320]{1,0:T(8,128)S(1)}, f32[80,320]{1,0:T(8,128)S(1)}, u32[]{:S(2)}, u32[]{:S(2)}) collective-permute-start(f32[80,320]{1,0:T(8,128)S(1)} %get-tuple-element.38), channel_id=1, source_target_pairs={{0,64},{64,0},{1,65},{65,1},{2,66},{66,2},{3,67},{67,3},{4,68},{68... | collective-permute-start | bytes 307208 | tf_op jit(solution)/shard_map/ppermute | solution.py:308
  64.9 22.5 %all-to-all-start.2 = ((f32[8,24,384]{2,1,0:T(8,128)}), f32[8,24,384]{2,1,0:T(8,128)S(1)}, u32[]{:S(2)}, u32[]{:S(2)}) async-start(f32[8,24,384]{2,1,0:T(8,128)} %stack.25), calls=%async_computation.2 | async-start | bytes 589824 | tf_op jit(solution)/shard_map/all_to_all | solution.py:487
  72.9 6.3 %copy-start.4 = (bf16[768,768]{1,0:T(8,128)(2,1)S(1)}, bf16[768,768]{1,0:T(8,128)(2,1)}, u32[]{:S(2)}) copy-start(bf16[768,768]{1,0:T(8,128)(2,1)} %constant.37.clone.top_ref) | copy-start | bytes 3538948
  72.9 6.3 %copy-start.5 = (bf16[768,768]{1,0:T(8,128)(2,1)S(1)}, bf16[768,768]{1,0:T(8,128)(2,1)}, u32[]{:S(2)}) copy-start(bf16[768,768]{1,0:T(8,128)(2,1)} %constant.38.clone.low_ref) | copy-start | bytes 3538948
  73.9 7.9 %collective-permute-start.3 = (f32[30,768]{1,0:T(8,128)S(1)}, f32[30,768]{1,0:T(8,128)S(1)}, u32[]{:S(2)}, u32[]{:S(2)}) collective-permute-start(f32[30,768]{1,0:T(8,128)S(1)} %get-tuple-element.26), channel_id=1, source_target_pairs={{0,64},{64,128},{128,192},{1,65},{65,129},{129,193},{2,66},{66,130... | collective-permute-start | bytes 276488 | tf_op jit(solution)/shard_map/ppermute | solution.py:479
  77.2 5.9 %collective-permute-start.4 = (f32[30,768]{1,0:T(8,128)S(1)}, f32[30,768]{1,0:T(8,128)S(1)}, u32[]{:S(2)}, u32[]{:S(2)}) collective-permute-start(f32[30,768]{1,0:T(8,128)S(1)} %get-tuple-element.27), channel_id=1, source_target_pairs={{64,0},{128,64},{192,128},{65,1},{129,65},{193,129},{66,2},{130,66... | collective-permute-start | bytes 276488 | tf_op jit(solution)/shard_map/ppermute | solution.py:480
  79.2 1.2 %copy-start.6 = (f32[3,16,7,768]{3,1,2,0:T(8,128)S(1)}, f32[3,16,7,768]{3,1,2,0:T(8,128)}, u32[]{:S(2)}) copy-start(f32[3,16,7,768]{3,1,2,0:T(8,128)} %param.16) | copy-start | bytes 3096580
  80.4 2.8 %copy-start = (bf16[768,768]{1,0:T(8,128)(2,1)S(1)}, bf16[768,768]{1,0:T(8,128)(2,1)}, u32[]{:S(2)}) copy-start(bf16[768,768]{1,0:T(8,128)(2,1)} %constant.41.clone.top_ref) | copy-start | bytes 3538948
  80.4 2.8 %copy-start.1 = (bf16[768,768]{1,0:T(8,128)(2,1)S(1)}, bf16[768,768]{1,0:T(8,128)(2,1)}, u32[]{:S(2)}) copy-start(bf16[768,768]{1,0:T(8,128)(2,1)} %constant.42.clone.low_ref) | copy-start | bytes 3538948
  87.4 29.5 %all-to-all-start.1 = ((f32[64,16,128]{2,1,0:T(8,128)}), f32[64,16,128]{2,1,0:T(8,128)S(1)}, u32[]{:S(2)}, u32[]{:S(2)}) async-start(f32[64,16,128]{2,1,0:T(8,128)} %filter.1), calls=%async_computation.1 | async-start | bytes 1048576 | tf_op jit(solution)/shard_map/all_to_all | solution.py:460
  116.9 0.8 copy-start.15

commit v6 on v5

--- a/solution.py
+++ b/solution.py
@@ -41,6 +41,9 @@
 
 def whole(n):
     return [pl.BlockSpec(memory_space=pltpu.VMEM)] * n
+
+
+EARLIER = [pl.BlockSpec(memory_space=pl.ANY)]
 
 
 def params(mib):
@@ -100,7 +103,7 @@
     out_ref[:, 15, :] = weights
 
 
-def pack_kernel(place_ref, mixing_ref, unit_ref, arrived_ref, block_ref):
+def pack_kernel(place_ref, mixing_ref, _, unit_ref, arrived_ref, block_ref):
     pack(unit_ref[...] + arrived_ref[...], mixing_ref, place_ref[0], block_ref)
 
 
@@ -246,7 +249,7 @@
         outs[m][...] = kept_ref[index]
 
 
-def pair_kernel(place_ref, *refs):
+def pair_kernel(place_ref, _, *refs):
     ins, (mine_ref, send_ref) = refs[:4], refs[4:]
     total = (ins[0][...] + ins[1][...]) + (ins[2][...] + ins[3][...])
     even = jnp.concatenate([total[:, 0:160], total[:, 320:480]], axis=1)
@@ -256,35 +259,39 @@
     send_ref[...] = jnp.where(first, odd, even)
 
 
-def stack_kernel(place_ref, mine_ref, arrived_ref, out_ref):
-    out_ref[...] = jnp.zeros(out_ref.shape, F32)
+def stack_kernel(place_ref, mine_ref, arrived_ref, *refs):
+    outs, kept_ref = refs[:8], refs[8]
     first = place_ref[1] == 0
     mine, arrived = mine_ref[...], arrived_ref[...]
     below, above = jnp.where(first, mine, arrived), jnp.where(first, arrived, mine)
     for z in range(4):
-        out_ref[z, 0:20, 0:320] = below[20 * z : 20 * z + 20]
-        out_ref[4 + z, 0:20, 0:320] = above[20 * z : 20 * z + 20]
-
-
-def last_kernel(blocks_ref, first_ref, second_ref):
-    total = blocks_ref[0, 0:20, 0:320]
-    for z in range(1, 8):
-        total += blocks_ref[z, 0:20, 0:320]
+        kept_ref[z, 0:20, :] = below[20 * z : 20 * z + 20]
+        kept_ref[4 + z, 0:20, :] = above[20 * z : 20 * z + 20]
+    for m in range(8):
+        outs[m][...] = kept_ref[lax.rem(place_ref[5] + m, 8), 0:20, :]
+
+
+def last_kernel(*refs):
+    first_ref, second_ref = refs[8:]
+    a, b, c, d = (refs[m][...] + refs[m + 4][...] for m in range(4))
+    total = (a + b) + (c + d)
     first_ref[...] = total[:, 0:160]
     second_ref[...] = total[:, 160:320]
 
 
-def small(kernel, operands, shapes, scalars=0, scratch=(), name=None):
+def small(kernel, operands, shapes, scalars=0, scratch=(), earlier=(), name=None, flops=0):
     return pl.pallas_call(
         kernel,
         in_specs=[pl.BlockSpec(memory_space=pltpu.SMEM)] * scalars
+        + EARLIER * len(earlier)
         + whole(len(operands) - scalars),
         out_specs=whole(len(shapes)),
         out_shape=[jax.ShapeDtypeStruct(shape, F32) for shape in shapes],
         scratch_shapes=scratch,
         compiler_params=params(32),
+        cost_estimate=cost(flops, 4_000_000) if flops else None,
         name=name,
-    )(*operands)
+    )(*operands[:scalars], *earlier, *operands[scalars:])
 
 
 def exchange(pieces, cores):
@@ -308,12 +315,8 @@
     return lax.ppermute(value, "co", [(0, 1), (1, 0)])
 
 
-def after(value, earlier):
-    return lax.optimization_barrier((value, earlier))[0]
-
-
 def spectrum_kernel(
-    block_ref, top_ref, low_ref, out_ref, first_ref, final_ref, mixing_ref, flat_ref
+    block_ref, top_ref, low_ref, _, out_ref, first_ref, final_ref, mixing_ref, flat_ref
 ):
     for p in range(COLS // 2):
         pair = jnp.concatenate([block_ref[:, 2 * p, :], block_ref[:, 2 * p + 1, :]], axis=0)
@@ -329,12 +332,12 @@
         final_ref[3 * r : 3 * r + 3, :] = result[ROWS * r + 13 : ROWS * r + 16, :]
 
 
-def spectrum(block):
+def spectrum(block, earlier):
     top, low = forward_table(shard_order())
     rows = OWN * ROWS
     return pl.pallas_call(
         spectrum_kernel,
-        in_specs=whole(3),
+        in_specs=whole(3) + EARLIER,
         out_specs=whole(4),
         out_shape=[
             jax.ShapeDtypeStruct((rows, CIRCLE), F32),
@@ -346,7 +349,7 @@
         compiler_params=params(24),
         cost_estimate=cost(6 * rows * CIRCLE * CIRCLE, 4_000_000),
         name="spectrum",
-    )(block, jnp.asarray(top), jnp.asarray(low))
+    )(block, jnp.asarray(top), jnp.asarray(low), earlier)
 
 
 def kernel_spectrum_kernel(kernel_ref, top_ref, low_ref, out_ref):
@@ -369,8 +372,9 @@
 
 
 def filter_kernel(
-    mixing_ref, data_ref, before_ref, after_ref, kernel_ref, top_ref, low_ref, out_ref, rows_ref, sum_ref
+    mixing_ref, data_ref, before_ref, after_ref, kernel_ref, top_ref, low_ref, *refs
 ):
+    out_ref, rows_ref, sum_ref = refs[-3:]
     for r in range(OWN):
         rows_ref[r, 0:3, :] = before_ref[3 * r : 3 * r + 3, :]
         rows_ref[r, 3 : 3 + ROWS, :] = data_ref[ROWS * r : ROWS * (r + 1), :]
@@ -412,11 +416,11 @@
     out_ref[:, 15, :] = jnp.zeros((SHARDS, 128), F32)
 
 
-def filtered(mixing, data, before, after, kernel):
+def filtered(mixing, data, before, beyond, kernel, earlier):
     top, low = backward_table(shard_order())
     return pl.pallas_call(
         filter_kernel,
-        in_specs=[pl.BlockSpec(memory_space=pltpu.SMEM)] + whole(6),
+        in_specs=[pl.BlockSpec(memory_space=pltpu.SMEM)] + whole(6) + EARLIER * len(earlier),
         out_specs=whole(1)[0],
         out_shape=jax.ShapeDtypeStruct((SHARDS, 16, 128), F32),
         scratch_shapes=[
@@ -426,7 +430,7 @@
         compiler_params=params(32),
         cost_estimate=cost(6 * OWN * ROWS * CIRCLE * CIRCLE, 5_000_000),
         name="filter",
-    )(mixing, data, before, after, kernel, jnp.asarray(top), jnp.asarray(low))
+    )(mixing, data, before, beyond, kernel, jnp.asarray(top), jnp.asarray(low), *earlier)
 
 
 def unpack_kernel(block_ref, out_ref):
@@ -465,27 +469,32 @@
     width = activation.shape[2]
     act = activation.transpose(1, 0, 2).reshape(points, width)
     cot = cotangent.transpose(1, 0, 2).reshape(points, width)
-    place = jnp.stack([lax.axis_index(axis) for axis in (LON, "co", "yl", "yh", "x")])
+    place = jnp.stack([lax.axis_index(axis) for axis in (LON, "co", "yl", "yh", "x", "z")])
     unit, other, *pieces = mlp(place, act, to_core(act), cot, to_core(cot), weight_in, weight_out)
-    (block,) = small(
-        pack_kernel, (place, mixing.T, unit, to_core(other)), [(SHARDS, 16, 128)], 2, name="pack"
-    )
+    kernel = kernel_spectrum(kernels)
+    operands = (place, mixing.T, unit, to_core(other))
+    (block,) = small(pack_kernel, operands, [(SHARDS, 16, 128)], 2, (), (kernel,), "pack")
     moved = exchange(pieces, "xy")
     spread = across(block)
-    kernel = after(kernel_spectrum(kernels), moved)
-    data, first, final, own_mixing = spectrum(spread)
+    kept = (pltpu.VMEM((4, 80, 640), F32),)
+    swapped = small(swap_kernel, (place, *moved), [(80, 640)] * 4, 1, kept, (), "swap", 10**10)
+    data, first, final, own_mixing = spectrum(spread, swapped[0])
     forward = [(i, i + 1) for i in range(3)]
     backward = [(target, source) for source, target in forward]
     before = lax.ppermute(final, LAT, forward)
     beyond = lax.ppermute(first, LAT, backward)
-    result = across(filtered(own_mixing, data, before, beyond, kernel))
-    kept = (pltpu.VMEM((4, 80, 640), F32),)
-    swapped = small(swap_kernel, (place, *moved), [(80, 640)] * 4, 1, kept, "swap")
     moved = exchange(swapped, "yx")
-    mine, send = small(pair_kernel, (place, *moved), [(80, 320)] * 2, 1, name="pair")
-    (blocks,) = small(stack_kernel, (place, mine, to_core(send)), [(8, 24, 384)], 1, name="stack")
-    blocks = lax.all_to_all(blocks, "z", split_axis=0, concat_axis=0, tiled=True)
-    grad_in, grad_out = small(last_kernel, (blocks,), [(20, 160)] * 2, name="last")
+    sent = filtered(own_mixing, data, before, beyond, kernel, moved)
+    result = across(sent)
+    mine, send = small(pair_kernel, (place, *moved), [(80, 320)] * 2, 1, (), (sent,), "pair")
+    kept = (pltpu.VMEM((8, 24, 320), F32),)
+    stacked = small(
+        stack_kernel, (place, mine, to_core(send)), [(20, 320)] * 8, 1, kept, name="stack"
+    )
+    moved = [stacked[0]] + [
+        lax.ppermute(stacked[m], "z", [(i, (i + m) % 8) for i in range(8)]) for m in range(1, 8)
+    ]
+    grad_in, grad_out = small(last_kernel, moved, [(20, 160)] * 2, name="last")
     field = unpack(result).reshape(COLS, ROWS, width).transpose(1, 0, 2)
     return (field, grad_in, grad_out)
 

time: 121 us -> 109 us (0.901)
  waiting for transfers between devices: 30.3 us -> 21.1 us
  local copies, waits for them, and re-layouts: 8.58 us -> 5.83 us
    ppermute x0 -> x7, starting transfers between devices: none -> 14.8 us  [per_device(): lax.ppermute(stacked[m], 'z', [(i, (i + m) % 8) for i in range(8)])]
    all_to_all x2, waiting for transfers between devices: 16.9 us -> 8.76 us  [across(): return lax.all_to_all(block, LON, split_axis=0, concat_axis=0, tiled=True)]
    all_to_all x1 -> x0, starting transfers between devices: 7.96 us -> none  [per_device(): lax.all_to_all(blocks, 'z', split_axis=0, concat_axis=0, tiled=True)]
    ppermute x6, waiting for transfers between devices: 9.4 us -> 1.55 us  [exchange(): moved.append(lax.ppermute(pieces[m], AXES, pairs))]
    all_to_all x2, starting transfers between devices: 24.5 us -> 18.2 us  [across(): return lax.all_to_all(block, LON, split_axis=0, concat_axis=0, tiled=True)]
    ppermute x0 -> x7, waiting for transfers between devices: none -> 3.79 us  [per_device(): lax.ppermute(stacked[m], 'z', [(i, (i + m) % 8) for i in range(8)])]
    unnamed x36 -> x30, local copies, waits for them, and re-layouts: 7.95 us -> 5.22 us
    ppermute x1, waiting for transfers between devices: 1.36 us -> 3.97 us  [per_device(): beyond = lax.ppermute(first, LAT, backward)]
  transfers between devices with their start and end apart: 15 -> 21, of which waited for: 9 -> 10; matrix products, arithmetic and copies ran while one was open for 1% -> 1% of each run, Pallas kernels for 11% -> 9%
where the time goes in v6:
time: 109 us
  starting transfers between devices  50.2 us (46%)
  Pallas kernels  30.7 us (28%)
  waiting for transfers between devices  21.1 us (19%)
  local copies, waits for them, and re-layouts  5.83 us (5%)
    all_to_all x2, starting transfers between devices, across(): return lax.all_to_all(block, LON, split_axis=0, concat_axis=0, tiled=True)  18.2 us
    ppermute x7, starting transfers between devices, per_device(): lax.ppermute(stacked[m], 'z', [(i, (i + m) % 8) for i in range(8)])  14.8 us
    pallas_call x1, Pallas kernels, mlp(): pl.pallas_call(mlp_kernel, grid_spec=pltpu.PrefetchScalarGridSpec(num_sca...  14.7 us
    all_to_all x2, waiting for transfers between devices, across(): return lax.all_to_all(block, LON, split_axis=0, concat_axis=0, tiled=True)  8.76 us
    pallas_call x5, Pallas kernels, small(): pl.pallas_call(kernel, in_specs=[pl.BlockSpec(memory_space=pltpu.SMEM)] *...  7.05 us
    ppermute x6, starting transfers between devices, exchange(): moved.append(lax.ppermute(pieces[m], AXES, pairs))  6.11 us
    unnamed x30, local copies, waits for them, and re-layouts  5.22 us
    ppermute x1, starting transfers between devices, per_device(): before = lax.ppermute(final, LAT, forward)  5.01 us
  transfers between devices with their start and end apart: 21, of which 10 were waited for; matrix products, arithmetic and copies ran while one was open for 1% of the time, Pallas kernels for 9%

profile of v6, /device:TPU:1, one launch (start us, length us, event | category | flops | bytes accessed | tf_op | source)
XLA Modules:
  0.0 108.6 jit_solution(11601698375413753732)
XLA Ops:
  0.6 3.3 %collective-permute-start = (f32[192,640]{1,0:T(8,128)}, f32[192,640]{1,0:T(8,128)S(1)}, u32[]{:S(2)}, u32[]{:S(2)}) collective-permute-start(f32[192,640]{1,0:T(8,128)} %bitcast.26), channel_id=1, source_target_pairs={{0,64},{64,0},{1,65},{65,1},{2,66},{66,2},{3,67},{67,3},{4,68},{68... | collective-permute-start | bytes 1474568 | tf_op jit(solution)/shard_map/ppermute | solution.py:315
  4.0 0.1 collective-permute-start.1
  4.1 0.6 stack.28.place_ref
  4.7 1.0 collective-permute-done.act_other_ref
  5.7 0.7 collective-permute-done.1.cot_other_ref
  6.4 0.1 copy-done.13
  6.4 0.7 copy-done.14
  7.1 14.7 %mlp.1 = (f32[192,640]{1,0:T(8,128)}, f32[192,640]{1,0:T(8,128)}, f32[160,1280]{1,0:T(8,128)}, f32[160,1280]{1,0:T(8,128)}, f32[160,1280]{1,0:T(8,128)}, /*index=5*/f32[160,1280]{1,0:T(8,128)}) custom-call(s32[6]{0:T(128)} %stack.28.place_ref, f32[192,640]{1,0:T(8,128)} %bitcast.27, f32[192,640]{1,0:T(8,128)} %copy-done.13, f32[192,640]{1,0:T(8,128)} %bitcast.29, ...), custom_call_target="tpu_custom_call" | custom-call | flops 4718592000 | bytes 12000000 | tf_op jit(solution)/shard_map/mlp/pallas_call | solution.py:201
  21.9 1.2 %collective-permute-start.3 = (f32[160,1280]{1,0:T(8,128)}, f32[160,1280]{1,0:T(8,128)}, u32[]{:S(2)}, u32[]{:S(2)}) collective-permute-start(f32[160,1280]{1,0:T(8,128)} %get-tuple-element.32), channel_id=1, source_target_pairs={{0,16},{1,17},{2,18},{3,19},{4,20},{5,21},{6,22},{7,23},{8,24},{9,... | collective-permute-start | bytes 2457608 | tf_op jit(solution)/shard_map/ppermute | solution.py:310
  23.1 0.4 collective-permute-start.4
  23.5 1.7 %collective-permute-start.5 = (f32[160,1280]{1,0:T(8,128)}, f32[160,1280]{1,0:T(8,128)}, u32[]{:S(2)}, u32[]{:S(2)}) collective-permute-start(f32[160,1280]{1,0:T(8,128)} %get-tuple-element.34), channel_id=1, source_target_pairs={{0,48},{1,49},{2,50},{3,51},{4,52},{5,53},{6,54},{7,55},{8,56},{9,... | collective-permute-start | bytes 2457608 | tf_op jit(solution)/shard_map/ppermute | solution.py:310
  25.1 0.6 collective-permute-start.2
  25.7 0.0 copy-done.4
  25.7 0.0 copy-done.5
  25.7 1.2 %copy-done.6 = f32[3,16,7,768]{3,1,2,0:T(8,128)S(1)} copy-done((f32[3,16,7,768]{3,1,2,0:T(8,128)S(1)}, f32[3,16,7,768]{3,1,2,0:T(8,128)}, u32[]{:S(2)}) %copy-start.6) | copy-done | bytes 1032216
  27.0 1.4 %kernel_spectrum.1._.kernel_ref = f32[336,768]{1,0:T(8,128)S(1)} custom-call(f32[336,768]{1,0:T(8,128)S(1)} %bitcast.21, bf16[768,768]{1,0:T(8,128)(2,1)S(1)} %copy-done.4, bf16[768,768]{1,0:T(8,128)(2,1)S(1)} %copy-done.5), custom_call_target="tpu_custom_call" | custom-call | flops 1189085184 | bytes 5000000 | tf_op jit(solution)/shard_map/kernel_spectrum/pallas_call | solution.py:363
  28.3 0.0 collective-permute-done.2.arrived_ref
  28.4 0.0 copy-done.7
  28.4 0.0 copy-done.8
  28.4 0.0 copy-done.10
  28.4 2.0 %pack.1 = f32[64,16,128]{2,1,0:T(8,128)} custom-call(s32[6]{0:T(128)S(1)} %copy-done.8, f32[3,10]{1,0:T(4,128)S(1)} %bitcast.22, f32[336,768]{1,0:T(8,128)S(1)} %kernel_spectrum.1._.kernel_ref, f32[192,640]{1,0:T(8,128)S(1)} %copy-done.7, f32[192,640]{1,0:T(8,128)S(1)} %collective-permute-done.2.arrived_ref), custom_call_target="tpu_custom_call" | custom-call | tf_op jit(solution)/shard_map/pack/pallas_call | solution.py:283
  30.4 12.0 %all-to-all-start = ((f32[64,16,128]{2,1,0:T(8,128)}), f32[64,16,128]{2,1,0:T(8,128)S(1)}, u32[]{:S(2)}, u32[]{:S(2)}) async-start(f32[64,16,128]{2,1,0:T(8,128)} %pack.1), calls=%async_computation | async-start | bytes 1048576 | tf_op jit(solution)/shard_map/all_to_all | solution.py:464
  42.4 0.0 collective-permute-done.3.refs_1_
  42.4 0.2 collective-permute-done.4.refs_2_
  42.6 1.3 %collective-permute-done.5.refs_3_ = f32[160,1280]{1,0:T(8,128)} collective-permute-done((f32[160,1280]{1,0:T(8,128)}, f32[160,1280]{1,0:T(8,128)}, u32[]{:S(2)}, u32[]{:S(2)}) %collective-permute-start.5) | collective-permute-done | bytes 819232 | tf_op jit(solution)/shard_map/ppermute | solution.py:310
  44.0 1.1 %copy-done.11 = f32[160,1280]{1,0:T(8,128)S(1)} copy-done((f32[160,1280]{1,0:T(8,128)S(1)}, f32[160,1280]{1,0:T(8,128)}, u32[]{:S(2)}) %copy-start.11) | copy-done | bytes 819224
  45.1 3.1 %swap.1 = (f32[80,640]{1,0:T(8,128)S(1)}, f32[80,640]{1,0:T(8,128)}, f32[80,640]{1,0:T(8,128)}, f32[80,640]{1,0:T(8,128)}) custom-call(s32[6]{0:T(128)S(1)} %copy-done.8, f32[160,1280]{1,0:T(8,128)S(1)} %copy-done.11, f32[160,1280]{1,0:T(8,128)} %collective-permute-done.3.refs_1_, f32[160,1280]{1,0:T(8,128)} %collective-permute-done.4.refs_2_, ...), custom_call_target="tpu_custom_call" | custom-call | flops 10000000000 | bytes 4000000 | tf_op jit(solution)/shard_map/swap/pallas_call | solution.py:283
  48.2 1.1 %collective-permute-start.10 = (f32[80,640]{1,0:T(8,128)}, f32[80,640]{1,0:T(8,128)S(1)}, u32[]{:S(2)}, u32[]{:S(2)}) collective-permute-start(f32[80,640]{1,0:T(8,128)} %get-tuple-element.42), channel_id=1, source_target_pairs={{0,129},{1,128},{2,131},{3,130},{4,133},{5,132},{6,135},{7,134},{8... | collective-permute-start | bytes 614408 | tf_op jit(solution)/shard_map/ppermute | solution.py:310
  49.3 0.3 collective-permute-start.8
  49.6 1.4 %collective-permute-start.9 = (f32[80,640]{1,0:T(8,128)}, f32[80,640]{1,0:T(8,128)S(1)}, u32[]{:S(2)}, u32[]{:S(2)}) collective-permute-start(f32[80,640]{1,0:T(8,128)} %get-tuple-element.41), channel_id=1, source_target_pairs={{0,128},{1,129},{2,130},{3,131},{4,132},{5,133},{6,134},{7,135},{8... | collective-permute-start | bytes 614408 | tf_op jit(solution)/shard_map/ppermute | solution.py:310
  51.0 8.8 %all-to-all-done.block_ref = f32[64,16,128]{2,1,0:T(8,128)S(1)} async-done(((f32[64,16,128]{2,1,0:T(8,128)}), f32[64,16,128]{2,1,0:T(8,128)S(1)}, u32[]{:S(2)}, u32[]{:S(2)}) %all-to-all-start) | async-done | bytes 524320 | tf_op jit(solution)/shard_map/all_to_all | solution.py:464
  59.8 1.3 %copy-done.1 = bf16[768,768]{1,0:T(8,128)(2,1)S(1)} copy-done((bf16[768,768]{1,0:T(8,128)(2,1)S(1)}, bf16[768,768]{1,0:T(8,128)(2,1)}, u32[]{:S(2)}) %copy-start.1) | copy-done | bytes 1179672
  61.1 1.0 spectrum.1
  62.1 5.0 %collective-permute-start.6 = (f32[30,768]{1,0:T(8,128)S(1)}, f32[30,768]{1,0:T(8,128)S(1)}, u32[]{:S(2)}, u32[]{:S(2)}) collective-permute-start(f32[30,768]{1,0:T(8,128)S(1)} %get-tuple-element.38), channel_id=1, source_target_pairs={{0,64},{64,128},{128,192},{1,65},{65,129},{129,193},{2,66},{66,130... | collective-permute-start | bytes 276488 | tf_op jit(solution)/shard_map/ppermute | solution.py:484
  67.1 1.9 %collective-permute-start.7 = (f32[30,768]{1,0:T(8,128)S(1)}, f32[30,768]{1,0:T(8,128)S(1)}, u32[]{:S(2)}, u32[]{:S(2)}) collective-permute-start(f32[30,768]{1,0:T(8,128)S(1)} %get-tuple-element.39), channel_id=1, source_target_pairs={{64,0},{128,64},{192,128},{65,1},{129,65},{193,129},{66,2},{130,66... | collective-permute-start | bytes 276488 | tf_op jit(solution)/shard_map/ppermute | solution.py:485
  69.0 0.0 collective-permute-done.10.refs_3_
  69.0 0.0 collective-permute-done.8.refs_1_
  69.1 0.0 collective-permute-done.9.refs_2_
  69.1 0.0 collective-permute-done.6.before_ref
  69.1 4.0 %collective-permute-done.7.after_ref = f32[30,768]{1,0:T(8,128)S(1)} collective-permute-done((f32[30,768]{1,0:T(8,128)S(1)}, f32[30,768]{1,0:T(8,128)S(1)}, u32[]{:S(2)}, u32[]{:S(2)}) %collective-permute-start.7) | collective-permute-done | bytes 92192 | tf_op jit(solution)/shard_map/ppermute | solution.py:485
  73.1 4.2 %filter.1._ = f32[64,16,128]{2,1,0:T(8,128)} custom-call(f32[1,128]{1,0:T(1,128)S(1)} %get-tuple-element.36.mixing_ref, f32[160,768]{1,0:T(8,128)S(1)} %get-tuple-element.37.data_ref, f32[30,768]{1,0:T(8,128)S(1)} %collective-permute-done.6.before_ref, f32[30,768]{1,0:T(8,128)S(1)} %collective-permute-done.7.after_ref, ...), custom_call_target="tpu_custom_call" | custom-call | flops 566231040 | bytes 5000000 | tf_op jit(solution)/shard_map/filter/pallas_call | solution.py:421
  77.2 6.3 %all-to-all-start.1 = ((f32[64,16,128]{2,1,0:T(8,128)}), f32[64,16,128]{2,1,0:T(8,128)S(1)}, u32[]{:S(2)}, u32[]{:S(2)}) async-start(f32[64,16,128]{2,1,0:T(8,128)} %filter.1._), calls=%async_computation.1 | async-start | bytes 1048576 | tf_op jit(solution)/shard_map/all_to_all | solution.py:464
  83.5 0.7 pair.1
  84.2 0.1 collective-permute-start.11
  84.3 1.3 %collective-permute-done.11.arrived_ref = f32[80,320]{1,0:T(8,128)S(1)} collective-permute-done((f32[80,320]{1,0:T(8,128)S(1)}, f32[80,320]{1,0:T(8,128)S(1)}, u32[]{:S(2)}, u32[]{:S(2)}) %collective-permute-start.11) | collective-permute-done | bytes 102432 | tf_op jit(solution)/shard_map/ppermute | solution.py:315
  85.6 0.6 stack.29
  86.2 1.1 %collective-permute-start.12 = (f32[20,320]{1,0:T(8,128)S(1)}, f32[20,320]{1,0:T(8,128)S(1)}, u32[]{:S(2)}, u32[]{:S(2)}) collective-permute-start(f32[20,320]{1,0:T(8,128)S(1)} %get-tuple-element.46), channel_id=1, source_target_pairs={{0,2},{2,4},{4,6},{6,8},{8,10},{10,12},{12,14},{14,0},{1,3},{3,5},... | collective-permute-start | bytes 76808 | tf_op jit(solution)/shard_map/ppermute | solution.py:495
  87.3 2.1 %collective-permute-start.13 = (f32[20,320]{1,0:T(8,128)S(1)}, f32[20,320]{1,0:T(8,128)S(1)}, u32[]{:S(2)}, u32[]{:S(2)}) collective-permute-start(f32[20,320]{1,0:T(8,128)S(1)} %get-tuple-element.47), channel_id=1, source_target_pairs={{0,4},{2,6},{4,8},{6,10},{8,12},{10,14},{12,0},{14,2},{1,5},{3,7},... | collective-permute-start | bytes 76808 | tf_op jit(solution)/shard_map/ppermute | solution.py:495
  89.3 2.4 %collective-permute-start.14 = (f32[20,320]{1,0:T(8,128)S(1)}, f32[20,320]{1,0:T(8,128)S(1)}, u32[]{:S(2)}, u32[]{:S(2)}) collective-permute-start(f32[20,320]{1,0:T(8,128)S(1)} %get-tuple-element.48), channel_id=1, source_target_pairs={{0,6},{2,8},{4,10},{6,12},{8,14},{10,0},{12,2},{14,4},{1,7},{3,9},... | collective-permute-start | bytes 76808 | tf_op jit(solution)/shard_map/ppermute | solution.py:495
  91.7 2.1 %collective-permute-start.15 = (f32[20,320]{1,0:T(8,128)S(1)}, f32[20,320]{1,0:T(8,128)S(1)}, u32[]{:S(2)}, u32[]{:S(2)}) collective-permute-start(f32[20,320]{1,0:T(8,128)S(1)} %get-tuple-element.49), channel_id=1, source_target_pairs={{0,8},{2,10},{4,12},{6,14},{8,0},{10,2},{12,4},{14,6},{1,9},{3,11}... | collective-permute-start | bytes 76808 | tf_op jit(solution)/shard_map/ppermute | solution.py:495
  93.8 2.4 %collective-permute-start.16 = (f32[20,320]{1,0:T(8,128)S(1)}, f32[20,320]{1,0:T(8,128)S(1)}, u32[]{:S(2)}, u32[]{:S(2)}) collective-permute-start(f32[20,320]{1,0:T(8,128)S(1)} %get-tuple-element.50), channel_id=1, source_target_pairs={{0,10},{2,12},{4,14},{6,0},{8,2},{10,4},{12,6},{14,8},{1,11},{3,13... | collective-permute-start | bytes 76808 | tf_op jit(solution)/shard_map/ppermute | solution.py:495
  96.2 1.2 %collective-permute-done.12.refs_1_ = f32[20,320]{1,0:T(8,128)S(1)} collective-permute-done((f32[20,320]{1,0:T(8,128)S(1)}, f32[20,320]{1,0:T(8,128)S(1)}, u32[]{:S(2)}, u32[]{:S(2)}) %collective-permute-start.12) | collective-permute-done | bytes 25632 | tf_op jit(solution)/shard_map/ppermute | solution.py:495
  97.5 2.5 %collective-permute-start.17 = (f32[20,320]{1,0:T(8,128)S(1)}, f32[20,320]{1,0:T(8,128)S(1)}, u32[]{:S(2)}, u32[]{:S(2)}) collective-permute-start(f32[20,320]{1,0:T(8,128)S(1)} %get-tuple-element.51), channel_id=1, source_target_pairs={{0,12},{2,14},{4,0},{6,2},{8,4},{10,6},{12,8},{14,10},{1,13},{3,15... | collective-permute-start | bytes 76808 | tf_op jit(solution)/shard_map/ppermute | solution.py:495
  100.0 0.2 collective-permute-done.13.refs_2_
  100.2 2.2 %collective-permute-start.18 = (f32[20,320]{1,0:T(8,128)S(1)}, f32[20,320]{1,0:T(8,128)S(1)}, u32[]{:S(2)}, u32[]{:S(2)}) collective-permute-start(f32[20,320]{1,0:T(8,128)S(1)} %get-tuple-element.52), channel_id=1, source_target_pairs={{0,14},{2,0},{4,2},{6,4},{8,6},{10,8},{12,10},{14,12},{1,15},{3,1}... | collective-permute-start | bytes 76808 | tf_op jit(solution)/shard_map/ppermute | solution.py:495
  102.4 0.0 collective-permute-done.14.refs_3_
  102.4 2.3 %collective-permute-done.15.refs_4_ = f32[20,320]{1,0:T(8,128)S(1)} collective-permute-done((f32[20,320]{1,0:T(8,128)S(1)}, f32[20,320]{1,0:T(8,128)S(1)}, u32[]{:S(2)}, u32[]{:S(2)}) %collective-permute-start.15) | collective-permute-done | bytes 25632 | tf_op jit(solution)/shard_map/ppermute | solution.py:495
  104.8 0.0 collective-permute-done.16.refs_5_
  104.8 0.0 collective-permute-done.17.refs_6_
  104.8 0.0 collective-permute-done.18.refs_7_
  104.8 0.7 last.1
  105.5 0.0 all-to-all-done.1.block_ref
  105.5 0.8 copy-done.12
  106.2 2.3 %unpack.1 = f32[192,640]{1,0:T(8,128)} custom-call(f32[64,16,128]{2,1,0:T(8,128)} %copy-done.12), custom_call_target="tpu_custom_call" | custom-call | tf_op jit(solution)/shard_map/unpack/pallas_call | solution.py:454
  (19 shorter events, 0.0 us)
Async XLA Ops:
  0.6 5.0 %collective-permute-start = (f32[192,640]{1,0:T(8,128)}, f32[192,640]{1,0:T(8,128)S(1)}, u32[]{:S(2)}, u32[]{:S(2)}) collective-permute-start(f32[192,640]{1,0:T(8,128)} %bitcast.26), channel_id=1, source_target_pairs={{0,64},{64,0},{1,65},{65,1},{2,66},{66,2},{3,67},{67,3},{4,68},{68... | collective-permute-start | bytes 1474568 | tf_op jit(solution)/shard_map/ppermute | solution.py:315
  4.0 2.4 %collective-permute-start.1 = (f32[192,640]{1,0:T(8,128)}, f32[192,640]{1,0:T(8,128)S(1)}, u32[]{:S(2)}, u32[]{:S(2)}) collective-permute-start(f32[192,640]{1,0:T(8,128)} %bitcast.28), channel_id=1, source_target_pairs={{0,64},{64,0},{1,65},{65,1},{2,66},{66,2},{3,67},{67,3},{4,68},{68... | collective-permute-start | bytes 1474568 | tf_op jit(solution)/shard_map/ppermute | solution.py:315
  5.7 0.8 copy-start.13
  6.4 0.8 copy-start.14
  7.1 18.6 %copy-start.4 = (bf16[768,768]{1,0:T(8,128)(2,1)S(1)}, bf16[768,768]{1,0:T(8,128)(2,1)}, u32[]{:S(2)}) copy-start(bf16[768,768]{1,0:T(8,128)(2,1)} %constant.37.clone.top_ref) | copy-start | bytes 3538948
  7.1 18.6 %copy-start.5 = (bf16[768,768]{1,0:T(8,128)(2,1)S(1)}, bf16[768,768]{1,0:T(8,128)(2,1)}, u32[]{:S(2)}) copy-start(bf16[768,768]{1,0:T(8,128)(2,1)} %constant.38.clone.low_ref) | copy-start | bytes 3538948
  21.9 20.5 %collective-permute-start.3 = (f32[160,1280]{1,0:T(8,128)}, f32[160,1280]{1,0:T(8,128)}, u32[]{:S(2)}, u32[]{:S(2)}) collective-permute-start(f32[160,1280]{1,0:T(8,128)} %get-tuple-element.32), channel_id=1, source_target_pairs={{0,16},{1,17},{2,18},{3,19},{4,20},{5,21},{6,22},{7,23},{8,24},{9,... | collective-permute-start | bytes 2457608 | tf_op jit(solution)/shard_map/ppermute | solution.py:310
  23.1 19.6 %collective-permute-start.4 = (f32[160,1280]{1,0:T(8,128)}, f32[160,1280]{1,0:T(8,128)}, u32[]{:S(2)}, u32[]{:S(2)}) collective-permute-start(f32[160,1280]{1,0:T(8,128)} %get-tuple-element.33), channel_id=1, source_target_pairs={{0,32},{1,33},{2,34},{3,35},{4,36},{5,37},{6,38},{7,39},{8,40},{9,... | collective-permute-start | bytes 2457608 | tf_op jit(solution)/shard_map/ppermute | solution.py:310
  23.5 20.5 %collective-permute-start.5 = (f32[160,1280]{1,0:T(8,128)}, f32[160,1280]{1,0:T(8,128)}, u32[]{:S(2)}, u32[]{:S(2)}) collective-permute-start(f32[160,1280]{1,0:T(8,128)} %get-tuple-element.34), channel_id=1, source_target_pairs={{0,48},{1,49},{2,50},{3,51},{4,52},{5,53},{6,54},{7,55},{8,56},{9,... | collective-permute-start | bytes 2457608 | tf_op jit(solution)/shard_map/ppermute | solution.py:310
  25.1 3.2 %collective-permute-start.2 = (f32[192,640]{1,0:T(8,128)}, f32[192,640]{1,0:T(8,128)S(1)}, u32[]{:S(2)}, u32[]{:S(2)}) collective-permute-start(f32[192,640]{1,0:T(8,128)} %get-tuple-element.30), channel_id=1, source_target_pairs={{0,64},{64,0},{1,65},{65,1},{2,66},{66,2},{3,67},{67,3},{4,68},{68... | collective-permute-start | bytes 1474568 | tf_op jit(solution)/shard_map/ppermute | solution.py:315
  25.7 1.2 %copy-start.6 = (f32[3,16,7,768]{3,1,2,0:T(8,128)S(1)}, f32[3,16,7,768]{3,1,2,0:T(8,128)}, u32[]{:S(2)}) copy-start(f32[3,16,7,768]{3,1,2,0:T(8,128)} %param.16) | copy-start | bytes 3096580
  27.0 1.4 %copy-start.7 = (f32[192,640]{1,0:T(8,128)S(1)}, f32[192,640]{1,0:T(8,128)}, u32[]{:S(2)}) copy-start(f32[192,640]{1,0:T(8,128)} %get-tuple-element.29.unit_ref) | copy-start | bytes 1474564
  27.0 1.4 %copy-start.8 = (s32[6]{0:T(128)S(1)}, s32[6]{0:T(128)}, u32[]{:S(2)}) copy-start(s32[6]{0:T(128)} %stack.28.place_ref) | copy-start | bytes 76
  27.0 1.4 %copy-start.10 = (f32[10,3]{0,1:T(4,128)S(1)}, f32[10,3]{0,1:T(4,128)}, u32[]{:S(2)}) copy-start(f32[10,3]{0,1:T(4,128)} %param.17) | copy-start | bytes 364
  30.4 29.3 %all-to-all-start = ((f32[64,16,128]{2,1,0:T(8,128)}), f32[64,16,128]{2,1,0:T(8,128)S(1)}, u32[]{:S(2)}, u32[]{:S(2)}) async-start(f32[64,16,128]{2,1,0:T(8,128)} %pack.1), calls=%async_computation | async-start | bytes 1048576 | tf_op jit(solution)/shard_map/all_to_all | solution.py:464
  44.0 1.1 %copy-start.11 = (f32[160,1280]{1,0:T(8,128)S(1)}, f32[160,1280]{1,0:T(8,128)}, u32[]{:S(2)}) copy-start(f32[160,1280]{1,0:T(8,128)} %get-tuple-element.31.refs_0_) | copy-start | bytes 2457604
  45.1 14.7 %copy-start = (bf16[768,768]{1,0:T(8,128)(2,1)S(1)}, bf16[768,768]{1,0:T(8,128)(2,1)}, u32[]{:S(2)}) copy-start(bf16[768,768]{1,0:T(8,128)(2,1)} %constant.39.clone.top_ref) | copy-start | bytes 3538948
  48.2 20.9 %collective-permute-start.10 = (f32[80,640]{1,0:T(8,128)}, f32[80,640]{1,0:T(8,128)S(1)}, u32[]{:S(2)}, u32[]{:S(2)}) collective-permute-start(f32[80,640]{1,0:T(8,128)} %get-tuple-element.42), channel_id=1, source_target_pairs={{0,129},{1,128},{2,131},{3,130},{4,133},{5,132},{6,135},{7,134},{8... | collective-permute-start | bytes 614408 | tf_op jit(solution)/shard_map/ppermute | solution.py:310
  49.3 19.8 %collective-permute-start.8 = (f32[80,640]{1,0:T(8,128)}, f32[80,640]{1,0:T(8,128)S(1)}, u32[]{:S(2)}, u32[]{:S(2)}) collective-permute-start(f32[80,640]{1,0:T(8,128)} %get-tuple-element.40), channel_id=1, source_target_pairs={{0,1},{1,0},{2,3},{3,2},{4,5},{5,4},{6,7},{7,6},{8,9},{9,8},{10,11... | collective-permute-start | bytes 614408 | tf_op jit(solution)/shard_map/ppermute | solution.py:310
  49.6 19.4 %collective-permute-start.9 = (f32[80,640]{1,0:T(8,128)}, f32[80,640]{1,0:T(8,128)S(1)}, u32[]{:S(2)}, u32[]{:S(2)}) collective-permute-start(f32[80,640]{1,0:T(8,128)} %get-tuple-element.41), channel_id=1, source_target_pairs={{0,128},{1,129},{2,130},{3,131},{4,132},{5,133},{6,134},{7,135},{8... | collective-permute-start | bytes 614408 | tf_op jit(solution)/shard_map/ppermute | solution.py:310
  59.8 1.3 %copy-start.1 = (bf16[768,768]{1,0:T(8,128)(2,1)S(1)}, bf16[768,768]{1,0:T(8,128)(2,1)}, u32[]{:S(2)}) copy-start(bf16[768,768]{1,0:T(8,128)(2,1)} %constant.40.clone.low_ref) | copy-start | bytes 3538948
  61.0 12.0 %copy-start.2 = (bf16[768,768]{1,0:T(8,128)(2,1)S(1)}, bf16[768,768]{1,0:T(8,128)(2,1)}, u32[]{:S(2)}) copy-start(bf16[768,768]{1,0:T(8,128)(2,1)} %constant.41.clone.top_ref) | copy-start | bytes 3538948
  61.1 12.0 %copy-start.3 = (bf16[768,768]{1,0:T(8,128)(2,1)S(1)}, bf16[768,768]{1,0:T(8,128)(2,1)}, u32[]{:S(2)}) copy-start(bf16[768,768]{1,0:T(8,128)(2,1)} %constant.42.clone.low_ref) | copy-start | bytes 3538948
  62.1 7.0 %collective-permute-start.6 = (f32[30,768]{1,0:T(8,128)S(1)}, f32[30,768]{1,0:T(8,128)S(1)}, u32[]{:S(2)}, u32[]{:S(2)}) collective-permute-start(f32[30,768]{1,0:T(8,128)S(1)} %get-tuple-element.38), channel_id=1, source_target_pairs={{0,64},{64,128},{128,192},{1,65},{65,129},{129,193},{2,66},{66,130... | collective-permute-start | bytes 276488 | tf_op jit(solution)/shard_map/ppermute | solution.py:484
  67.1 5.9 %collective-permute-start.7 = (f32[30,768]{1,0:T(8,128)S(1)}, f32[30,768]{1,0:T(8,128)S(1)}, u32[]{:S(2)}, u32[]{:S(2)}) collective-permute-start(f32[30,768]{1,0:T(8,128)S(1)} %get-tuple-element.39), channel_id=1, source_target_pairs={{64,0},{128,64},{192,128},{65,1},{129,65},{193,129},{66,2},{130,66... | collective-permute-start | bytes 276488 | tf_op jit(solution)/shard_map/ppermute | solution.py:485
  73.0 10.4 %copy-start.9 = (s32[6]{0:T(128)S(1)}, s32[6]{0:T(128)}, u32[]{:S(2)}) copy-start(s32[6]{0:T(128)} %stack.28.place_ref) | copy-start | bytes 76
  77.2 28.3 %all-to-all-start.1 = ((f32[64,16,128]{2,1,0:T(8,128)}), f32[64,16,128]{2,1,0:T(8,128)S(1)}, u32[]{:S(2)}, u32[]{:S(2)}) async-start(f32[64,16,128]{2,1,0:T(8,128)} %filter.1._), calls=%async_computation.1 | async-start | bytes 1048576 | tf_op jit(solution)/shard_map/all_to_all | solution.py:464
  84.2 1.4 %collective-permute-start.11 = (f32[80,320]{1,0:T(8,128)S(1)}, f32[80,320]{1,0:T(8,128)S(1)}, u32[]{:S(2)}, u32[]{:S(2)}) collective-permute-start(f32[80,320]{1,0:T(8,128)S(1)} %get-tuple-element.44), channel_id=1, source_target_pairs={{0,64},{64,0},{1,65},{65,1},{2,66},{66,2},{3,67},{67,3},{4,68},{68... | collective-permute-start | bytes 307208 | tf_op jit(solution)/shard_map/ppermute | solution.py:315
  86.2 11.3 %collective-permute-start.12 = (f32[20,320]{1,0:T(8,128)S(1)}, f32[20,320]{1,0:T(8,128)S(1)}, u32[]{:S(2)}, u32[]{:S(2)}) collective-permute-start(f32[20,320]{1,0:T(8,128)S(1)} %get-tuple-element.46), channel_id=1, source_target_pairs={{0,2},{2,4},{4,6},{6,8},{8,10},{10,12},{12,14},{14,0},{1,3},{3,5},... | collective-permute-start | bytes 76808 | tf_op jit(solution)/shard_map/ppermute | solution.py:495
  87.3 12.9 %collective-permute-start.13 = (f32[20,320]{1,0:T(8,128)S(1)}, f32[20,320]{1,0:T(8,128)S(1)}, u32[]{:S(2)}, u32[]{:S(2)}) collective-permute-start(f32[20,320]{1,0:T(8,128)S(1)} %get-tuple-element.47), channel_id=1, source_target_pairs={{0,4},{2,6},{4,8},{6,10},{8,12},{10,14},{12,0},{14,2},{1,5},{3,7},... | collective-permute-start | bytes 76808 | tf_op jit(solution)/shard_map/ppermute | solution.py:495
  89.3 13.1 %collective-permute-start.14 = (f32[20,320]{1,0:T(8,128)S(1)}, f32[20,320]{1,0:T(8,128)S(1)}, u32[]{:S(2)}, u32[]{:S(2)}) collective-permute-start(f32[20,320]{1,0:T(8,128)S(1)} %get-tuple-element.48), channel_id=1, source_target_pairs={{0,6},{2,8},{4,10},{6,12},{8,14},{10,0},{12,2},{14,4},{1,7},{3,9},... | collective-permute-start | bytes 76808 | tf_op jit(solution)/shard_map/ppermute | solution.py:495
  91.7 13.0 %collective-permute-start.15 = (f32[20,320]{1,0:T(8,128)S(1)}, f32[20,320]{1,0:T(8,128)S(1)}, u32[]{:S(2)}, u32[]{:S(2)}) collective-permute-start(f32[20,320]{1,0:T(8,128)S(1)} %get-tuple-element.49), channel_id=1, source_target_pairs={{0,8},{2,10},{4,12},{6,14},{8,0},{10,2},{12,4},{14,6},{1,9},{3,11}... | collective-permute-start | bytes 76808 | tf_op jit(solution)/shard_map/ppermute | solution.py:495
  93.8 10.9 %collective-permute-start.16 = (f32[20,320]{1,0:T(8,128)S(1)}, f32[20,320]{1,0:T(8,128)S(1)}, u32[]{:S(2)}, u32[]{:S(2)}) collective-permute-start(f32[20,320]{1,0:T(8,128)S(1)} %get-tuple-element.50), channel_id=1, source_target_pairs={{0,10},{2,12},{4,14},{6,0},{8,2},{10,4},{12,6},{14,8},{1,11},{3,13... | collective-permute-start | bytes 76808 | tf_op jit(solution)/shard_map/ppermute | solution.py:495
  97.5 7.3 %collective-permute-start.17 = (f32[20,320]{1,0:T(8,128)S(1)}, f32[20,320]{1,0:T(8,128)S(1)}, u32[]{:S(2)}, u32[]{:S(2)}) collective-permute-start(f32[20,320]{1,0:T(8,128)S(1)} %get-tuple-element.51), channel_id=1, source_target_pairs={{0,12},{2,14},{4,0},{6,2},{8,4},{10,6},{12,8},{14,10},{1,13},{3,15... | collective-permute-start | bytes 76808 | tf_op jit(solution)/shard_map/ppermute | solution.py:495
  100.2 4.6 %collective-permute-start.18 = (f32[20,320]{1,0:T(8,128)S(1)}, f32[20,320]{1,0:T(8,128)S(1)}, u32[]{:S(2)}, u32[]{:S(2)}) collective-permute-start(f32[20,320]{1,0:T(8,128)S(1)} %get-tuple-element.52), channel_id=1, source_target_pairs={{0,14},{2,0},{4,2},{6,4},{8,6},{10,8},{12,10},{14,12},{1,15},{3,1}... | collective-permute-start | bytes 76808 | tf_op jit(solution)/shard_map/ppermute | solution.py:495
  105.5 0.8 copy-start.12

commit v7 on v6

--- a/solution.py
+++ b/solution.py
@@ -34,9 +34,13 @@
 
 def dot3(left, right, dims):
     (a, b), (c, d) = left, right
-    numbers = (dims, ((), ()))
-    one = functools.partial(lax.dot_general, dimension_numbers=numbers, preferred_element_type=F32)
-    return one(a, c) + (one(a, d) + one(b, c))
+    (at,), (to,) = dims
+    return lax.dot_general(
+        jnp.concatenate([a, b, a], axis=at),
+        jnp.concatenate([c, c, d], axis=to),
+        dimension_numbers=(dims, ((), ())),
+        preferred_element_type=F32,
+    )
 
 
 def whole(n):
@@ -103,7 +107,7 @@
     out_ref[:, 15, :] = weights
 
 
-def pack_kernel(place_ref, mixing_ref, _, unit_ref, arrived_ref, block_ref):
+def pack_kernel(place_ref, mixing_ref, unit_ref, arrived_ref, block_ref):
     pack(unit_ref[...] + arrived_ref[...], mixing_ref, place_ref[0], block_ref)
 
 
@@ -134,21 +138,13 @@
     other_ref,
     *refs,
 ):
-    outs, (unit_ref, act_top, act_low, cot_top, cot_low, kept_ref) = refs[:4], refs[4:]
-    step = pl.program_id(0)
+    outs, kept_ref = refs[:4], refs[4]
     core = place_ref[1]
     points = act_ref.shape[0]
-
-    @pl.when(step == 0)
-    def _():
-        act_top[0:points, :], act_low[0:points, :] = split(act_ref[...])
-        act_top[points:, :], act_low[points:, :] = split(act_other_ref[...])
-        cot_top[0:points, :], cot_low[0:points, :] = split(cot_ref[...])
-        cot_top[points:, :], cot_low[points:, :] = split(cot_other_ref[...])
-
-    act, cot = (act_top[...], act_low[...]), (cot_top[...], cot_low[...])
-    w_in = split(in_ref[...].reshape(320, 640))
-    w_out = split(out_ref[...].reshape(320, 640))
+    act = split(jnp.concatenate([act_ref[...], act_other_ref[...]], axis=0))
+    cot = split(jnp.concatenate([cot_ref[...], cot_other_ref[...]], axis=0))
+    w_in = split(in_ref[...].reshape(640, 640))
+    w_out = split(out_ref[...].reshape(640, 640))
     preact = dot3(act, w_in, ((1,), (1,)))
     cdf = 0.5 * (1.0 + lax.erf(preact * (1.0 / math.sqrt(2.0))))
     density = jnp.exp(-0.5 * preact * preact) * (1.0 / math.sqrt(2.0 * math.pi))
@@ -156,58 +152,49 @@
     slope = cdf + preact * density
     grad = split(dot3(cot, w_out, ((1,), (1,))) * slope)
     term = dot3(grad, w_in, ((1,), (0,)))
+    own_ref[...] = cot_ref[...] + term[0:points]
+    other_ref[...] = term[points:]
     contract = ((0,), (0,))
     first = dot3(grad, act, contract)
     second = dot3(hidden, cot, contract)
 
-    @pl.when(step == 0)
-    def _():
-        unit_ref[...] = term
-
     @pl.when(core == 0)
     def _():
-        for x in range(2):
+        for x in range(4):
             rows = slice(160 * x, 160 * x + 160)
-            kept_ref[2 * step + x, :, 0:640] = first[rows]
-            kept_ref[2 * step + x, :, 640:1280] = second[rows]
+            kept_ref[x, :, 0:640] = first[rows]
+            kept_ref[x, :, 640:1280] = second[rows]
 
     @pl.when(core == 1)
     def _():
-        lanes = pl.ds(pl.multiple_of(640 * step, 128), 640)
-        for x in range(2):
+        for x in range(4):
             rows = slice(160 * x, 160 * x + 160)
+            row, lane = 80 * (x % 2), 640 * (x // 2)
             parts = zip(low_high(first[rows]), low_high(second[rows]))
             for right, (a, b) in enumerate(parts):
                 for upper in range(2):
                     cols = slice(320 * upper, 320 * upper + 320)
                     piece = jnp.concatenate([a[:, cols], b[:, cols]], axis=1)
-                    kept_ref[2 * upper + right, 80 * x : 80 * x + 80, lanes] = piece
-
-    @pl.when(step == 1)
-    def _():
-        total = unit_ref[...] + term
-        own_ref[...] = cot_ref[...] + total[0:points]
-        other_ref[...] = total[points:]
-        for m in range(4):
-            index = jnp.where(core == 0, along_x(place_ref, m), along_y(place_ref, m))
-            outs[m][...] = kept_ref[index]
+                    kept_ref[2 * upper + right, row : row + 80, lane : lane + 640] = piece
+
+    for m in range(4):
+        index = jnp.where(core == 0, along_x(place_ref, m), along_y(place_ref, m))
+        outs[m][...] = kept_ref[index]
 
 
 def mlp(place, act, act_other, cot, cot_other, weight_in, weight_out):
     points, width = act.shape
     units = weight_in.shape[0]
     full = lambda shape: pl.BlockSpec(shape, lambda i, place: (0,) * len(shape))
-    rows = pl.BlockSpec((2, None, 160, width), lambda i, place: (i, place[1], 0, 0))
+    rows = pl.BlockSpec((4, None, 160, width), lambda i, place: (0, place[1], 0, 0))
     return pl.pallas_call(
         mlp_kernel,
         grid_spec=pltpu.PrefetchScalarGridSpec(
             num_scalar_prefetch=1,
-            grid=(2,),
+            grid=(1,),
             in_specs=[full((points, width))] * 4 + [rows, rows],
             out_specs=[full((points, width))] * 2 + [full((160, 1280))] * 4,
-            scratch_shapes=[pltpu.VMEM((2 * points, width), F32)]
-            + [pltpu.VMEM((2 * points, width), BF16)] * 4
-            + [pltpu.VMEM((4, 160, 1280), F32)],
+            scratch_shapes=[pltpu.VMEM((4, 160, 1280), F32)],
         ),
         out_shape=[jax.ShapeDtypeStruct((points, width), F32)] * 2
         + [jax.ShapeDtypeStruct((160, 1280), F32)] * 4,
@@ -249,26 +236,19 @@
         outs[m][...] = kept_ref[index]
 
 
-def pair_kernel(place_ref, _, *refs):
-    ins, (mine_ref, send_ref) = refs[:4], refs[4:]
+def stack_kernel(place_ref, _, *refs):
+    ins, outs, kept_ref = refs[:4], refs[4:12], refs[12]
     total = (ins[0][...] + ins[1][...]) + (ins[2][...] + ins[3][...])
-    even = jnp.concatenate([total[:, 0:160], total[:, 320:480]], axis=1)
-    odd = jnp.concatenate([total[:, 160:320], total[:, 480:640]], axis=1)
-    first = place_ref[1] == 0
-    mine_ref[...] = jnp.where(first, even, odd)
-    send_ref[...] = jnp.where(first, odd, even)
-
-
-def stack_kernel(place_ref, mine_ref, arrived_ref, *refs):
-    outs, kept_ref = refs[:8], refs[8]
-    first = place_ref[1] == 0
-    mine, arrived = mine_ref[...], arrived_ref[...]
-    below, above = jnp.where(first, mine, arrived), jnp.where(first, arrived, mine)
-    for z in range(4):
-        kept_ref[z, 0:20, :] = below[20 * z : 20 * z + 20]
-        kept_ref[4 + z, 0:20, :] = above[20 * z : 20 * z + 20]
-    for m in range(8):
-        outs[m][...] = kept_ref[lax.rem(place_ref[5] + m, 8), 0:20, :]
+    for core in range(2):
+        at = 160 * core
+        part = jnp.concatenate([total[:, at : at + 160], total[:, 320 + at : 480 + at]], axis=1)
+        for z in range(4):
+            kept_ref[2 * z + core, 0:20, :] = part[20 * z : 20 * z + 20]
+    high, low = lax.div(place_ref[5], 4), lax.rem(place_ref[5], 4)
+    for a in range(4):
+        for b in range(2):
+            index = 2 * lax.rem(low + a, 4) + (1 - high if b else high)
+            outs[2 * a + b][...] = kept_ref[index, 0:20, :]
 
 
 def last_kernel(*refs):
@@ -294,6 +274,13 @@
     )(*operands[:scalars], *earlier, *operands[scalars:])
 
 
+def permute(value, target):
+    sizes = (2, 2, 4, 8, 2)
+    order = lambda at: int(np.ravel_multi_index(at, sizes))
+    pairs = [(order(at), order(target(*at))) for at in np.ndindex(*sizes)]
+    return lax.ppermute(value, AXES, pairs)
+
+
 def exchange(pieces, cores):
     def target(m, yl, co, x, z, yh):
         if cores[co] == "x":
@@ -302,13 +289,14 @@
             yl, yh = yl ^ (m >> 1), yh ^ (m & 1)
         return yl, co, x, z, yh
 
-    sizes = (2, 2, 4, 8, 2)
-    order = lambda at: int(np.ravel_multi_index(at, sizes))
-    moved = [pieces[0]]
-    for m in (1, 2, 3):
-        pairs = [(order(at), order(target(m, *at))) for at in np.ndindex(*sizes)]
-        moved.append(lax.ppermute(pieces[m], AXES, pairs))
-    return moved
+    return [pieces[0]] + [permute(pieces[m], functools.partial(target, m)) for m in (1, 2, 3)]
+
+
+def exchange_z(pieces):
+    def target(m, yl, co, x, z, yh):
+        return yl, (z // 4) ^ (m & 1), x, 4 * co + (z + (m >> 1)) % 4, yh
+
+    return [permute(pieces[m], functools.partial(target, m)) for m in range(8)]
 
 
 def to_core(value):
@@ -352,23 +340,23 @@
     )(block, jnp.asarray(top), jnp.asarray(low), earlier)
 
 
-def kernel_spectrum_kernel(kernel_ref, top_ref, low_ref, out_ref):
+def kernel_spectrum_kernel(kernel_ref, top_ref, low_ref, _, out_ref):
     out_ref[...] = dot3(split(kernel_ref[...]), (top_ref[...], low_ref[...]), ((1,), (0,)))
 
 
-def kernel_spectrum(kernels):
+def kernel_spectrum(kernels, earlier):
     top, low = forward_table(np.arange(CIRCLE))
     rows = BASIS * TAPS * ROWS
     flat = kernels.transpose(0, 2, 1, 3).reshape(rows, CIRCLE)
     return pl.pallas_call(
         kernel_spectrum_kernel,
-        in_specs=whole(3),
+        in_specs=whole(3) + EARLIER,
         out_specs=whole(1)[0],
         out_shape=jax.ShapeDtypeStruct((rows, CIRCLE), F32),
         compiler_params=params(24),
         cost_estimate=cost(6 * rows * CIRCLE * CIRCLE, 5_000_000),
         name="kernel_spectrum",
-    )(flat, jnp.asarray(top), jnp.asarray(low))
+    )(flat, jnp.asarray(top), jnp.asarray(low), earlier)
 
 
 def filter_kernel(
@@ -471,30 +459,24 @@
     cot = cotangent.transpose(1, 0, 2).reshape(points, width)
     place = jnp.stack([lax.axis_index(axis) for axis in (LON, "co", "yl", "yh", "x", "z")])
     unit, other, *pieces = mlp(place, act, to_core(act), cot, to_core(cot), weight_in, weight_out)
-    kernel = kernel_spectrum(kernels)
     operands = (place, mixing.T, unit, to_core(other))
-    (block,) = small(pack_kernel, operands, [(SHARDS, 16, 128)], 2, (), (kernel,), "pack")
+    (block,) = small(pack_kernel, operands, [(SHARDS, 16, 128)], 2, name="pack")
     moved = exchange(pieces, "xy")
     spread = across(block)
     kept = (pltpu.VMEM((4, 80, 640), F32),)
     swapped = small(swap_kernel, (place, *moved), [(80, 640)] * 4, 1, kept, (), "swap", 10**10)
-    data, first, final, own_mixing = spectrum(spread, swapped[0])
+    kernel = kernel_spectrum(kernels, swapped[0])
+    moved = exchange(swapped, "yx")
+    kept = (pltpu.VMEM((8, 24, 320), F32),)
+    stacked = small(stack_kernel, (place, *moved), [(20, 320)] * 8, 1, kept, (kernel,), "stack")
+    data, first, final, own_mixing = spectrum(spread, stacked[0])
     forward = [(i, i + 1) for i in range(3)]
     backward = [(target, source) for source, target in forward]
     before = lax.ppermute(final, LAT, forward)
     beyond = lax.ppermute(first, LAT, backward)
-    moved = exchange(swapped, "yx")
-    sent = filtered(own_mixing, data, before, beyond, kernel, moved)
+    sent = filtered(own_mixing, data, before, beyond, kernel, ())
     result = across(sent)
-    mine, send = small(pair_kernel, (place, *moved), [(80, 320)] * 2, 1, (), (sent,), "pair")
-    kept = (pltpu.VMEM((8, 24, 320), F32),)
-    stacked = small(
-        stack_kernel, (place, mine, to_core(send)), [(20, 320)] * 8, 1, kept, name="stack"
-    )
-    moved = [stacked[0]] + [
-        lax.ppermute(stacked[m], "z", [(i, (i + m) % 8) for i in range(8)]) for m in range(1, 8)
-    ]
-    grad_in, grad_out = small(last_kernel, moved, [(20, 160)] * 2, name="last")
+    grad_in, grad_out = small(last_kernel, exchange_z(stacked), [(20, 160)] * 2, name="last")
     field = unpack(result).reshape(COLS, ROWS, width).transpose(1, 0, 2)
     return (field, grad_in, grad_out)
 

time: 109 us -> 117 us (1.073)
  starting transfers between devices: 50.2 us -> 61.7 us
  Pallas kernels: 30.7 us -> 26.5 us
    all_to_all x2, waiting for transfers between devices: 8.76 us -> 0.59 us  [across(): return lax.all_to_all(block, LON, split_axis=0, concat_axis=0, tiled=True)]
    ppermute x13 -> x14, waiting for transfers between devices: 5.34 us -> 13.4 us  [permute(): return lax.ppermute(value, AXES, pairs)]
    ppermute x13 -> x14, starting transfers between devices: 20.9 us -> 28.5 us  [permute(): return lax.ppermute(value, AXES, pairs)]
    all_to_all x2, starting transfers between devices: 18.2 us -> 22.5 us  [across(): return lax.all_to_all(block, LON, split_axis=0, concat_axis=0, tiled=True)]
    pallas_call x1, Pallas kernels: 14.7 us -> 12.5 us  [mlp(): pl.pallas_call(mlp_kernel, grid_spec=pltpu.PrefetchScalarGridSpec(num_sca...]
    pallas_call x5 -> x4, Pallas kernels: 7.05 us -> 5.07 us  [small(): pl.pallas_call(kernel, in_specs=[pl.BlockSpec(memory_space=pltpu.SMEM)] *...]
    ppermute x4 -> x3, waiting for transfers between devices: 3.01 us -> 3.32 us  [to_core(): return lax.ppermute(value, 'co', [(0, 1), (1, 0)])]
    unnamed x30 -> x28, local copies, waits for them, and re-layouts: 5.22 us -> 5.05 us
  transfers between devices with their start and end apart: 21 -> 21, of which waited for: 10 -> 9; matrix products, arithmetic and copies ran while one was open for 1% -> 1% of each run, Pallas kernels for 9% -> 6%
where the time goes in v7:
time: 117 us; the launch traced here: 116 us
  starting transfers between devices  61.7 us (53%)
  Pallas kernels  26.5 us (23%)
  waiting for transfers between devices  21.3 us (18%)
  local copies, waits for them, and re-layouts  5.73 us (5%)
    ppermute x14, starting transfers between devices, permute(): return lax.ppermute(value, AXES, pairs)  28.5 us
    all_to_all x2, starting transfers between devices, across(): return lax.all_to_all(block, LON, split_axis=0, concat_axis=0, tiled=True)  22.5 us
    ppermute x14, waiting for transfers between devices, permute(): return lax.ppermute(value, AXES, pairs)  13.4 us
    pallas_call x1, Pallas kernels, mlp(): pl.pallas_call(mlp_kernel, grid_spec=pltpu.PrefetchScalarGridSpec(num_sca...  12.5 us
    pallas_call x4, Pallas kernels, small(): pl.pallas_call(kernel, in_specs=[pl.BlockSpec(memory_space=pltpu.SMEM)] *...  5.07 us
    unnamed x28, local copies, waits for them, and re-layouts  5.05 us
    ppermute x1, starting transfers between devices, per_device(): before = lax.ppermute(final, LAT, forward)  4.59 us
    pallas_call x1, Pallas kernels, filtered(): pl.pallas_call(filter_kernel, in_specs=[pl.BlockSpec(memory_space=pltpu.S...  4.17 us
  transfers between devices with their start and end apart: 21, of which 9 were waited for; matrix products, arithmetic and copies ran while one was open for 1% of the time, Pallas kernels for 6%

profile of v7, /device:TPU:1, one launch (start us, length us, event | category | flops | bytes accessed | tf_op | source)
XLA Modules:
  0.0 115.9 jit_solution(2186900944044940412)
XLA Ops:
  0.6 3.3 %collective-permute-start = (f32[192,640]{1,0:T(8,128)}, f32[192,640]{1,0:T(8,128)S(1)}, u32[]{:S(2)}, u32[]{:S(2)}) collective-permute-start(f32[192,640]{1,0:T(8,128)} %bitcast.26), channel_id=1, source_target_pairs={{0,64},{64,0},{1,65},{65,1},{2,66},{66,2},{3,67},{67,3},{4,68},{68... | collective-permute-start | bytes 1474568 | tf_op jit(solution)/shard_map/ppermute | solution.py:303
  4.0 0.1 collective-permute-start.1
  4.1 0.7 stack.28.place_ref
  4.7 0.9 collective-permute-done.act_other_ref
  5.7 0.7 collective-permute-done.1.cot_other_ref
  6.4 0.1 copy-done.12
  6.4 0.7 copy-done.13
  7.2 12.5 %mlp.1 = (f32[192,640]{1,0:T(8,128)}, f32[192,640]{1,0:T(8,128)}, f32[160,1280]{1,0:T(8,128)}, f32[160,1280]{1,0:T(8,128)}, f32[160,1280]{1,0:T(8,128)}, /*index=5*/f32[160,1280]{1,0:T(8,128)}) custom-call(s32[6]{0:T(128)} %stack.28.place_ref, f32[192,640]{1,0:T(8,128)} %bitcast.27, f32[192,640]{1,0:T(8,128)} %copy-done.12, f32[192,640]{1,0:T(8,128)} %bitcast.29, ...), custom_call_target="tpu_custom_call" | custom-call | flops 4718592000 | bytes 12000000 | tf_op jit(solution)/shard_map/mlp/pallas_call | solution.py:190
  19.6 1.2 %collective-permute-start.3 = (f32[160,1280]{1,0:T(8,128)}, f32[160,1280]{1,0:T(8,128)S(1)}, u32[]{:S(2)}, u32[]{:S(2)}) collective-permute-start(f32[160,1280]{1,0:T(8,128)} %get-tuple-element.30), channel_id=1, source_target_pairs={{0,16},{1,17},{2,18},{3,19},{4,20},{5,21},{6,22},{7,23},{8,24},{9,... | collective-permute-start | bytes 2457608 | tf_op jit(solution)/shard_map/ppermute | solution.py:281
  20.8 0.4 collective-permute-start.4
  21.2 1.7 %collective-permute-start.5 = (f32[160,1280]{1,0:T(8,128)}, f32[160,1280]{1,0:T(8,128)}, u32[]{:S(2)}, u32[]{:S(2)}) collective-permute-start(f32[160,1280]{1,0:T(8,128)} %get-tuple-element.32), channel_id=1, source_target_pairs={{0,48},{1,49},{2,50},{3,51},{4,52},{5,53},{6,54},{7,55},{8,56},{9,... | collective-permute-start | bytes 2457608 | tf_op jit(solution)/shard_map/ppermute | solution.py:281
  22.9 0.6 collective-permute-start.2
  23.5 1.7 %collective-permute-done.2.arrived_ref = f32[192,640]{1,0:T(8,128)S(1)} collective-permute-done((f32[192,640]{1,0:T(8,128)}, f32[192,640]{1,0:T(8,128)S(1)}, u32[]{:S(2)}, u32[]{:S(2)}) %collective-permute-start.2) | collective-permute-done | bytes 491552 | tf_op jit(solution)/shard_map/ppermute | solution.py:303
  25.2 0.0 copy-done.8
  25.2 0.0 copy-done.9
  25.2 1.0 copy-done.7
  26.3 2.0 %pack.1 = f32[64,16,128]{2,1,0:T(8,128)} custom-call(s32[6]{0:T(128)S(1)} %copy-done.8, f32[3,10]{1,0:T(4,128)S(1)} %bitcast.22, f32[192,640]{1,0:T(8,128)S(1)} %copy-done.7, f32[192,640]{1,0:T(8,128)S(1)} %collective-permute-done.2.arrived_ref), custom_call_target="tpu_custom_call" | custom-call | tf_op jit(solution)/shard_map/pack/pallas_call | solution.py:263
  28.3 12.5 %all-to-all-start = ((f32[64,16,128]{2,1,0:T(8,128)}), f32[64,16,128]{2,1,0:T(8,128)S(1)}, u32[]{:S(2)}, u32[]{:S(2)}) async-start(f32[64,16,128]{2,1,0:T(8,128)} %pack.1), calls=%async_computation | async-start | bytes 1048576 | tf_op jit(solution)/shard_map/all_to_all | solution.py:452
  40.8 0.0 collective-permute-done.3.refs_1_
  40.8 0.0 collective-permute-done.4.refs_2_
  40.8 0.8 collective-permute-done.5.refs_3_
  41.6 1.1 copy-done.10
  42.8 1.7 %swap.1 = (f32[80,640]{1,0:T(8,128)S(1)}, f32[80,640]{1,0:T(8,128)S(1)}, f32[80,640]{1,0:T(8,128)S(1)}, f32[80,640]{1,0:T(8,128)S(1)}) custom-call(s32[6]{0:T(128)S(1)} %copy-done.8, f32[160,1280]{1,0:T(8,128)S(1)} %copy-done.10, f32[160,1280]{1,0:T(8,128)S(1)} %collective-permute-done.3.refs_1_, f32[160,1280]{1,0:T(8,128)S(1)} %collective-permute-done.4.refs_2_, ...), custom_call_target="tpu_custom_call" | custom-call | flops 10000000000 | bytes 4000000 | tf_op jit(solution)/shard_map/swap/pallas_call | solution.py:263
  44.4 0.1 collective-permute-start.6
  44.6 2.6 %collective-permute-start.7 = (f32[80,640]{1,0:T(8,128)S(1)}, f32[80,640]{1,0:T(8,128)S(1)}, u32[]{:S(2)}, u32[]{:S(2)}) collective-permute-start(f32[80,640]{1,0:T(8,128)S(1)} %get-tuple-element.35), channel_id=1, source_target_pairs={{0,128},{1,129},{2,130},{3,131},{4,132},{5,133},{6,134},{7,135},{8... | collective-permute-start | bytes 614408 | tf_op jit(solution)/shard_map/ppermute | solution.py:281
  47.2 1.1 collective-permute-start.8
  48.2 0.0 copy-done.2
  48.2 0.0 copy-done.3
  48.2 1.4 %kernel_spectrum.1._.kernel_ref = f32[336,768]{1,0:T(8,128)S(1)} custom-call(f32[336,768]{1,0:T(8,128)S(1)} %bitcast.21, bf16[768,768]{1,0:T(8,128)(2,1)S(1)} %copy-done.3, bf16[768,768]{1,0:T(8,128)(2,1)S(1)} %copy-done.2, f32[80,640]{1,0:T(8,128)S(1)} %get-tuple-element.33._.refs_0_), custom_call_target="tpu_custom_call" | custom-call | flops 1189085184 | bytes 5000000 | tf_op jit(solution)/shard_map/kernel_spectrum/pallas_call | solution.py:351
  49.6 0.0 copy-start.4
  49.6 3.1 %collective-permute-done.6.refs_1_ = f32[80,640]{1,0:T(8,128)S(1)} collective-permute-done((f32[80,640]{1,0:T(8,128)S(1)}, f32[80,640]{1,0:T(8,128)S(1)}, u32[]{:S(2)}, u32[]{:S(2)}) %collective-permute-start.6) | collective-permute-done | bytes 204832 | tf_op jit(solution)/shard_map/ppermute | solution.py:281
  52.8 4.3 %collective-permute-done.7.refs_2_ = f32[80,640]{1,0:T(8,128)S(1)} collective-permute-done((f32[80,640]{1,0:T(8,128)S(1)}, f32[80,640]{1,0:T(8,128)S(1)}, u32[]{:S(2)}, u32[]{:S(2)}) %collective-permute-start.7) | collective-permute-done | bytes 204832 | tf_op jit(solution)/shard_map/ppermute | solution.py:281
  57.1 0.0 collective-permute-done.8.refs_3_
  57.1 0.7 stack.29
  57.8 0.6 all-to-all-done.block_ref
  58.4 1.3 %copy-done.5 = bf16[768,768]{1,0:T(8,128)(2,1)S(1)} copy-done((bf16[768,768]{1,0:T(8,128)(2,1)S(1)}, bf16[768,768]{1,0:T(8,128)(2,1)}, u32[]{:S(2)}) %copy-start.5) | copy-done | bytes 1179672
  59.7 1.0 spectrum.1
  60.7 4.6 %collective-permute-start.9 = (f32[30,768]{1,0:T(8,128)S(1)}, f32[30,768]{1,0:T(8,128)S(1)}, u32[]{:S(2)}, u32[]{:S(2)}) collective-permute-start(f32[30,768]{1,0:T(8,128)S(1)} %get-tuple-element.40), channel_id=1, source_target_pairs={{0,64},{64,128},{128,192},{1,65},{65,129},{129,193},{2,66},{66,130... | collective-permute-start | bytes 276488 | tf_op jit(solution)/shard_map/ppermute | solution.py:475
  65.3 1.9 %collective-permute-start.10 = (f32[30,768]{1,0:T(8,128)S(1)}, f32[30,768]{1,0:T(8,128)S(1)}, u32[]{:S(2)}, u32[]{:S(2)}) collective-permute-start(f32[30,768]{1,0:T(8,128)S(1)} %get-tuple-element.41), channel_id=1, source_target_pairs={{64,0},{128,64},{192,128},{65,1},{129,65},{193,129},{66,2},{130,66... | collective-permute-start | bytes 276488 | tf_op jit(solution)/shard_map/ppermute | solution.py:476
  67.2 0.0 collective-permute-done.9.before_ref
  67.2 4.0 %collective-permute-done.10.after_ref = f32[30,768]{1,0:T(8,128)S(1)} collective-permute-done((f32[30,768]{1,0:T(8,128)S(1)}, f32[30,768]{1,0:T(8,128)S(1)}, u32[]{:S(2)}, u32[]{:S(2)}) %collective-permute-start.10) | collective-permute-done | bytes 92192 | tf_op jit(solution)/shard_map/ppermute | solution.py:476
  71.2 0.0 copy-done
  71.2 4.2 %filter.1 = f32[64,16,128]{2,1,0:T(8,128)} custom-call(f32[1,128]{1,0:T(1,128)S(1)} %get-tuple-element.38.mixing_ref, f32[160,768]{1,0:T(8,128)S(1)} %get-tuple-element.39.data_ref, f32[30,768]{1,0:T(8,128)S(1)} %collective-permute-done.9.before_ref, f32[30,768]{1,0:T(8,128)S(1)} %collective-permute-done.10.after_ref, ...), custom_call_target="tpu_custom_call" | custom-call | flops 566231040 | bytes 5000000 | tf_op jit(solution)/shard_map/filter/pallas_call | solution.py:409
  75.4 10.1 %all-to-all-start.1 = ((f32[64,16,128]{2,1,0:T(8,128)}), f32[64,16,128]{2,1,0:T(8,128)S(1)}, u32[]{:S(2)}, u32[]{:S(2)}) async-start(f32[64,16,128]{2,1,0:T(8,128)} %filter.1), calls=%async_computation.1 | async-start | bytes 1048576 | tf_op jit(solution)/shard_map/all_to_all | solution.py:452
  85.5 5.0 %collective-permute-start.12 = (f32[20,320]{1,0:T(8,128)S(1)}, f32[20,320]{1,0:T(8,128)S(1)}, u32[]{:S(2)}, u32[]{:S(2)}) collective-permute-start(f32[20,320]{1,0:T(8,128)S(1)} %get-tuple-element.42), channel_id=1, source_target_pairs={{0,64},{1,65},{2,66},{3,67},{4,68},{5,69},{6,70},{7,71},{8,0},{9,1... | collective-permute-start | bytes 76808 | tf_op jit(solution)/shard_map/ppermute | solution.py:281
  90.5 0.0 collective-permute-start.13
  90.5 0.0 collective-permute-start.14
  90.5 3.0 %collective-permute-start.15 = (f32[20,320]{1,0:T(8,128)S(1)}, f32[20,320]{1,0:T(8,128)S(1)}, u32[]{:S(2)}, u32[]{:S(2)}) collective-permute-start(f32[20,320]{1,0:T(8,128)S(1)} %get-tuple-element.45), channel_id=1, source_target_pairs={{0,4},{1,5},{2,6},{3,7},{4,0},{5,1},{6,2},{7,3},{8,68},{9,69},{10,... | collective-permute-start | bytes 76808 | tf_op jit(solution)/shard_map/ppermute | solution.py:281
  93.5 2.4 %collective-permute-start.16 = (f32[20,320]{1,0:T(8,128)S(1)}, f32[20,320]{1,0:T(8,128)S(1)}, u32[]{:S(2)}, u32[]{:S(2)}) collective-permute-start(f32[20,320]{1,0:T(8,128)S(1)} %get-tuple-element.46), channel_id=1, source_target_pairs={{0,68},{1,69},{2,70},{3,71},{4,64},{5,65},{6,66},{7,67},{8,4},{9,5... | collective-permute-start | bytes 76808 | tf_op jit(solution)/shard_map/ppermute | solution.py:281
  95.8 0.0 collective-permute-done.12.refs_1_
  95.8 2.7 %collective-permute-start.17 = (f32[20,320]{1,0:T(8,128)S(1)}, f32[20,320]{1,0:T(8,128)S(1)}, u32[]{:S(2)}, u32[]{:S(2)}) collective-permute-start(f32[20,320]{1,0:T(8,128)S(1)} %get-tuple-element.47), channel_id=1, source_target_pairs={{0,6},{1,7},{2,0},{3,1},{4,2},{5,3},{6,4},{7,5},{8,70},{9,71},{10,... | collective-permute-start | bytes 76808 | tf_op jit(solution)/shard_map/ppermute | solution.py:281
  98.5 0.0 collective-permute-done.13.refs_2_
  98.5 4.4 %collective-permute-start.18 = (f32[20,320]{1,0:T(8,128)S(1)}, f32[20,320]{1,0:T(8,128)S(1)}, u32[]{:S(2)}, u32[]{:S(2)}) collective-permute-start(f32[20,320]{1,0:T(8,128)S(1)} %get-tuple-element.48), channel_id=1, source_target_pairs={{0,70},{1,71},{2,64},{3,65},{4,66},{5,67},{6,68},{7,69},{8,6},{9,7... | collective-permute-start | bytes 76808 | tf_op jit(solution)/shard_map/ppermute | solution.py:281
  103.0 0.0 collective-permute-done.14.refs_3_
  103.0 4.1 %collective-permute-start.11 = (f32[20,320]{1,0:T(8,128)S(1)}, f32[20,320]{1,0:T(8,128)S(1)}, u32[]{:S(2)}, u32[]{:S(2)}) collective-permute-start(f32[20,320]{1,0:T(8,128)S(1)} %get-tuple-element.37._), channel_id=1, source_target_pairs={{0,0},{1,1},{2,2},{3,3},{4,4},{5,5},{6,6},{7,7},{8,64},{9,65},{10,... | collective-permute-start | bytes 76808 | tf_op jit(solution)/shard_map/ppermute | solution.py:281
  107.0 0.0 collective-permute-done.15.refs_4_
  107.0 0.0 collective-permute-done.16.refs_5_
  107.0 0.0 collective-permute-done.17.refs_6_
  107.1 0.0 collective-permute-done.18.refs_7_
  107.1 5.1 %collective-permute-done.11.refs_0_ = f32[20,320]{1,0:T(8,128)S(1)} collective-permute-done((f32[20,320]{1,0:T(8,128)S(1)}, f32[20,320]{1,0:T(8,128)S(1)}, u32[]{:S(2)}, u32[]{:S(2)}) %collective-permute-start.11) | collective-permute-done | bytes 25632 | tf_op jit(solution)/shard_map/ppermute | solution.py:281
  112.1 0.7 last.1
  112.8 0.0 all-to-all-done.1.block_ref
  112.8 0.8 copy-done.11
  113.6 2.3 %unpack.1 = f32[192,640]{1,0:T(8,128)} custom-call(f32[64,16,128]{2,1,0:T(8,128)} %copy-done.11), custom_call_target="tpu_custom_call" | custom-call | tf_op jit(solution)/shard_map/unpack/pallas_call | solution.py:442
  (16 shorter events, 0.0 us)
Async XLA Ops:
  0.6 5.0 %collective-permute-start = (f32[192,640]{1,0:T(8,128)}, f32[192,640]{1,0:T(8,128)S(1)}, u32[]{:S(2)}, u32[]{:S(2)}) collective-permute-start(f32[192,640]{1,0:T(8,128)} %bitcast.26), channel_id=1, source_target_pairs={{0,64},{64,0},{1,65},{65,1},{2,66},{66,2},{3,67},{67,3},{4,68},{68... | collective-permute-start | bytes 1474568 | tf_op jit(solution)/shard_map/ppermute | solution.py:303
  4.0 2.4 %collective-permute-start.1 = (f32[192,640]{1,0:T(8,128)}, f32[192,640]{1,0:T(8,128)S(1)}, u32[]{:S(2)}, u32[]{:S(2)}) collective-permute-start(f32[192,640]{1,0:T(8,128)} %bitcast.28), channel_id=1, source_target_pairs={{0,64},{64,0},{1,65},{65,1},{2,66},{66,2},{3,67},{67,3},{4,68},{68... | collective-permute-start | bytes 1474568 | tf_op jit(solution)/shard_map/ppermute | solution.py:303
  5.7 0.8 copy-start.12
  6.4 0.8 copy-start.13
  7.1 18.1 %copy-start.8 = (s32[6]{0:T(128)S(1)}, s32[6]{0:T(128)}, u32[]{:S(2)}) copy-start(s32[6]{0:T(128)} %stack.28.place_ref) | copy-start | bytes 76
  7.1 18.1 %copy-start.9 = (f32[10,3]{0,1:T(4,128)S(1)}, f32[10,3]{0,1:T(4,128)}, u32[]{:S(2)}) copy-start(f32[10,3]{0,1:T(4,128)} %param.17) | copy-start | bytes 364
  19.6 21.1 %collective-permute-start.3 = (f32[160,1280]{1,0:T(8,128)}, f32[160,1280]{1,0:T(8,128)S(1)}, u32[]{:S(2)}, u32[]{:S(2)}) collective-permute-start(f32[160,1280]{1,0:T(8,128)} %get-tuple-element.30), channel_id=1, source_target_pairs={{0,16},{1,17},{2,18},{3,19},{4,20},{5,21},{6,22},{7,23},{8,24},{9,... | collective-permute-start | bytes 2457608 | tf_op jit(solution)/shard_map/ppermute | solution.py:281
  20.8 20.0 %collective-permute-start.4 = (f32[160,1280]{1,0:T(8,128)}, f32[160,1280]{1,0:T(8,128)S(1)}, u32[]{:S(2)}, u32[]{:S(2)}) collective-permute-start(f32[160,1280]{1,0:T(8,128)} %get-tuple-element.31), channel_id=1, source_target_pairs={{0,32},{1,33},{2,34},{3,35},{4,36},{5,37},{6,38},{7,39},{8,40},{9,... | collective-permute-start | bytes 2457608 | tf_op jit(solution)/shard_map/ppermute | solution.py:281
  21.2 20.4 %collective-permute-start.5 = (f32[160,1280]{1,0:T(8,128)}, f32[160,1280]{1,0:T(8,128)}, u32[]{:S(2)}, u32[]{:S(2)}) collective-permute-start(f32[160,1280]{1,0:T(8,128)} %get-tuple-element.32), channel_id=1, source_target_pairs={{0,48},{1,49},{2,50},{3,51},{4,52},{5,53},{6,54},{7,55},{8,56},{9,... | collective-permute-start | bytes 2457608 | tf_op jit(solution)/shard_map/ppermute | solution.py:281
  22.9 2.3 %collective-permute-start.2 = (f32[192,640]{1,0:T(8,128)}, f32[192,640]{1,0:T(8,128)S(1)}, u32[]{:S(2)}, u32[]{:S(2)}) collective-permute-start(f32[192,640]{1,0:T(8,128)} %get-tuple-element.28), channel_id=1, source_target_pairs={{0,64},{64,0},{1,65},{65,1},{2,66},{66,2},{3,67},{67,3},{4,68},{68... | collective-permute-start | bytes 1474568 | tf_op jit(solution)/shard_map/ppermute | solution.py:303
  25.2 1.0 copy-start.7
  28.3 30.1 %all-to-all-start = ((f32[64,16,128]{2,1,0:T(8,128)}), f32[64,16,128]{2,1,0:T(8,128)S(1)}, u32[]{:S(2)}, u32[]{:S(2)}) async-start(f32[64,16,128]{2,1,0:T(8,128)} %pack.1), calls=%async_computation | async-start | bytes 1048576 | tf_op jit(solution)/shard_map/all_to_all | solution.py:452
  41.6 1.1 copy-start.10
  42.8 5.5 %copy-start.2 = (bf16[768,768]{1,0:T(8,128)(2,1)S(1)}, bf16[768,768]{1,0:T(8,128)(2,1)}, u32[]{:S(2)}) copy-start(bf16[768,768]{1,0:T(8,128)(2,1)} %constant.38.clone.low_ref) | copy-start | bytes 3538948
  42.8 5.5 %copy-start.3 = (bf16[768,768]{1,0:T(8,128)(2,1)S(1)}, bf16[768,768]{1,0:T(8,128)(2,1)}, u32[]{:S(2)}) copy-start(bf16[768,768]{1,0:T(8,128)(2,1)} %constant.37.clone.top_ref) | copy-start | bytes 3538948
  42.8 5.5 %copy-start.6 = (f32[3,16,7,768]{3,1,2,0:T(8,128)S(1)}, f32[3,16,7,768]{3,1,2,0:T(8,128)}, u32[]{:S(2)}) copy-start(f32[3,16,7,768]{3,1,2,0:T(8,128)} %param.16) | copy-start | bytes 3096580
  44.4 8.3 %collective-permute-start.6 = (f32[80,640]{1,0:T(8,128)S(1)}, f32[80,640]{1,0:T(8,128)S(1)}, u32[]{:S(2)}, u32[]{:S(2)}) collective-permute-start(f32[80,640]{1,0:T(8,128)S(1)} %get-tuple-element.34), channel_id=1, source_target_pairs={{0,1},{1,0},{2,3},{3,2},{4,5},{5,4},{6,7},{7,6},{8,9},{9,8},{10,11... | collective-permute-start | bytes 614408 | tf_op jit(solution)/shard_map/ppermute | solution.py:281
  44.6 12.6 %collective-permute-start.7 = (f32[80,640]{1,0:T(8,128)S(1)}, f32[80,640]{1,0:T(8,128)S(1)}, u32[]{:S(2)}, u32[]{:S(2)}) collective-permute-start(f32[80,640]{1,0:T(8,128)S(1)} %get-tuple-element.35), channel_id=1, source_target_pairs={{0,128},{1,129},{2,130},{3,131},{4,132},{5,133},{6,134},{7,135},{8... | collective-permute-start | bytes 614408 | tf_op jit(solution)/shard_map/ppermute | solution.py:281
  47.2 10.0 %collective-permute-start.8 = (f32[80,640]{1,0:T(8,128)S(1)}, f32[80,640]{1,0:T(8,128)S(1)}, u32[]{:S(2)}, u32[]{:S(2)}) collective-permute-start(f32[80,640]{1,0:T(8,128)S(1)} %get-tuple-element.36), channel_id=1, source_target_pairs={{0,129},{1,128},{2,131},{3,130},{4,133},{5,132},{6,135},{7,134},{8... | collective-permute-start | bytes 614408 | tf_op jit(solution)/shard_map/ppermute | solution.py:281
  49.6 8.8 %copy-start.4 = (bf16[768,768]{1,0:T(8,128)(2,1)S(1)}, bf16[768,768]{1,0:T(8,128)(2,1)}, u32[]{:S(2)}) copy-start(bf16[768,768]{1,0:T(8,128)(2,1)} %constant.40.clone.low_ref) | copy-start | bytes 3538948
  58.4 1.3 %copy-start.5 = (bf16[768,768]{1,0:T(8,128)(2,1)S(1)}, bf16[768,768]{1,0:T(8,128)(2,1)}, u32[]{:S(2)}) copy-start(bf16[768,768]{1,0:T(8,128)(2,1)} %constant.39.clone.top_ref) | copy-start | bytes 3538948
  59.7 11.6 %copy-start = (bf16[768,768]{1,0:T(8,128)(2,1)S(1)}, bf16[768,768]{1,0:T(8,128)(2,1)}, u32[]{:S(2)}) copy-start(bf16[768,768]{1,0:T(8,128)(2,1)} %constant.42.clone.low_ref) | copy-start | bytes 3538948
  59.7 11.6 %copy-start.1 = (bf16[768,768]{1,0:T(8,128)(2,1)S(1)}, bf16[768,768]{1,0:T(8,128)(2,1)}, u32[]{:S(2)}) copy-start(bf16[768,768]{1,0:T(8,128)(2,1)} %constant.41.clone.top_ref) | copy-start | bytes 3538948
  60.7 6.5 %collective-permute-start.9 = (f32[30,768]{1,0:T(8,128)S(1)}, f32[30,768]{1,0:T(8,128)S(1)}, u32[]{:S(2)}, u32[]{:S(2)}) collective-permute-start(f32[30,768]{1,0:T(8,128)S(1)} %get-tuple-element.40), channel_id=1, source_target_pairs={{0,64},{64,128},{128,192},{1,65},{65,129},{129,193},{2,66},{66,130... | collective-permute-start | bytes 276488 | tf_op jit(solution)/shard_map/ppermute | solution.py:475
  65.3 5.9 %collective-permute-start.10 = (f32[30,768]{1,0:T(8,128)S(1)}, f32[30,768]{1,0:T(8,128)S(1)}, u32[]{:S(2)}, u32[]{:S(2)}) collective-permute-start(f32[30,768]{1,0:T(8,128)S(1)} %get-tuple-element.41), channel_id=1, source_target_pairs={{64,0},{128,64},{192,128},{65,1},{129,65},{193,129},{66,2},{130,66... | collective-permute-start | bytes 276488 | tf_op jit(solution)/shard_map/ppermute | solution.py:476
  75.4 37.4 %all-to-all-start.1 = ((f32[64,16,128]{2,1,0:T(8,128)}), f32[64,16,128]{2,1,0:T(8,128)S(1)}, u32[]{:S(2)}, u32[]{:S(2)}) async-start(f32[64,16,128]{2,1,0:T(8,128)} %filter.1), calls=%async_computation.1 | async-start | bytes 1048576 | tf_op jit(solution)/shard_map/all_to_all | solution.py:452
  85.5 10.3 %collective-permute-start.12 = (f32[20,320]{1,0:T(8,128)S(1)}, f32[20,320]{1,0:T(8,128)S(1)}, u32[]{:S(2)}, u32[]{:S(2)}) collective-permute-start(f32[20,320]{1,0:T(8,128)S(1)} %get-tuple-element.42), channel_id=1, source_target_pairs={{0,64},{1,65},{2,66},{3,67},{4,68},{5,69},{6,70},{7,71},{8,0},{9,1... | collective-permute-start | bytes 76808 | tf_op jit(solution)/shard_map/ppermute | solution.py:281
  90.5 8.0 %collective-permute-start.13 = (f32[20,320]{1,0:T(8,128)S(1)}, f32[20,320]{1,0:T(8,128)S(1)}, u32[]{:S(2)}, u32[]{:S(2)}) collective-permute-start(f32[20,320]{1,0:T(8,128)S(1)} %get-tuple-element.43), channel_id=1, source_target_pairs={{0,2},{1,3},{2,4},{3,5},{4,6},{5,7},{6,0},{7,1},{8,66},{9,67},{10,... | collective-permute-start | bytes 76808 | tf_op jit(solution)/shard_map/ppermute | solution.py:281
  90.5 12.5 %collective-permute-start.14 = (f32[20,320]{1,0:T(8,128)S(1)}, f32[20,320]{1,0:T(8,128)S(1)}, u32[]{:S(2)}, u32[]{:S(2)}) collective-permute-start(f32[20,320]{1,0:T(8,128)S(1)} %get-tuple-element.44), channel_id=1, source_target_pairs={{0,66},{1,67},{2,68},{3,69},{4,70},{5,71},{6,64},{7,65},{8,2},{9,3... | collective-permute-start | bytes 76808 | tf_op jit(solution)/shard_map/ppermute | solution.py:281
  90.5 16.5 %collective-permute-start.15 = (f32[20,320]{1,0:T(8,128)S(1)}, f32[20,320]{1,0:T(8,128)S(1)}, u32[]{:S(2)}, u32[]{:S(2)}) collective-permute-start(f32[20,320]{1,0:T(8,128)S(1)} %get-tuple-element.45), channel_id=1, source_target_pairs={{0,4},{1,5},{2,6},{3,7},{4,0},{5,1},{6,2},{7,3},{8,68},{9,69},{10,... | collective-permute-start | bytes 76808 | tf_op jit(solution)/shard_map/ppermute | solution.py:281
  93.5 13.6 %collective-permute-start.16 = (f32[20,320]{1,0:T(8,128)S(1)}, f32[20,320]{1,0:T(8,128)S(1)}, u32[]{:S(2)}, u32[]{:S(2)}) collective-permute-start(f32[20,320]{1,0:T(8,128)S(1)} %get-tuple-element.46), channel_id=1, source_target_pairs={{0,68},{1,69},{2,70},{3,71},{4,64},{5,65},{6,66},{7,67},{8,4},{9,5... | collective-permute-start | bytes 76808 | tf_op jit(solution)/shard_map/ppermute | solution.py:281
  95.8 11.2 %collective-permute-start.17 = (f32[20,320]{1,0:T(8,128)S(1)}, f32[20,320]{1,0:T(8,128)S(1)}, u32[]{:S(2)}, u32[]{:S(2)}) collective-permute-start(f32[20,320]{1,0:T(8,128)S(1)} %get-tuple-element.47), channel_id=1, source_target_pairs={{0,6},{1,7},{2,0},{3,1},{4,2},{5,3},{6,4},{7,5},{8,70},{9,71},{10,... | collective-permute-start | bytes 76808 | tf_op jit(solution)/shard_map/ppermute | solution.py:281
  98.5 8.6 %collective-permute-start.18 = (f32[20,320]{1,0:T(8,128)S(1)}, f32[20,320]{1,0:T(8,128)S(1)}, u32[]{:S(2)}, u32[]{:S(2)}) collective-permute-start(f32[20,320]{1,0:T(8,128)S(1)} %get-tuple-element.48), channel_id=1, source_target_pairs={{0,70},{1,71},{2,64},{3,65},{4,66},{5,67},{6,68},{7,69},{8,6},{9,7... | collective-permute-start | bytes 76808 | tf_op jit(solution)/shard_map/ppermute | solution.py:281
  103.0 9.2 %collective-permute-start.11 = (f32[20,320]{1,0:T(8,128)S(1)}, f32[20,320]{1,0:T(8,128)S(1)}, u32[]{:S(2)}, u32[]{:S(2)}) collective-permute-start(f32[20,320]{1,0:T(8,128)S(1)} %get-tuple-element.37._), channel_id=1, source_target_pairs={{0,0},{1,1},{2,2},{3,3},{4,4},{5,5},{6,6},{7,7},{8,64},{9,65},{10,... | collective-permute-start | bytes 76808 | tf_op jit(solution)/shard_map/ppermute | solution.py:281
  112.8 0.8 copy-start.11

commit v8 on v7

--- a/solution.py
+++ b/solution.py
@@ -198,7 +198,7 @@
         ),
         out_shape=[jax.ShapeDtypeStruct((points, width), F32)] * 2
         + [jax.ShapeDtypeStruct((160, 1280), F32)] * 4,
-        compiler_params=params(60),
+        compiler_params=params(57),
         cost_estimate=cost(30 * points * width * units, 12_000_000),
         name="mlp",
     )(
@@ -236,25 +236,38 @@
         outs[m][...] = kept_ref[index]
 
 
-def stack_kernel(place_ref, _, *refs):
-    ins, outs, kept_ref = refs[:4], refs[4:12], refs[12]
+def pair_kernel(place_ref, _, *refs):
+    ins, (mine_ref, send_ref) = refs[:4], refs[4:]
     total = (ins[0][...] + ins[1][...]) + (ins[2][...] + ins[3][...])
-    for core in range(2):
-        at = 160 * core
-        part = jnp.concatenate([total[:, at : at + 160], total[:, 320 + at : 480 + at]], axis=1)
-        for z in range(4):
-            kept_ref[2 * z + core, 0:20, :] = part[20 * z : 20 * z + 20]
-    high, low = lax.div(place_ref[5], 4), lax.rem(place_ref[5], 4)
-    for a in range(4):
-        for b in range(2):
-            index = 2 * lax.rem(low + a, 4) + (1 - high if b else high)
-            outs[2 * a + b][...] = kept_ref[index, 0:20, :]
-
-
-def last_kernel(*refs):
-    first_ref, second_ref = refs[8:]
-    a, b, c, d = (refs[m][...] + refs[m + 4][...] for m in range(4))
-    total = (a + b) + (c + d)
+    even = jnp.concatenate([total[:, 0:160], total[:, 320:480]], axis=1)
+    odd = jnp.concatenate([total[:, 160:320], total[:, 480:640]], axis=1)
+    first = place_ref[1] == 0
+    mine_ref[...] = jnp.where(first, even, odd)
+    send_ref[...] = jnp.where(first, odd, even)
+
+
+def stack_kernel(place_ref, _, mine_ref, arrived_ref, *refs):
+    outs, kept_ref = refs[:4], refs[4]
+    first = place_ref[1] == 0
+    mine, arrived = mine_ref[...], arrived_ref[...]
+    below, above = jnp.where(first, mine, arrived), jnp.where(first, arrived, mine)
+    for r in range(4):
+        rows = slice(20 * r, 20 * r + 20)
+        kept_ref[r] = jnp.concatenate([below[rows], above[rows]], axis=0)
+    for m in range(4):
+        outs[m][...] = kept_ref[lax.rem(place_ref[5] + m, 4)]
+
+
+def half_kernel(place_ref, *refs):
+    ins, (mine_ref, send_ref) = refs[:4], refs[4:]
+    total = (ins[0][...] + ins[1][...]) + (ins[2][...] + ins[3][...])
+    below = place_ref[5] < 4
+    mine_ref[...] = jnp.where(below, total[0:20], total[20:40])
+    send_ref[...] = jnp.where(below, total[20:40], total[0:20])
+
+
+def last_kernel(mine_ref, arrived_ref, first_ref, second_ref):
+    total = mine_ref[...] + arrived_ref[...]
     first_ref[...] = total[:, 0:160]
     second_ref[...] = total[:, 160:320]
 
@@ -293,10 +306,10 @@
 
 
 def exchange_z(pieces):
-    def target(m, yl, co, x, z, yh):
-        return yl, (z // 4) ^ (m & 1), x, 4 * co + (z + (m >> 1)) % 4, yh
-
-    return [permute(pieces[m], functools.partial(target, m)) for m in range(8)]
+    def pairs(m):
+        return [(z, 4 * (z // 4) + (z + m) % 4) for z in range(8)]
+
+    return [pieces[0]] + [lax.ppermute(pieces[m], "z", pairs(m)) for m in (1, 2, 3)]
 
 
 def to_core(value):
@@ -444,6 +457,7 @@
         in_specs=whole(1),
         out_specs=whole(1)[0],
         out_shape=jax.ShapeDtypeStruct((ROWS * COLS, SHARDS * OWN), F32),
+        compiler_params=params(16),
         name="unpack",
     )(block)
 
@@ -467,16 +481,24 @@
     swapped = small(swap_kernel, (place, *moved), [(80, 640)] * 4, 1, kept, (), "swap", 10**10)
     kernel = kernel_spectrum(kernels, swapped[0])
     moved = exchange(swapped, "yx")
-    kept = (pltpu.VMEM((8, 24, 320), F32),)
-    stacked = small(stack_kernel, (place, *moved), [(20, 320)] * 8, 1, kept, (kernel,), "stack")
-    data, first, final, own_mixing = spectrum(spread, stacked[0])
+    mine, send = small(
+        pair_kernel, (place, *moved), [(80, 320)] * 2, 1, (), (kernel,), "pair"
+    )
+    data, first, final, own_mixing = spectrum(spread, mine)
     forward = [(i, i + 1) for i in range(3)]
     backward = [(target, source) for source, target in forward]
     before = lax.ppermute(final, LAT, forward)
     beyond = lax.ppermute(first, LAT, backward)
-    sent = filtered(own_mixing, data, before, beyond, kernel, ())
+    paired = to_core(send)
+    sent = filtered(own_mixing, data, before, beyond, kernel, (paired,))
     result = across(sent)
-    grad_in, grad_out = small(last_kernel, exchange_z(stacked), [(20, 160)] * 2, name="last")
+    kept = (pltpu.VMEM((4, 40, 320), F32),)
+    operands = (place, mine, paired)
+    stacked = small(stack_kernel, operands, [(40, 320)] * 4, 1, kept, (sent,), "stack")
+    moved = exchange_z(stacked)
+    mine, send = small(half_kernel, (place, *moved), [(20, 320)] * 2, 1, name="half")
+    arrived = lax.ppermute(send, "z", [(z, z ^ 4) for z in range(8)])
+    grad_in, grad_out = small(last_kernel, (mine, arrived), [(20, 160)] * 2, name="last")
     field = unpack(result).reshape(COLS, ROWS, width).transpose(1, 0, 2)
     return (field, grad_in, grad_out)
 

time: 117 us -> 112 us (0.957)
  starting transfers between devices: 61.7 us -> 48.7 us
  waiting for transfers between devices: 21.3 us -> 30.4 us
    ppermute x14 -> x6, starting transfers between devices: 28.5 us -> 7.03 us  [permute(): return lax.ppermute(value, AXES, pairs)]
    ppermute x0 -> x4, waiting for transfers between devices: none -> 14.8 us  [the longest x3 11.4 us: exchange_z(): lax.ppermute(pieces[m], 'z', pairs(m))]
    ppermute x0 -> x4, starting transfers between devices: none -> 7.82 us  [the longest x3 4.35 us: exchange_z(): lax.ppermute(pieces[m], 'z', pairs(m))]
    ppermute x14 -> x6, waiting for transfers between devices: 13.4 us -> 8.27 us  [permute(): return lax.ppermute(value, AXES, pairs)]
    ppermute x3 -> x4, starting transfers between devices: 4.06 us -> 6.03 us  [to_core(): return lax.ppermute(value, 'co', [(0, 1), (1, 0)])]
    ppermute x1, starting transfers between devices: 4.59 us -> 3.3 us  [per_device(): before = lax.ppermute(final, LAT, forward)]
    pallas_call x4 -> x6, Pallas kernels: 5.07 us -> 6.16 us  [small(): pl.pallas_call(kernel, in_specs=[pl.BlockSpec(memory_space=pltpu.SMEM)] *...]
    unnamed x28 -> x26, local copies, waits for them, and re-layouts: 5.05 us -> 4.26 us
  transfers between devices with their start and end apart: 21 -> 18, of which waited for: 9 -> 10; matrix products, arithmetic and copies ran while one was open for 1% -> 1% of each run, Pallas kernels for 6% -> 8%
where the time goes in v8:
time: 112 us; the launch traced here: 111 us
  starting transfers between devices  48.7 us (43%)
  waiting for transfers between devices  30.4 us (27%)
  Pallas kernels  26.5 us (24%)
  local copies, waits for them, and re-layouts  4.86 us (4%)
    all_to_all x2, starting transfers between devices, across(): return lax.all_to_all(block, LON, split_axis=0, concat_axis=0, tiled=True)  22.6 us
    pallas_call x1, Pallas kernels, mlp(): pl.pallas_call(mlp_kernel, grid_spec=pltpu.PrefetchScalarGridSpec(num_sca...  12.5 us
    ppermute x3, waiting for transfers between devices, exchange_z(): lax.ppermute(pieces[m], 'z', pairs(m))  11.4 us
    ppermute x6, waiting for transfers between devices, permute(): return lax.ppermute(value, AXES, pairs)  8.27 us
    ppermute x6, starting transfers between devices, permute(): return lax.ppermute(value, AXES, pairs)  7.03 us
    pallas_call x6, Pallas kernels, small(): pl.pallas_call(kernel, in_specs=[pl.BlockSpec(memory_space=pltpu.SMEM)] *...  6.16 us
    ppermute x4, starting transfers between devices, to_core(): return lax.ppermute(value, 'co', [(0, 1), (1, 0)])  6.03 us
    ppermute x3, starting transfers between devices, exchange_z(): lax.ppermute(pieces[m], 'z', pairs(m))  4.35 us
  transfers between devices with their start and end apart: 18, of which 10 were waited for; matrix products, arithmetic and copies ran while one was open for 1% of the time, Pallas kernels for 8%

profile of v8, /device:TPU:1, one launch (start us, length us, event | category | flops | bytes accessed | tf_op | source)
XLA Modules:
  0.0 111.3 jit_solution(16030810389974973377)
XLA Ops:
  0.6 3.3 %collective-permute-start = (f32[192,640]{1,0:T(8,128)}, f32[192,640]{1,0:T(8,128)S(1)}, u32[]{:S(2)}, u32[]{:S(2)}) collective-permute-start(f32[192,640]{1,0:T(8,128)} %bitcast.26), channel_id=1, source_target_pairs={{0,64},{64,0},{1,65},{65,1},{2,66},{66,2},{3,67},{67,3},{4,68},{68... | collective-permute-start | bytes 1474568 | tf_op jit(solution)/shard_map/ppermute | solution.py:316
  4.0 0.1 collective-permute-start.1
  4.1 0.6 stack.28.place_ref
  4.7 1.0 collective-permute-done.act_other_ref
  5.7 0.0 copy-start.11
  5.7 0.7 collective-permute-done.1.cot_other_ref
  6.4 0.0 copy-start.12
  6.4 0.1 copy-done.11
  6.4 0.7 copy-done.12
  7.1 12.5 %mlp.1 = (f32[192,640]{1,0:T(8,128)}, f32[192,640]{1,0:T(8,128)}, f32[160,1280]{1,0:T(8,128)}, f32[160,1280]{1,0:T(8,128)}, f32[160,1280]{1,0:T(8,128)}, /*index=5*/f32[160,1280]{1,0:T(8,128)}) custom-call(s32[6]{0:T(128)} %stack.28.place_ref, f32[192,640]{1,0:T(8,128)} %bitcast.27, f32[192,640]{1,0:T(8,128)} %copy-done.11, f32[192,640]{1,0:T(8,128)} %bitcast.29, ...), custom_call_target="tpu_custom_call" | custom-call | flops 4718592000 | bytes 12000000 | tf_op jit(solution)/shard_map/mlp/pallas_call | solution.py:190
  19.6 1.2 %collective-permute-start.3 = (f32[160,1280]{1,0:T(8,128)}, f32[160,1280]{1,0:T(8,128)S(1)}, u32[]{:S(2)}, u32[]{:S(2)}) collective-permute-start(f32[160,1280]{1,0:T(8,128)} %get-tuple-element.30), channel_id=1, source_target_pairs={{0,16},{1,17},{2,18},{3,19},{4,20},{5,21},{6,22},{7,23},{8,24},{9,... | collective-permute-start | bytes 2457608 | tf_op jit(solution)/shard_map/ppermute | solution.py:294
  20.8 0.4 collective-permute-start.4
  21.2 1.7 %collective-permute-start.5 = (f32[160,1280]{1,0:T(8,128)}, f32[160,1280]{1,0:T(8,128)}, u32[]{:S(2)}, u32[]{:S(2)}) collective-permute-start(f32[160,1280]{1,0:T(8,128)} %get-tuple-element.32), channel_id=1, source_target_pairs={{0,48},{1,49},{2,50},{3,51},{4,52},{5,53},{6,54},{7,55},{8,56},{9,... | collective-permute-start | bytes 2457608 | tf_op jit(solution)/shard_map/ppermute | solution.py:294
  22.9 0.6 collective-permute-start.2
  23.5 1.7 %collective-permute-done.2.arrived_ref = f32[192,640]{1,0:T(8,128)S(1)} collective-permute-done((f32[192,640]{1,0:T(8,128)}, f32[192,640]{1,0:T(8,128)S(1)}, u32[]{:S(2)}, u32[]{:S(2)}) %collective-permute-start.2) | collective-permute-done | bytes 491552 | tf_op jit(solution)/shard_map/ppermute | solution.py:316
  25.2 0.0 copy-done.8
  25.2 0.0 copy-done.9
  25.2 1.0 copy-done.7
  26.3 2.0 %pack.1 = f32[64,16,128]{2,1,0:T(8,128)} custom-call(s32[6]{0:T(128)S(1)} %copy-done.8, f32[3,10]{1,0:T(4,128)S(1)} %bitcast.22, f32[192,640]{1,0:T(8,128)S(1)} %copy-done.7, f32[192,640]{1,0:T(8,128)S(1)} %collective-permute-done.2.arrived_ref), custom_call_target="tpu_custom_call" | custom-call | tf_op jit(solution)/shard_map/pack/pallas_call | solution.py:276
  28.3 12.5 %all-to-all-start = ((f32[64,16,128]{2,1,0:T(8,128)}), f32[64,16,128]{2,1,0:T(8,128)S(1)}, u32[]{:S(2)}, u32[]{:S(2)}) async-start(f32[64,16,128]{2,1,0:T(8,128)} %pack.1), calls=%async_computation | async-start | bytes 1048576 | tf_op jit(solution)/shard_map/all_to_all | solution.py:466
  40.8 0.0 collective-permute-done.3.refs_1_
  40.8 0.0 collective-permute-done.4.refs_2_
  40.8 0.8 collective-permute-done.5.refs_3_
  41.6 1.1 %copy-done.10 = f32[160,1280]{1,0:T(8,128)S(1)} copy-done((f32[160,1280]{1,0:T(8,128)S(1)}, f32[160,1280]{1,0:T(8,128)}, u32[]{:S(2)}) %copy-start.10) | copy-done | bytes 819224
  42.8 1.6 %swap.1 = (f32[80,640]{1,0:T(8,128)S(1)}, f32[80,640]{1,0:T(8,128)S(1)}, f32[80,640]{1,0:T(8,128)S(1)}, f32[80,640]{1,0:T(8,128)S(1)}) custom-call(s32[6]{0:T(128)S(1)} %copy-done.8, f32[160,1280]{1,0:T(8,128)S(1)} %copy-done.10, f32[160,1280]{1,0:T(8,128)S(1)} %collective-permute-done.3.refs_1_, f32[160,1280]{1,0:T(8,128)S(1)} %collective-permute-done.4.refs_2_, ...), custom_call_target="tpu_custom_call" | custom-call | flops 10000000000 | bytes 4000000 | tf_op jit(solution)/shard_map/swap/pallas_call | solution.py:276
  44.4 0.1 collective-permute-start.6
  44.5 2.6 %collective-permute-start.7 = (f32[80,640]{1,0:T(8,128)S(1)}, f32[80,640]{1,0:T(8,128)S(1)}, u32[]{:S(2)}, u32[]{:S(2)}) collective-permute-start(f32[80,640]{1,0:T(8,128)S(1)} %get-tuple-element.35), channel_id=1, source_target_pairs={{0,128},{1,129},{2,130},{3,131},{4,132},{5,133},{6,134},{7,135},{8... | collective-permute-start | bytes 614408 | tf_op jit(solution)/shard_map/ppermute | solution.py:294
  47.1 1.1 collective-permute-start.8
  48.2 0.0 copy-done.2
  48.2 0.0 copy-done.3
  48.2 0.0 copy-done.6
  48.2 1.4 %kernel_spectrum.1._.kernel_ref = f32[336,768]{1,0:T(8,128)S(1)} custom-call(f32[336,768]{1,0:T(8,128)S(1)} %bitcast.21, bf16[768,768]{1,0:T(8,128)(2,1)S(1)} %copy-done.3, bf16[768,768]{1,0:T(8,128)(2,1)S(1)} %copy-done.2, f32[80,640]{1,0:T(8,128)S(1)} %get-tuple-element.33._.refs_0_), custom_call_target="tpu_custom_call" | custom-call | flops 1189085184 | bytes 5000000 | tf_op jit(solution)/shard_map/kernel_spectrum/pallas_call | solution.py:364
  49.6 0.0 copy-start.4
  49.6 3.1 %collective-permute-done.6.refs_1_ = f32[80,640]{1,0:T(8,128)S(1)} collective-permute-done((f32[80,640]{1,0:T(8,128)S(1)}, f32[80,640]{1,0:T(8,128)S(1)}, u32[]{:S(2)}, u32[]{:S(2)}) %collective-permute-start.6) | collective-permute-done | bytes 204832 | tf_op jit(solution)/shard_map/ppermute | solution.py:294
  52.7 4.3 %collective-permute-done.7.refs_2_ = f32[80,640]{1,0:T(8,128)S(1)} collective-permute-done((f32[80,640]{1,0:T(8,128)S(1)}, f32[80,640]{1,0:T(8,128)S(1)}, u32[]{:S(2)}, u32[]{:S(2)}) %collective-permute-start.7) | collective-permute-done | bytes 204832 | tf_op jit(solution)/shard_map/ppermute | solution.py:294
  57.0 0.0 collective-permute-done.8.refs_3_
  57.0 0.7 pair.1
  57.7 2.0 %collective-permute-start.11 = (f32[80,320]{1,0:T(8,128)S(1)}, f32[80,320]{1,0:T(8,128)S(1)}, u32[]{:S(2)}, u32[]{:S(2)}) collective-permute-start(f32[80,320]{1,0:T(8,128)S(1)} %get-tuple-element.42), channel_id=1, source_target_pairs={{0,64},{64,0},{1,65},{65,1},{2,66},{66,2},{3,67},{67,3},{4,68},{68... | collective-permute-start | bytes 307208 | tf_op jit(solution)/shard_map/ppermute | solution.py:316
  59.7 0.0 all-to-all-done.block_ref
  59.7 0.0 copy-done.4
  59.7 1.3 %copy-done.5 = bf16[768,768]{1,0:T(8,128)(2,1)S(1)} copy-done((bf16[768,768]{1,0:T(8,128)(2,1)S(1)}, bf16[768,768]{1,0:T(8,128)(2,1)}, u32[]{:S(2)}) %copy-start.5) | copy-done | bytes 1179672
  61.0 1.0 spectrum.1
  62.0 3.3 %collective-permute-start.9 = (f32[30,768]{1,0:T(8,128)S(1)}, f32[30,768]{1,0:T(8,128)S(1)}, u32[]{:S(2)}, u32[]{:S(2)}) collective-permute-start(f32[30,768]{1,0:T(8,128)S(1)} %get-tuple-element.40), channel_id=1, source_target_pairs={{0,64},{64,128},{128,192},{1,65},{65,129},{129,193},{2,66},{66,130... | collective-permute-start | bytes 276488 | tf_op jit(solution)/shard_map/ppermute | solution.py:490
  65.3 1.9 %collective-permute-start.10 = (f32[30,768]{1,0:T(8,128)S(1)}, f32[30,768]{1,0:T(8,128)S(1)}, u32[]{:S(2)}, u32[]{:S(2)}) collective-permute-start(f32[30,768]{1,0:T(8,128)S(1)} %get-tuple-element.41), channel_id=1, source_target_pairs={{64,0},{128,64},{192,128},{65,1},{129,65},{193,129},{66,2},{130,66... | collective-permute-start | bytes 276488 | tf_op jit(solution)/shard_map/ppermute | solution.py:491
  67.2 0.0 collective-permute-done.11.refs_0_.arrived_ref
  67.3 0.0 collective-permute-done.9.before_ref
  67.3 4.0 %collective-permute-done.10.after_ref = f32[30,768]{1,0:T(8,128)S(1)} collective-permute-done((f32[30,768]{1,0:T(8,128)S(1)}, f32[30,768]{1,0:T(8,128)S(1)}, u32[]{:S(2)}, u32[]{:S(2)}) %collective-permute-start.10) | collective-permute-done | bytes 92192 | tf_op jit(solution)/shard_map/ppermute | solution.py:491
  71.3 0.0 copy-done
  71.3 0.0 copy-done.1
  71.3 4.2 %filter.1._ = f32[64,16,128]{2,1,0:T(8,128)} custom-call(f32[1,128]{1,0:T(1,128)S(1)} %get-tuple-element.38.mixing_ref, f32[160,768]{1,0:T(8,128)S(1)} %get-tuple-element.39.data_ref, f32[30,768]{1,0:T(8,128)S(1)} %collective-permute-done.9.before_ref, f32[30,768]{1,0:T(8,128)S(1)} %collective-permute-done.10.after_ref, ...), custom_call_target="tpu_custom_call" | custom-call | flops 566231040 | bytes 5000000 | tf_op jit(solution)/shard_map/filter/pallas_call | solution.py:422
  75.4 10.1 %all-to-all-start.1 = ((f32[64,16,128]{2,1,0:T(8,128)}), f32[64,16,128]{2,1,0:T(8,128)S(1)}, u32[]{:S(2)}, u32[]{:S(2)}) async-start(f32[64,16,128]{2,1,0:T(8,128)} %filter.1._), calls=%async_computation.1 | async-start | bytes 1048576 | tf_op jit(solution)/shard_map/all_to_all | solution.py:466
  85.6 0.6 stack.29
  86.2 1.1 collective-permute-start.12
  87.2 2.1 %collective-permute-start.13 = (f32[40,320]{1,0:T(8,128)S(1)}, f32[40,320]{1,0:T(8,128)S(1)}, u32[]{:S(2)}, u32[]{:S(2)}) collective-permute-start(f32[40,320]{1,0:T(8,128)S(1)} %get-tuple-element.45), channel_id=1, source_target_pairs={{0,4},{2,6},{4,0},{6,2},{8,12},{10,14},{12,8},{14,10},{1,5},{3,7},... | collective-permute-start | bytes 153608 | tf_op jit(solution)/shard_map/ppermute | solution.py:312
  89.3 1.2 %collective-permute-start.14 = (f32[40,320]{1,0:T(8,128)S(1)}, f32[40,320]{1,0:T(8,128)S(1)}, u32[]{:S(2)}, u32[]{:S(2)}) collective-permute-start(f32[40,320]{1,0:T(8,128)S(1)} %get-tuple-element.46), channel_id=1, source_target_pairs={{0,6},{2,0},{4,2},{6,4},{8,14},{10,8},{12,10},{14,12},{1,7},{3,1},... | collective-permute-start | bytes 153608 | tf_op jit(solution)/shard_map/ppermute | solution.py:312
  90.5 10.1 %collective-permute-done.12.refs_1_ = f32[40,320]{1,0:T(8,128)S(1)} collective-permute-done((f32[40,320]{1,0:T(8,128)S(1)}, f32[40,320]{1,0:T(8,128)S(1)}, u32[]{:S(2)}, u32[]{:S(2)}) %collective-permute-start.12) | collective-permute-done | bytes 51232 | tf_op jit(solution)/shard_map/ppermute | solution.py:312
  100.6 1.3 %collective-permute-done.13.refs_2_ = f32[40,320]{1,0:T(8,128)S(1)} collective-permute-done((f32[40,320]{1,0:T(8,128)S(1)}, f32[40,320]{1,0:T(8,128)S(1)}, u32[]{:S(2)}, u32[]{:S(2)}) %collective-permute-start.13) | collective-permute-done | bytes 51232 | tf_op jit(solution)/shard_map/ppermute | solution.py:312
  101.9 0.0 collective-permute-done.14.refs_3_
  101.9 0.6 half.1
  102.5 3.5 %collective-permute-start.15 = (f32[20,320]{1,0:T(8,128)S(1)}, f32[20,320]{1,0:T(8,128)S(1)}, u32[]{:S(2)}, u32[]{:S(2)}) collective-permute-start(f32[20,320]{1,0:T(8,128)S(1)} %get-tuple-element.48), channel_id=1, source_target_pairs={{0,8},{2,10},{4,12},{6,14},{8,0},{10,2},{12,4},{14,6},{1,9},{3,11}... | collective-permute-start | bytes 76808 | tf_op jit(solution)/shard_map/ppermute | solution.py:500
  106.0 3.3 %collective-permute-done.15.arrived_ref = f32[20,320]{1,0:T(8,128)S(1)} collective-permute-done((f32[20,320]{1,0:T(8,128)S(1)}, f32[20,320]{1,0:T(8,128)S(1)}, u32[]{:S(2)}, u32[]{:S(2)}) %collective-permute-start.15) | collective-permute-done | bytes 25632 | tf_op jit(solution)/shard_map/ppermute | solution.py:500
  109.3 0.7 last.1
  110.0 0.0 all-to-all-done.1.block_ref
  110.0 1.3 %unpack.1 = f32[192,640]{1,0:T(8,128)} custom-call(f32[64,16,128]{2,1,0:T(8,128)S(1)} %all-to-all-done.1.block_ref), custom_call_target="tpu_custom_call" | custom-call | tf_op jit(solution)/shard_map/unpack/pallas_call | solution.py:455
  (10 shorter events, 0.0 us)
Async XLA Ops:
  0.6 5.0 %collective-permute-start = (f32[192,640]{1,0:T(8,128)}, f32[192,640]{1,0:T(8,128)S(1)}, u32[]{:S(2)}, u32[]{:S(2)}) collective-permute-start(f32[192,640]{1,0:T(8,128)} %bitcast.26), channel_id=1, source_target_pairs={{0,64},{64,0},{1,65},{65,1},{2,66},{66,2},{3,67},{67,3},{4,68},{68... | collective-permute-start | bytes 1474568 | tf_op jit(solution)/shard_map/ppermute | solution.py:316
  4.0 2.4 %collective-permute-start.1 = (f32[192,640]{1,0:T(8,128)}, f32[192,640]{1,0:T(8,128)S(1)}, u32[]{:S(2)}, u32[]{:S(2)}) collective-permute-start(f32[192,640]{1,0:T(8,128)} %bitcast.28), channel_id=1, source_target_pairs={{0,64},{64,0},{1,65},{65,1},{2,66},{66,2},{3,67},{67,3},{4,68},{68... | collective-permute-start | bytes 1474568 | tf_op jit(solution)/shard_map/ppermute | solution.py:316
  5.7 0.8 copy-start.11
  6.4 0.8 copy-start.12
  7.1 18.1 %copy-start.8 = (s32[6]{0:T(128)S(1)}, s32[6]{0:T(128)}, u32[]{:S(2)}) copy-start(s32[6]{0:T(128)} %stack.28.place_ref) | copy-start | bytes 76
  7.1 18.1 %copy-start.9 = (f32[10,3]{0,1:T(4,128)S(1)}, f32[10,3]{0,1:T(4,128)}, u32[]{:S(2)}) copy-start(f32[10,3]{0,1:T(4,128)} %param.17) | copy-start | bytes 364
  19.6 21.1 %collective-permute-start.3 = (f32[160,1280]{1,0:T(8,128)}, f32[160,1280]{1,0:T(8,128)S(1)}, u32[]{:S(2)}, u32[]{:S(2)}) collective-permute-start(f32[160,1280]{1,0:T(8,128)} %get-tuple-element.30), channel_id=1, source_target_pairs={{0,16},{1,17},{2,18},{3,19},{4,20},{5,21},{6,22},{7,23},{8,24},{9,... | collective-permute-start | bytes 2457608 | tf_op jit(solution)/shard_map/ppermute | solution.py:294
  20.8 20.0 %collective-permute-start.4 = (f32[160,1280]{1,0:T(8,128)}, f32[160,1280]{1,0:T(8,128)S(1)}, u32[]{:S(2)}, u32[]{:S(2)}) collective-permute-start(f32[160,1280]{1,0:T(8,128)} %get-tuple-element.31), channel_id=1, source_target_pairs={{0,32},{1,33},{2,34},{3,35},{4,36},{5,37},{6,38},{7,39},{8,40},{9,... | collective-permute-start | bytes 2457608 | tf_op jit(solution)/shard_map/ppermute | solution.py:294
  21.2 20.4 %collective-permute-start.5 = (f32[160,1280]{1,0:T(8,128)}, f32[160,1280]{1,0:T(8,128)}, u32[]{:S(2)}, u32[]{:S(2)}) collective-permute-start(f32[160,1280]{1,0:T(8,128)} %get-tuple-element.32), channel_id=1, source_target_pairs={{0,48},{1,49},{2,50},{3,51},{4,52},{5,53},{6,54},{7,55},{8,56},{9,... | collective-permute-start | bytes 2457608 | tf_op jit(solution)/shard_map/ppermute | solution.py:294
  22.9 2.3 %collective-permute-start.2 = (f32[192,640]{1,0:T(8,128)}, f32[192,640]{1,0:T(8,128)S(1)}, u32[]{:S(2)}, u32[]{:S(2)}) collective-permute-start(f32[192,640]{1,0:T(8,128)} %get-tuple-element.28), channel_id=1, source_target_pairs={{0,64},{64,0},{1,65},{65,1},{2,66},{66,2},{3,67},{67,3},{4,68},{68... | collective-permute-start | bytes 1474568 | tf_op jit(solution)/shard_map/ppermute | solution.py:316
  25.2 1.0 copy-start.7
  28.3 31.4 %all-to-all-start = ((f32[64,16,128]{2,1,0:T(8,128)}), f32[64,16,128]{2,1,0:T(8,128)S(1)}, u32[]{:S(2)}, u32[]{:S(2)}) async-start(f32[64,16,128]{2,1,0:T(8,128)} %pack.1), calls=%async_computation | async-start | bytes 1048576 | tf_op jit(solution)/shard_map/all_to_all | solution.py:466
  41.6 1.1 %copy-start.10 = (f32[160,1280]{1,0:T(8,128)S(1)}, f32[160,1280]{1,0:T(8,128)}, u32[]{:S(2)}) copy-start(f32[160,1280]{1,0:T(8,128)} %get-tuple-element.29.refs_0_) | copy-start | bytes 2457604
  42.8 5.4 %copy-start.2 = (bf16[768,768]{1,0:T(8,128)(2,1)S(1)}, bf16[768,768]{1,0:T(8,128)(2,1)}, u32[]{:S(2)}) copy-start(bf16[768,768]{1,0:T(8,128)(2,1)} %constant.38.clone.low_ref) | copy-start | bytes 3538948
  42.8 5.4 %copy-start.3 = (bf16[768,768]{1,0:T(8,128)(2,1)S(1)}, bf16[768,768]{1,0:T(8,128)(2,1)}, u32[]{:S(2)}) copy-start(bf16[768,768]{1,0:T(8,128)(2,1)} %constant.37.clone.top_ref) | copy-start | bytes 3538948
  42.8 5.4 %copy-start.6 = (f32[3,16,7,768]{3,1,2,0:T(8,128)S(1)}, f32[3,16,7,768]{3,1,2,0:T(8,128)}, u32[]{:S(2)}) copy-start(f32[3,16,7,768]{3,1,2,0:T(8,128)} %param.16) | copy-start | bytes 3096580
  44.4 8.3 %collective-permute-start.6 = (f32[80,640]{1,0:T(8,128)S(1)}, f32[80,640]{1,0:T(8,128)S(1)}, u32[]{:S(2)}, u32[]{:S(2)}) collective-permute-start(f32[80,640]{1,0:T(8,128)S(1)} %get-tuple-element.34), channel_id=1, source_target_pairs={{0,1},{1,0},{2,3},{3,2},{4,5},{5,4},{6,7},{7,6},{8,9},{9,8},{10,11... | collective-permute-start | bytes 614408 | tf_op jit(solution)/shard_map/ppermute | solution.py:294
  44.5 12.5 %collective-permute-start.7 = (f32[80,640]{1,0:T(8,128)S(1)}, f32[80,640]{1,0:T(8,128)S(1)}, u32[]{:S(2)}, u32[]{:S(2)}) collective-permute-start(f32[80,640]{1,0:T(8,128)S(1)} %get-tuple-element.35), channel_id=1, source_target_pairs={{0,128},{1,129},{2,130},{3,131},{4,132},{5,133},{6,134},{7,135},{8... | collective-permute-start | bytes 614408 | tf_op jit(solution)/shard_map/ppermute | solution.py:294
  47.1 9.9 %collective-permute-start.8 = (f32[80,640]{1,0:T(8,128)S(1)}, f32[80,640]{1,0:T(8,128)S(1)}, u32[]{:S(2)}, u32[]{:S(2)}) collective-permute-start(f32[80,640]{1,0:T(8,128)S(1)} %get-tuple-element.36), channel_id=1, source_target_pairs={{0,129},{1,128},{2,131},{3,130},{4,133},{5,132},{6,135},{7,134},{8... | collective-permute-start | bytes 614408 | tf_op jit(solution)/shard_map/ppermute | solution.py:294
  49.6 10.1 %copy-start.4 = (bf16[768,768]{1,0:T(8,128)(2,1)S(1)}, bf16[768,768]{1,0:T(8,128)(2,1)}, u32[]{:S(2)}) copy-start(bf16[768,768]{1,0:T(8,128)(2,1)} %constant.40.clone.low_ref) | copy-start | bytes 3538948
  57.7 9.5 %collective-permute-start.11 = (f32[80,320]{1,0:T(8,128)S(1)}, f32[80,320]{1,0:T(8,128)S(1)}, u32[]{:S(2)}, u32[]{:S(2)}) collective-permute-start(f32[80,320]{1,0:T(8,128)S(1)} %get-tuple-element.42), channel_id=1, source_target_pairs={{0,64},{64,0},{1,65},{65,1},{2,66},{66,2},{3,67},{67,3},{4,68},{68... | collective-permute-start | bytes 307208 | tf_op jit(solution)/shard_map/ppermute | solution.py:316
  59.7 1.3 %copy-start.5 = (bf16[768,768]{1,0:T(8,128)(2,1)S(1)}, bf16[768,768]{1,0:T(8,128)(2,1)}, u32[]{:S(2)}) copy-start(bf16[768,768]{1,0:T(8,128)(2,1)} %constant.39.clone.top_ref) | copy-start | bytes 3538948
  61.0 10.3 %copy-start = (bf16[768,768]{1,0:T(8,128)(2,1)S(1)}, bf16[768,768]{1,0:T(8,128)(2,1)}, u32[]{:S(2)}) copy-start(bf16[768,768]{1,0:T(8,128)(2,1)} %constant.42.clone.low_ref) | copy-start | bytes 3538948
  61.0 10.3 %copy-start.1 = (bf16[768,768]{1,0:T(8,128)(2,1)S(1)}, bf16[768,768]{1,0:T(8,128)(2,1)}, u32[]{:S(2)}) copy-start(bf16[768,768]{1,0:T(8,128)(2,1)} %constant.41.clone.top_ref) | copy-start | bytes 3538948
  62.0 5.2 %collective-permute-start.9 = (f32[30,768]{1,0:T(8,128)S(1)}, f32[30,768]{1,0:T(8,128)S(1)}, u32[]{:S(2)}, u32[]{:S(2)}) collective-permute-start(f32[30,768]{1,0:T(8,128)S(1)} %get-tuple-element.40), channel_id=1, source_target_pairs={{0,64},{64,128},{128,192},{1,65},{65,129},{129,193},{2,66},{66,130... | collective-permute-start | bytes 276488 | tf_op jit(solution)/shard_map/ppermute | solution.py:490
  65.3 5.9 %collective-permute-start.10 = (f32[30,768]{1,0:T(8,128)S(1)}, f32[30,768]{1,0:T(8,128)S(1)}, u32[]{:S(2)}, u32[]{:S(2)}) collective-permute-start(f32[30,768]{1,0:T(8,128)S(1)} %get-tuple-element.41), channel_id=1, source_target_pairs={{64,0},{128,64},{192,128},{65,1},{129,65},{193,129},{66,2},{130,66... | collective-permute-start | bytes 276488 | tf_op jit(solution)/shard_map/ppermute | solution.py:491
  75.4 34.6 %all-to-all-start.1 = ((f32[64,16,128]{2,1,0:T(8,128)}), f32[64,16,128]{2,1,0:T(8,128)S(1)}, u32[]{:S(2)}, u32[]{:S(2)}) async-start(f32[64,16,128]{2,1,0:T(8,128)} %filter.1._), calls=%async_computation.1 | async-start | bytes 1048576 | tf_op jit(solution)/shard_map/all_to_all | solution.py:466
  86.2 14.5 %collective-permute-start.12 = (f32[40,320]{1,0:T(8,128)S(1)}, f32[40,320]{1,0:T(8,128)S(1)}, u32[]{:S(2)}, u32[]{:S(2)}) collective-permute-start(f32[40,320]{1,0:T(8,128)S(1)} %get-tuple-element.44), channel_id=1, source_target_pairs={{0,2},{2,4},{4,6},{6,0},{8,10},{10,12},{12,14},{14,8},{1,3},{3,5},... | collective-permute-start | bytes 153608 | tf_op jit(solution)/shard_map/ppermute | solution.py:312
  87.2 14.7 %collective-permute-start.13 = (f32[40,320]{1,0:T(8,128)S(1)}, f32[40,320]{1,0:T(8,128)S(1)}, u32[]{:S(2)}, u32[]{:S(2)}) collective-permute-start(f32[40,320]{1,0:T(8,128)S(1)} %get-tuple-element.45), channel_id=1, source_target_pairs={{0,4},{2,6},{4,0},{6,2},{8,12},{10,14},{12,8},{14,10},{1,5},{3,7},... | collective-permute-start | bytes 153608 | tf_op jit(solution)/shard_map/ppermute | solution.py:312
  89.3 12.6 %collective-permute-start.14 = (f32[40,320]{1,0:T(8,128)S(1)}, f32[40,320]{1,0:T(8,128)S(1)}, u32[]{:S(2)}, u32[]{:S(2)}) collective-permute-start(f32[40,320]{1,0:T(8,128)S(1)} %get-tuple-element.46), channel_id=1, source_target_pairs={{0,6},{2,0},{4,2},{6,4},{8,14},{10,8},{12,10},{14,12},{1,7},{3,1},... | collective-permute-start | bytes 153608 | tf_op jit(solution)/shard_map/ppermute | solution.py:312
  102.5 6.8 %collective-permute-start.15 = (f32[20,320]{1,0:T(8,128)S(1)}, f32[20,320]{1,0:T(8,128)S(1)}, u32[]{:S(2)}, u32[]{:S(2)}) collective-permute-start(f32[20,320]{1,0:T(8,128)S(1)} %get-tuple-element.48), channel_id=1, source_target_pairs={{0,8},{2,10},{4,12},{6,14},{8,0},{10,2},{12,4},{14,6},{1,9},{3,11}... | collective-permute-start | bytes 76808 | tf_op jit(solution)/shard_map/ppermute | solution.py:500

commit v9 on v8

--- a/solution.py
+++ b/solution.py
@@ -237,37 +237,27 @@
 
 
 def pair_kernel(place_ref, _, *refs):
-    ins, (mine_ref, send_ref) = refs[:4], refs[4:]
+    ins, outs = refs[:4], refs[4:]
     total = (ins[0][...] + ins[1][...]) + (ins[2][...] + ins[3][...])
     even = jnp.concatenate([total[:, 0:160], total[:, 320:480]], axis=1)
     odd = jnp.concatenate([total[:, 160:320], total[:, 480:640]], axis=1)
-    first = place_ref[1] == 0
-    mine_ref[...] = jnp.where(first, even, odd)
-    send_ref[...] = jnp.where(first, odd, even)
-
-
-def stack_kernel(place_ref, _, mine_ref, arrived_ref, *refs):
+    below = place_ref[5] < 4
+    outs[0][...] = jnp.where(below, even, odd)
+    outs[1][...] = jnp.where(below, odd, even)
+
+
+def stack_kernel(place_ref, _, first_ref, second_ref, *refs):
     outs, kept_ref = refs[:4], refs[4]
-    first = place_ref[1] == 0
-    mine, arrived = mine_ref[...], arrived_ref[...]
-    below, above = jnp.where(first, mine, arrived), jnp.where(first, arrived, mine)
+    total = first_ref[...] + second_ref[...]
     for r in range(4):
-        rows = slice(20 * r, 20 * r + 20)
-        kept_ref[r] = jnp.concatenate([below[rows], above[rows]], axis=0)
+        kept_ref[r, 0:20, :] = total[20 * r : 20 * r + 20]
     for m in range(4):
-        outs[m][...] = kept_ref[lax.rem(place_ref[5] + m, 4)]
-
-
-def half_kernel(place_ref, *refs):
-    ins, (mine_ref, send_ref) = refs[:4], refs[4:]
+        outs[m][...] = kept_ref[lax.rem(place_ref[5] + m, 4), 0:20, :]
+
+
+def last_kernel(*refs):
+    ins, (first_ref, second_ref) = refs[:4], refs[4:]
     total = (ins[0][...] + ins[1][...]) + (ins[2][...] + ins[3][...])
-    below = place_ref[5] < 4
-    mine_ref[...] = jnp.where(below, total[0:20], total[20:40])
-    send_ref[...] = jnp.where(below, total[20:40], total[0:20])
-
-
-def last_kernel(mine_ref, arrived_ref, first_ref, second_ref):
-    total = mine_ref[...] + arrived_ref[...]
     first_ref[...] = total[:, 0:160]
     second_ref[...] = total[:, 160:320]
 
@@ -281,7 +271,7 @@
         out_specs=whole(len(shapes)),
         out_shape=[jax.ShapeDtypeStruct(shape, F32) for shape in shapes],
         scratch_shapes=scratch,
-        compiler_params=params(32),
+        compiler_params=params(16),
         cost_estimate=cost(flops, 4_000_000) if flops else None,
         name=name,
     )(*operands[:scalars], *earlier, *operands[scalars:])
@@ -303,6 +293,13 @@
         return yl, co, x, z, yh
 
     return [pieces[0]] + [permute(pieces[m], functools.partial(target, m)) for m in (1, 2, 3)]
+
+
+def exchange_pair(pieces):
+    def target(b, yl, co, x, z, yh):
+        return yl, (z // 4) ^ b, x, 4 * co + z % 4, yh
+
+    return [permute(pieces[b], functools.partial(target, b)) for b in range(2)]
 
 
 def exchange_z(pieces):
@@ -481,24 +478,18 @@
     swapped = small(swap_kernel, (place, *moved), [(80, 640)] * 4, 1, kept, (), "swap", 10**10)
     kernel = kernel_spectrum(kernels, swapped[0])
     moved = exchange(swapped, "yx")
-    mine, send = small(
-        pair_kernel, (place, *moved), [(80, 320)] * 2, 1, (), (kernel,), "pair"
-    )
-    data, first, final, own_mixing = spectrum(spread, mine)
+    pair = small(pair_kernel, (place, *moved), [(80, 320)] * 2, 1, (), (kernel,), "pair")
+    paired = exchange_pair(pair)
+    data, first, final, own_mixing = spectrum(spread, pair[0])
     forward = [(i, i + 1) for i in range(3)]
     backward = [(target, source) for source, target in forward]
     before = lax.ppermute(final, LAT, forward)
     beyond = lax.ppermute(first, LAT, backward)
-    paired = to_core(send)
-    sent = filtered(own_mixing, data, before, beyond, kernel, (paired,))
+    sent = filtered(own_mixing, data, before, beyond, kernel, paired)
     result = across(sent)
-    kept = (pltpu.VMEM((4, 40, 320), F32),)
-    operands = (place, mine, paired)
-    stacked = small(stack_kernel, operands, [(40, 320)] * 4, 1, kept, (sent,), "stack")
-    moved = exchange_z(stacked)
-    mine, send = small(half_kernel, (place, *moved), [(20, 320)] * 2, 1, name="half")
-    arrived = lax.ppermute(send, "z", [(z, z ^ 4) for z in range(8)])
-    grad_in, grad_out = small(last_kernel, (mine, arrived), [(20, 160)] * 2, name="last")
+    kept = (pltpu.VMEM((4, 24, 320), F32),)
+    stacked = small(stack_kernel, (place, *paired), [(20, 320)] * 4, 1, kept, (sent,), "stack")
+    grad_in, grad_out = small(last_kernel, exchange_z(stacked), [(20, 160)] * 2, name="last")
     field = unpack(result).reshape(COLS, ROWS, width).transpose(1, 0, 2)
     return (field, grad_in, grad_out)
 

time: 112 us -> 113 us (level)
  starting transfers between devices: 48.7 us -> 52 us
  waiting for transfers between devices: 30.4 us -> 27.7 us
  local copies, waits for them, and re-layouts: 4.86 us -> 6.19 us
    ppermute x6 -> x8, starting transfers between devices: 7.03 us -> 16.6 us  [permute(): return lax.ppermute(value, AXES, pairs)]
    ppermute x1 -> x0, starting transfers between devices: 3.47 us -> none  [per_device(): arrived = lax.ppermute(send, 'z', [(z, z ^ 4) for z in range(8)])]
    ppermute x1 -> x0, waiting for transfers between devices: 3.33 us -> none  [per_device(): arrived = lax.ppermute(send, 'z', [(z, z ^ 4) for z in range(8)])]
    all_to_all x2, waiting for transfers between devices: 0.01 us -> 2.77 us  [across(): return lax.all_to_all(block, LON, split_axis=0, concat_axis=0, tiled=True)]
    ppermute x4 -> x3, starting transfers between devices: 6.03 us -> 4.06 us  [to_core(): return lax.ppermute(value, 'co', [(0, 1), (1, 0)])]
    ppermute x3, waiting for transfers between devices: 11.4 us -> 9.82 us  [exchange_z(): lax.ppermute(pieces[m], 'z', pairs(m))]
    ppermute x1, starting transfers between devices: 3.3 us -> 1.92 us  [per_device(): before = lax.ppermute(final, LAT, forward)]
    unnamed x26, local copies, waits for them, and re-layouts: 4.26 us -> 5.52 us
  transfers between devices with their start and end apart: 18 -> 18, of which waited for: 10 -> 10; matrix products, arithmetic and copies ran while one was open for 1% -> 1% of each run, Pallas kernels for 8% -> 7%
where the time goes in v9:
time: 113 us
  starting transfers between devices  52 us (46%)
  waiting for transfers between devices  27.7 us (25%)
  Pallas kernels  26 us (23%)
  local copies, waits for them, and re-layouts  6.19 us (5%)
    all_to_all x2, starting transfers between devices, across(): return lax.all_to_all(block, LON, split_axis=0, concat_axis=0, tiled=True)  22.7 us
    ppermute x8, starting transfers between devices, permute(): return lax.ppermute(value, AXES, pairs)  16.6 us
    pallas_call x1, Pallas kernels, mlp(): pl.pallas_call(mlp_kernel, grid_spec=pltpu.PrefetchScalarGridSpec(num_sca...  12.5 us
    ppermute x3, waiting for transfers between devices, exchange_z(): lax.ppermute(pieces[m], 'z', pairs(m))  9.82 us
    ppermute x8, waiting for transfers between devices, permute(): return lax.ppermute(value, AXES, pairs)  8.27 us
    pallas_call x5, Pallas kernels, small(): pl.pallas_call(kernel, in_specs=[pl.BlockSpec(memory_space=pltpu.SMEM)] *...  5.59 us
    unnamed x26, local copies, waits for them, and re-layouts  5.52 us
    ppermute x3, starting transfers between devices, exchange_z(): lax.ppermute(pieces[m], 'z', pairs(m))  4.35 us
  transfers between devices with their start and end apart: 18, of which 10 were waited for; matrix products, arithmetic and copies ran while one was open for 1% of the time, Pallas kernels for 7%

profile of v9, /device:TPU:1, one launch (start us, length us, event | category | flops | bytes accessed | tf_op | source)
XLA Modules:
  0.0 112.7 jit_solution(4392275118985865477)
XLA Ops:
  0.6 3.3 %collective-permute-start = (f32[192,640]{1,0:T(8,128)}, f32[192,640]{1,0:T(8,128)S(1)}, u32[]{:S(2)}, u32[]{:S(2)}) collective-permute-start(f32[192,640]{1,0:T(8,128)} %bitcast.26), channel_id=1, source_target_pairs={{0,64},{64,0},{1,65},{65,1},{2,66},{66,2},{3,67},{67,3},{4,68},{68... | collective-permute-start | bytes 1474568 | tf_op jit(solution)/shard_map/ppermute | solution.py:313
  4.0 0.1 collective-permute-start.1
  4.1 0.7 stack.28.place_ref
  4.7 0.9 collective-permute-done.act_other_ref
  5.7 0.0 copy-start.11
  5.7 0.7 collective-permute-done.1.cot_other_ref
  6.4 0.0 copy-start.12
  6.4 0.1 copy-done.11
  6.4 0.7 copy-done.12
  7.1 0.0 copy-start.8
  7.1 12.5 %mlp.1 = (f32[192,640]{1,0:T(8,128)}, f32[192,640]{1,0:T(8,128)}, f32[160,1280]{1,0:T(8,128)}, f32[160,1280]{1,0:T(8,128)}, f32[160,1280]{1,0:T(8,128)}, /*index=5*/f32[160,1280]{1,0:T(8,128)}) custom-call(s32[6]{0:T(128)} %stack.28.place_ref, f32[192,640]{1,0:T(8,128)} %bitcast.27, f32[192,640]{1,0:T(8,128)} %copy-done.11, f32[192,640]{1,0:T(8,128)} %bitcast.29, ...), custom_call_target="tpu_custom_call" | custom-call | flops 4718592000 | bytes 12000000 | tf_op jit(solution)/shard_map/mlp/pallas_call | solution.py:190
  19.7 1.2 %collective-permute-start.3 = (f32[160,1280]{1,0:T(8,128)}, f32[160,1280]{1,0:T(8,128)S(1)}, u32[]{:S(2)}, u32[]{:S(2)}) collective-permute-start(f32[160,1280]{1,0:T(8,128)} %get-tuple-element.28), channel_id=1, source_target_pairs={{0,16},{1,17},{2,18},{3,19},{4,20},{5,21},{6,22},{7,23},{8,24},{9,... | collective-permute-start | bytes 2457608 | tf_op jit(solution)/shard_map/ppermute | solution.py:284
  20.8 0.4 collective-permute-start.4
  21.2 1.7 %collective-permute-start.5 = (f32[160,1280]{1,0:T(8,128)}, f32[160,1280]{1,0:T(8,128)}, u32[]{:S(2)}, u32[]{:S(2)}) collective-permute-start(f32[160,1280]{1,0:T(8,128)} %get-tuple-element.30), channel_id=1, source_target_pairs={{0,48},{1,49},{2,50},{3,51},{4,52},{5,53},{6,54},{7,55},{8,56},{9,... | collective-permute-start | bytes 2457608 | tf_op jit(solution)/shard_map/ppermute | solution.py:284
  22.9 0.6 collective-permute-start.2
  23.5 1.7 %collective-permute-done.2.arrived_ref = f32[192,640]{1,0:T(8,128)S(1)} collective-permute-done((f32[192,640]{1,0:T(8,128)}, f32[192,640]{1,0:T(8,128)S(1)}, u32[]{:S(2)}, u32[]{:S(2)}) %collective-permute-start.2) | collective-permute-done | bytes 491552 | tf_op jit(solution)/shard_map/ppermute | solution.py:313
  25.2 0.0 copy-done.8
  25.3 0.0 copy-done.9
  25.3 1.0 copy-done.7
  26.3 2.0 %pack.1 = f32[64,16,128]{2,1,0:T(8,128)} custom-call(s32[6]{0:T(128)S(1)} %copy-done.8, f32[3,10]{1,0:T(4,128)S(1)} %bitcast.22, f32[192,640]{1,0:T(8,128)S(1)} %copy-done.7, f32[192,640]{1,0:T(8,128)S(1)} %collective-permute-done.2.arrived_ref), custom_call_target="tpu_custom_call" | custom-call | tf_op jit(solution)/shard_map/pack/pallas_call | solution.py:266
  28.3 12.5 %all-to-all-start = ((f32[64,16,128]{2,1,0:T(8,128)}), f32[64,16,128]{2,1,0:T(8,128)S(1)}, u32[]{:S(2)}, u32[]{:S(2)}) async-start(f32[64,16,128]{2,1,0:T(8,128)} %pack.1), calls=%async_computation | async-start | bytes 1048576 | tf_op jit(solution)/shard_map/all_to_all | solution.py:463
  40.8 0.0 collective-permute-done.3.refs_1_
  40.8 0.0 collective-permute-done.4.refs_2_
  40.8 0.8 collective-permute-done.5.refs_3_
  41.6 1.1 %copy-done.10 = f32[160,1280]{1,0:T(8,128)S(1)} copy-done((f32[160,1280]{1,0:T(8,128)S(1)}, f32[160,1280]{1,0:T(8,128)}, u32[]{:S(2)}) %copy-start.10) | copy-done | bytes 819224
  42.8 1.6 %swap.1 = (f32[80,640]{1,0:T(8,128)S(1)}, f32[80,640]{1,0:T(8,128)S(1)}, f32[80,640]{1,0:T(8,128)S(1)}, f32[80,640]{1,0:T(8,128)S(1)}) custom-call(s32[6]{0:T(128)S(1)} %copy-done.8, f32[160,1280]{1,0:T(8,128)S(1)} %copy-done.10, f32[160,1280]{1,0:T(8,128)S(1)} %collective-permute-done.3.refs_1_, f32[160,1280]{1,0:T(8,128)S(1)} %collective-permute-done.4.refs_2_, ...), custom_call_target="tpu_custom_call" | custom-call | flops 10000000000 | bytes 4000000 | tf_op jit(solution)/shard_map/swap/pallas_call | solution.py:266
  44.4 0.1 collective-permute-start.6
  44.5 2.6 %collective-permute-start.7 = (f32[80,640]{1,0:T(8,128)S(1)}, f32[80,640]{1,0:T(8,128)S(1)}, u32[]{:S(2)}, u32[]{:S(2)}) collective-permute-start(f32[80,640]{1,0:T(8,128)S(1)} %get-tuple-element.33), channel_id=1, source_target_pairs={{0,128},{1,129},{2,130},{3,131},{4,132},{5,133},{6,134},{7,135},{8... | collective-permute-start | bytes 614408 | tf_op jit(solution)/shard_map/ppermute | solution.py:284
  47.1 1.1 collective-permute-start.8
  48.2 0.0 copy-done.2
  48.2 0.0 copy-done.3
  48.2 0.0 copy-done.6
  48.2 1.4 %kernel_spectrum.1._.kernel_ref = f32[336,768]{1,0:T(8,128)S(1)} custom-call(f32[336,768]{1,0:T(8,128)S(1)} %bitcast.21, bf16[768,768]{1,0:T(8,128)(2,1)S(1)} %copy-done.3, bf16[768,768]{1,0:T(8,128)(2,1)S(1)} %copy-done.2, f32[80,640]{1,0:T(8,128)S(1)} %get-tuple-element.31._.refs_0_), custom_call_target="tpu_custom_call" | custom-call | flops 1189085184 | bytes 5000000 | tf_op jit(solution)/shard_map/kernel_spectrum/pallas_call | solution.py:361
  49.6 3.1 %collective-permute-done.6.refs_1_ = f32[80,640]{1,0:T(8,128)S(1)} collective-permute-done((f32[80,640]{1,0:T(8,128)S(1)}, f32[80,640]{1,0:T(8,128)S(1)}, u32[]{:S(2)}, u32[]{:S(2)}) %collective-permute-start.6) | collective-permute-done | bytes 204832 | tf_op jit(solution)/shard_map/ppermute | solution.py:284
  52.7 4.3 %collective-permute-done.7.refs_2_ = f32[80,640]{1,0:T(8,128)S(1)} collective-permute-done((f32[80,640]{1,0:T(8,128)S(1)}, f32[80,640]{1,0:T(8,128)S(1)}, u32[]{:S(2)}, u32[]{:S(2)}) %collective-permute-start.7) | collective-permute-done | bytes 204832 | tf_op jit(solution)/shard_map/ppermute | solution.py:284
  57.1 0.0 collective-permute-done.8.refs_3_
  57.1 0.7 pair.1
  57.7 4.8 %collective-permute-start.12 = (f32[80,320]{1,0:T(8,128)S(1)}, f32[80,320]{1,0:T(8,128)S(1)}, u32[]{:S(2)}, u32[]{:S(2)}) collective-permute-start(f32[80,320]{1,0:T(8,128)S(1)} %get-tuple-element.40), channel_id=1, source_target_pairs={{0,64},{1,65},{2,66},{3,67},{4,68},{5,69},{6,70},{7,71},{8,0},{9,1... | collective-permute-start | bytes 307208 | tf_op jit(solution)/shard_map/ppermute | solution.py:284
  62.6 4.7 %collective-permute-start.11 = (f32[80,320]{1,0:T(8,128)S(1)}, f32[80,320]{1,0:T(8,128)S(1)}, u32[]{:S(2)}, u32[]{:S(2)}) collective-permute-start(f32[80,320]{1,0:T(8,128)S(1)} %get-tuple-element.35._), channel_id=1, source_target_pairs={{0,0},{1,1},{2,2},{3,3},{4,4},{5,5},{6,6},{7,7},{8,64},{9,65},{10,... | collective-permute-start | bytes 307208 | tf_op jit(solution)/shard_map/ppermute | solution.py:284
  67.3 0.0 all-to-all-done.block_ref
  67.3 0.0 copy-start.4
  67.3 1.3 %copy-done.4 = bf16[768,768]{1,0:T(8,128)(2,1)S(1)} copy-done((bf16[768,768]{1,0:T(8,128)(2,1)S(1)}, bf16[768,768]{1,0:T(8,128)(2,1)}, u32[]{:S(2)}) %copy-start.4) | copy-done | bytes 1179672
  68.6 1.3 %copy-done.5 = bf16[768,768]{1,0:T(8,128)(2,1)S(1)} copy-done((bf16[768,768]{1,0:T(8,128)(2,1)S(1)}, bf16[768,768]{1,0:T(8,128)(2,1)}, u32[]{:S(2)}) %copy-start.5) | copy-done | bytes 1179672
  69.8 1.0 spectrum.1
  70.9 1.9 %collective-permute-start.9 = (f32[30,768]{1,0:T(8,128)S(1)}, f32[30,768]{1,0:T(8,128)S(1)}, u32[]{:S(2)}, u32[]{:S(2)}) collective-permute-start(f32[30,768]{1,0:T(8,128)S(1)} %get-tuple-element.38), channel_id=1, source_target_pairs={{0,64},{64,128},{128,192},{1,65},{65,129},{129,193},{2,66},{66,130... | collective-permute-start | bytes 276488 | tf_op jit(solution)/shard_map/ppermute | solution.py:486
  72.8 2.4 %collective-permute-start.10 = (f32[30,768]{1,0:T(8,128)S(1)}, f32[30,768]{1,0:T(8,128)S(1)}, u32[]{:S(2)}, u32[]{:S(2)}) collective-permute-start(f32[30,768]{1,0:T(8,128)S(1)} %get-tuple-element.39), channel_id=1, source_target_pairs={{64,0},{128,64},{192,128},{65,1},{129,65},{193,129},{66,2},{130,66... | collective-permute-start | bytes 276488 | tf_op jit(solution)/shard_map/ppermute | solution.py:487
  75.2 0.0 collective-permute-done.12.refs_1_.second_ref
  75.2 0.0 collective-permute-done.11.refs_0_.first_ref
  75.3 0.0 collective-permute-done.9.before_ref
  75.3 3.5 %collective-permute-done.10.after_ref = f32[30,768]{1,0:T(8,128)S(1)} collective-permute-done((f32[30,768]{1,0:T(8,128)S(1)}, f32[30,768]{1,0:T(8,128)S(1)}, u32[]{:S(2)}, u32[]{:S(2)}) %collective-permute-start.10) | collective-permute-done | bytes 92192 | tf_op jit(solution)/shard_map/ppermute | solution.py:487
  78.8 0.0 copy-done
  78.8 0.0 copy-done.1
  78.8 4.2 %filter.1._ = f32[64,16,128]{2,1,0:T(8,128)} custom-call(f32[1,128]{1,0:T(1,128)S(1)} %get-tuple-element.36.mixing_ref, f32[160,768]{1,0:T(8,128)S(1)} %get-tuple-element.37.data_ref, f32[30,768]{1,0:T(8,128)S(1)} %collective-permute-done.9.before_ref, f32[30,768]{1,0:T(8,128)S(1)} %collective-permute-done.10.after_ref, ...), custom_call_target="tpu_custom_call" | custom-call | flops 566231040 | bytes 5000000 | tf_op jit(solution)/shard_map/filter/pallas_call | solution.py:419
  82.9 10.3 %all-to-all-start.1 = ((f32[64,16,128]{2,1,0:T(8,128)}), f32[64,16,128]{2,1,0:T(8,128)S(1)}, u32[]{:S(2)}, u32[]{:S(2)}) async-start(f32[64,16,128]{2,1,0:T(8,128)} %filter.1._), calls=%async_computation.1 | async-start | bytes 1048576 | tf_op jit(solution)/shard_map/all_to_all | solution.py:463
  93.2 0.6 stack.29
  93.8 1.1 collective-permute-start.13
  94.9 2.1 %collective-permute-start.14 = (f32[20,320]{1,0:T(8,128)S(1)}, f32[20,320]{1,0:T(8,128)S(1)}, u32[]{:S(2)}, u32[]{:S(2)}) collective-permute-start(f32[20,320]{1,0:T(8,128)S(1)} %get-tuple-element.43), channel_id=1, source_target_pairs={{0,4},{2,6},{4,0},{6,2},{8,12},{10,14},{12,8},{14,10},{1,5},{3,7},... | collective-permute-start | bytes 76808 | tf_op jit(solution)/shard_map/ppermute | solution.py:309
  97.0 1.2 %collective-permute-start.15 = (f32[20,320]{1,0:T(8,128)S(1)}, f32[20,320]{1,0:T(8,128)S(1)}, u32[]{:S(2)}, u32[]{:S(2)}) collective-permute-start(f32[20,320]{1,0:T(8,128)S(1)} %get-tuple-element.44), channel_id=1, source_target_pairs={{0,6},{2,0},{4,2},{6,4},{8,14},{10,8},{12,10},{14,12},{1,7},{3,1},... | collective-permute-start | bytes 76808 | tf_op jit(solution)/shard_map/ppermute | solution.py:309
  98.1 9.4 %collective-permute-done.13.refs_1_ = f32[20,320]{1,0:T(8,128)S(1)} collective-permute-done((f32[20,320]{1,0:T(8,128)S(1)}, f32[20,320]{1,0:T(8,128)S(1)}, u32[]{:S(2)}, u32[]{:S(2)}) %collective-permute-start.13) | collective-permute-done | bytes 25632 | tf_op jit(solution)/shard_map/ppermute | solution.py:309
  107.5 0.5 collective-permute-done.14.refs_2_
  108.0 0.0 collective-permute-done.15.refs_3_
  108.0 0.7 last.1
  108.6 2.8 %all-to-all-done.1.block_ref = f32[64,16,128]{2,1,0:T(8,128)S(1)} async-done(((f32[64,16,128]{2,1,0:T(8,128)}), f32[64,16,128]{2,1,0:T(8,128)S(1)}, u32[]{:S(2)}, u32[]{:S(2)}) %all-to-all-start.1) | async-done | bytes 524320 | tf_op jit(solution)/shard_map/all_to_all | solution.py:463
  111.4 1.3 %unpack.1 = f32[192,640]{1,0:T(8,128)} custom-call(f32[64,16,128]{2,1,0:T(8,128)S(1)} %all-to-all-done.1.block_ref), custom_call_target="tpu_custom_call" | custom-call | tf_op jit(solution)/shard_map/unpack/pallas_call | solution.py:452
  (9 shorter events, 0.0 us)
Async XLA Ops:
  0.6 5.0 %collective-permute-start = (f32[192,640]{1,0:T(8,128)}, f32[192,640]{1,0:T(8,128)S(1)}, u32[]{:S(2)}, u32[]{:S(2)}) collective-permute-start(f32[192,640]{1,0:T(8,128)} %bitcast.26), channel_id=1, source_target_pairs={{0,64},{64,0},{1,65},{65,1},{2,66},{66,2},{3,67},{67,3},{4,68},{68... | collective-permute-start | bytes 1474568 | tf_op jit(solution)/shard_map/ppermute | solution.py:313
  4.0 2.4 %collective-permute-start.1 = (f32[192,640]{1,0:T(8,128)}, f32[192,640]{1,0:T(8,128)S(1)}, u32[]{:S(2)}, u32[]{:S(2)}) collective-permute-start(f32[192,640]{1,0:T(8,128)} %bitcast.28), channel_id=1, source_target_pairs={{0,64},{64,0},{1,65},{65,1},{2,66},{66,2},{3,67},{67,3},{4,68},{68... | collective-permute-start | bytes 1474568 | tf_op jit(solution)/shard_map/ppermute | solution.py:313
  5.7 0.8 copy-start.11
  6.4 0.8 copy-start.12
  7.1 18.1 %copy-start.8 = (s32[6]{0:T(128)S(1)}, s32[6]{0:T(128)}, u32[]{:S(2)}) copy-start(s32[6]{0:T(128)} %stack.28.place_ref) | copy-start | bytes 76
  7.1 18.1 %copy-start.9 = (f32[10,3]{0,1:T(4,128)S(1)}, f32[10,3]{0,1:T(4,128)}, u32[]{:S(2)}) copy-start(f32[10,3]{0,1:T(4,128)} %param.17) | copy-start | bytes 364
  19.7 21.1 %collective-permute-start.3 = (f32[160,1280]{1,0:T(8,128)}, f32[160,1280]{1,0:T(8,128)S(1)}, u32[]{:S(2)}, u32[]{:S(2)}) collective-permute-start(f32[160,1280]{1,0:T(8,128)} %get-tuple-element.28), channel_id=1, source_target_pairs={{0,16},{1,17},{2,18},{3,19},{4,20},{5,21},{6,22},{7,23},{8,24},{9,... | collective-permute-start | bytes 2457608 | tf_op jit(solution)/shard_map/ppermute | solution.py:284
  20.8 20.0 %collective-permute-start.4 = (f32[160,1280]{1,0:T(8,128)}, f32[160,1280]{1,0:T(8,128)S(1)}, u32[]{:S(2)}, u32[]{:S(2)}) collective-permute-start(f32[160,1280]{1,0:T(8,128)} %get-tuple-element.29), channel_id=1, source_target_pairs={{0,32},{1,33},{2,34},{3,35},{4,36},{5,37},{6,38},{7,39},{8,40},{9,... | collective-permute-start | bytes 2457608 | tf_op jit(solution)/shard_map/ppermute | solution.py:284
  21.2 20.4 %collective-permute-start.5 = (f32[160,1280]{1,0:T(8,128)}, f32[160,1280]{1,0:T(8,128)}, u32[]{:S(2)}, u32[]{:S(2)}) collective-permute-start(f32[160,1280]{1,0:T(8,128)} %get-tuple-element.30), channel_id=1, source_target_pairs={{0,48},{1,49},{2,50},{3,51},{4,52},{5,53},{6,54},{7,55},{8,56},{9,... | collective-permute-start | bytes 2457608 | tf_op jit(solution)/shard_map/ppermute | solution.py:284
  22.9 2.3 %collective-permute-start.2 = (f32[192,640]{1,0:T(8,128)}, f32[192,640]{1,0:T(8,128)S(1)}, u32[]{:S(2)}, u32[]{:S(2)}) collective-permute-start(f32[192,640]{1,0:T(8,128)} %get-tuple-element.26), channel_id=1, source_target_pairs={{0,64},{64,0},{1,65},{65,1},{2,66},{66,2},{3,67},{67,3},{4,68},{68... | collective-permute-start | bytes 1474568 | tf_op jit(solution)/shard_map/ppermute | solution.py:313
  25.3 1.0 copy-start.7
  28.3 39.0 %all-to-all-start = ((f32[64,16,128]{2,1,0:T(8,128)}), f32[64,16,128]{2,1,0:T(8,128)S(1)}, u32[]{:S(2)}, u32[]{:S(2)}) async-start(f32[64,16,128]{2,1,0:T(8,128)} %pack.1), calls=%async_computation | async-start | bytes 1048576 | tf_op jit(solution)/shard_map/all_to_all | solution.py:463
  41.6 1.1 %copy-start.10 = (f32[160,1280]{1,0:T(8,128)S(1)}, f32[160,1280]{1,0:T(8,128)}, u32[]{:S(2)}) copy-start(f32[160,1280]{1,0:T(8,128)} %get-tuple-element.27.refs_0_) | copy-start | bytes 2457604
  42.8 5.4 %copy-start.2 = (bf16[768,768]{1,0:T(8,128)(2,1)S(1)}, bf16[768,768]{1,0:T(8,128)(2,1)}, u32[]{:S(2)}) copy-start(bf16[768,768]{1,0:T(8,128)(2,1)} %constant.38.clone.low_ref) | copy-start | bytes 3538948
  42.8 5.4 %copy-start.3 = (bf16[768,768]{1,0:T(8,128)(2,1)S(1)}, bf16[768,768]{1,0:T(8,128)(2,1)}, u32[]{:S(2)}) copy-start(bf16[768,768]{1,0:T(8,128)(2,1)} %constant.37.clone.top_ref) | copy-start | bytes 3538948
  42.8 5.4 %copy-start.6 = (f32[3,16,7,768]{3,1,2,0:T(8,128)S(1)}, f32[3,16,7,768]{3,1,2,0:T(8,128)}, u32[]{:S(2)}) copy-start(f32[3,16,7,768]{3,1,2,0:T(8,128)} %param.16) | copy-start | bytes 3096580
  44.4 8.3 %collective-permute-start.6 = (f32[80,640]{1,0:T(8,128)S(1)}, f32[80,640]{1,0:T(8,128)S(1)}, u32[]{:S(2)}, u32[]{:S(2)}) collective-permute-start(f32[80,640]{1,0:T(8,128)S(1)} %get-tuple-element.32), channel_id=1, source_target_pairs={{0,1},{1,0},{2,3},{3,2},{4,5},{5,4},{6,7},{7,6},{8,9},{9,8},{10,11... | collective-permute-start | bytes 614408 | tf_op jit(solution)/shard_map/ppermute | solution.py:284
  44.5 12.5 %collective-permute-start.7 = (f32[80,640]{1,0:T(8,128)S(1)}, f32[80,640]{1,0:T(8,128)S(1)}, u32[]{:S(2)}, u32[]{:S(2)}) collective-permute-start(f32[80,640]{1,0:T(8,128)S(1)} %get-tuple-element.33), channel_id=1, source_target_pairs={{0,128},{1,129},{2,130},{3,131},{4,132},{5,133},{6,134},{7,135},{8... | collective-permute-start | bytes 614408 | tf_op jit(solution)/shard_map/ppermute | solution.py:284
  47.1 9.9 %collective-permute-start.8 = (f32[80,640]{1,0:T(8,128)S(1)}, f32[80,640]{1,0:T(8,128)S(1)}, u32[]{:S(2)}, u32[]{:S(2)}) collective-permute-start(f32[80,640]{1,0:T(8,128)S(1)} %get-tuple-element.34), channel_id=1, source_target_pairs={{0,129},{1,128},{2,131},{3,130},{4,133},{5,132},{6,135},{7,134},{8... | collective-permute-start | bytes 614408 | tf_op jit(solution)/shard_map/ppermute | solution.py:284
  57.7 17.5 %collective-permute-start.12 = (f32[80,320]{1,0:T(8,128)S(1)}, f32[80,320]{1,0:T(8,128)S(1)}, u32[]{:S(2)}, u32[]{:S(2)}) collective-permute-start(f32[80,320]{1,0:T(8,128)S(1)} %get-tuple-element.40), channel_id=1, source_target_pairs={{0,64},{1,65},{2,66},{3,67},{4,68},{5,69},{6,70},{7,71},{8,0},{9,1... | collective-permute-start | bytes 307208 | tf_op jit(solution)/shard_map/ppermute | solution.py:284
  62.5 16.2 %copy-start = (bf16[768,768]{1,0:T(8,128)(2,1)S(1)}, bf16[768,768]{1,0:T(8,128)(2,1)}, u32[]{:S(2)}) copy-start(bf16[768,768]{1,0:T(8,128)(2,1)} %constant.42.clone.low_ref) | copy-start | bytes 3538948
  62.6 12.7 %collective-permute-start.11 = (f32[80,320]{1,0:T(8,128)S(1)}, f32[80,320]{1,0:T(8,128)S(1)}, u32[]{:S(2)}, u32[]{:S(2)}) collective-permute-start(f32[80,320]{1,0:T(8,128)S(1)} %get-tuple-element.35._), channel_id=1, source_target_pairs={{0,0},{1,1},{2,2},{3,3},{4,4},{5,5},{6,6},{7,7},{8,64},{9,65},{10,... | collective-permute-start | bytes 307208 | tf_op jit(solution)/shard_map/ppermute | solution.py:284
  67.3 1.3 %copy-start.4 = (bf16[768,768]{1,0:T(8,128)(2,1)S(1)}, bf16[768,768]{1,0:T(8,128)(2,1)}, u32[]{:S(2)}) copy-start(bf16[768,768]{1,0:T(8,128)(2,1)} %constant.40.clone.low_ref) | copy-start | bytes 3538948
  68.6 1.3 %copy-start.5 = (bf16[768,768]{1,0:T(8,128)(2,1)S(1)}, bf16[768,768]{1,0:T(8,128)(2,1)}, u32[]{:S(2)}) copy-start(bf16[768,768]{1,0:T(8,128)(2,1)} %constant.39.clone.top_ref) | copy-start | bytes 3538948
  69.8 8.9 %copy-start.1 = (bf16[768,768]{1,0:T(8,128)(2,1)S(1)}, bf16[768,768]{1,0:T(8,128)(2,1)}, u32[]{:S(2)}) copy-start(bf16[768,768]{1,0:T(8,128)(2,1)} %constant.41.clone.top_ref) | copy-start | bytes 3538948
  70.9 4.4 %collective-permute-start.9 = (f32[30,768]{1,0:T(8,128)S(1)}, f32[30,768]{1,0:T(8,128)S(1)}, u32[]{:S(2)}, u32[]{:S(2)}) collective-permute-start(f32[30,768]{1,0:T(8,128)S(1)} %get-tuple-element.38), channel_id=1, source_target_pairs={{0,64},{64,128},{128,192},{1,65},{65,129},{129,193},{2,66},{66,130... | collective-permute-start | bytes 276488 | tf_op jit(solution)/shard_map/ppermute | solution.py:486
  72.8 5.9 %collective-permute-start.10 = (f32[30,768]{1,0:T(8,128)S(1)}, f32[30,768]{1,0:T(8,128)S(1)}, u32[]{:S(2)}, u32[]{:S(2)}) collective-permute-start(f32[30,768]{1,0:T(8,128)S(1)} %get-tuple-element.39), channel_id=1, source_target_pairs={{64,0},{128,64},{192,128},{65,1},{129,65},{193,129},{66,2},{130,66... | collective-permute-start | bytes 276488 | tf_op jit(solution)/shard_map/ppermute | solution.py:487
  82.9 28.5 %all-to-all-start.1 = ((f32[64,16,128]{2,1,0:T(8,128)}), f32[64,16,128]{2,1,0:T(8,128)S(1)}, u32[]{:S(2)}, u32[]{:S(2)}) async-start(f32[64,16,128]{2,1,0:T(8,128)} %filter.1._), calls=%async_computation.1 | async-start | bytes 1048576 | tf_op jit(solution)/shard_map/all_to_all | solution.py:463
  93.8 13.7 %collective-permute-start.13 = (f32[20,320]{1,0:T(8,128)S(1)}, f32[20,320]{1,0:T(8,128)S(1)}, u32[]{:S(2)}, u32[]{:S(2)}) collective-permute-start(f32[20,320]{1,0:T(8,128)S(1)} %get-tuple-element.42), channel_id=1, source_target_pairs={{0,2},{2,4},{4,6},{6,0},{8,10},{10,12},{12,14},{14,8},{1,3},{3,5},... | collective-permute-start | bytes 76808 | tf_op jit(solution)/shard_map/ppermute | solution.py:309
  94.9 13.1 %collective-permute-start.14 = (f32[20,320]{1,0:T(8,128)S(1)}, f32[20,320]{1,0:T(8,128)S(1)}, u32[]{:S(2)}, u32[]{:S(2)}) collective-permute-start(f32[20,320]{1,0:T(8,128)S(1)} %get-tuple-element.43), channel_id=1, source_target_pairs={{0,4},{2,6},{4,0},{6,2},{8,12},{10,14},{12,8},{14,10},{1,5},{3,7},... | collective-permute-start | bytes 76808 | tf_op jit(solution)/shard_map/ppermute | solution.py:309
  97.0 11.0 %collective-permute-start.15 = (f32[20,320]{1,0:T(8,128)S(1)}, f32[20,320]{1,0:T(8,128)S(1)}, u32[]{:S(2)}, u32[]{:S(2)}) collective-permute-start(f32[20,320]{1,0:T(8,128)S(1)} %get-tuple-element.44), channel_id=1, source_target_pairs={{0,6},{2,0},{4,2},{6,4},{8,14},{10,8},{12,10},{14,12},{1,7},{3,1},... | collective-permute-start | bytes 76808 | tf_op jit(solution)/shard_map/ppermute | solution.py:309

commit v10 on v8

--- a/solution.py
+++ b/solution.py
@@ -247,27 +247,21 @@
 
 
 def stack_kernel(place_ref, _, mine_ref, arrived_ref, *refs):
-    outs, kept_ref = refs[:4], refs[4]
+    outs, kept_ref = refs[:8], refs[8]
     first = place_ref[1] == 0
     mine, arrived = mine_ref[...], arrived_ref[...]
     below, above = jnp.where(first, mine, arrived), jnp.where(first, arrived, mine)
-    for r in range(4):
-        rows = slice(20 * r, 20 * r + 20)
-        kept_ref[r] = jnp.concatenate([below[rows], above[rows]], axis=0)
-    for m in range(4):
-        outs[m][...] = kept_ref[lax.rem(place_ref[5] + m, 4)]
-
-
-def half_kernel(place_ref, *refs):
-    ins, (mine_ref, send_ref) = refs[:4], refs[4:]
-    total = (ins[0][...] + ins[1][...]) + (ins[2][...] + ins[3][...])
-    below = place_ref[5] < 4
-    mine_ref[...] = jnp.where(below, total[0:20], total[20:40])
-    send_ref[...] = jnp.where(below, total[20:40], total[0:20])
-
-
-def last_kernel(mine_ref, arrived_ref, first_ref, second_ref):
-    total = mine_ref[...] + arrived_ref[...]
+    for z in range(4):
+        kept_ref[z, 0:20, :] = below[20 * z : 20 * z + 20]
+        kept_ref[4 + z, 0:20, :] = above[20 * z : 20 * z + 20]
+    for m in range(8):
+        outs[m][...] = kept_ref[lax.rem(place_ref[5] + m, 8), 0:20, :]
+
+
+def last_kernel(*refs):
+    first_ref, second_ref = refs[8:]
+    a, b, c, d = (refs[m][...] + refs[m + 4][...] for m in range(4))
+    total = (a + b) + (c + d)
     first_ref[...] = total[:, 0:160]
     second_ref[...] = total[:, 160:320]
 
@@ -306,10 +300,10 @@
 
 
 def exchange_z(pieces):
-    def pairs(m):
-        return [(z, 4 * (z // 4) + (z + m) % 4) for z in range(8)]
-
-    return [pieces[0]] + [lax.ppermute(pieces[m], "z", pairs(m)) for m in (1, 2, 3)]
+    far = (1, 7, 4, 3, 5, 2, 6)
+    return [pieces[0]] + [
+        lax.ppermute(pieces[m], "z", [(z, (z + m) % 8) for z in range(8)]) for m in far
+    ]
 
 
 def to_core(value):
@@ -492,13 +486,10 @@
     paired = to_core(send)
     sent = filtered(own_mixing, data, before, beyond, kernel, (paired,))
     result = across(sent)
-    kept = (pltpu.VMEM((4, 40, 320), F32),)
+    kept = (pltpu.VMEM((8, 24, 320), F32),)
     operands = (place, mine, paired)
-    stacked = small(stack_kernel, operands, [(40, 320)] * 4, 1, kept, (sent,), "stack")
-    moved = exchange_z(stacked)
-    mine, send = small(half_kernel, (place, *moved), [(20, 320)] * 2, 1, name="half")
-    arrived = lax.ppermute(send, "z", [(z, z ^ 4) for z in range(8)])
-    grad_in, grad_out = small(last_kernel, (mine, arrived), [(20, 160)] * 2, name="last")
+    stacked = small(stack_kernel, operands, [(20, 320)] * 8, 1, kept, (sent,), "stack")
+    grad_in, grad_out = small(last_kernel, exchange_z(stacked), [(20, 160)] * 2, name="last")
     field = unpack(result).reshape(COLS, ROWS, width).transpose(1, 0, 2)
     return (field, grad_in, grad_out)
 

time: 112 us -> 109 us (0.973)
  waiting for transfers between devices: 30.4 us -> 19.9 us
  starting transfers between devices: 48.7 us -> 56.6 us
    ppermute x4 -> x7, waiting for transfers between devices: 14.8 us -> 4.27 us  [exchange_z(): lax.ppermute(pieces[m], 'z', [(z, (z + m) % 8) for z in range(8)])]
    ppermute x4 -> x7, starting transfers between devices: 7.82 us -> 15.7 us  [exchange_z(): lax.ppermute(pieces[m], 'z', [(z, (z + m) % 8) for z in range(8)])]
    pallas_call x6 -> x5, Pallas kernels: 6.16 us -> 5.62 us  [small(): pl.pallas_call(kernel, in_specs=[pl.BlockSpec(memory_space=pltpu.SMEM)] *...]
  transfers between devices with their start and end apart: 18 -> 21, of which waited for: 10 -> 10; matrix products, arithmetic and copies ran while one was open for 1% -> 1% of each run, Pallas kernels for 8% -> 7%
where the time goes in v10:
time: 109 us; the launch traced here: 108 us
  starting transfers between devices  56.6 us (52%)
  Pallas kernels  26 us (24%)
  waiting for transfers between devices  19.9 us (18%)
  local copies, waits for them, and re-layouts  4.95 us (5%)
    all_to_all x2, starting transfers between devices, across(): return lax.all_to_all(block, LON, split_axis=0, concat_axis=0, tiled=True)  22.6 us
    ppermute x7, starting transfers between devices, exchange_z(): lax.ppermute(pieces[m], 'z', [(z, (z + m) % 8) for z in range(8)])  15.7 us
    pallas_call x1, Pallas kernels, mlp(): pl.pallas_call(mlp_kernel, grid_spec=pltpu.PrefetchScalarGridSpec(num_sca...  12.5 us
    ppermute x6, waiting for transfers between devices, permute(): return lax.ppermute(value, AXES, pairs)  8.26 us
    ppermute x6, starting transfers between devices, permute(): return lax.ppermute(value, AXES, pairs)  7.04 us
    ppermute x4, starting transfers between devices, to_core(): return lax.ppermute(value, 'co', [(0, 1), (1, 0)])  6.03 us
    pallas_call x5, Pallas kernels, small(): pl.pallas_call(kernel, in_specs=[pl.BlockSpec(memory_space=pltpu.SMEM)] *...  5.62 us
    ppermute x7, waiting for transfers between devices, exchange_z(): lax.ppermute(pieces[m], 'z', [(z, (z + m) % 8) for z in range(8)])  4.27 us
  transfers between devices with their start and end apart: 21, of which 10 were waited for; matrix products, arithmetic and copies ran while one was open for 1% of the time, Pallas kernels for 7%

profile of v10, /device:TPU:1, one launch (start us, length us, event | category | flops | bytes accessed | tf_op | source)
XLA Modules:
  0.0 108.2 jit_solution(215449171041516985)
XLA Ops:
  0.6 3.3 %collective-permute-start = (f32[192,640]{1,0:T(8,128)}, f32[192,640]{1,0:T(8,128)S(1)}, u32[]{:S(2)}, u32[]{:S(2)}) collective-permute-start(f32[192,640]{1,0:T(8,128)} %bitcast.26), channel_id=1, source_target_pairs={{0,64},{64,0},{1,65},{65,1},{2,66},{66,2},{3,67},{67,3},{4,68},{68... | collective-permute-start | bytes 1474568 | tf_op jit(solution)/shard_map/ppermute | solution.py:310
  4.0 0.1 collective-permute-start.1
  4.1 0.7 stack.28.place_ref
  4.7 0.9 collective-permute-done.act_other_ref
  5.7 0.7 collective-permute-done.1.cot_other_ref
  6.4 0.1 copy-done.11
  6.4 0.7 copy-done.12
  7.2 12.5 %mlp.1 = (f32[192,640]{1,0:T(8,128)}, f32[192,640]{1,0:T(8,128)}, f32[160,1280]{1,0:T(8,128)}, f32[160,1280]{1,0:T(8,128)}, f32[160,1280]{1,0:T(8,128)}, /*index=5*/f32[160,1280]{1,0:T(8,128)}) custom-call(s32[6]{0:T(128)} %stack.28.place_ref, f32[192,640]{1,0:T(8,128)} %bitcast.27, f32[192,640]{1,0:T(8,128)} %copy-done.11, f32[192,640]{1,0:T(8,128)} %bitcast.29, ...), custom_call_target="tpu_custom_call" | custom-call | flops 4718592000 | bytes 12000000 | tf_op jit(solution)/shard_map/mlp/pallas_call | solution.py:190
  19.6 1.2 %collective-permute-start.3 = (f32[160,1280]{1,0:T(8,128)}, f32[160,1280]{1,0:T(8,128)S(1)}, u32[]{:S(2)}, u32[]{:S(2)}) collective-permute-start(f32[160,1280]{1,0:T(8,128)} %get-tuple-element.32), channel_id=1, source_target_pairs={{0,16},{1,17},{2,18},{3,19},{4,20},{5,21},{6,22},{7,23},{8,24},{9,... | collective-permute-start | bytes 2457608 | tf_op jit(solution)/shard_map/ppermute | solution.py:288
  20.8 0.4 collective-permute-start.4
  21.2 1.7 %collective-permute-start.5 = (f32[160,1280]{1,0:T(8,128)}, f32[160,1280]{1,0:T(8,128)}, u32[]{:S(2)}, u32[]{:S(2)}) collective-permute-start(f32[160,1280]{1,0:T(8,128)} %get-tuple-element.34), channel_id=1, source_target_pairs={{0,48},{1,49},{2,50},{3,51},{4,52},{5,53},{6,54},{7,55},{8,56},{9,... | collective-permute-start | bytes 2457608 | tf_op jit(solution)/shard_map/ppermute | solution.py:288
  22.9 0.6 collective-permute-start.2
  23.5 1.7 %collective-permute-done.2.arrived_ref = f32[192,640]{1,0:T(8,128)S(1)} collective-permute-done((f32[192,640]{1,0:T(8,128)}, f32[192,640]{1,0:T(8,128)S(1)}, u32[]{:S(2)}, u32[]{:S(2)}) %collective-permute-start.2) | collective-permute-done | bytes 491552 | tf_op jit(solution)/shard_map/ppermute | solution.py:310
  25.2 0.0 copy-done.8
  25.2 0.0 copy-done.9
  25.2 1.0 copy-done.7
  26.3 2.0 %pack.1 = f32[64,16,128]{2,1,0:T(8,128)} custom-call(s32[6]{0:T(128)S(1)} %copy-done.8, f32[3,10]{1,0:T(4,128)S(1)} %bitcast.22, f32[192,640]{1,0:T(8,128)S(1)} %copy-done.7, f32[192,640]{1,0:T(8,128)S(1)} %collective-permute-done.2.arrived_ref), custom_call_target="tpu_custom_call" | custom-call | tf_op jit(solution)/shard_map/pack/pallas_call | solution.py:270
  28.3 12.5 %all-to-all-start = ((f32[64,16,128]{2,1,0:T(8,128)}), f32[64,16,128]{2,1,0:T(8,128)S(1)}, u32[]{:S(2)}, u32[]{:S(2)}) async-start(f32[64,16,128]{2,1,0:T(8,128)} %pack.1), calls=%async_computation | async-start | bytes 1048576 | tf_op jit(solution)/shard_map/all_to_all | solution.py:460
  40.8 0.0 collective-permute-done.3.refs_1_
  40.8 0.0 collective-permute-done.4.refs_2_
  40.8 0.8 collective-permute-done.5.refs_3_
  41.6 1.1 %copy-done.10 = f32[160,1280]{1,0:T(8,128)S(1)} copy-done((f32[160,1280]{1,0:T(8,128)S(1)}, f32[160,1280]{1,0:T(8,128)}, u32[]{:S(2)}) %copy-start.10) | copy-done | bytes 819224
  42.8 1.6 %swap.1 = (f32[80,640]{1,0:T(8,128)S(1)}, f32[80,640]{1,0:T(8,128)S(1)}, f32[80,640]{1,0:T(8,128)S(1)}, f32[80,640]{1,0:T(8,128)S(1)}) custom-call(s32[6]{0:T(128)S(1)} %copy-done.8, f32[160,1280]{1,0:T(8,128)S(1)} %copy-done.10, f32[160,1280]{1,0:T(8,128)S(1)} %collective-permute-done.3.refs_1_, f32[160,1280]{1,0:T(8,128)S(1)} %collective-permute-done.4.refs_2_, ...), custom_call_target="tpu_custom_call" | custom-call | flops 10000000000 | bytes 4000000 | tf_op jit(solution)/shard_map/swap/pallas_call | solution.py:270
  44.4 0.1 collective-permute-start.6
  44.5 2.6 %collective-permute-start.7 = (f32[80,640]{1,0:T(8,128)S(1)}, f32[80,640]{1,0:T(8,128)S(1)}, u32[]{:S(2)}, u32[]{:S(2)}) collective-permute-start(f32[80,640]{1,0:T(8,128)S(1)} %get-tuple-element.37), channel_id=1, source_target_pairs={{0,128},{1,129},{2,130},{3,131},{4,132},{5,133},{6,134},{7,135},{8... | collective-permute-start | bytes 614408 | tf_op jit(solution)/shard_map/ppermute | solution.py:288
  47.1 1.1 collective-permute-start.8
  48.2 0.0 copy-done.2
  48.2 0.0 copy-done.3
  48.2 1.4 %kernel_spectrum.1._.kernel_ref = f32[336,768]{1,0:T(8,128)S(1)} custom-call(f32[336,768]{1,0:T(8,128)S(1)} %bitcast.21, bf16[768,768]{1,0:T(8,128)(2,1)S(1)} %copy-done.3, bf16[768,768]{1,0:T(8,128)(2,1)S(1)} %copy-done.2, f32[80,640]{1,0:T(8,128)S(1)} %get-tuple-element.35._.refs_0_), custom_call_target="tpu_custom_call" | custom-call | flops 1189085184 | bytes 5000000 | tf_op jit(solution)/shard_map/kernel_spectrum/pallas_call | solution.py:358
  49.6 0.0 copy-start.4
  49.6 3.1 %collective-permute-done.6.refs_1_ = f32[80,640]{1,0:T(8,128)S(1)} collective-permute-done((f32[80,640]{1,0:T(8,128)S(1)}, f32[80,640]{1,0:T(8,128)S(1)}, u32[]{:S(2)}, u32[]{:S(2)}) %collective-permute-start.6) | collective-permute-done | bytes 204832 | tf_op jit(solution)/shard_map/ppermute | solution.py:288
  52.7 4.3 %collective-permute-done.7.refs_2_ = f32[80,640]{1,0:T(8,128)S(1)} collective-permute-done((f32[80,640]{1,0:T(8,128)S(1)}, f32[80,640]{1,0:T(8,128)S(1)}, u32[]{:S(2)}, u32[]{:S(2)}) %collective-permute-start.7) | collective-permute-done | bytes 204832 | tf_op jit(solution)/shard_map/ppermute | solution.py:288
  57.1 0.0 collective-permute-done.8.refs_3_
  57.1 0.7 pair.1
  57.7 2.0 %collective-permute-start.11 = (f32[80,320]{1,0:T(8,128)S(1)}, f32[80,320]{1,0:T(8,128)S(1)}, u32[]{:S(2)}, u32[]{:S(2)}) collective-permute-start(f32[80,320]{1,0:T(8,128)S(1)} %get-tuple-element.44), channel_id=1, source_target_pairs={{0,64},{64,0},{1,65},{65,1},{2,66},{66,2},{3,67},{67,3},{4,68},{68... | collective-permute-start | bytes 307208 | tf_op jit(solution)/shard_map/ppermute | solution.py:310
  59.7 0.0 all-to-all-done.block_ref
  59.7 0.0 copy-done.4
  59.7 1.3 %copy-done.5 = bf16[768,768]{1,0:T(8,128)(2,1)S(1)} copy-done((bf16[768,768]{1,0:T(8,128)(2,1)S(1)}, bf16[768,768]{1,0:T(8,128)(2,1)}, u32[]{:S(2)}) %copy-start.5) | copy-done | bytes 1179672
  61.0 1.0 spectrum.1
  62.0 3.3 %collective-permute-start.9 = (f32[30,768]{1,0:T(8,128)S(1)}, f32[30,768]{1,0:T(8,128)S(1)}, u32[]{:S(2)}, u32[]{:S(2)}) collective-permute-start(f32[30,768]{1,0:T(8,128)S(1)} %get-tuple-element.42), channel_id=1, source_target_pairs={{0,64},{64,128},{128,192},{1,65},{65,129},{129,193},{2,66},{66,130... | collective-permute-start | bytes 276488 | tf_op jit(solution)/shard_map/ppermute | solution.py:484
  65.3 1.9 %collective-permute-start.10 = (f32[30,768]{1,0:T(8,128)S(1)}, f32[30,768]{1,0:T(8,128)S(1)}, u32[]{:S(2)}, u32[]{:S(2)}) collective-permute-start(f32[30,768]{1,0:T(8,128)S(1)} %get-tuple-element.43), channel_id=1, source_target_pairs={{64,0},{128,64},{192,128},{65,1},{129,65},{193,129},{66,2},{130,66... | collective-permute-start | bytes 276488 | tf_op jit(solution)/shard_map/ppermute | solution.py:485
  67.3 0.0 collective-permute-done.11.refs_0_.arrived_ref
  67.3 0.0 collective-permute-done.9.before_ref
  67.3 4.0 %collective-permute-done.10.after_ref = f32[30,768]{1,0:T(8,128)S(1)} collective-permute-done((f32[30,768]{1,0:T(8,128)S(1)}, f32[30,768]{1,0:T(8,128)S(1)}, u32[]{:S(2)}, u32[]{:S(2)}) %collective-permute-start.10) | collective-permute-done | bytes 92192 | tf_op jit(solution)/shard_map/ppermute | solution.py:485
  71.3 4.2 %filter.1._ = f32[64,16,128]{2,1,0:T(8,128)} custom-call(f32[1,128]{1,0:T(1,128)S(1)} %get-tuple-element.40.mixing_ref, f32[160,768]{1,0:T(8,128)S(1)} %get-tuple-element.41.data_ref, f32[30,768]{1,0:T(8,128)S(1)} %collective-permute-done.9.before_ref, f32[30,768]{1,0:T(8,128)S(1)} %collective-permute-done.10.after_ref, ...), custom_call_target="tpu_custom_call" | custom-call | flops 566231040 | bytes 5000000 | tf_op jit(solution)/shard_map/filter/pallas_call | solution.py:416
  75.4 10.1 %all-to-all-start.1 = ((f32[64,16,128]{2,1,0:T(8,128)}), f32[64,16,128]{2,1,0:T(8,128)S(1)}, u32[]{:S(2)}, u32[]{:S(2)}) async-start(f32[64,16,128]{2,1,0:T(8,128)} %filter.1._), calls=%async_computation.1 | async-start | bytes 1048576 | tf_op jit(solution)/shard_map/all_to_all | solution.py:460
  85.6 0.6 stack.29
  86.2 1.1 %collective-permute-start.12 = (f32[20,320]{1,0:T(8,128)S(1)}, f32[20,320]{1,0:T(8,128)S(1)}, u32[]{:S(2)}, u32[]{:S(2)}) collective-permute-start(f32[20,320]{1,0:T(8,128)S(1)} %get-tuple-element.46), channel_id=1, source_target_pairs={{0,2},{2,4},{4,6},{6,8},{8,10},{10,12},{12,14},{14,0},{1,3},{3,5},... | collective-permute-start | bytes 76808 | tf_op jit(solution)/shard_map/ppermute | solution.py:305
  87.2 1.7 %collective-permute-start.13 = (f32[20,320]{1,0:T(8,128)S(1)}, f32[20,320]{1,0:T(8,128)S(1)}, u32[]{:S(2)}, u32[]{:S(2)}) collective-permute-start(f32[20,320]{1,0:T(8,128)S(1)} %get-tuple-element.47), channel_id=1, source_target_pairs={{0,14},{2,0},{4,2},{6,4},{8,6},{10,8},{12,10},{14,12},{1,15},{3,1}... | collective-permute-start | bytes 76808 | tf_op jit(solution)/shard_map/ppermute | solution.py:305
  88.9 4.9 %collective-permute-start.14 = (f32[20,320]{1,0:T(8,128)S(1)}, f32[20,320]{1,0:T(8,128)S(1)}, u32[]{:S(2)}, u32[]{:S(2)}) collective-permute-start(f32[20,320]{1,0:T(8,128)S(1)} %get-tuple-element.48), channel_id=1, source_target_pairs={{0,8},{2,10},{4,12},{6,14},{8,0},{10,2},{12,4},{14,6},{1,9},{3,11}... | collective-permute-start | bytes 76808 | tf_op jit(solution)/shard_map/ppermute | solution.py:305
  93.8 0.0 collective-permute-start.15
  93.8 4.5 %collective-permute-start.16 = (f32[20,320]{1,0:T(8,128)S(1)}, f32[20,320]{1,0:T(8,128)S(1)}, u32[]{:S(2)}, u32[]{:S(2)}) collective-permute-start(f32[20,320]{1,0:T(8,128)S(1)} %get-tuple-element.50), channel_id=1, source_target_pairs={{0,10},{2,12},{4,14},{6,0},{8,2},{10,4},{12,6},{14,8},{1,11},{3,13... | collective-permute-start | bytes 76808 | tf_op jit(solution)/shard_map/ppermute | solution.py:305
  98.3 2.1 %collective-permute-done.12.refs_1_ = f32[20,320]{1,0:T(8,128)S(1)} collective-permute-done((f32[20,320]{1,0:T(8,128)S(1)}, f32[20,320]{1,0:T(8,128)S(1)}, u32[]{:S(2)}, u32[]{:S(2)}) %collective-permute-start.12) | collective-permute-done | bytes 25632 | tf_op jit(solution)/shard_map/ppermute | solution.py:305
  100.4 0.8 collective-permute-start.17
  101.1 0.0 collective-permute-done.13.refs_2_
  101.1 2.8 %collective-permute-start.18 = (f32[20,320]{1,0:T(8,128)S(1)}, f32[20,320]{1,0:T(8,128)S(1)}, u32[]{:S(2)}, u32[]{:S(2)}) collective-permute-start(f32[20,320]{1,0:T(8,128)S(1)} %get-tuple-element.52), channel_id=1, source_target_pairs={{0,12},{2,14},{4,0},{6,2},{8,4},{10,6},{12,8},{14,10},{1,13},{3,15... | collective-permute-start | bytes 76808 | tf_op jit(solution)/shard_map/ppermute | solution.py:305
  104.0 1.7 %collective-permute-done.14.refs_3_ = f32[20,320]{1,0:T(8,128)S(1)} collective-permute-done((f32[20,320]{1,0:T(8,128)S(1)}, f32[20,320]{1,0:T(8,128)S(1)}, u32[]{:S(2)}, u32[]{:S(2)}) %collective-permute-start.14) | collective-permute-done | bytes 25632 | tf_op jit(solution)/shard_map/ppermute | solution.py:305
  105.7 0.0 collective-permute-done.15.refs_4_
  105.7 0.0 collective-permute-done.16.refs_5_
  105.7 0.5 collective-permute-done.17.refs_6_
  106.2 0.0 collective-permute-done.18.refs_7_
  106.2 0.7 last.1
  106.9 0.0 all-to-all-done.1.block_ref
  106.9 1.3 %unpack.1 = f32[192,640]{1,0:T(8,128)} custom-call(f32[64,16,128]{2,1,0:T(8,128)S(1)} %all-to-all-done.1.block_ref), custom_call_target="tpu_custom_call" | custom-call | tf_op jit(solution)/shard_map/unpack/pallas_call | solution.py:449
  (15 shorter events, 0.0 us)
Async XLA Ops:
  0.6 5.0 %collective-permute-start = (f32[192,640]{1,0:T(8,128)}, f32[192,640]{1,0:T(8,128)S(1)}, u32[]{:S(2)}, u32[]{:S(2)}) collective-permute-start(f32[192,640]{1,0:T(8,128)} %bitcast.26), channel_id=1, source_target_pairs={{0,64},{64,0},{1,65},{65,1},{2,66},{66,2},{3,67},{67,3},{4,68},{68... | collective-permute-start | bytes 1474568 | tf_op jit(solution)/shard_map/ppermute | solution.py:310
  4.0 2.4 %collective-permute-start.1 = (f32[192,640]{1,0:T(8,128)}, f32[192,640]{1,0:T(8,128)S(1)}, u32[]{:S(2)}, u32[]{:S(2)}) collective-permute-start(f32[192,640]{1,0:T(8,128)} %bitcast.28), channel_id=1, source_target_pairs={{0,64},{64,0},{1,65},{65,1},{2,66},{66,2},{3,67},{67,3},{4,68},{68... | collective-permute-start | bytes 1474568 | tf_op jit(solution)/shard_map/ppermute | solution.py:310
  5.7 0.8 copy-start.11
  6.4 0.8 copy-start.12
  7.1 18.1 %copy-start.8 = (s32[6]{0:T(128)S(1)}, s32[6]{0:T(128)}, u32[]{:S(2)}) copy-start(s32[6]{0:T(128)} %stack.28.place_ref) | copy-start | bytes 76
  7.1 18.1 %copy-start.9 = (f32[10,3]{0,1:T(4,128)S(1)}, f32[10,3]{0,1:T(4,128)}, u32[]{:S(2)}) copy-start(f32[10,3]{0,1:T(4,128)} %param.17) | copy-start | bytes 364
  19.6 21.1 %collective-permute-start.3 = (f32[160,1280]{1,0:T(8,128)}, f32[160,1280]{1,0:T(8,128)S(1)}, u32[]{:S(2)}, u32[]{:S(2)}) collective-permute-start(f32[160,1280]{1,0:T(8,128)} %get-tuple-element.32), channel_id=1, source_target_pairs={{0,16},{1,17},{2,18},{3,19},{4,20},{5,21},{6,22},{7,23},{8,24},{9,... | collective-permute-start | bytes 2457608 | tf_op jit(solution)/shard_map/ppermute | solution.py:288
  20.8 20.0 %collective-permute-start.4 = (f32[160,1280]{1,0:T(8,128)}, f32[160,1280]{1,0:T(8,128)S(1)}, u32[]{:S(2)}, u32[]{:S(2)}) collective-permute-start(f32[160,1280]{1,0:T(8,128)} %get-tuple-element.33), channel_id=1, source_target_pairs={{0,32},{1,33},{2,34},{3,35},{4,36},{5,37},{6,38},{7,39},{8,40},{9,... | collective-permute-start | bytes 2457608 | tf_op jit(solution)/shard_map/ppermute | solution.py:288
  21.2 20.4 %collective-permute-start.5 = (f32[160,1280]{1,0:T(8,128)}, f32[160,1280]{1,0:T(8,128)}, u32[]{:S(2)}, u32[]{:S(2)}) collective-permute-start(f32[160,1280]{1,0:T(8,128)} %get-tuple-element.34), channel_id=1, source_target_pairs={{0,48},{1,49},{2,50},{3,51},{4,52},{5,53},{6,54},{7,55},{8,56},{9,... | collective-permute-start | bytes 2457608 | tf_op jit(solution)/shard_map/ppermute | solution.py:288
  22.9 2.3 %collective-permute-start.2 = (f32[192,640]{1,0:T(8,128)}, f32[192,640]{1,0:T(8,128)S(1)}, u32[]{:S(2)}, u32[]{:S(2)}) collective-permute-start(f32[192,640]{1,0:T(8,128)} %get-tuple-element.30), channel_id=1, source_target_pairs={{0,64},{64,0},{1,65},{65,1},{2,66},{66,2},{3,67},{67,3},{4,68},{68... | collective-permute-start | bytes 1474568 | tf_op jit(solution)/shard_map/ppermute | solution.py:310
  25.2 1.0 copy-start.7
  28.3 31.4 %all-to-all-start = ((f32[64,16,128]{2,1,0:T(8,128)}), f32[64,16,128]{2,1,0:T(8,128)S(1)}, u32[]{:S(2)}, u32[]{:S(2)}) async-start(f32[64,16,128]{2,1,0:T(8,128)} %pack.1), calls=%async_computation | async-start | bytes 1048576 | tf_op jit(solution)/shard_map/all_to_all | solution.py:460
  41.6 1.1 %copy-start.10 = (f32[160,1280]{1,0:T(8,128)S(1)}, f32[160,1280]{1,0:T(8,128)}, u32[]{:S(2)}) copy-start(f32[160,1280]{1,0:T(8,128)} %get-tuple-element.31.refs_0_) | copy-start | bytes 2457604
  42.8 5.4 %copy-start.2 = (bf16[768,768]{1,0:T(8,128)(2,1)S(1)}, bf16[768,768]{1,0:T(8,128)(2,1)}, u32[]{:S(2)}) copy-start(bf16[768,768]{1,0:T(8,128)(2,1)} %constant.38.clone.low_ref) | copy-start | bytes 3538948
  42.8 5.4 %copy-start.3 = (bf16[768,768]{1,0:T(8,128)(2,1)S(1)}, bf16[768,768]{1,0:T(8,128)(2,1)}, u32[]{:S(2)}) copy-start(bf16[768,768]{1,0:T(8,128)(2,1)} %constant.37.clone.top_ref) | copy-start | bytes 3538948
  42.8 5.4 %copy-start.6 = (f32[3,16,7,768]{3,1,2,0:T(8,128)S(1)}, f32[3,16,7,768]{3,1,2,0:T(8,128)}, u32[]{:S(2)}) copy-start(f32[3,16,7,768]{3,1,2,0:T(8,128)} %param.16) | copy-start | bytes 3096580
  44.4 8.3 %collective-permute-start.6 = (f32[80,640]{1,0:T(8,128)S(1)}, f32[80,640]{1,0:T(8,128)S(1)}, u32[]{:S(2)}, u32[]{:S(2)}) collective-permute-start(f32[80,640]{1,0:T(8,128)S(1)} %get-tuple-element.36), channel_id=1, source_target_pairs={{0,1},{1,0},{2,3},{3,2},{4,5},{5,4},{6,7},{7,6},{8,9},{9,8},{10,11... | collective-permute-start | bytes 614408 | tf_op jit(solution)/shard_map/ppermute | solution.py:288
  44.5 12.5 %collective-permute-start.7 = (f32[80,640]{1,0:T(8,128)S(1)}, f32[80,640]{1,0:T(8,128)S(1)}, u32[]{:S(2)}, u32[]{:S(2)}) collective-permute-start(f32[80,640]{1,0:T(8,128)S(1)} %get-tuple-element.37), channel_id=1, source_target_pairs={{0,128},{1,129},{2,130},{3,131},{4,132},{5,133},{6,134},{7,135},{8... | collective-permute-start | bytes 614408 | tf_op jit(solution)/shard_map/ppermute | solution.py:288
  47.1 9.9 %collective-permute-start.8 = (f32[80,640]{1,0:T(8,128)S(1)}, f32[80,640]{1,0:T(8,128)S(1)}, u32[]{:S(2)}, u32[]{:S(2)}) collective-permute-start(f32[80,640]{1,0:T(8,128)S(1)} %get-tuple-element.38), channel_id=1, source_target_pairs={{0,129},{1,128},{2,131},{3,130},{4,133},{5,132},{6,135},{7,134},{8... | collective-permute-start | bytes 614408 | tf_op jit(solution)/shard_map/ppermute | solution.py:288
  49.6 10.1 %copy-start.4 = (bf16[768,768]{1,0:T(8,128)(2,1)S(1)}, bf16[768,768]{1,0:T(8,128)(2,1)}, u32[]{:S(2)}) copy-start(bf16[768,768]{1,0:T(8,128)(2,1)} %constant.40.clone.low_ref) | copy-start | bytes 3538948
  57.7 9.5 %collective-permute-start.11 = (f32[80,320]{1,0:T(8,128)S(1)}, f32[80,320]{1,0:T(8,128)S(1)}, u32[]{:S(2)}, u32[]{:S(2)}) collective-permute-start(f32[80,320]{1,0:T(8,128)S(1)} %get-tuple-element.44), channel_id=1, source_target_pairs={{0,64},{64,0},{1,65},{65,1},{2,66},{66,2},{3,67},{67,3},{4,68},{68... | collective-permute-start | bytes 307208 | tf_op jit(solution)/shard_map/ppermute | solution.py:310
  59.7 1.3 %copy-start.5 = (bf16[768,768]{1,0:T(8,128)(2,1)S(1)}, bf16[768,768]{1,0:T(8,128)(2,1)}, u32[]{:S(2)}) copy-start(bf16[768,768]{1,0:T(8,128)(2,1)} %constant.39.clone.top_ref) | copy-start | bytes 3538948
  61.0 10.3 %copy-start = (bf16[768,768]{1,0:T(8,128)(2,1)S(1)}, bf16[768,768]{1,0:T(8,128)(2,1)}, u32[]{:S(2)}) copy-start(bf16[768,768]{1,0:T(8,128)(2,1)} %constant.42.clone.low_ref) | copy-start | bytes 3538948
  61.0 10.3 %copy-start.1 = (bf16[768,768]{1,0:T(8,128)(2,1)S(1)}, bf16[768,768]{1,0:T(8,128)(2,1)}, u32[]{:S(2)}) copy-start(bf16[768,768]{1,0:T(8,128)(2,1)} %constant.41.clone.top_ref) | copy-start | bytes 3538948
  62.0 5.3 %collective-permute-start.9 = (f32[30,768]{1,0:T(8,128)S(1)}, f32[30,768]{1,0:T(8,128)S(1)}, u32[]{:S(2)}, u32[]{:S(2)}) collective-permute-start(f32[30,768]{1,0:T(8,128)S(1)} %get-tuple-element.42), channel_id=1, source_target_pairs={{0,64},{64,128},{128,192},{1,65},{65,129},{129,193},{2,66},{66,130... | collective-permute-start | bytes 276488 | tf_op jit(solution)/shard_map/ppermute | solution.py:484
  65.3 5.9 %collective-permute-start.10 = (f32[30,768]{1,0:T(8,128)S(1)}, f32[30,768]{1,0:T(8,128)S(1)}, u32[]{:S(2)}, u32[]{:S(2)}) collective-permute-start(f32[30,768]{1,0:T(8,128)S(1)} %get-tuple-element.43), channel_id=1, source_target_pairs={{64,0},{128,64},{192,128},{65,1},{129,65},{193,129},{66,2},{130,66... | collective-permute-start | bytes 276488 | tf_op jit(solution)/shard_map/ppermute | solution.py:485
  75.4 31.4 %all-to-all-start.1 = ((f32[64,16,128]{2,1,0:T(8,128)}), f32[64,16,128]{2,1,0:T(8,128)S(1)}, u32[]{:S(2)}, u32[]{:S(2)}) async-start(f32[64,16,128]{2,1,0:T(8,128)} %filter.1._), calls=%async_computation.1 | async-start | bytes 1048576 | tf_op jit(solution)/shard_map/all_to_all | solution.py:460
  86.2 14.2 %collective-permute-start.12 = (f32[20,320]{1,0:T(8,128)S(1)}, f32[20,320]{1,0:T(8,128)S(1)}, u32[]{:S(2)}, u32[]{:S(2)}) collective-permute-start(f32[20,320]{1,0:T(8,128)S(1)} %get-tuple-element.46), channel_id=1, source_target_pairs={{0,2},{2,4},{4,6},{6,8},{8,10},{10,12},{12,14},{14,0},{1,3},{3,5},... | collective-permute-start | bytes 76808 | tf_op jit(solution)/shard_map/ppermute | solution.py:305
  87.2 13.9 %collective-permute-start.13 = (f32[20,320]{1,0:T(8,128)S(1)}, f32[20,320]{1,0:T(8,128)S(1)}, u32[]{:S(2)}, u32[]{:S(2)}) collective-permute-start(f32[20,320]{1,0:T(8,128)S(1)} %get-tuple-element.47), channel_id=1, source_target_pairs={{0,14},{2,0},{4,2},{6,4},{8,6},{10,8},{12,10},{14,12},{1,15},{3,1}... | collective-permute-start | bytes 76808 | tf_op jit(solution)/shard_map/ppermute | solution.py:305
  88.9 16.7 %collective-permute-start.14 = (f32[20,320]{1,0:T(8,128)S(1)}, f32[20,320]{1,0:T(8,128)S(1)}, u32[]{:S(2)}, u32[]{:S(2)}) collective-permute-start(f32[20,320]{1,0:T(8,128)S(1)} %get-tuple-element.48), channel_id=1, source_target_pairs={{0,8},{2,10},{4,12},{6,14},{8,0},{10,2},{12,4},{14,6},{1,9},{3,11}... | collective-permute-start | bytes 76808 | tf_op jit(solution)/shard_map/ppermute | solution.py:305
  93.8 11.8 %collective-permute-start.15 = (f32[20,320]{1,0:T(8,128)S(1)}, f32[20,320]{1,0:T(8,128)S(1)}, u32[]{:S(2)}, u32[]{:S(2)}) collective-permute-start(f32[20,320]{1,0:T(8,128)S(1)} %get-tuple-element.49), channel_id=1, source_target_pairs={{0,6},{2,8},{4,10},{6,12},{8,14},{10,0},{12,2},{14,4},{1,7},{3,9},... | collective-permute-start | bytes 76808 | tf_op jit(solution)/shard_map/ppermute | solution.py:305
  93.8 11.8 %collective-permute-start.16 = (f32[20,320]{1,0:T(8,128)S(1)}, f32[20,320]{1,0:T(8,128)S(1)}, u32[]{:S(2)}, u32[]{:S(2)}) collective-permute-start(f32[20,320]{1,0:T(8,128)S(1)} %get-tuple-element.50), channel_id=1, source_target_pairs={{0,10},{2,12},{4,14},{6,0},{8,2},{10,4},{12,6},{14,8},{1,11},{3,13... | collective-permute-start | bytes 76808 | tf_op jit(solution)/shard_map/ppermute | solution.py:305
  100.4 5.8 %collective-permute-start.17 = (f32[20,320]{1,0:T(8,128)S(1)}, f32[20,320]{1,0:T(8,128)S(1)}, u32[]{:S(2)}, u32[]{:S(2)}) collective-permute-start(f32[20,320]{1,0:T(8,128)S(1)} %get-tuple-element.51), channel_id=1, source_target_pairs={{0,4},{2,6},{4,8},{6,10},{8,12},{10,14},{12,0},{14,2},{1,5},{3,7},... | collective-permute-start | bytes 76808 | tf_op jit(solution)/shard_map/ppermute | solution.py:305
  101.1 5.0 %collective-permute-start.18 = (f32[20,320]{1,0:T(8,128)S(1)}, f32[20,320]{1,0:T(8,128)S(1)}, u32[]{:S(2)}, u32[]{:S(2)}) collective-permute-start(f32[20,320]{1,0:T(8,128)S(1)} %get-tuple-element.52), channel_id=1, source_target_pairs={{0,12},{2,14},{4,0},{6,2},{8,4},{10,6},{12,8},{14,10},{1,13},{3,15... | collective-permute-start | bytes 76808 | tf_op jit(solution)/shard_map/ppermute | solution.py:305

commit v11 on v10

--- a/solution.py
+++ b/solution.py
@@ -246,7 +246,7 @@
     send_ref[...] = jnp.where(first, odd, even)
 
 
-def stack_kernel(place_ref, _, mine_ref, arrived_ref, *refs):
+def stack_kernel(place_ref, mine_ref, arrived_ref, *refs):
     outs, kept_ref = refs[:8], refs[8]
     first = place_ref[1] == 0
     mine, arrived = mine_ref[...], arrived_ref[...]
@@ -300,9 +300,9 @@
 
 
 def exchange_z(pieces):
-    far = (1, 7, 4, 3, 5, 2, 6)
+    order = (4, 1, 3, 5, 2, 6, 7)
     return [pieces[0]] + [
-        lax.ppermute(pieces[m], "z", [(z, (z + m) % 8) for z in range(8)]) for m in far
+        lax.ppermute(pieces[m], "z", [(z, (z + m) % 8) for z in range(8)]) for m in order
     ]
 
 
@@ -478,18 +478,19 @@
     mine, send = small(
         pair_kernel, (place, *moved), [(80, 320)] * 2, 1, (), (kernel,), "pair"
     )
-    data, first, final, own_mixing = spectrum(spread, mine)
+    data, first, final, own_mixing = spectrum(spread, kernel)
     forward = [(i, i + 1) for i in range(3)]
     backward = [(target, source) for source, target in forward]
     before = lax.ppermute(final, LAT, forward)
     beyond = lax.ppermute(first, LAT, backward)
     paired = to_core(send)
-    sent = filtered(own_mixing, data, before, beyond, kernel, (paired,))
-    result = across(sent)
     kept = (pltpu.VMEM((8, 24, 320), F32),)
     operands = (place, mine, paired)
-    stacked = small(stack_kernel, operands, [(20, 320)] * 8, 1, kept, (sent,), "stack")
-    grad_in, grad_out = small(last_kernel, exchange_z(stacked), [(20, 160)] * 2, name="last")
+    stacked = small(stack_kernel, operands, [(20, 320)] * 8, 1, kept, name="stack")
+    moved = exchange_z(stacked)
+    sent = filtered(own_mixing, data, before, beyond, kernel, moved[1:3])
+    result = across(sent)
+    grad_in, grad_out = small(last_kernel, moved, [(20, 160)] * 2, name="last")
     field = unpack(result).reshape(COLS, ROWS, width).transpose(1, 0, 2)
     return (field, grad_in, grad_out)
 

time: 109 us -> 112 us (1.028)
  the two profiles are of different devices: /device:TPU:1 before, /device:TPU:2 now
where the time goes in v11:
time: 112 us
  starting transfers between devices  52.5 us (47%)
  waiting for transfers between devices  26.7 us (24%)
  Pallas kernels  25.7 us (23%)
  local copies, waits for them, and re-layouts  6.21 us (6%)
    all_to_all x2, starting transfers between devices, across(): return lax.all_to_all(block, LON, split_axis=0, concat_axis=0, tiled=True)  23 us
    ppermute x7, starting transfers between devices, exchange_z(): lax.ppermute(pieces[m], 'z', [(z, (z + m) % 8) for z in range(8)])  17.3 us
    ppermute x7, waiting for transfers between devices, exchange_z(): lax.ppermute(pieces[m], 'z', [(z, (z + m) % 8) for z in range(8)])  12.4 us
    pallas_call x1, Pallas kernels, mlp(): pl.pallas_call(mlp_kernel, grid_spec=pltpu.PrefetchScalarGridSpec(num_sca...  12.1 us
    ppermute x6, starting transfers between devices, permute(): return lax.ppermute(value, AXES, pairs)  8.92 us
    ppermute x6, waiting for transfers between devices, permute(): return lax.ppermute(value, AXES, pairs)  8.39 us
    pallas_call x5, Pallas kernels, small(): pl.pallas_call(kernel, in_specs=[pl.BlockSpec(memory_space=pltpu.SMEM)] *...  5.77 us
    unnamed x26, local copies, waits for them, and re-layouts  5.53 us
  transfers between devices with their start and end apart: 21, of which 13 were waited for; matrix products, arithmetic and copies ran while one was open for 1% of the time, Pallas kernels for 7%

profile of v11, /device:TPU:2, one launch (start us, length us, event | category | flops | bytes accessed | tf_op | source)
XLA Modules:
  0.0 111.9 jit_solution(7578776622373317892)
XLA Ops:
  0.6 0.1 collective-permute-start
  0.7 0.5 collective-permute-start.1
  1.2 0.7 stack.28.place_ref
  1.9 0.9 collective-permute-done.act_other_ref
  2.8 0.7 collective-permute-done.1.cot_other_ref
  3.5 0.1 copy-done.11
  3.6 0.7 copy-done.12
  4.3 12.1 %mlp.1 = (f32[192,640]{1,0:T(8,128)}, f32[192,640]{1,0:T(8,128)}, f32[160,1280]{1,0:T(8,128)}, f32[160,1280]{1,0:T(8,128)}, f32[160,1280]{1,0:T(8,128)}, /*index=5*/f32[160,1280]{1,0:T(8,128)}) custom-call(s32[6]{0:T(128)} %stack.28.place_ref, f32[192,640]{1,0:T(8,128)} %bitcast.27, f32[192,640]{1,0:T(8,128)} %copy-done.11, f32[192,640]{1,0:T(8,128)} %bitcast.29, ...), custom_call_target="tpu_custom_call" | custom-call | flops 4718592000 | bytes 12000000 | tf_op jit(solution)/shard_map/mlp/pallas_call | solution.py:190
  16.4 1.5 %collective-permute-start.3 = (f32[160,1280]{1,0:T(8,128)}, f32[160,1280]{1,0:T(8,128)S(1)}, u32[]{:S(2)}, u32[]{:S(2)}) collective-permute-start(f32[160,1280]{1,0:T(8,128)} %get-tuple-element.32), channel_id=1, source_target_pairs={{0,16},{1,17},{2,18},{3,19},{4,20},{5,21},{6,22},{7,23},{8,24},{9,... | collective-permute-start | bytes 2457608 | tf_op jit(solution)/shard_map/ppermute | solution.py:288
  17.9 2.8 %collective-permute-start.4 = (f32[160,1280]{1,0:T(8,128)}, f32[160,1280]{1,0:T(8,128)S(1)}, u32[]{:S(2)}, u32[]{:S(2)}) collective-permute-start(f32[160,1280]{1,0:T(8,128)} %get-tuple-element.33), channel_id=1, source_target_pairs={{0,32},{1,33},{2,34},{3,35},{4,36},{5,37},{6,38},{7,39},{8,40},{9,... | collective-permute-start | bytes 2457608 | tf_op jit(solution)/shard_map/ppermute | solution.py:288
  20.7 0.4 collective-permute-start.5
  21.1 0.0 collective-permute-start.2
  21.1 2.1 %collective-permute-done.2.arrived_ref = f32[192,640]{1,0:T(8,128)S(1)} collective-permute-done((f32[192,640]{1,0:T(8,128)}, f32[192,640]{1,0:T(8,128)S(1)}, u32[]{:S(2)}, u32[]{:S(2)}) %collective-permute-start.2) | collective-permute-done | bytes 491552 | tf_op jit(solution)/shard_map/ppermute | solution.py:310
  23.2 0.0 copy-done.8
  23.2 0.0 copy-done.9
  23.2 1.0 copy-done.7
  24.2 2.0 %pack.1 = f32[64,16,128]{2,1,0:T(8,128)} custom-call(s32[6]{0:T(128)S(1)} %copy-done.8, f32[3,10]{1,0:T(4,128)S(1)} %bitcast.22, f32[192,640]{1,0:T(8,128)S(1)} %copy-done.7, f32[192,640]{1,0:T(8,128)S(1)} %collective-permute-done.2.arrived_ref), custom_call_target="tpu_custom_call" | custom-call | tf_op jit(solution)/shard_map/pack/pallas_call | solution.py:270
  26.3 13.3 %all-to-all-start = ((f32[64,16,128]{2,1,0:T(8,128)}), f32[64,16,128]{2,1,0:T(8,128)S(1)}, u32[]{:S(2)}, u32[]{:S(2)}) async-start(f32[64,16,128]{2,1,0:T(8,128)} %pack.1), calls=%async_computation | async-start | bytes 1048576 | tf_op jit(solution)/shard_map/all_to_all | solution.py:460
  39.6 0.0 collective-permute-done.3.refs_1_
  39.6 0.0 collective-permute-done.4.refs_2_
  39.7 1.2 %collective-permute-done.5.refs_3_ = f32[160,1280]{1,0:T(8,128)} collective-permute-done((f32[160,1280]{1,0:T(8,128)}, f32[160,1280]{1,0:T(8,128)}, u32[]{:S(2)}, u32[]{:S(2)}) %collective-permute-start.5) | collective-permute-done | bytes 819232 | tf_op jit(solution)/shard_map/ppermute | solution.py:288
  40.8 1.1 %copy-done.10 = f32[160,1280]{1,0:T(8,128)S(1)} copy-done((f32[160,1280]{1,0:T(8,128)S(1)}, f32[160,1280]{1,0:T(8,128)}, u32[]{:S(2)}) %copy-start.10) | copy-done | bytes 819224
  42.0 1.8 %swap.1 = (f32[80,640]{1,0:T(8,128)S(1)}, f32[80,640]{1,0:T(8,128)S(1)}, f32[80,640]{1,0:T(8,128)S(1)}, f32[80,640]{1,0:T(8,128)S(1)}) custom-call(s32[6]{0:T(128)S(1)} %copy-done.8, f32[160,1280]{1,0:T(8,128)S(1)} %copy-done.10, f32[160,1280]{1,0:T(8,128)S(1)} %collective-permute-done.3.refs_1_, f32[160,1280]{1,0:T(8,128)S(1)} %collective-permute-done.4.refs_2_, ...), custom_call_target="tpu_custom_call" | custom-call | flops 10000000000 | bytes 4000000 | tf_op jit(solution)/shard_map/swap/pallas_call | solution.py:270
  43.7 2.9 %collective-permute-start.8 = (f32[80,640]{1,0:T(8,128)S(1)}, f32[80,640]{1,0:T(8,128)S(1)}, u32[]{:S(2)}, u32[]{:S(2)}) collective-permute-start(f32[80,640]{1,0:T(8,128)S(1)} %get-tuple-element.40), channel_id=1, source_target_pairs={{0,1},{1,0},{2,3},{3,2},{4,5},{5,4},{6,7},{7,6},{8,9},{9,8},{10,11... | collective-permute-start | bytes 614408 | tf_op jit(solution)/shard_map/ppermute | solution.py:288
  46.6 0.7 collective-permute-start.9
  47.3 0.6 collective-permute-start.10
  47.9 0.0 copy-done.2
  47.9 0.0 copy-done.3
  47.9 1.4 %kernel_spectrum.1._.kernel_ref = f32[336,768]{1,0:T(8,128)S(1)} custom-call(f32[336,768]{1,0:T(8,128)S(1)} %bitcast.21, bf16[768,768]{1,0:T(8,128)(2,1)S(1)} %copy-done.3, bf16[768,768]{1,0:T(8,128)(2,1)S(1)} %copy-done.2, f32[80,640]{1,0:T(8,128)S(1)} %get-tuple-element.35._.refs_0_), custom_call_target="tpu_custom_call" | custom-call | flops 1189085184 | bytes 5000000 | tf_op jit(solution)/shard_map/kernel_spectrum/pallas_call | solution.py:358
  49.3 3.2 %collective-permute-done.8.refs_1_ = f32[80,640]{1,0:T(8,128)S(1)} collective-permute-done((f32[80,640]{1,0:T(8,128)S(1)}, f32[80,640]{1,0:T(8,128)S(1)}, u32[]{:S(2)}, u32[]{:S(2)}) %collective-permute-start.8) | collective-permute-done | bytes 204832 | tf_op jit(solution)/shard_map/ppermute | solution.py:288
  52.5 3.2 %collective-permute-done.9.refs_2_ = f32[80,640]{1,0:T(8,128)S(1)} collective-permute-done((f32[80,640]{1,0:T(8,128)S(1)}, f32[80,640]{1,0:T(8,128)S(1)}, u32[]{:S(2)}, u32[]{:S(2)}) %collective-permute-start.9) | collective-permute-done | bytes 204832 | tf_op jit(solution)/shard_map/ppermute | solution.py:288
  55.7 0.9 collective-permute-done.10.refs_3_
  56.5 0.7 pair.1
  57.2 0.0 copy-start
  57.2 0.1 collective-permute-start.11
  57.3 1.2 %all-to-all-done.block_ref = f32[64,16,128]{2,1,0:T(8,128)S(1)} async-done(((f32[64,16,128]{2,1,0:T(8,128)}), f32[64,16,128]{2,1,0:T(8,128)S(1)}, u32[]{:S(2)}, u32[]{:S(2)}) %all-to-all-start) | async-done | bytes 524320 | tf_op jit(solution)/shard_map/all_to_all | solution.py:460
  58.5 1.3 %copy-done.4 = bf16[768,768]{1,0:T(8,128)(2,1)S(1)} copy-done((bf16[768,768]{1,0:T(8,128)(2,1)S(1)}, bf16[768,768]{1,0:T(8,128)(2,1)}, u32[]{:S(2)}) %copy-start.4) | copy-done | bytes 1179672
  59.8 1.3 %copy-done.5 = bf16[768,768]{1,0:T(8,128)(2,1)S(1)} copy-done((bf16[768,768]{1,0:T(8,128)(2,1)S(1)}, bf16[768,768]{1,0:T(8,128)(2,1)}, u32[]{:S(2)}) %copy-start.5) | copy-done | bytes 1179672
  61.0 1.0 spectrum.1
  62.1 1.3 %collective-permute-start.6 = (f32[30,768]{1,0:T(8,128)S(1)}, f32[30,768]{1,0:T(8,128)S(1)}, u32[]{:S(2)}, u32[]{:S(2)}) collective-permute-start(f32[30,768]{1,0:T(8,128)S(1)} %get-tuple-element.38), channel_id=1, source_target_pairs={{0,64},{64,128},{128,192},{1,65},{65,129},{129,193},{2,66},{66,130... | collective-permute-start | bytes 276488 | tf_op jit(solution)/shard_map/ppermute | solution.py:484
  63.4 1.3 %collective-permute-start.7 = (f32[30,768]{1,0:T(8,128)S(1)}, f32[30,768]{1,0:T(8,128)S(1)}, u32[]{:S(2)}, u32[]{:S(2)}) collective-permute-start(f32[30,768]{1,0:T(8,128)S(1)} %get-tuple-element.39), channel_id=1, source_target_pairs={{64,0},{128,64},{192,128},{65,1},{129,65},{193,129},{66,2},{130,66... | collective-permute-start | bytes 276488 | tf_op jit(solution)/shard_map/ppermute | solution.py:485
  64.7 0.0 collective-permute-done.11.arrived_ref
  64.7 0.6 stack.29
  65.3 5.9 %collective-permute-start.12 = (f32[20,320]{1,0:T(8,128)S(1)}, f32[20,320]{1,0:T(8,128)S(1)}, u32[]{:S(2)}, u32[]{:S(2)}) collective-permute-start(f32[20,320]{1,0:T(8,128)S(1)} %get-tuple-element.45), channel_id=1, source_target_pairs={{0,8},{2,10},{4,12},{6,14},{8,0},{10,2},{12,4},{14,6},{1,9},{3,11}... | collective-permute-start | bytes 76808 | tf_op jit(solution)/shard_map/ppermute | solution.py:305
  71.2 1.2 %collective-permute-start.13 = (f32[20,320]{1,0:T(8,128)S(1)}, f32[20,320]{1,0:T(8,128)S(1)}, u32[]{:S(2)}, u32[]{:S(2)}) collective-permute-start(f32[20,320]{1,0:T(8,128)S(1)} %get-tuple-element.46), channel_id=1, source_target_pairs={{0,2},{2,4},{4,6},{6,8},{8,10},{10,12},{12,14},{14,0},{1,3},{3,5},... | collective-permute-start | bytes 76808 | tf_op jit(solution)/shard_map/ppermute | solution.py:305
  72.4 0.9 collective-permute-done.12.refs_0_.refs_1_
  73.3 3.1 %collective-permute-done.13.refs_1_.refs_2_ = f32[20,320]{1,0:T(8,128)S(1)} collective-permute-done((f32[20,320]{1,0:T(8,128)S(1)}, f32[20,320]{1,0:T(8,128)S(1)}, u32[]{:S(2)}, u32[]{:S(2)}) %collective-permute-start.13) | collective-permute-done | bytes 25632 | tf_op jit(solution)/shard_map/ppermute | solution.py:305
  76.4 0.0 collective-permute-done.6.before_ref
  76.4 0.0 collective-permute-done.7.after_ref
  76.4 4.2 %filter.1 = f32[64,16,128]{2,1,0:T(8,128)} custom-call(f32[1,128]{1,0:T(1,128)S(1)} %get-tuple-element.36.mixing_ref, f32[160,768]{1,0:T(8,128)S(1)} %get-tuple-element.37.data_ref, f32[30,768]{1,0:T(8,128)S(1)} %collective-permute-done.6.before_ref, f32[30,768]{1,0:T(8,128)S(1)} %collective-permute-done.7.after_ref, ...), custom_call_target="tpu_custom_call" | custom-call | flops 566231040 | bytes 5000000 | tf_op jit(solution)/shard_map/filter/pallas_call | solution.py:416
  80.5 9.7 %all-to-all-start.1 = ((f32[64,16,128]{2,1,0:T(8,128)}), f32[64,16,128]{2,1,0:T(8,128)S(1)}, u32[]{:S(2)}, u32[]{:S(2)}) async-start(f32[64,16,128]{2,1,0:T(8,128)} %filter.1), calls=%async_computation.1 | async-start | bytes 1048576 | tf_op jit(solution)/shard_map/all_to_all | solution.py:460
  90.3 3.4 %collective-permute-start.14 = (f32[20,320]{1,0:T(8,128)S(1)}, f32[20,320]{1,0:T(8,128)S(1)}, u32[]{:S(2)}, u32[]{:S(2)}) collective-permute-start(f32[20,320]{1,0:T(8,128)S(1)} %get-tuple-element.48), channel_id=1, source_target_pairs={{0,6},{2,8},{4,10},{6,12},{8,14},{10,0},{12,2},{14,4},{1,7},{3,9},... | collective-permute-start | bytes 76808 | tf_op jit(solution)/shard_map/ppermute | solution.py:305
  93.6 1.8 %collective-permute-start.15 = (f32[20,320]{1,0:T(8,128)S(1)}, f32[20,320]{1,0:T(8,128)S(1)}, u32[]{:S(2)}, u32[]{:S(2)}) collective-permute-start(f32[20,320]{1,0:T(8,128)S(1)} %get-tuple-element.49), channel_id=1, source_target_pairs={{0,10},{2,12},{4,14},{6,0},{8,2},{10,4},{12,6},{14,8},{1,11},{3,13... | collective-permute-start | bytes 76808 | tf_op jit(solution)/shard_map/ppermute | solution.py:305
  95.4 2.4 %collective-permute-start.16 = (f32[20,320]{1,0:T(8,128)S(1)}, f32[20,320]{1,0:T(8,128)S(1)}, u32[]{:S(2)}, u32[]{:S(2)}) collective-permute-start(f32[20,320]{1,0:T(8,128)S(1)} %get-tuple-element.50), channel_id=1, source_target_pairs={{0,4},{2,6},{4,8},{6,10},{8,12},{10,14},{12,0},{14,2},{1,5},{3,7},... | collective-permute-start | bytes 76808 | tf_op jit(solution)/shard_map/ppermute | solution.py:305
  97.7 1.8 %collective-permute-start.17 = (f32[20,320]{1,0:T(8,128)S(1)}, f32[20,320]{1,0:T(8,128)S(1)}, u32[]{:S(2)}, u32[]{:S(2)}) collective-permute-start(f32[20,320]{1,0:T(8,128)S(1)} %get-tuple-element.51), channel_id=1, source_target_pairs={{0,12},{2,14},{4,0},{6,2},{8,4},{10,6},{12,8},{14,10},{1,13},{3,15... | collective-permute-start | bytes 76808 | tf_op jit(solution)/shard_map/ppermute | solution.py:305
  99.5 1.0 collective-permute-start.18
  100.5 7.5 %collective-permute-done.14.refs_3_ = f32[20,320]{1,0:T(8,128)S(1)} collective-permute-done((f32[20,320]{1,0:T(8,128)S(1)}, f32[20,320]{1,0:T(8,128)S(1)}, u32[]{:S(2)}, u32[]{:S(2)}) %collective-permute-start.14) | collective-permute-done | bytes 25632 | tf_op jit(solution)/shard_map/ppermute | solution.py:305
  107.9 0.0 collective-permute-done.15.refs_4_
  107.9 0.9 collective-permute-done.16.refs_5_
  108.8 0.0 collective-permute-done.17.refs_6_
  108.8 0.0 collective-permute-done.18.refs_7_
  108.9 0.7 last.1
  109.5 1.1 all-to-all-done.1.block_ref
  110.6 1.3 %unpack.1 = f32[192,640]{1,0:T(8,128)} custom-call(f32[64,16,128]{2,1,0:T(8,128)S(1)} %all-to-all-done.1.block_ref), custom_call_target="tpu_custom_call" | custom-call | tf_op jit(solution)/shard_map/unpack/pallas_call | solution.py:449
  (15 shorter events, 0.0 us)
Async XLA Ops:
  0.6 2.2 %collective-permute-start = (f32[192,640]{1,0:T(8,128)}, f32[192,640]{1,0:T(8,128)S(1)}, u32[]{:S(2)}, u32[]{:S(2)}) collective-permute-start(f32[192,640]{1,0:T(8,128)} %bitcast.26), channel_id=1, source_target_pairs={{0,64},{64,0},{1,65},{65,1},{2,66},{66,2},{3,67},{67,3},{4,68},{68... | collective-permute-start | bytes 1474568 | tf_op jit(solution)/shard_map/ppermute | solution.py:310
  0.7 2.8 %collective-permute-start.1 = (f32[192,640]{1,0:T(8,128)}, f32[192,640]{1,0:T(8,128)S(1)}, u32[]{:S(2)}, u32[]{:S(2)}) collective-permute-start(f32[192,640]{1,0:T(8,128)} %bitcast.28), channel_id=1, source_target_pairs={{0,64},{64,0},{1,65},{65,1},{2,66},{66,2},{3,67},{67,3},{4,68},{68... | collective-permute-start | bytes 1474568 | tf_op jit(solution)/shard_map/ppermute | solution.py:310
  2.8 0.8 copy-start.11
  3.5 0.8 copy-start.12
  4.3 18.9 %copy-start.8 = (s32[6]{0:T(128)S(1)}, s32[6]{0:T(128)}, u32[]{:S(2)}) copy-start(s32[6]{0:T(128)} %stack.28.place_ref) | copy-start | bytes 76
  4.3 18.9 %copy-start.9 = (f32[10,3]{0,1:T(4,128)S(1)}, f32[10,3]{0,1:T(4,128)}, u32[]{:S(2)}) copy-start(f32[10,3]{0,1:T(4,128)} %param.17) | copy-start | bytes 364
  16.4 23.3 %collective-permute-start.3 = (f32[160,1280]{1,0:T(8,128)}, f32[160,1280]{1,0:T(8,128)S(1)}, u32[]{:S(2)}, u32[]{:S(2)}) collective-permute-start(f32[160,1280]{1,0:T(8,128)} %get-tuple-element.32), channel_id=1, source_target_pairs={{0,16},{1,17},{2,18},{3,19},{4,20},{5,21},{6,22},{7,23},{8,24},{9,... | collective-permute-start | bytes 2457608 | tf_op jit(solution)/shard_map/ppermute | solution.py:288
  17.9 21.8 %collective-permute-start.4 = (f32[160,1280]{1,0:T(8,128)}, f32[160,1280]{1,0:T(8,128)S(1)}, u32[]{:S(2)}, u32[]{:S(2)}) collective-permute-start(f32[160,1280]{1,0:T(8,128)} %get-tuple-element.33), channel_id=1, source_target_pairs={{0,32},{1,33},{2,34},{3,35},{4,36},{5,37},{6,38},{7,39},{8,40},{9,... | collective-permute-start | bytes 2457608 | tf_op jit(solution)/shard_map/ppermute | solution.py:288
  20.7 20.1 %collective-permute-start.5 = (f32[160,1280]{1,0:T(8,128)}, f32[160,1280]{1,0:T(8,128)}, u32[]{:S(2)}, u32[]{:S(2)}) collective-permute-start(f32[160,1280]{1,0:T(8,128)} %get-tuple-element.34), channel_id=1, source_target_pairs={{0,48},{1,49},{2,50},{3,51},{4,52},{5,53},{6,54},{7,55},{8,56},{9,... | collective-permute-start | bytes 2457608 | tf_op jit(solution)/shard_map/ppermute | solution.py:288
  21.1 2.1 %collective-permute-start.2 = (f32[192,640]{1,0:T(8,128)}, f32[192,640]{1,0:T(8,128)S(1)}, u32[]{:S(2)}, u32[]{:S(2)}) collective-permute-start(f32[192,640]{1,0:T(8,128)} %get-tuple-element.30), channel_id=1, source_target_pairs={{0,64},{64,0},{1,65},{65,1},{2,66},{66,2},{3,67},{67,3},{4,68},{68... | collective-permute-start | bytes 1474568 | tf_op jit(solution)/shard_map/ppermute | solution.py:310
  23.2 1.0 copy-start.7
  26.3 32.2 %all-to-all-start = ((f32[64,16,128]{2,1,0:T(8,128)}), f32[64,16,128]{2,1,0:T(8,128)S(1)}, u32[]{:S(2)}, u32[]{:S(2)}) async-start(f32[64,16,128]{2,1,0:T(8,128)} %pack.1), calls=%async_computation | async-start | bytes 1048576 | tf_op jit(solution)/shard_map/all_to_all | solution.py:460
  40.8 1.1 %copy-start.10 = (f32[160,1280]{1,0:T(8,128)S(1)}, f32[160,1280]{1,0:T(8,128)}, u32[]{:S(2)}) copy-start(f32[160,1280]{1,0:T(8,128)} %get-tuple-element.31.refs_0_) | copy-start | bytes 2457604
  42.0 6.0 %copy-start.2 = (bf16[768,768]{1,0:T(8,128)(2,1)S(1)}, bf16[768,768]{1,0:T(8,128)(2,1)}, u32[]{:S(2)}) copy-start(bf16[768,768]{1,0:T(8,128)(2,1)} %constant.38.clone.low_ref) | copy-start | bytes 3538948
  42.0 6.0 %copy-start.3 = (bf16[768,768]{1,0:T(8,128)(2,1)S(1)}, bf16[768,768]{1,0:T(8,128)(2,1)}, u32[]{:S(2)}) copy-start(bf16[768,768]{1,0:T(8,128)(2,1)} %constant.37.clone.top_ref) | copy-start | bytes 3538948
  42.0 6.0 %copy-start.6 = (f32[3,16,7,768]{3,1,2,0:T(8,128)S(1)}, f32[3,16,7,768]{3,1,2,0:T(8,128)}, u32[]{:S(2)}) copy-start(f32[3,16,7,768]{3,1,2,0:T(8,128)} %param.16) | copy-start | bytes 3096580
  43.7 8.8 %collective-permute-start.8 = (f32[80,640]{1,0:T(8,128)S(1)}, f32[80,640]{1,0:T(8,128)S(1)}, u32[]{:S(2)}, u32[]{:S(2)}) collective-permute-start(f32[80,640]{1,0:T(8,128)S(1)} %get-tuple-element.40), channel_id=1, source_target_pairs={{0,1},{1,0},{2,3},{3,2},{4,5},{5,4},{6,7},{7,6},{8,9},{9,8},{10,11... | collective-permute-start | bytes 614408 | tf_op jit(solution)/shard_map/ppermute | solution.py:288
  46.6 9.0 %collective-permute-start.9 = (f32[80,640]{1,0:T(8,128)S(1)}, f32[80,640]{1,0:T(8,128)S(1)}, u32[]{:S(2)}, u32[]{:S(2)}) collective-permute-start(f32[80,640]{1,0:T(8,128)S(1)} %get-tuple-element.41), channel_id=1, source_target_pairs={{0,128},{1,129},{2,130},{3,131},{4,132},{5,133},{6,134},{7,135},{8... | collective-permute-start | bytes 614408 | tf_op jit(solution)/shard_map/ppermute | solution.py:288
  47.3 9.2 %collective-permute-start.10 = (f32[80,640]{1,0:T(8,128)S(1)}, f32[80,640]{1,0:T(8,128)S(1)}, u32[]{:S(2)}, u32[]{:S(2)}) collective-permute-start(f32[80,640]{1,0:T(8,128)S(1)} %get-tuple-element.42), channel_id=1, source_target_pairs={{0,129},{1,128},{2,131},{3,130},{4,133},{5,132},{6,135},{7,134},{8... | collective-permute-start | bytes 614408 | tf_op jit(solution)/shard_map/ppermute | solution.py:288
  57.2 19.2 %copy-start = (bf16[768,768]{1,0:T(8,128)(2,1)S(1)}, bf16[768,768]{1,0:T(8,128)(2,1)}, u32[]{:S(2)}) copy-start(bf16[768,768]{1,0:T(8,128)(2,1)} %constant.42.clone.low_ref) | copy-start | bytes 3538948
  57.2 7.4 %collective-permute-start.11 = (f32[80,320]{1,0:T(8,128)S(1)}, f32[80,320]{1,0:T(8,128)S(1)}, u32[]{:S(2)}, u32[]{:S(2)}) collective-permute-start(f32[80,320]{1,0:T(8,128)S(1)} %get-tuple-element.44), channel_id=1, source_target_pairs={{0,64},{64,0},{1,65},{65,1},{2,66},{66,2},{3,67},{67,3},{4,68},{68... | collective-permute-start | bytes 307208 | tf_op jit(solution)/shard_map/ppermute | solution.py:310
  58.5 1.3 %copy-start.4 = (bf16[768,768]{1,0:T(8,128)(2,1)S(1)}, bf16[768,768]{1,0:T(8,128)(2,1)}, u32[]{:S(2)}) copy-start(bf16[768,768]{1,0:T(8,128)(2,1)} %constant.40.clone.low_ref) | copy-start | bytes 3538948
  59.8 1.3 %copy-start.5 = (bf16[768,768]{1,0:T(8,128)(2,1)S(1)}, bf16[768,768]{1,0:T(8,128)(2,1)}, u32[]{:S(2)}) copy-start(bf16[768,768]{1,0:T(8,128)(2,1)} %constant.39.clone.top_ref) | copy-start | bytes 3538948
  61.0 15.3 %copy-start.1 = (bf16[768,768]{1,0:T(8,128)(2,1)S(1)}, bf16[768,768]{1,0:T(8,128)(2,1)}, u32[]{:S(2)}) copy-start(bf16[768,768]{1,0:T(8,128)(2,1)} %constant.41.clone.top_ref) | copy-start | bytes 3538948
  62.1 14.3 %collective-permute-start.6 = (f32[30,768]{1,0:T(8,128)S(1)}, f32[30,768]{1,0:T(8,128)S(1)}, u32[]{:S(2)}, u32[]{:S(2)}) collective-permute-start(f32[30,768]{1,0:T(8,128)S(1)} %get-tuple-element.38), channel_id=1, source_target_pairs={{0,64},{64,128},{128,192},{1,65},{65,129},{129,193},{2,66},{66,130... | collective-permute-start | bytes 276488 | tf_op jit(solution)/shard_map/ppermute | solution.py:484
  63.4 13.0 %collective-permute-start.7 = (f32[30,768]{1,0:T(8,128)S(1)}, f32[30,768]{1,0:T(8,128)S(1)}, u32[]{:S(2)}, u32[]{:S(2)}) collective-permute-start(f32[30,768]{1,0:T(8,128)S(1)} %get-tuple-element.39), channel_id=1, source_target_pairs={{64,0},{128,64},{192,128},{65,1},{129,65},{193,129},{66,2},{130,66... | collective-permute-start | bytes 276488 | tf_op jit(solution)/shard_map/ppermute | solution.py:485
  65.3 8.0 %collective-permute-start.12 = (f32[20,320]{1,0:T(8,128)S(1)}, f32[20,320]{1,0:T(8,128)S(1)}, u32[]{:S(2)}, u32[]{:S(2)}) collective-permute-start(f32[20,320]{1,0:T(8,128)S(1)} %get-tuple-element.45), channel_id=1, source_target_pairs={{0,8},{2,10},{4,12},{6,14},{8,0},{10,2},{12,4},{14,6},{1,9},{3,11}... | collective-permute-start | bytes 76808 | tf_op jit(solution)/shard_map/ppermute | solution.py:305
  71.2 5.2 %collective-permute-start.13 = (f32[20,320]{1,0:T(8,128)S(1)}, f32[20,320]{1,0:T(8,128)S(1)}, u32[]{:S(2)}, u32[]{:S(2)}) collective-permute-start(f32[20,320]{1,0:T(8,128)S(1)} %get-tuple-element.46), channel_id=1, source_target_pairs={{0,2},{2,4},{4,6},{6,8},{8,10},{10,12},{12,14},{14,0},{1,3},{3,5},... | collective-permute-start | bytes 76808 | tf_op jit(solution)/shard_map/ppermute | solution.py:305
  80.5 30.1 %all-to-all-start.1 = ((f32[64,16,128]{2,1,0:T(8,128)}), f32[64,16,128]{2,1,0:T(8,128)S(1)}, u32[]{:S(2)}, u32[]{:S(2)}) async-start(f32[64,16,128]{2,1,0:T(8,128)} %filter.1), calls=%async_computation.1 | async-start | bytes 1048576 | tf_op jit(solution)/shard_map/all_to_all | solution.py:460
  90.3 17.7 %collective-permute-start.14 = (f32[20,320]{1,0:T(8,128)S(1)}, f32[20,320]{1,0:T(8,128)S(1)}, u32[]{:S(2)}, u32[]{:S(2)}) collective-permute-start(f32[20,320]{1,0:T(8,128)S(1)} %get-tuple-element.48), channel_id=1, source_target_pairs={{0,6},{2,8},{4,10},{6,12},{8,14},{10,0},{12,2},{14,4},{1,7},{3,9},... | collective-permute-start | bytes 76808 | tf_op jit(solution)/shard_map/ppermute | solution.py:305
  93.6 14.3 %collective-permute-start.15 = (f32[20,320]{1,0:T(8,128)S(1)}, f32[20,320]{1,0:T(8,128)S(1)}, u32[]{:S(2)}, u32[]{:S(2)}) collective-permute-start(f32[20,320]{1,0:T(8,128)S(1)} %get-tuple-element.49), channel_id=1, source_target_pairs={{0,10},{2,12},{4,14},{6,0},{8,2},{10,4},{12,6},{14,8},{1,11},{3,13... | collective-permute-start | bytes 76808 | tf_op jit(solution)/shard_map/ppermute | solution.py:305
  95.4 13.5 %collective-permute-start.16 = (f32[20,320]{1,0:T(8,128)S(1)}, f32[20,320]{1,0:T(8,128)S(1)}, u32[]{:S(2)}, u32[]{:S(2)}) collective-permute-start(f32[20,320]{1,0:T(8,128)S(1)} %get-tuple-element.50), channel_id=1, source_target_pairs={{0,4},{2,6},{4,8},{6,10},{8,12},{10,14},{12,0},{14,2},{1,5},{3,7},... | collective-permute-start | bytes 76808 | tf_op jit(solution)/shard_map/ppermute | solution.py:305
  97.7 11.1 %collective-permute-start.17 = (f32[20,320]{1,0:T(8,128)S(1)}, f32[20,320]{1,0:T(8,128)S(1)}, u32[]{:S(2)}, u32[]{:S(2)}) collective-permute-start(f32[20,320]{1,0:T(8,128)S(1)} %get-tuple-element.51), channel_id=1, source_target_pairs={{0,12},{2,14},{4,0},{6,2},{8,4},{10,6},{12,8},{14,10},{1,13},{3,15... | collective-permute-start | bytes 76808 | tf_op jit(solution)/shard_map/ppermute | solution.py:305
  99.5 9.3 %collective-permute-start.18 = (f32[20,320]{1,0:T(8,128)S(1)}, f32[20,320]{1,0:T(8,128)S(1)}, u32[]{:S(2)}, u32[]{:S(2)}) collective-permute-start(f32[20,320]{1,0:T(8,128)S(1)} %get-tuple-element.52), channel_id=1, source_target_pairs={{0,14},{2,0},{4,2},{6,4},{8,6},{10,8},{12,10},{14,12},{1,15},{3,1}... | collective-permute-start | bytes 76808 | tf_op jit(solution)/shard_map/ppermute | solution.py:305

commit v12 on v10

--- a/solution.py
+++ b/solution.py
@@ -311,7 +311,7 @@
 
 
 def spectrum_kernel(
-    block_ref, top_ref, low_ref, _, out_ref, first_ref, final_ref, mixing_ref, flat_ref
+    place_ref, block_ref, top_ref, low_ref, _, out_ref, near_ref, cross_ref, mixing_ref, flat_ref
 ):
     for p in range(COLS // 2):
         pair = jnp.concatenate([block_ref[:, 2 * p, :], block_ref[:, 2 * p + 1, :]], axis=0)
@@ -322,17 +322,20 @@
     result = dot3(split(flat_ref[...]), (top_ref[...], low_ref[...]), ((1,), (0,)))
     out_ref[...] = result
     mixing_ref[...] = jnp.sum(block_ref[:, 15, :], axis=0, keepdims=True)
+    even = place_ref[1] == 0
     for r in range(OWN):
-        first_ref[3 * r : 3 * r + 3, :] = result[ROWS * r : ROWS * r + 3, :]
-        final_ref[3 * r : 3 * r + 3, :] = result[ROWS * r + 13 : ROWS * r + 16, :]
-
-
-def spectrum(block, earlier):
+        first = result[ROWS * r : ROWS * r + 3, :]
+        final = result[ROWS * r + 13 : ROWS * r + 16, :]
+        near_ref[3 * r : 3 * r + 3, :] = jnp.where(even, final, first)
+        cross_ref[3 * r : 3 * r + 3, :] = jnp.where(even, first, final)
+
+
+def spectrum(place, block, earlier):
     top, low = forward_table(shard_order())
     rows = OWN * ROWS
     return pl.pallas_call(
         spectrum_kernel,
-        in_specs=whole(3) + EARLIER,
+        in_specs=[pl.BlockSpec(memory_space=pltpu.SMEM)] + whole(3) + EARLIER,
         out_specs=whole(4),
         out_shape=[
             jax.ShapeDtypeStruct((rows, CIRCLE), F32),
@@ -344,7 +347,7 @@
         compiler_params=params(24),
         cost_estimate=cost(6 * rows * CIRCLE * CIRCLE, 4_000_000),
         name="spectrum",
-    )(block, jnp.asarray(top), jnp.asarray(low), earlier)
+    )(place, block, jnp.asarray(top), jnp.asarray(low), earlier)
 
 
 def kernel_spectrum_kernel(kernel_ref, top_ref, low_ref, _, out_ref):
@@ -367,13 +370,15 @@
 
 
 def filter_kernel(
-    mixing_ref, data_ref, before_ref, after_ref, kernel_ref, top_ref, low_ref, *refs
+    place_ref, mixing_ref, data_ref, near_ref, cross_ref, kernel_ref, top_ref, low_ref, *refs
 ):
     out_ref, rows_ref, sum_ref = refs[-3:]
+    even = place_ref[1] == 0
     for r in range(OWN):
-        rows_ref[r, 0:3, :] = before_ref[3 * r : 3 * r + 3, :]
+        near, cross = near_ref[3 * r : 3 * r + 3, :], cross_ref[3 * r : 3 * r + 3, :]
+        rows_ref[r, 0:3, :] = jnp.where(even, cross, near)
         rows_ref[r, 3 : 3 + ROWS, :] = data_ref[ROWS * r : ROWS * (r + 1), :]
-        rows_ref[r, 3 + ROWS : 6 + ROWS, :] = after_ref[3 * r : 3 * r + 3, :]
+        rows_ref[r, 3 + ROWS : 6 + ROWS, :] = jnp.where(even, near, cross)
     lane = lax.broadcasted_iota(jnp.int32, (ROWS, HALF), 1)
     ends = lane == 0
 
@@ -411,11 +416,11 @@
     out_ref[:, 15, :] = jnp.zeros((SHARDS, 128), F32)
 
 
-def filtered(mixing, data, before, beyond, kernel, earlier):
+def filtered(place, mixing, data, near, cross, kernel, earlier):
     top, low = backward_table(shard_order())
     return pl.pallas_call(
         filter_kernel,
-        in_specs=[pl.BlockSpec(memory_space=pltpu.SMEM)] + whole(6) + EARLIER * len(earlier),
+        in_specs=[pl.BlockSpec(memory_space=pltpu.SMEM)] * 2 + whole(6) + EARLIER,
         out_specs=whole(1)[0],
         out_shape=jax.ShapeDtypeStruct((SHARDS, 16, 128), F32),
         scratch_shapes=[
@@ -425,7 +430,7 @@
         compiler_params=params(32),
         cost_estimate=cost(6 * OWN * ROWS * CIRCLE * CIRCLE, 5_000_000),
         name="filter",
-    )(mixing, data, before, beyond, kernel, jnp.asarray(top), jnp.asarray(low), *earlier)
+    )(place, mixing, data, near, cross, kernel, jnp.asarray(top), jnp.asarray(low), earlier)
 
 
 def unpack_kernel(block_ref, out_ref):
@@ -475,16 +480,12 @@
     swapped = small(swap_kernel, (place, *moved), [(80, 640)] * 4, 1, kept, (), "swap", 10**10)
     kernel = kernel_spectrum(kernels, swapped[0])
     moved = exchange(swapped, "yx")
-    mine, send = small(
-        pair_kernel, (place, *moved), [(80, 320)] * 2, 1, (), (kernel,), "pair"
-    )
-    data, first, final, own_mixing = spectrum(spread, mine)
-    forward = [(i, i + 1) for i in range(3)]
-    backward = [(target, source) for source, target in forward]
-    before = lax.ppermute(final, LAT, forward)
-    beyond = lax.ppermute(first, LAT, backward)
+    data, near, cross, own_mixing = spectrum(place, spread, kernel)
+    near = to_core(near)
+    cross = lax.ppermute(cross, LAT, [(1, 2), (2, 1)])
+    mine, send = small(pair_kernel, (place, *moved), [(80, 320)] * 2, 1, (), (data,), "pair")
     paired = to_core(send)
-    sent = filtered(own_mixing, data, before, beyond, kernel, (paired,))
+    sent = filtered(place, own_mixing, data, near, cross, kernel, paired)
     result = across(sent)
     kept = (pltpu.VMEM((8, 24, 320), F32),)
     operands = (place, mine, paired)

time: 109 us -> 104 us (0.954)
  starting transfers between devices: 56.6 us -> 51.1 us
  waiting for transfers between devices: 19.9 us -> 16.8 us
  local copies, waits for them, and re-layouts: 4.95 us -> 7.45 us
    ppermute x6, waiting for transfers between devices: 8.26 us -> 0.86 us  [permute(): return lax.ppermute(value, AXES, pairs)]
    all_to_all x2, waiting for transfers between devices: 0.01 us -> 6.78 us  [across(): return lax.all_to_all(block, LON, split_axis=0, concat_axis=0, tiled=True)]
    all_to_all x2, starting transfers between devices: 22.6 us -> 19.2 us  [across(): return lax.all_to_all(block, LON, split_axis=0, concat_axis=0, tiled=True)]
    ppermute x2 -> x1, starting transfers between devices: 5.22 us -> 2.59 us  [per_device(): cross = lax.ppermute(cross, LAT, [(1, 2), (2, 1)])]
    unnamed x26 -> x34, local copies, waits for them, and re-layouts: 4.27 us -> 6.88 us
    ppermute x7, waiting for transfers between devices: 4.27 us -> 2.46 us  [exchange_z(): lax.ppermute(pieces[m], 'z', [(z, (z + m) % 8) for z in range(8)])]
    ppermute x2 -> x1, waiting for transfers between devices: 3.99 us -> 3.31 us  [per_device(): cross = lax.ppermute(cross, LAT, [(1, 2), (2, 1)])]
    ppermute x4 -> x5, starting transfers between devices: 6.03 us -> 6.65 us  [to_core(): return lax.ppermute(value, 'co', [(0, 1), (1, 0)])]
  transfers between devices with their start and end apart: 21 -> 21, of which waited for: 10 -> 9; matrix products, arithmetic and copies ran while one was open for 1% -> 1% of each run, Pallas kernels for 7% -> 8%
where the time goes in v12:
time: 104 us; the launch traced here: 103 us
  starting transfers between devices  51.1 us (49%)
  Pallas kernels  26.6 us (26%)
  waiting for transfers between devices  16.8 us (16%)
  local copies, waits for them, and re-layouts  7.45 us (7%)
    all_to_all x2, starting transfers between devices, across(): return lax.all_to_all(block, LON, split_axis=0, concat_axis=0, tiled=True)  19.2 us
    ppermute x7, starting transfers between devices, exchange_z(): lax.ppermute(pieces[m], 'z', [(z, (z + m) % 8) for z in range(8)])  15.7 us
    pallas_call x1, Pallas kernels, mlp(): pl.pallas_call(mlp_kernel, grid_spec=pltpu.PrefetchScalarGridSpec(num_sca...  12.5 us
    ppermute x6, starting transfers between devices, permute(): return lax.ppermute(value, AXES, pairs)  6.93 us
    unnamed x34, local copies, waits for them, and re-layouts  6.88 us
    all_to_all x2, waiting for transfers between devices, across(): return lax.all_to_all(block, LON, split_axis=0, concat_axis=0, tiled=True)  6.78 us
    ppermute x5, starting transfers between devices, to_core(): return lax.ppermute(value, 'co', [(0, 1), (1, 0)])  6.65 us
    pallas_call x5, Pallas kernels, small(): pl.pallas_call(kernel, in_specs=[pl.BlockSpec(memory_space=pltpu.SMEM)] *...  5.65 us
  transfers between devices with their start and end apart: 21, of which 9 were waited for; matrix products, arithmetic and copies ran while one was open for 1% of the time, Pallas kernels for 8%

profile of v12, /device:TPU:1, one launch (start us, length us, event | category | flops | bytes accessed | tf_op | source)
XLA Modules:
  0.0 102.8 jit_solution(5235511891773789470)
XLA Ops:
  0.6 3.3 %collective-permute-start = (f32[192,640]{1,0:T(8,128)}, f32[192,640]{1,0:T(8,128)S(1)}, u32[]{:S(2)}, u32[]{:S(2)}) collective-permute-start(f32[192,640]{1,0:T(8,128)} %bitcast.26), channel_id=1, source_target_pairs={{0,64},{64,0},{1,65},{65,1},{2,66},{66,2},{3,67},{67,3},{4,68},{68... | collective-permute-start | bytes 1474568 | tf_op jit(solution)/shard_map/ppermute | solution.py:310
  4.0 0.1 collective-permute-start.1
  4.1 0.6 stack.28.place_ref
  4.6 1.0 %collective-permute-done.act_other_ref = f32[192,640]{1,0:T(8,128)S(1)} collective-permute-done((f32[192,640]{1,0:T(8,128)}, f32[192,640]{1,0:T(8,128)S(1)}, u32[]{:S(2)}, u32[]{:S(2)}) %collective-permute-start) | collective-permute-done | bytes 491552 | tf_op jit(solution)/shard_map/ppermute | solution.py:310
  5.7 0.7 collective-permute-done.1.cot_other_ref
  6.4 0.1 copy-done.15
  6.4 0.7 copy-done.16
  7.1 12.5 %mlp.1 = (f32[192,640]{1,0:T(8,128)}, f32[192,640]{1,0:T(8,128)}, f32[160,1280]{1,0:T(8,128)}, f32[160,1280]{1,0:T(8,128)}, f32[160,1280]{1,0:T(8,128)}, /*index=5*/f32[160,1280]{1,0:T(8,128)}) custom-call(s32[6]{0:T(128)} %stack.28.place_ref, f32[192,640]{1,0:T(8,128)} %bitcast.27, f32[192,640]{1,0:T(8,128)} %copy-done.15, f32[192,640]{1,0:T(8,128)} %bitcast.29, ...), custom_call_target="tpu_custom_call" | custom-call | flops 4718592000 | bytes 12000000 | tf_op jit(solution)/shard_map/mlp/pallas_call | solution.py:190
  19.6 1.2 %collective-permute-start.3 = (f32[160,1280]{1,0:T(8,128)}, f32[160,1280]{1,0:T(8,128)S(1)}, u32[]{:S(2)}, u32[]{:S(2)}) collective-permute-start(f32[160,1280]{1,0:T(8,128)} %get-tuple-element.32), channel_id=1, source_target_pairs={{0,16},{1,17},{2,18},{3,19},{4,20},{5,21},{6,22},{7,23},{8,24},{9,... | collective-permute-start | bytes 2457608 | tf_op jit(solution)/shard_map/ppermute | solution.py:288
  20.8 0.4 collective-permute-start.4
  21.2 1.7 %collective-permute-start.5 = (f32[160,1280]{1,0:T(8,128)}, f32[160,1280]{1,0:T(8,128)S(1)}, u32[]{:S(2)}, u32[]{:S(2)}) collective-permute-start(f32[160,1280]{1,0:T(8,128)} %get-tuple-element.34), channel_id=1, source_target_pairs={{0,48},{1,49},{2,50},{3,51},{4,52},{5,53},{6,54},{7,55},{8,56},{9,... | collective-permute-start | bytes 2457608 | tf_op jit(solution)/shard_map/ppermute | solution.py:288
  22.9 0.6 collective-permute-start.2
  23.5 1.7 %collective-permute-done.2.arrived_ref = f32[192,640]{1,0:T(8,128)S(1)} collective-permute-done((f32[192,640]{1,0:T(8,128)}, f32[192,640]{1,0:T(8,128)S(1)}, u32[]{:S(2)}, u32[]{:S(2)}) %collective-permute-start.2) | collective-permute-done | bytes 491552 | tf_op jit(solution)/shard_map/ppermute | solution.py:310
  25.2 0.0 copy-done.8
  25.2 1.0 %copy-done.7 = f32[192,640]{1,0:T(8,128)S(1)} copy-done((f32[192,640]{1,0:T(8,128)S(1)}, f32[192,640]{1,0:T(8,128)}, u32[]{:S(2)}) %copy-start.7) | copy-done | bytes 491544
  26.3 2.0 %pack.1 = f32[64,16,128]{2,1,0:T(8,128)} custom-call(s32[6]{0:T(128)S(1)} %copy-done.8, f32[3,10]{1,0:T(4,128)S(1)} %bitcast.22, f32[192,640]{1,0:T(8,128)S(1)} %copy-done.7, f32[192,640]{1,0:T(8,128)S(1)} %collective-permute-done.2.arrived_ref), custom_call_target="tpu_custom_call" | custom-call | tf_op jit(solution)/shard_map/pack/pallas_call | solution.py:270
  28.3 12.5 %all-to-all-start = ((f32[64,16,128]{2,1,0:T(8,128)}), f32[64,16,128]{2,1,0:T(8,128)S(1)}, u32[]{:S(2)}, u32[]{:S(2)}) async-start(f32[64,16,128]{2,1,0:T(8,128)} %pack.1), calls=%async_computation | async-start | bytes 1048576 | tf_op jit(solution)/shard_map/all_to_all | solution.py:465
  40.8 0.0 collective-permute-done.3.refs_1_
  40.8 0.0 collective-permute-done.4.refs_2_
  40.8 0.8 collective-permute-done.5.refs_3_
  41.6 0.9 copy-done.12
  42.5 1.1 %copy-done.13 = f32[160,1280]{1,0:T(8,128)S(1)} copy-done((f32[160,1280]{1,0:T(8,128)S(1)}, f32[160,1280]{1,0:T(8,128)}, u32[]{:S(2)}) %copy-start.13) | copy-done | bytes 819224
  43.7 1.1 %copy-done.14 = f32[160,1280]{1,0:T(8,128)S(1)} copy-done((f32[160,1280]{1,0:T(8,128)S(1)}, f32[160,1280]{1,0:T(8,128)}, u32[]{:S(2)}) %copy-start.14) | copy-done | bytes 819224
  44.8 1.7 %swap.1 = (f32[80,640]{1,0:T(8,128)S(1)}, f32[80,640]{1,0:T(8,128)}, f32[80,640]{1,0:T(8,128)}, f32[80,640]{1,0:T(8,128)}) custom-call(s32[6]{0:T(128)S(1)} %copy-done.8, f32[160,1280]{1,0:T(8,128)S(1)} %copy-done.14, f32[160,1280]{1,0:T(8,128)S(1)} %collective-permute-done.3.refs_1_, f32[160,1280]{1,0:T(8,128)S(1)} %collective-permute-done.4.refs_2_, ...), custom_call_target="tpu_custom_call" | custom-call | flops 10000000000 | bytes 4000000 | tf_op jit(solution)/shard_map/swap/pallas_call | solution.py:270
  46.5 0.0 collective-permute-start.8
  46.5 2.6 %collective-permute-start.9 = (f32[80,640]{1,0:T(8,128)}, f32[80,640]{1,0:T(8,128)S(1)}, u32[]{:S(2)}, u32[]{:S(2)}) collective-permute-start(f32[80,640]{1,0:T(8,128)} %get-tuple-element.41), channel_id=1, source_target_pairs={{0,128},{1,129},{2,130},{3,131},{4,132},{5,133},{6,134},{7,135},{8... | collective-permute-start | bytes 614408 | tf_op jit(solution)/shard_map/ppermute | solution.py:288
  49.1 1.1 %collective-permute-start.10 = (f32[80,640]{1,0:T(8,128)}, f32[80,640]{1,0:T(8,128)S(1)}, u32[]{:S(2)}, u32[]{:S(2)}) collective-permute-start(f32[80,640]{1,0:T(8,128)} %get-tuple-element.42), channel_id=1, source_target_pairs={{0,129},{1,128},{2,131},{3,130},{4,133},{5,132},{6,135},{7,134},{8... | collective-permute-start | bytes 614408 | tf_op jit(solution)/shard_map/ppermute | solution.py:288
  50.2 0.0 copy-done.1
  50.2 1.4 %kernel_spectrum.1._.kernel_ref = f32[336,768]{1,0:T(8,128)S(1)} custom-call(f32[336,768]{1,0:T(8,128)S(1)} %bitcast.21, bf16[768,768]{1,0:T(8,128)(2,1)S(1)} %copy-done.1, bf16[768,768]{1,0:T(8,128)(2,1)S(1)} %copy-done, f32[80,640]{1,0:T(8,128)S(1)} %get-tuple-element.35._.refs_0_), custom_call_target="tpu_custom_call" | custom-call | flops 1189085184 | bytes 5000000 | tf_op jit(solution)/shard_map/kernel_spectrum/pallas_call | solution.py:361
  51.6 6.8 %all-to-all-done.block_ref = f32[64,16,128]{2,1,0:T(8,128)S(1)} async-done(((f32[64,16,128]{2,1,0:T(8,128)}), f32[64,16,128]{2,1,0:T(8,128)S(1)}, u32[]{:S(2)}, u32[]{:S(2)}) %all-to-all-start) | async-done | bytes 524320 | tf_op jit(solution)/shard_map/all_to_all | solution.py:465
  58.4 1.3 %copy-done.5 = bf16[768,768]{1,0:T(8,128)(2,1)S(1)} copy-done((bf16[768,768]{1,0:T(8,128)(2,1)S(1)}, bf16[768,768]{1,0:T(8,128)(2,1)}, u32[]{:S(2)}) %copy-start.5) | copy-done | bytes 1179672
  59.7 0.6 copy-done.9
  60.2 1.6 %spectrum.1 = (f32[160,768]{1,0:T(8,128)S(1)}, f32[30,768]{1,0:T(8,128)S(1)}, f32[30,768]{1,0:T(8,128)S(1)}, f32[1,128]{1,0:T(1,128)S(1)}) custom-call(s32[6]{0:T(128)S(1)} %copy-done.9, f32[64,16,128]{2,1,0:T(8,128)S(1)} %all-to-all-done.block_ref, bf16[768,768]{1,0:T(8,128)(2,1)S(1)} %copy-done.5, bf16[768,768]{1,0:T(8,128)(2,1)S(1)} %copy-done.4, ...), custom_call_target="tpu_custom_call" | custom-call | flops 566231040 | bytes 4000000 | tf_op jit(solution)/shard_map/spectrum/pallas_call | solution.py:336
  61.8 0.0 copy-start.2
  61.8 0.0 collective-permute-done.8.refs_1_
  61.8 0.0 collective-permute-done.9.refs_2_
  61.9 0.0 collective-permute-done.10.refs_3_
  61.9 0.7 pair.1
  62.5 2.5 %collective-permute-start.11 = (f32[80,320]{1,0:T(8,128)S(1)}, f32[80,320]{1,0:T(8,128)S(1)}, u32[]{:S(2)}, u32[]{:S(2)}) collective-permute-start(f32[80,320]{1,0:T(8,128)S(1)} %get-tuple-element.43), channel_id=1, source_target_pairs={{0,64},{64,0},{1,65},{65,1},{2,66},{66,2},{3,67},{67,3},{4,68},{68... | collective-permute-start | bytes 307208 | tf_op jit(solution)/shard_map/ppermute | solution.py:310
  65.0 0.1 collective-permute-start.6
  65.1 2.6 %collective-permute-start.7 = (f32[30,768]{1,0:T(8,128)S(1)}, f32[30,768]{1,0:T(8,128)S(1)}, u32[]{:S(2)}, u32[]{:S(2)}) collective-permute-start(f32[30,768]{1,0:T(8,128)S(1)} %get-tuple-element.39), channel_id=1, source_target_pairs={{64,128},{128,64},{65,129},{129,65},{66,130},{130,66},{67,131},{13... | collective-permute-start | bytes 276488 | tf_op jit(solution)/shard_map/ppermute | solution.py:485
  67.7 0.0 collective-permute-done.6.near_ref
  67.7 3.3 %collective-permute-done.7.cross_ref = f32[30,768]{1,0:T(8,128)S(1)} collective-permute-done((f32[30,768]{1,0:T(8,128)S(1)}, f32[30,768]{1,0:T(8,128)S(1)}, u32[]{:S(2)}, u32[]{:S(2)}) %collective-permute-start.7) | collective-permute-done | bytes 92192 | tf_op jit(solution)/shard_map/ppermute | solution.py:485
  71.1 0.0 collective-permute-done.11.refs_0_.arrived_ref
  71.1 4.2 %filter.1._ = f32[64,16,128]{2,1,0:T(8,128)} custom-call(s32[6]{0:T(128)S(1)} %copy-done.9, f32[1,128]{1,0:T(1,128)S(1)} %get-tuple-element.36.mixing_ref, f32[160,768]{1,0:T(8,128)S(1)} %get-tuple-element.37._.data_ref, f32[30,768]{1,0:T(8,128)S(1)} %collective-permute-done.6.near_ref, f32[30,768]{1,0:T(8,128)S(1)} %collective-permute-done.7.cross_ref, ...), custom_call_target="tpu_custom_call" | custom-call | flops 566231040 | bytes 5000000 | tf_op jit(solution)/shard_map/filter/pallas_call | solution.py:421
  75.3 6.7 %all-to-all-start.1 = ((f32[64,16,128]{2,1,0:T(8,128)}), f32[64,16,128]{2,1,0:T(8,128)S(1)}, u32[]{:S(2)}, u32[]{:S(2)}) async-start(f32[64,16,128]{2,1,0:T(8,128)} %filter.1._), calls=%async_computation.1 | async-start | bytes 1048576 | tf_op jit(solution)/shard_map/all_to_all | solution.py:465
  82.0 0.6 stack.29
  82.6 1.1 %collective-permute-start.12 = (f32[20,320]{1,0:T(8,128)S(1)}, f32[20,320]{1,0:T(8,128)S(1)}, u32[]{:S(2)}, u32[]{:S(2)}) collective-permute-start(f32[20,320]{1,0:T(8,128)S(1)} %get-tuple-element.46), channel_id=1, source_target_pairs={{0,2},{2,4},{4,6},{6,8},{8,10},{10,12},{12,14},{14,0},{1,3},{3,5},... | collective-permute-start | bytes 76808 | tf_op jit(solution)/shard_map/ppermute | solution.py:305
  83.7 1.7 %collective-permute-start.13 = (f32[20,320]{1,0:T(8,128)S(1)}, f32[20,320]{1,0:T(8,128)S(1)}, u32[]{:S(2)}, u32[]{:S(2)}) collective-permute-start(f32[20,320]{1,0:T(8,128)S(1)} %get-tuple-element.47), channel_id=1, source_target_pairs={{0,14},{2,0},{4,2},{6,4},{8,6},{10,8},{12,10},{14,12},{1,15},{3,1}... | collective-permute-start | bytes 76808 | tf_op jit(solution)/shard_map/ppermute | solution.py:305
  85.3 4.9 %collective-permute-start.14 = (f32[20,320]{1,0:T(8,128)S(1)}, f32[20,320]{1,0:T(8,128)S(1)}, u32[]{:S(2)}, u32[]{:S(2)}) collective-permute-start(f32[20,320]{1,0:T(8,128)S(1)} %get-tuple-element.48), channel_id=1, source_target_pairs={{0,8},{2,10},{4,12},{6,14},{8,0},{10,2},{12,4},{14,6},{1,9},{3,11}... | collective-permute-start | bytes 76808 | tf_op jit(solution)/shard_map/ppermute | solution.py:305
  90.3 0.0 collective-permute-start.15
  90.3 4.5 %collective-permute-start.16 = (f32[20,320]{1,0:T(8,128)S(1)}, f32[20,320]{1,0:T(8,128)S(1)}, u32[]{:S(2)}, u32[]{:S(2)}) collective-permute-start(f32[20,320]{1,0:T(8,128)S(1)} %get-tuple-element.50), channel_id=1, source_target_pairs={{0,10},{2,12},{4,14},{6,0},{8,2},{10,4},{12,6},{14,8},{1,11},{3,13... | collective-permute-start | bytes 76808 | tf_op jit(solution)/shard_map/ppermute | solution.py:305
  94.7 0.0 collective-permute-done.12.refs_1_
  94.7 1.1 %collective-permute-start.17 = (f32[20,320]{1,0:T(8,128)S(1)}, f32[20,320]{1,0:T(8,128)S(1)}, u32[]{:S(2)}, u32[]{:S(2)}) collective-permute-start(f32[20,320]{1,0:T(8,128)S(1)} %get-tuple-element.51), channel_id=1, source_target_pairs={{0,4},{2,6},{4,8},{6,10},{8,12},{10,14},{12,0},{14,2},{1,5},{3,7},... | collective-permute-start | bytes 76808 | tf_op jit(solution)/shard_map/ppermute | solution.py:305
  95.8 0.0 collective-permute-done.13.refs_2_
  95.8 2.5 %collective-permute-start.18 = (f32[20,320]{1,0:T(8,128)S(1)}, f32[20,320]{1,0:T(8,128)S(1)}, u32[]{:S(2)}, u32[]{:S(2)}) collective-permute-start(f32[20,320]{1,0:T(8,128)S(1)} %get-tuple-element.52), channel_id=1, source_target_pairs={{0,12},{2,14},{4,0},{6,2},{8,4},{10,6},{12,8},{14,10},{1,13},{3,15... | collective-permute-start | bytes 76808 | tf_op jit(solution)/shard_map/ppermute | solution.py:305
  98.3 0.9 collective-permute-done.14.refs_3_
  99.3 0.0 collective-permute-done.15.refs_4_
  99.3 0.0 collective-permute-done.16.refs_5_
  99.3 0.7 collective-permute-done.17.refs_6_
  100.0 0.8 collective-permute-done.18.refs_7_
  100.8 0.7 last.1
  101.5 0.0 all-to-all-done.1.block_ref
  101.5 1.3 %unpack.1 = f32[192,640]{1,0:T(8,128)} custom-call(f32[64,16,128]{2,1,0:T(8,128)S(1)} %all-to-all-done.1.block_ref), custom_call_target="tpu_custom_call" | custom-call | tf_op jit(solution)/shard_map/unpack/pallas_call | solution.py:454
  (23 shorter events, 0.0 us)
Async XLA Ops:
  0.6 5.0 %collective-permute-start = (f32[192,640]{1,0:T(8,128)}, f32[192,640]{1,0:T(8,128)S(1)}, u32[]{:S(2)}, u32[]{:S(2)}) collective-permute-start(f32[192,640]{1,0:T(8,128)} %bitcast.26), channel_id=1, source_target_pairs={{0,64},{64,0},{1,65},{65,1},{2,66},{66,2},{3,67},{67,3},{4,68},{68... | collective-permute-start | bytes 1474568 | tf_op jit(solution)/shard_map/ppermute | solution.py:310
  4.0 2.4 %collective-permute-start.1 = (f32[192,640]{1,0:T(8,128)}, f32[192,640]{1,0:T(8,128)S(1)}, u32[]{:S(2)}, u32[]{:S(2)}) collective-permute-start(f32[192,640]{1,0:T(8,128)} %bitcast.28), channel_id=1, source_target_pairs={{0,64},{64,0},{1,65},{65,1},{2,66},{66,2},{3,67},{67,3},{4,68},{68... | collective-permute-start | bytes 1474568 | tf_op jit(solution)/shard_map/ppermute | solution.py:310
  5.7 0.8 copy-start.15
  6.4 0.8 copy-start.16
  7.1 18.1 %copy-start.8 = (s32[6]{0:T(128)S(1)}, s32[6]{0:T(128)}, u32[]{:S(2)}) copy-start(s32[6]{0:T(128)} %stack.28.place_ref) | copy-start | bytes 76
  7.1 18.1 %copy-start.11 = (f32[10,3]{0,1:T(4,128)S(1)}, f32[10,3]{0,1:T(4,128)}, u32[]{:S(2)}) copy-start(f32[10,3]{0,1:T(4,128)} %param.17) | copy-start | bytes 364
  19.6 21.1 %collective-permute-start.3 = (f32[160,1280]{1,0:T(8,128)}, f32[160,1280]{1,0:T(8,128)S(1)}, u32[]{:S(2)}, u32[]{:S(2)}) collective-permute-start(f32[160,1280]{1,0:T(8,128)} %get-tuple-element.32), channel_id=1, source_target_pairs={{0,16},{1,17},{2,18},{3,19},{4,20},{5,21},{6,22},{7,23},{8,24},{9,... | collective-permute-start | bytes 2457608 | tf_op jit(solution)/shard_map/ppermute | solution.py:288
  20.8 19.9 %collective-permute-start.4 = (f32[160,1280]{1,0:T(8,128)}, f32[160,1280]{1,0:T(8,128)S(1)}, u32[]{:S(2)}, u32[]{:S(2)}) collective-permute-start(f32[160,1280]{1,0:T(8,128)} %get-tuple-element.33), channel_id=1, source_target_pairs={{0,32},{1,33},{2,34},{3,35},{4,36},{5,37},{6,38},{7,39},{8,40},{9,... | collective-permute-start | bytes 2457608 | tf_op jit(solution)/shard_map/ppermute | solution.py:288
  21.2 20.4 %collective-permute-start.5 = (f32[160,1280]{1,0:T(8,128)}, f32[160,1280]{1,0:T(8,128)S(1)}, u32[]{:S(2)}, u32[]{:S(2)}) collective-permute-start(f32[160,1280]{1,0:T(8,128)} %get-tuple-element.34), channel_id=1, source_target_pairs={{0,48},{1,49},{2,50},{3,51},{4,52},{5,53},{6,54},{7,55},{8,56},{9,... | collective-permute-start | bytes 2457608 | tf_op jit(solution)/shard_map/ppermute | solution.py:288
  22.9 2.3 %collective-permute-start.2 = (f32[192,640]{1,0:T(8,128)}, f32[192,640]{1,0:T(8,128)S(1)}, u32[]{:S(2)}, u32[]{:S(2)}) collective-permute-start(f32[192,640]{1,0:T(8,128)} %get-tuple-element.30), channel_id=1, source_target_pairs={{0,64},{64,0},{1,65},{65,1},{2,66},{66,2},{3,67},{67,3},{4,68},{68... | collective-permute-start | bytes 1474568 | tf_op jit(solution)/shard_map/ppermute | solution.py:310
  25.2 1.0 %copy-start.7 = (f32[192,640]{1,0:T(8,128)S(1)}, f32[192,640]{1,0:T(8,128)}, u32[]{:S(2)}) copy-start(f32[192,640]{1,0:T(8,128)} %get-tuple-element.29.unit_ref) | copy-start | bytes 1474564
  28.3 30.1 %all-to-all-start = ((f32[64,16,128]{2,1,0:T(8,128)}), f32[64,16,128]{2,1,0:T(8,128)S(1)}, u32[]{:S(2)}, u32[]{:S(2)}) async-start(f32[64,16,128]{2,1,0:T(8,128)} %pack.1), calls=%async_computation | async-start | bytes 1048576 | tf_op jit(solution)/shard_map/all_to_all | solution.py:465
  41.6 0.9 copy-start.12
  42.5 1.1 %copy-start.13 = (f32[160,1280]{1,0:T(8,128)S(1)}, f32[160,1280]{1,0:T(8,128)}, u32[]{:S(2)}) copy-start(f32[160,1280]{1,0:T(8,128)} %copy-done.12) | copy-start | bytes 2457604
  43.7 1.1 %copy-start.14 = (f32[160,1280]{1,0:T(8,128)S(1)}, f32[160,1280]{1,0:T(8,128)}, u32[]{:S(2)}) copy-start(f32[160,1280]{1,0:T(8,128)} %get-tuple-element.31.refs_0_) | copy-start | bytes 2457604
  44.8 5.4 %copy-start = (bf16[768,768]{1,0:T(8,128)(2,1)S(1)}, bf16[768,768]{1,0:T(8,128)(2,1)}, u32[]{:S(2)}) copy-start(bf16[768,768]{1,0:T(8,128)(2,1)} %constant.38.clone.low_ref) | copy-start | bytes 3538948
  44.8 5.4 %copy-start.1 = (bf16[768,768]{1,0:T(8,128)(2,1)S(1)}, bf16[768,768]{1,0:T(8,128)(2,1)}, u32[]{:S(2)}) copy-start(bf16[768,768]{1,0:T(8,128)(2,1)} %constant.37.clone.top_ref) | copy-start | bytes 3538948
  44.8 5.4 %copy-start.6 = (f32[3,16,7,768]{3,1,2,0:T(8,128)S(1)}, f32[3,16,7,768]{3,1,2,0:T(8,128)}, u32[]{:S(2)}) copy-start(f32[3,16,7,768]{3,1,2,0:T(8,128)} %param.16) | copy-start | bytes 3096580
  46.5 15.3 %collective-permute-start.8 = (f32[80,640]{1,0:T(8,128)}, f32[80,640]{1,0:T(8,128)S(1)}, u32[]{:S(2)}, u32[]{:S(2)}) collective-permute-start(f32[80,640]{1,0:T(8,128)} %get-tuple-element.40), channel_id=1, source_target_pairs={{0,1},{1,0},{2,3},{3,2},{4,5},{5,4},{6,7},{7,6},{8,9},{9,8},{10,11... | collective-permute-start | bytes 614408 | tf_op jit(solution)/shard_map/ppermute | solution.py:288
  46.5 15.3 %collective-permute-start.9 = (f32[80,640]{1,0:T(8,128)}, f32[80,640]{1,0:T(8,128)S(1)}, u32[]{:S(2)}, u32[]{:S(2)}) collective-permute-start(f32[80,640]{1,0:T(8,128)} %get-tuple-element.41), channel_id=1, source_target_pairs={{0,128},{1,129},{2,130},{3,131},{4,132},{5,133},{6,134},{7,135},{8... | collective-permute-start | bytes 614408 | tf_op jit(solution)/shard_map/ppermute | solution.py:288
  49.1 12.7 %collective-permute-start.10 = (f32[80,640]{1,0:T(8,128)}, f32[80,640]{1,0:T(8,128)S(1)}, u32[]{:S(2)}, u32[]{:S(2)}) collective-permute-start(f32[80,640]{1,0:T(8,128)} %get-tuple-element.42), channel_id=1, source_target_pairs={{0,129},{1,128},{2,131},{3,130},{4,133},{5,132},{6,135},{7,134},{8... | collective-permute-start | bytes 614408 | tf_op jit(solution)/shard_map/ppermute | solution.py:288
  50.2 8.2 %copy-start.4 = (bf16[768,768]{1,0:T(8,128)(2,1)S(1)}, bf16[768,768]{1,0:T(8,128)(2,1)}, u32[]{:S(2)}) copy-start(bf16[768,768]{1,0:T(8,128)(2,1)} %constant.40.clone.low_ref) | copy-start | bytes 3538948
  58.4 1.3 %copy-start.5 = (bf16[768,768]{1,0:T(8,128)(2,1)S(1)}, bf16[768,768]{1,0:T(8,128)(2,1)}, u32[]{:S(2)}) copy-start(bf16[768,768]{1,0:T(8,128)(2,1)} %constant.39.clone.top_ref) | copy-start | bytes 3538948
  59.7 0.6 copy-start.9
  60.2 10.8 %copy-start.3 = (bf16[768,768]{1,0:T(8,128)(2,1)S(1)}, bf16[768,768]{1,0:T(8,128)(2,1)}, u32[]{:S(2)}) copy-start(bf16[768,768]{1,0:T(8,128)(2,1)} %constant.41.clone.top_ref) | copy-start | bytes 3538948
  61.8 9.2 %copy-start.2 = (bf16[768,768]{1,0:T(8,128)(2,1)S(1)}, bf16[768,768]{1,0:T(8,128)(2,1)}, u32[]{:S(2)}) copy-start(bf16[768,768]{1,0:T(8,128)(2,1)} %constant.42.clone.low_ref) | copy-start | bytes 3538948
  62.5 8.5 %collective-permute-start.11 = (f32[80,320]{1,0:T(8,128)S(1)}, f32[80,320]{1,0:T(8,128)S(1)}, u32[]{:S(2)}, u32[]{:S(2)}) collective-permute-start(f32[80,320]{1,0:T(8,128)S(1)} %get-tuple-element.43), channel_id=1, source_target_pairs={{0,64},{64,0},{1,65},{65,1},{2,66},{66,2},{3,67},{67,3},{4,68},{68... | collective-permute-start | bytes 307208 | tf_op jit(solution)/shard_map/ppermute | solution.py:310
  65.0 2.7 %collective-permute-start.6 = (f32[30,768]{1,0:T(8,128)S(1)}, f32[30,768]{1,0:T(8,128)S(1)}, u32[]{:S(2)}, u32[]{:S(2)}) collective-permute-start(f32[30,768]{1,0:T(8,128)S(1)} %get-tuple-element.38), channel_id=1, source_target_pairs={{0,64},{64,0},{1,65},{65,1},{2,66},{66,2},{3,67},{67,3},{4,68},{68... | collective-permute-start | bytes 276488 | tf_op jit(solution)/shard_map/ppermute | solution.py:310
  65.1 5.9 %collective-permute-start.7 = (f32[30,768]{1,0:T(8,128)S(1)}, f32[30,768]{1,0:T(8,128)S(1)}, u32[]{:S(2)}, u32[]{:S(2)}) collective-permute-start(f32[30,768]{1,0:T(8,128)S(1)} %get-tuple-element.39), channel_id=1, source_target_pairs={{64,128},{128,64},{65,129},{129,65},{66,130},{130,66},{67,131},{13... | collective-permute-start | bytes 276488 | tf_op jit(solution)/shard_map/ppermute | solution.py:485
  71.1 10.9 %copy-start.10 = (s32[6]{0:T(128)S(1)}, s32[6]{0:T(128)}, u32[]{:S(2)}) copy-start(s32[6]{0:T(128)} %stack.28.place_ref) | copy-start | bytes 76
  75.3 26.2 %all-to-all-start.1 = ((f32[64,16,128]{2,1,0:T(8,128)}), f32[64,16,128]{2,1,0:T(8,128)S(1)}, u32[]{:S(2)}, u32[]{:S(2)}) async-start(f32[64,16,128]{2,1,0:T(8,128)} %filter.1._), calls=%async_computation.1 | async-start | bytes 1048576 | tf_op jit(solution)/shard_map/all_to_all | solution.py:465
  82.6 12.2 %collective-permute-start.12 = (f32[20,320]{1,0:T(8,128)S(1)}, f32[20,320]{1,0:T(8,128)S(1)}, u32[]{:S(2)}, u32[]{:S(2)}) collective-permute-start(f32[20,320]{1,0:T(8,128)S(1)} %get-tuple-element.46), channel_id=1, source_target_pairs={{0,2},{2,4},{4,6},{6,8},{8,10},{10,12},{12,14},{14,0},{1,3},{3,5},... | collective-permute-start | bytes 76808 | tf_op jit(solution)/shard_map/ppermute | solution.py:305
  83.7 12.2 %collective-permute-start.13 = (f32[20,320]{1,0:T(8,128)S(1)}, f32[20,320]{1,0:T(8,128)S(1)}, u32[]{:S(2)}, u32[]{:S(2)}) collective-permute-start(f32[20,320]{1,0:T(8,128)S(1)} %get-tuple-element.47), channel_id=1, source_target_pairs={{0,14},{2,0},{4,2},{6,4},{8,6},{10,8},{12,10},{14,12},{1,15},{3,1}... | collective-permute-start | bytes 76808 | tf_op jit(solution)/shard_map/ppermute | solution.py:305
  85.3 13.9 %collective-permute-start.14 = (f32[20,320]{1,0:T(8,128)S(1)}, f32[20,320]{1,0:T(8,128)S(1)}, u32[]{:S(2)}, u32[]{:S(2)}) collective-permute-start(f32[20,320]{1,0:T(8,128)S(1)} %get-tuple-element.48), channel_id=1, source_target_pairs={{0,8},{2,10},{4,12},{6,14},{8,0},{10,2},{12,4},{14,6},{1,9},{3,11}... | collective-permute-start | bytes 76808 | tf_op jit(solution)/shard_map/ppermute | solution.py:305
  90.3 9.0 %collective-permute-start.15 = (f32[20,320]{1,0:T(8,128)S(1)}, f32[20,320]{1,0:T(8,128)S(1)}, u32[]{:S(2)}, u32[]{:S(2)}) collective-permute-start(f32[20,320]{1,0:T(8,128)S(1)} %get-tuple-element.49), channel_id=1, source_target_pairs={{0,6},{2,8},{4,10},{6,12},{8,14},{10,0},{12,2},{14,4},{1,7},{3,9},... | collective-permute-start | bytes 76808 | tf_op jit(solution)/shard_map/ppermute | solution.py:305
  90.3 9.0 %collective-permute-start.16 = (f32[20,320]{1,0:T(8,128)S(1)}, f32[20,320]{1,0:T(8,128)S(1)}, u32[]{:S(2)}, u32[]{:S(2)}) collective-permute-start(f32[20,320]{1,0:T(8,128)S(1)} %get-tuple-element.50), channel_id=1, source_target_pairs={{0,10},{2,12},{4,14},{6,0},{8,2},{10,4},{12,6},{14,8},{1,11},{3,13... | collective-permute-start | bytes 76808 | tf_op jit(solution)/shard_map/ppermute | solution.py:305
  94.7 5.2 %collective-permute-start.17 = (f32[20,320]{1,0:T(8,128)S(1)}, f32[20,320]{1,0:T(8,128)S(1)}, u32[]{:S(2)}, u32[]{:S(2)}) collective-permute-start(f32[20,320]{1,0:T(8,128)S(1)} %get-tuple-element.51), channel_id=1, source_target_pairs={{0,4},{2,6},{4,8},{6,10},{8,12},{10,14},{12,0},{14,2},{1,5},{3,7},... | collective-permute-start | bytes 76808 | tf_op jit(solution)/shard_map/ppermute | solution.py:305
  95.8 4.9 %collective-permute-start.18 = (f32[20,320]{1,0:T(8,128)S(1)}, f32[20,320]{1,0:T(8,128)S(1)}, u32[]{:S(2)}, u32[]{:S(2)}) collective-permute-start(f32[20,320]{1,0:T(8,128)S(1)} %get-tuple-element.52), channel_id=1, source_target_pairs={{0,12},{2,14},{4,0},{6,2},{8,4},{10,6},{12,8},{14,10},{1,13},{3,15... | collective-permute-start | bytes 76808 | tf_op jit(solution)/shard_map/ppermute | solution.py:305

commit v13 on v12

--- a/solution.py
+++ b/solution.py
@@ -258,7 +258,7 @@
         outs[m][...] = kept_ref[lax.rem(place_ref[5] + m, 8), 0:20, :]
 
 
-def last_kernel(*refs):
+def last_kernel(_, *refs):
     first_ref, second_ref = refs[8:]
     a, b, c, d = (refs[m][...] + refs[m + 4][...] for m in range(4))
     total = (a + b) + (c + d)
@@ -266,19 +266,26 @@
     second_ref[...] = total[:, 160:320]
 
 
-def small(kernel, operands, shapes, scalars=0, scratch=(), earlier=(), name=None, flops=0):
+def small(
+    kernel, operands, shapes, scalars=0, scratch=(), earlier=(), name=None, flops=0, piped=False
+):
+    def full(shape):
+        return pl.BlockSpec(shape, lambda i: (0,) * len(shape))
+
+    arrays = operands[scalars:]
     return pl.pallas_call(
         kernel,
+        grid=(1,) if piped else (),
         in_specs=[pl.BlockSpec(memory_space=pltpu.SMEM)] * scalars
         + EARLIER * len(earlier)
-        + whole(len(operands) - scalars),
-        out_specs=whole(len(shapes)),
+        + ([full(array.shape) for array in arrays] if piped else whole(len(arrays))),
+        out_specs=[full(shape) for shape in shapes] if piped else whole(len(shapes)),
         out_shape=[jax.ShapeDtypeStruct(shape, F32) for shape in shapes],
         scratch_shapes=scratch,
-        compiler_params=params(32),
+        compiler_params=params(57 if piped else 32),
         cost_estimate=cost(flops, 4_000_000) if flops else None,
         name=name,
-    )(*operands[:scalars], *earlier, *operands[scalars:])
+    )(*operands[:scalars], *earlier, *arrays)
 
 
 def permute(value, target):
@@ -433,7 +440,9 @@
     )(place, mixing, data, near, cross, kernel, jnp.asarray(top), jnp.asarray(low), earlier)
 
 
-def unpack_kernel(block_ref, out_ref):
+def unpack_kernel(block_ref, out_ref, token_ref):
+    token_ref[...] = jnp.zeros((8, 128), F32)
+
     def put(l, r, pair):
         out_ref[ROWS * l : ROWS * (l + 1), SHARDS * r : SHARDS * (r + 2)] = jnp.concatenate(
             pair, axis=1
@@ -454,8 +463,11 @@
     return pl.pallas_call(
         unpack_kernel,
         in_specs=whole(1),
-        out_specs=whole(1)[0],
-        out_shape=jax.ShapeDtypeStruct((ROWS * COLS, SHARDS * OWN), F32),
+        out_specs=whole(2),
+        out_shape=[
+            jax.ShapeDtypeStruct((ROWS * COLS, SHARDS * OWN), F32),
+            jax.ShapeDtypeStruct((8, 128), F32),
+        ],
         compiler_params=params(16),
         name="unpack",
     )(block)
@@ -473,11 +485,11 @@
     place = jnp.stack([lax.axis_index(axis) for axis in (LON, "co", "yl", "yh", "x", "z")])
     unit, other, *pieces = mlp(place, act, to_core(act), cot, to_core(cot), weight_in, weight_out)
     operands = (place, mixing.T, unit, to_core(other))
-    (block,) = small(pack_kernel, operands, [(SHARDS, 16, 128)], 2, name="pack")
+    (block,) = small(pack_kernel, operands, [(SHARDS, 16, 128)], 2, name="pack", piped=True)
     moved = exchange(pieces, "xy")
     spread = across(block)
     kept = (pltpu.VMEM((4, 80, 640), F32),)
-    swapped = small(swap_kernel, (place, *moved), [(80, 640)] * 4, 1, kept, (), "swap", 10**10)
+    swapped = small(swap_kernel, (place, *moved), [(80, 640)] * 4, 1, kept, (), "swap", 10**10, True)
     kernel = kernel_spectrum(kernels, swapped[0])
     moved = exchange(swapped, "yx")
     data, near, cross, own_mixing = spectrum(place, spread, kernel)
@@ -490,8 +502,10 @@
     kept = (pltpu.VMEM((8, 24, 320), F32),)
     operands = (place, mine, paired)
     stacked = small(stack_kernel, operands, [(20, 320)] * 8, 1, kept, (sent,), "stack")
-    grad_in, grad_out = small(last_kernel, exchange_z(stacked), [(20, 160)] * 2, name="last")
-    field = unpack(result).reshape(COLS, ROWS, width).transpose(1, 0, 2)
+    flat, token = unpack(result)
+    field = flat.reshape(COLS, ROWS, width).transpose(1, 0, 2)
+    moved = exchange_z(stacked)
+    grad_in, grad_out = small(last_kernel, moved, [(20, 160)] * 2, 0, (), (token,), "last")
     return (field, grad_in, grad_out)
 
 

time: 104 us -> 102 us (0.981)
  local copies, waits for them, and re-layouts: 7.45 us -> 5.33 us
  Pallas kernels: 26.6 us -> 28.6 us
  waiting for transfers between devices: 16.8 us -> 14.8 us
    ppermute x7, waiting for transfers between devices: 2.46 us -> 0.02 us  [exchange_z(): lax.ppermute(pieces[m], 'z', [(z, (z + m) % 8) for z in range(8)])]
    pallas_call x6, Pallas kernels: 6.94 us -> 9.13 us  [the longest x5 7.84 us: small(): pl.pallas_call(kernel, grid=(1,) if piped else (), in_specs=[pl.BlockSpec...]
    unnamed x34 -> x32, local copies, waits for them, and re-layouts: 6.88 us -> 4.72 us
  transfers between devices with their start and end apart: 21 -> 21, of which waited for: 9 -> 7; matrix products, arithmetic and copies ran while one was open for 1% -> 1% of each run, Pallas kernels for 8% -> 11%
where the time goes in v13:
time: 102 us; the launch traced here: 101 us
  starting transfers between devices  51.5 us (50%)
  Pallas kernels  28.6 us (28%)
  waiting for transfers between devices  14.8 us (15%)
  local copies, waits for them, and re-layouts  5.33 us (5%)
    all_to_all x2, starting transfers between devices, across(): return lax.all_to_all(block, LON, split_axis=0, concat_axis=0, tiled=True)  18.7 us
    ppermute x7, starting transfers between devices, exchange_z(): lax.ppermute(pieces[m], 'z', [(z, (z + m) % 8) for z in range(8)])  15.7 us
    pallas_call x1, Pallas kernels, mlp(): pl.pallas_call(mlp_kernel, grid_spec=pltpu.PrefetchScalarGridSpec(num_sca...  12.4 us
    pallas_call x5, Pallas kernels, small(): pl.pallas_call(kernel, grid=(1,) if piped else (), in_specs=[pl.BlockSpec...  7.84 us
    ppermute x6, starting transfers between devices, permute(): return lax.ppermute(value, AXES, pairs)  7.77 us
    all_to_all x2, waiting for transfers between devices, across(): return lax.all_to_all(block, LON, split_axis=0, concat_axis=0, tiled=True)  7.57 us
    ppermute x5, starting transfers between devices, to_core(): return lax.ppermute(value, 'co', [(0, 1), (1, 0)])  6.65 us
    unnamed x32, local copies, waits for them, and re-layouts  4.72 us
  transfers between devices with their start and end apart: 21, of which 7 were waited for; matrix products, arithmetic and copies ran while one was open for 1% of the time, Pallas kernels for 11%

profile of v13, /device:TPU:1, one launch (start us, length us, event | category | flops | bytes accessed | tf_op | source)
XLA Modules:
  0.0 101.0 jit_solution(7652321114459539217)
XLA Ops:
  0.6 3.3 %collective-permute-start = (f32[192,640]{1,0:T(8,128)}, f32[192,640]{1,0:T(8,128)S(1)}, u32[]{:S(2)}, u32[]{:S(2)}) collective-permute-start(f32[192,640]{1,0:T(8,128)} %bitcast.25), channel_id=1, source_target_pairs={{0,64},{64,0},{1,65},{65,1},{2,66},{66,2},{3,67},{67,3},{4,68},{68... | collective-permute-start | bytes 1474568 | tf_op jit(solution)/shard_map/ppermute | solution.py:317
  4.0 0.1 collective-permute-start.1
  4.1 0.6 stack.28.place_ref
  4.7 1.0 collective-permute-done.act_other_ref
  5.7 0.7 collective-permute-done.1.cot_other_ref
  6.4 0.1 copy-done.14
  6.4 0.7 copy-done.15
  7.1 12.4 %mlp.1 = (f32[192,640]{1,0:T(8,128)}, f32[192,640]{1,0:T(8,128)}, f32[160,1280]{1,0:T(8,128)}, f32[160,1280]{1,0:T(8,128)}, f32[160,1280]{1,0:T(8,128)}, /*index=5*/f32[160,1280]{1,0:T(8,128)}) custom-call(s32[6]{0:T(128)} %stack.28.place_ref, f32[192,640]{1,0:T(8,128)} %bitcast.26, f32[192,640]{1,0:T(8,128)} %copy-done.14, f32[192,640]{1,0:T(8,128)} %bitcast.28, ...), custom_call_target="tpu_custom_call" | custom-call | flops 4718592000 | bytes 12000000 | tf_op jit(solution)/shard_map/mlp/pallas_call | solution.py:190
  19.5 1.2 %collective-permute-start.3 = (f32[160,1280]{1,0:T(8,128)}, f32[160,1280]{1,0:T(8,128)S(1)}, u32[]{:S(2)}, u32[]{:S(2)}) collective-permute-start(f32[160,1280]{1,0:T(8,128)} %get-tuple-element.34), channel_id=1, source_target_pairs={{0,16},{1,17},{2,18},{3,19},{4,20},{5,21},{6,22},{7,23},{8,24},{9,... | collective-permute-start | bytes 2457608 | tf_op jit(solution)/shard_map/ppermute | solution.py:295
  20.7 0.4 collective-permute-start.4
  21.1 1.7 %collective-permute-start.5 = (f32[160,1280]{1,0:T(8,128)}, f32[160,1280]{1,0:T(8,128)S(1)}, u32[]{:S(2)}, u32[]{:S(2)}) collective-permute-start(f32[160,1280]{1,0:T(8,128)} %get-tuple-element.36), channel_id=1, source_target_pairs={{0,48},{1,49},{2,50},{3,51},{4,52},{5,53},{6,54},{7,55},{8,56},{9,... | collective-permute-start | bytes 2457608 | tf_op jit(solution)/shard_map/ppermute | solution.py:295
  22.8 0.6 collective-permute-start.2
  23.4 1.7 %collective-permute-done.2.arrived_ref = f32[192,640]{1,0:T(8,128)S(1)} collective-permute-done((f32[192,640]{1,0:T(8,128)}, f32[192,640]{1,0:T(8,128)S(1)}, u32[]{:S(2)}, u32[]{:S(2)}) %collective-permute-start.2) | collective-permute-done | bytes 491552 | tf_op jit(solution)/shard_map/ppermute | solution.py:317
  25.1 0.8 copy-done.10
  25.9 2.6 %pack.1 = f32[64,16,128]{2,1,0:T(8,128)} custom-call(s32[6]{0:T(128)} %stack.28.place_ref, f32[3,10]{1,0:T(4,128)} %bitcast.22, f32[192,640]{1,0:T(8,128)} %get-tuple-element.31.unit_ref, f32[192,640]{1,0:T(8,128)} %copy-done.10), custom_call_target="tpu_custom_call" | custom-call | tf_op jit(solution)/shard_map/pack/pallas_call | solution.py:276
  28.5 12.5 %all-to-all-start = ((f32[64,16,128]{2,1,0:T(8,128)}), f32[64,16,128]{2,1,0:T(8,128)S(1)}, u32[]{:S(2)}, u32[]{:S(2)}) async-start(f32[64,16,128]{2,1,0:T(8,128)} %pack.1), calls=%async_computation | async-start | bytes 1048576 | tf_op jit(solution)/shard_map/all_to_all | solution.py:477
  41.0 0.0 collective-permute-done.3.refs_1_
  41.0 0.0 copy-start.11
  41.0 0.0 collective-permute-done.4.refs_2_
  41.0 0.5 collective-permute-done.5.refs_3_
  41.5 0.4 copy-done.11
  41.9 0.3 copy-done.12
  42.2 0.3 copy-done.13
  42.4 3.3 %swap.1 = (f32[80,640]{1,0:T(8,128)}, f32[80,640]{1,0:T(8,128)}, f32[80,640]{1,0:T(8,128)}, f32[80,640]{1,0:T(8,128)}) custom-call(s32[6]{0:T(128)} %stack.28.place_ref, f32[160,1280]{1,0:T(8,128)} %get-tuple-element.33.refs_0_, f32[160,1280]{1,0:T(8,128)} %copy-done.11, f32[160,1280]{1,0:T(8,128)} %copy-done.12, f32[160,1280]{1,0:T(8,128)} %copy-done.13), custom_call_target="tpu_custom_call" | custom-call | flops 10000000000 | bytes 4000000 | tf_op jit(solution)/shard_map/swap/pallas_call | solution.py:276
  45.7 0.8 collective-permute-start.8
  46.5 2.6 %collective-permute-start.9 = (f32[80,640]{1,0:T(8,128)}, f32[80,640]{1,0:T(8,128)S(1)}, u32[]{:S(2)}, u32[]{:S(2)}) collective-permute-start(f32[80,640]{1,0:T(8,128)} %get-tuple-element.43), channel_id=1, source_target_pairs={{0,128},{1,129},{2,130},{3,131},{4,132},{5,133},{6,134},{7,135},{8... | collective-permute-start | bytes 614408 | tf_op jit(solution)/shard_map/ppermute | solution.py:295
  49.1 1.1 %collective-permute-start.10 = (f32[80,640]{1,0:T(8,128)}, f32[80,640]{1,0:T(8,128)S(1)}, u32[]{:S(2)}, u32[]{:S(2)}) collective-permute-start(f32[80,640]{1,0:T(8,128)} %get-tuple-element.44), channel_id=1, source_target_pairs={{0,129},{1,128},{2,131},{3,130},{4,133},{5,132},{6,135},{7,134},{8... | collective-permute-start | bytes 614408 | tf_op jit(solution)/shard_map/ppermute | solution.py:295
  50.2 0.0 copy-done.1
  50.2 0.9 copy-done.7
  51.1 1.4 %kernel_spectrum.1._.kernel_ref = f32[336,768]{1,0:T(8,128)S(1)} custom-call(f32[336,768]{1,0:T(8,128)S(1)} %bitcast.21, bf16[768,768]{1,0:T(8,128)(2,1)S(1)} %copy-done.1, bf16[768,768]{1,0:T(8,128)(2,1)S(1)} %copy-done, f32[80,640]{1,0:T(8,128)S(1)} %copy-done.7), custom_call_target="tpu_custom_call" | custom-call | flops 1189085184 | bytes 5000000 | tf_op jit(solution)/shard_map/kernel_spectrum/pallas_call | solution.py:368
  52.5 6.1 %all-to-all-done.block_ref = f32[64,16,128]{2,1,0:T(8,128)S(1)} async-done(((f32[64,16,128]{2,1,0:T(8,128)}), f32[64,16,128]{2,1,0:T(8,128)S(1)}, u32[]{:S(2)}, u32[]{:S(2)}) %all-to-all-start) | async-done | bytes 524320 | tf_op jit(solution)/shard_map/all_to_all | solution.py:477
  58.6 1.3 %copy-done.5 = bf16[768,768]{1,0:T(8,128)(2,1)S(1)} copy-done((bf16[768,768]{1,0:T(8,128)(2,1)S(1)}, bf16[768,768]{1,0:T(8,128)(2,1)}, u32[]{:S(2)}) %copy-start.5) | copy-done | bytes 1179672
  59.9 1.6 %spectrum.1 = (f32[160,768]{1,0:T(8,128)S(1)}, f32[30,768]{1,0:T(8,128)S(1)}, f32[30,768]{1,0:T(8,128)S(1)}, f32[1,128]{1,0:T(1,128)S(1)}) custom-call(s32[6]{0:T(128)S(1)} %copy-done.9, f32[64,16,128]{2,1,0:T(8,128)S(1)} %all-to-all-done.block_ref, bf16[768,768]{1,0:T(8,128)(2,1)S(1)} %copy-done.5, bf16[768,768]{1,0:T(8,128)(2,1)S(1)} %copy-done.4, ...), custom_call_target="tpu_custom_call" | custom-call | flops 566231040 | bytes 4000000 | tf_op jit(solution)/shard_map/spectrum/pallas_call | solution.py:343
  61.4 0.0 copy-start.2
  61.5 0.0 collective-permute-done.8.refs_1_
  61.5 0.0 collective-permute-done.9.refs_2_
  61.5 0.0 collective-permute-done.10.refs_3_
  61.5 0.7 pair.1
  62.2 2.5 %collective-permute-start.11 = (f32[80,320]{1,0:T(8,128)S(1)}, f32[80,320]{1,0:T(8,128)S(1)}, u32[]{:S(2)}, u32[]{:S(2)}) collective-permute-start(f32[80,320]{1,0:T(8,128)S(1)} %get-tuple-element.45), channel_id=1, source_target_pairs={{0,64},{64,0},{1,65},{65,1},{2,66},{66,2},{3,67},{67,3},{4,68},{68... | collective-permute-start | bytes 307208 | tf_op jit(solution)/shard_map/ppermute | solution.py:317
  64.7 0.1 collective-permute-start.6
  64.8 2.6 %collective-permute-start.7 = (f32[30,768]{1,0:T(8,128)S(1)}, f32[30,768]{1,0:T(8,128)S(1)}, u32[]{:S(2)}, u32[]{:S(2)}) collective-permute-start(f32[30,768]{1,0:T(8,128)S(1)} %get-tuple-element.41), channel_id=1, source_target_pairs={{64,128},{128,64},{65,129},{129,65},{66,130},{130,66},{67,131},{13... | collective-permute-start | bytes 276488 | tf_op jit(solution)/shard_map/ppermute | solution.py:497
  67.4 0.0 collective-permute-done.6.near_ref
  67.4 3.3 %collective-permute-done.7.cross_ref = f32[30,768]{1,0:T(8,128)S(1)} collective-permute-done((f32[30,768]{1,0:T(8,128)S(1)}, f32[30,768]{1,0:T(8,128)S(1)}, u32[]{:S(2)}, u32[]{:S(2)}) %collective-permute-start.7) | collective-permute-done | bytes 92192 | tf_op jit(solution)/shard_map/ppermute | solution.py:497
  70.7 0.0 collective-permute-done.11.refs_0_.arrived_ref
  70.7 4.2 %filter.1._ = f32[64,16,128]{2,1,0:T(8,128)} custom-call(s32[6]{0:T(128)S(1)} %copy-done.9, f32[1,128]{1,0:T(1,128)S(1)} %get-tuple-element.38.mixing_ref, f32[160,768]{1,0:T(8,128)S(1)} %get-tuple-element.39._.data_ref, f32[30,768]{1,0:T(8,128)S(1)} %collective-permute-done.6.near_ref, f32[30,768]{1,0:T(8,128)S(1)} %collective-permute-done.7.cross_ref, ...), custom_call_target="tpu_custom_call" | custom-call | flops 566231040 | bytes 5000000 | tf_op jit(solution)/shard_map/filter/pallas_call | solution.py:428
  74.9 6.2 %all-to-all-start.1 = ((f32[64,16,128]{2,1,0:T(8,128)}), f32[64,16,128]{2,1,0:T(8,128)S(1)}, u32[]{:S(2)}, u32[]{:S(2)}) async-start(f32[64,16,128]{2,1,0:T(8,128)} %filter.1._), calls=%async_computation.1 | async-start | bytes 1048576 | tf_op jit(solution)/shard_map/all_to_all | solution.py:477
  81.1 0.6 stack.29
  81.7 1.1 %collective-permute-start.12 = (f32[20,320]{1,0:T(8,128)S(1)}, f32[20,320]{1,0:T(8,128)S(1)}, u32[]{:S(2)}, u32[]{:S(2)}) collective-permute-start(f32[20,320]{1,0:T(8,128)S(1)} %get-tuple-element.50), channel_id=1, source_target_pairs={{0,2},{2,4},{4,6},{6,8},{8,10},{10,12},{12,14},{14,0},{1,3},{3,5},... | collective-permute-start | bytes 76808 | tf_op jit(solution)/shard_map/ppermute | solution.py:312
  82.8 1.7 %collective-permute-start.13 = (f32[20,320]{1,0:T(8,128)S(1)}, f32[20,320]{1,0:T(8,128)S(1)}, u32[]{:S(2)}, u32[]{:S(2)}) collective-permute-start(f32[20,320]{1,0:T(8,128)S(1)} %get-tuple-element.51), channel_id=1, source_target_pairs={{0,14},{2,0},{4,2},{6,4},{8,6},{10,8},{12,10},{14,12},{1,15},{3,1}... | collective-permute-start | bytes 76808 | tf_op jit(solution)/shard_map/ppermute | solution.py:312
  84.5 4.9 %collective-permute-start.14 = (f32[20,320]{1,0:T(8,128)S(1)}, f32[20,320]{1,0:T(8,128)S(1)}, u32[]{:S(2)}, u32[]{:S(2)}) collective-permute-start(f32[20,320]{1,0:T(8,128)S(1)} %get-tuple-element.52), channel_id=1, source_target_pairs={{0,8},{2,10},{4,12},{6,14},{8,0},{10,2},{12,4},{14,6},{1,9},{3,11}... | collective-permute-start | bytes 76808 | tf_op jit(solution)/shard_map/ppermute | solution.py:312
  89.4 0.0 collective-permute-start.15
  89.4 4.5 %collective-permute-start.16 = (f32[20,320]{1,0:T(8,128)S(1)}, f32[20,320]{1,0:T(8,128)S(1)}, u32[]{:S(2)}, u32[]{:S(2)}) collective-permute-start(f32[20,320]{1,0:T(8,128)S(1)} %get-tuple-element.54), channel_id=1, source_target_pairs={{0,10},{2,12},{4,14},{6,0},{8,2},{10,4},{12,6},{14,8},{1,11},{3,13... | collective-permute-start | bytes 76808 | tf_op jit(solution)/shard_map/ppermute | solution.py:312
  93.9 0.0 collective-permute-done.12.refs_1_
  93.9 1.1 %collective-permute-start.17 = (f32[20,320]{1,0:T(8,128)S(1)}, f32[20,320]{1,0:T(8,128)S(1)}, u32[]{:S(2)}, u32[]{:S(2)}) collective-permute-start(f32[20,320]{1,0:T(8,128)S(1)} %get-tuple-element.55), channel_id=1, source_target_pairs={{0,4},{2,6},{4,8},{6,10},{8,12},{10,14},{12,0},{14,2},{1,5},{3,7},... | collective-permute-start | bytes 76808 | tf_op jit(solution)/shard_map/ppermute | solution.py:312
  95.0 0.0 collective-permute-done.13.refs_2_
  95.0 2.5 %collective-permute-start.18 = (f32[20,320]{1,0:T(8,128)S(1)}, f32[20,320]{1,0:T(8,128)S(1)}, u32[]{:S(2)}, u32[]{:S(2)}) collective-permute-start(f32[20,320]{1,0:T(8,128)S(1)} %get-tuple-element.56), channel_id=1, source_target_pairs={{0,12},{2,14},{4,0},{6,2},{8,4},{10,6},{12,8},{14,10},{1,13},{3,15... | collective-permute-start | bytes 76808 | tf_op jit(solution)/shard_map/ppermute | solution.py:312
  97.5 1.5 %all-to-all-done.1.block_ref = f32[64,16,128]{2,1,0:T(8,128)S(1)} async-done(((f32[64,16,128]{2,1,0:T(8,128)}), f32[64,16,128]{2,1,0:T(8,128)S(1)}, u32[]{:S(2)}, u32[]{:S(2)}) %all-to-all-start.1) | async-done | bytes 524320 | tf_op jit(solution)/shard_map/all_to_all | solution.py:477
  99.0 1.3 %unpack.1 = (f32[192,640]{1,0:T(8,128)}, f32[8,128]{1,0:T(8,128)S(1)}) custom-call(f32[64,16,128]{2,1,0:T(8,128)S(1)} %all-to-all-done.1.block_ref), custom_call_target="tpu_custom_call" | custom-call | tf_op jit(solution)/shard_map/unpack/pallas_call | solution.py:463
  100.2 0.0 collective-permute-done.14.refs_3_
  100.3 0.0 collective-permute-done.15.refs_4_
  100.3 0.0 collective-permute-done.16.refs_5_
  100.3 0.0 collective-permute-done.17.refs_6_
  100.3 0.0 collective-permute-done.18.refs_7_
  100.3 0.7 last.1
  (21 shorter events, 0.0 us)
Async XLA Ops:
  0.6 5.0 %collective-permute-start = (f32[192,640]{1,0:T(8,128)}, f32[192,640]{1,0:T(8,128)S(1)}, u32[]{:S(2)}, u32[]{:S(2)}) collective-permute-start(f32[192,640]{1,0:T(8,128)} %bitcast.25), channel_id=1, source_target_pairs={{0,64},{64,0},{1,65},{65,1},{2,66},{66,2},{3,67},{67,3},{4,68},{68... | collective-permute-start | bytes 1474568 | tf_op jit(solution)/shard_map/ppermute | solution.py:317
  4.0 2.4 %collective-permute-start.1 = (f32[192,640]{1,0:T(8,128)}, f32[192,640]{1,0:T(8,128)S(1)}, u32[]{:S(2)}, u32[]{:S(2)}) collective-permute-start(f32[192,640]{1,0:T(8,128)} %bitcast.27), channel_id=1, source_target_pairs={{0,64},{64,0},{1,65},{65,1},{2,66},{66,2},{3,67},{67,3},{4,68},{68... | collective-permute-start | bytes 1474568 | tf_op jit(solution)/shard_map/ppermute | solution.py:317
  5.7 0.8 copy-start.14
  6.4 0.8 copy-start.15
  19.5 21.5 %collective-permute-start.3 = (f32[160,1280]{1,0:T(8,128)}, f32[160,1280]{1,0:T(8,128)S(1)}, u32[]{:S(2)}, u32[]{:S(2)}) collective-permute-start(f32[160,1280]{1,0:T(8,128)} %get-tuple-element.34), channel_id=1, source_target_pairs={{0,16},{1,17},{2,18},{3,19},{4,20},{5,21},{6,22},{7,23},{8,24},{9,... | collective-permute-start | bytes 2457608 | tf_op jit(solution)/shard_map/ppermute | solution.py:295
  20.7 20.3 %collective-permute-start.4 = (f32[160,1280]{1,0:T(8,128)}, f32[160,1280]{1,0:T(8,128)S(1)}, u32[]{:S(2)}, u32[]{:S(2)}) collective-permute-start(f32[160,1280]{1,0:T(8,128)} %get-tuple-element.35), channel_id=1, source_target_pairs={{0,32},{1,33},{2,34},{3,35},{4,36},{5,37},{6,38},{7,39},{8,40},{9,... | collective-permute-start | bytes 2457608 | tf_op jit(solution)/shard_map/ppermute | solution.py:295
  21.1 20.4 %collective-permute-start.5 = (f32[160,1280]{1,0:T(8,128)}, f32[160,1280]{1,0:T(8,128)S(1)}, u32[]{:S(2)}, u32[]{:S(2)}) collective-permute-start(f32[160,1280]{1,0:T(8,128)} %get-tuple-element.36), channel_id=1, source_target_pairs={{0,48},{1,49},{2,50},{3,51},{4,52},{5,53},{6,54},{7,55},{8,56},{9,... | collective-permute-start | bytes 2457608 | tf_op jit(solution)/shard_map/ppermute | solution.py:295
  22.8 2.3 %collective-permute-start.2 = (f32[192,640]{1,0:T(8,128)}, f32[192,640]{1,0:T(8,128)S(1)}, u32[]{:S(2)}, u32[]{:S(2)}) collective-permute-start(f32[192,640]{1,0:T(8,128)} %get-tuple-element.32), channel_id=1, source_target_pairs={{0,64},{64,0},{1,65},{65,1},{2,66},{66,2},{3,67},{67,3},{4,68},{68... | collective-permute-start | bytes 1474568 | tf_op jit(solution)/shard_map/ppermute | solution.py:317
  25.1 0.8 copy-start.10
  28.5 30.1 %all-to-all-start = ((f32[64,16,128]{2,1,0:T(8,128)}), f32[64,16,128]{2,1,0:T(8,128)S(1)}, u32[]{:S(2)}, u32[]{:S(2)}) async-start(f32[64,16,128]{2,1,0:T(8,128)} %pack.1), calls=%async_computation | async-start | bytes 1048576 | tf_op jit(solution)/shard_map/all_to_all | solution.py:477
  41.0 0.9 copy-start.11
  41.0 1.2 %copy-start.12 = (f32[160,1280]{1,0:T(8,128)}, f32[160,1280]{1,0:T(8,128)S(1)}, u32[]{:S(2)}) copy-start(f32[160,1280]{1,0:T(8,128)S(1)} %collective-permute-done.4.refs_2_) | copy-start | bytes 2457604
  41.5 0.9 copy-start.13
  42.4 7.8 %copy-start = (bf16[768,768]{1,0:T(8,128)(2,1)S(1)}, bf16[768,768]{1,0:T(8,128)(2,1)}, u32[]{:S(2)}) copy-start(bf16[768,768]{1,0:T(8,128)(2,1)} %constant.38.clone.low_ref) | copy-start | bytes 3538948
  42.4 7.8 %copy-start.1 = (bf16[768,768]{1,0:T(8,128)(2,1)S(1)}, bf16[768,768]{1,0:T(8,128)(2,1)}, u32[]{:S(2)}) copy-start(bf16[768,768]{1,0:T(8,128)(2,1)} %constant.37.clone.top_ref) | copy-start | bytes 3538948
  42.4 7.8 %copy-start.6 = (f32[3,16,7,768]{3,1,2,0:T(8,128)S(1)}, f32[3,16,7,768]{3,1,2,0:T(8,128)}, u32[]{:S(2)}) copy-start(f32[3,16,7,768]{3,1,2,0:T(8,128)} %param.16) | copy-start | bytes 3096580
  45.7 15.8 %collective-permute-start.8 = (f32[80,640]{1,0:T(8,128)}, f32[80,640]{1,0:T(8,128)S(1)}, u32[]{:S(2)}, u32[]{:S(2)}) collective-permute-start(f32[80,640]{1,0:T(8,128)} %get-tuple-element.42), channel_id=1, source_target_pairs={{0,1},{1,0},{2,3},{3,2},{4,5},{5,4},{6,7},{7,6},{8,9},{9,8},{10,11... | collective-permute-start | bytes 614408 | tf_op jit(solution)/shard_map/ppermute | solution.py:295
  46.5 14.9 %collective-permute-start.9 = (f32[80,640]{1,0:T(8,128)}, f32[80,640]{1,0:T(8,128)S(1)}, u32[]{:S(2)}, u32[]{:S(2)}) collective-permute-start(f32[80,640]{1,0:T(8,128)} %get-tuple-element.43), channel_id=1, source_target_pairs={{0,128},{1,129},{2,130},{3,131},{4,132},{5,133},{6,134},{7,135},{8... | collective-permute-start | bytes 614408 | tf_op jit(solution)/shard_map/ppermute | solution.py:295
  49.1 12.3 %collective-permute-start.10 = (f32[80,640]{1,0:T(8,128)}, f32[80,640]{1,0:T(8,128)S(1)}, u32[]{:S(2)}, u32[]{:S(2)}) collective-permute-start(f32[80,640]{1,0:T(8,128)} %get-tuple-element.44), channel_id=1, source_target_pairs={{0,129},{1,128},{2,131},{3,130},{4,133},{5,132},{6,135},{7,134},{8... | collective-permute-start | bytes 614408 | tf_op jit(solution)/shard_map/ppermute | solution.py:295
  50.2 0.9 copy-start.7
  51.1 7.4 %copy-start.4 = (bf16[768,768]{1,0:T(8,128)(2,1)S(1)}, bf16[768,768]{1,0:T(8,128)(2,1)}, u32[]{:S(2)}) copy-start(bf16[768,768]{1,0:T(8,128)(2,1)} %constant.40.clone.low_ref) | copy-start | bytes 3538948
  51.1 7.4 %copy-start.9 = (s32[6]{0:T(128)S(1)}, s32[6]{0:T(128)}, u32[]{:S(2)}) copy-start(s32[6]{0:T(128)} %stack.28.place_ref) | copy-start | bytes 76
  58.6 1.3 %copy-start.5 = (bf16[768,768]{1,0:T(8,128)(2,1)S(1)}, bf16[768,768]{1,0:T(8,128)(2,1)}, u32[]{:S(2)}) copy-start(bf16[768,768]{1,0:T(8,128)(2,1)} %constant.39.clone.top_ref) | copy-start | bytes 3538948
  59.9 1.6 %copy-start.8 = (f32[80,640]{1,0:T(8,128)S(1)}, f32[80,640]{1,0:T(8,128)}, u32[]{:S(2)}) copy-start(f32[80,640]{1,0:T(8,128)} %get-tuple-element.37._.refs_0_) | copy-start | bytes 614404
  59.9 10.8 %copy-start.3 = (bf16[768,768]{1,0:T(8,128)(2,1)S(1)}, bf16[768,768]{1,0:T(8,128)(2,1)}, u32[]{:S(2)}) copy-start(bf16[768,768]{1,0:T(8,128)(2,1)} %constant.41.clone.top_ref) | copy-start | bytes 3538948
  61.4 9.3 %copy-start.2 = (bf16[768,768]{1,0:T(8,128)(2,1)S(1)}, bf16[768,768]{1,0:T(8,128)(2,1)}, u32[]{:S(2)}) copy-start(bf16[768,768]{1,0:T(8,128)(2,1)} %constant.42.clone.low_ref) | copy-start | bytes 3538948
  62.2 8.5 %collective-permute-start.11 = (f32[80,320]{1,0:T(8,128)S(1)}, f32[80,320]{1,0:T(8,128)S(1)}, u32[]{:S(2)}, u32[]{:S(2)}) collective-permute-start(f32[80,320]{1,0:T(8,128)S(1)} %get-tuple-element.45), channel_id=1, source_target_pairs={{0,64},{64,0},{1,65},{65,1},{2,66},{66,2},{3,67},{67,3},{4,68},{68... | collective-permute-start | bytes 307208 | tf_op jit(solution)/shard_map/ppermute | solution.py:317
  64.7 2.7 %collective-permute-start.6 = (f32[30,768]{1,0:T(8,128)S(1)}, f32[30,768]{1,0:T(8,128)S(1)}, u32[]{:S(2)}, u32[]{:S(2)}) collective-permute-start(f32[30,768]{1,0:T(8,128)S(1)} %get-tuple-element.40), channel_id=1, source_target_pairs={{0,64},{64,0},{1,65},{65,1},{2,66},{66,2},{3,67},{67,3},{4,68},{68... | collective-permute-start | bytes 276488 | tf_op jit(solution)/shard_map/ppermute | solution.py:317
  64.8 5.9 %collective-permute-start.7 = (f32[30,768]{1,0:T(8,128)S(1)}, f32[30,768]{1,0:T(8,128)S(1)}, u32[]{:S(2)}, u32[]{:S(2)}) collective-permute-start(f32[30,768]{1,0:T(8,128)S(1)} %get-tuple-element.41), channel_id=1, source_target_pairs={{64,128},{128,64},{65,129},{129,65},{66,130},{130,66},{67,131},{13... | collective-permute-start | bytes 276488 | tf_op jit(solution)/shard_map/ppermute | solution.py:497
  74.9 24.1 %all-to-all-start.1 = ((f32[64,16,128]{2,1,0:T(8,128)}), f32[64,16,128]{2,1,0:T(8,128)S(1)}, u32[]{:S(2)}, u32[]{:S(2)}) async-start(f32[64,16,128]{2,1,0:T(8,128)} %filter.1._), calls=%async_computation.1 | async-start | bytes 1048576 | tf_op jit(solution)/shard_map/all_to_all | solution.py:477
  81.7 12.2 %collective-permute-start.12 = (f32[20,320]{1,0:T(8,128)S(1)}, f32[20,320]{1,0:T(8,128)S(1)}, u32[]{:S(2)}, u32[]{:S(2)}) collective-permute-start(f32[20,320]{1,0:T(8,128)S(1)} %get-tuple-element.50), channel_id=1, source_target_pairs={{0,2},{2,4},{4,6},{6,8},{8,10},{10,12},{12,14},{14,0},{1,3},{3,5},... | collective-permute-start | bytes 76808 | tf_op jit(solution)/shard_map/ppermute | solution.py:312
  82.8 12.2 %collective-permute-start.13 = (f32[20,320]{1,0:T(8,128)S(1)}, f32[20,320]{1,0:T(8,128)S(1)}, u32[]{:S(2)}, u32[]{:S(2)}) collective-permute-start(f32[20,320]{1,0:T(8,128)S(1)} %get-tuple-element.51), channel_id=1, source_target_pairs={{0,14},{2,0},{4,2},{6,4},{8,6},{10,8},{12,10},{14,12},{1,15},{3,1}... | collective-permute-start | bytes 76808 | tf_op jit(solution)/shard_map/ppermute | solution.py:312
  84.5 15.8 %collective-permute-start.14 = (f32[20,320]{1,0:T(8,128)S(1)}, f32[20,320]{1,0:T(8,128)S(1)}, u32[]{:S(2)}, u32[]{:S(2)}) collective-permute-start(f32[20,320]{1,0:T(8,128)S(1)} %get-tuple-element.52), channel_id=1, source_target_pairs={{0,8},{2,10},{4,12},{6,14},{8,0},{10,2},{12,4},{14,6},{1,9},{3,11}... | collective-permute-start | bytes 76808 | tf_op jit(solution)/shard_map/ppermute | solution.py:312
  89.4 10.9 %collective-permute-start.15 = (f32[20,320]{1,0:T(8,128)S(1)}, f32[20,320]{1,0:T(8,128)S(1)}, u32[]{:S(2)}, u32[]{:S(2)}) collective-permute-start(f32[20,320]{1,0:T(8,128)S(1)} %get-tuple-element.53), channel_id=1, source_target_pairs={{0,6},{2,8},{4,10},{6,12},{8,14},{10,0},{12,2},{14,4},{1,7},{3,9},... | collective-permute-start | bytes 76808 | tf_op jit(solution)/shard_map/ppermute | solution.py:312
  89.4 10.9 %collective-permute-start.16 = (f32[20,320]{1,0:T(8,128)S(1)}, f32[20,320]{1,0:T(8,128)S(1)}, u32[]{:S(2)}, u32[]{:S(2)}) collective-permute-start(f32[20,320]{1,0:T(8,128)S(1)} %get-tuple-element.54), channel_id=1, source_target_pairs={{0,10},{2,12},{4,14},{6,0},{8,2},{10,4},{12,6},{14,8},{1,11},{3,13... | collective-permute-start | bytes 76808 | tf_op jit(solution)/shard_map/ppermute | solution.py:312
  93.9 6.4 %collective-permute-start.17 = (f32[20,320]{1,0:T(8,128)S(1)}, f32[20,320]{1,0:T(8,128)S(1)}, u32[]{:S(2)}, u32[]{:S(2)}) collective-permute-start(f32[20,320]{1,0:T(8,128)S(1)} %get-tuple-element.55), channel_id=1, source_target_pairs={{0,4},{2,6},{4,8},{6,10},{8,12},{10,14},{12,0},{14,2},{1,5},{3,7},... | collective-permute-start | bytes 76808 | tf_op jit(solution)/shard_map/ppermute | solution.py:312
  95.0 5.3 %collective-permute-start.18 = (f32[20,320]{1,0:T(8,128)S(1)}, f32[20,320]{1,0:T(8,128)S(1)}, u32[]{:S(2)}, u32[]{:S(2)}) collective-permute-start(f32[20,320]{1,0:T(8,128)S(1)} %get-tuple-element.56), channel_id=1, source_target_pairs={{0,12},{2,14},{4,0},{6,2},{8,4},{10,6},{12,8},{14,10},{1,13},{3,15... | collective-permute-start | bytes 76808 | tf_op jit(solution)/shard_map/ppermute | solution.py:312

commit v14 on v13

--- a/solution.py
+++ b/solution.py
@@ -307,7 +307,7 @@
 
 
 def exchange_z(pieces):
-    far = (1, 7, 4, 3, 5, 2, 6)
+    far = (4, 3, 5, 1, 7, 2, 6)
     return [pieces[0]] + [
         lax.ppermute(pieces[m], "z", [(z, (z + m) % 8) for z in range(8)]) for m in far
     ]

time: 102 us -> 103 us (level)
  waiting for transfers between devices: 14.8 us -> 16.4 us
    ppermute x7, waiting for transfers between devices: 0.02 us -> 3.09 us  [exchange_z(): lax.ppermute(pieces[m], 'z', [(z, (z + m) % 8) for z in range(8)])]
    all_to_all x2, waiting for transfers between devices: 7.57 us -> 6.07 us  [across(): return lax.all_to_all(block, LON, split_axis=0, concat_axis=0, tiled=True)]
  transfers between devices with their start and end apart: 21 -> 21, of which waited for: 7 -> 7; matrix products, arithmetic and copies ran while one was open for 1% -> 1% of each run, Pallas kernels for 11% -> 10%
where the time goes in v14:
time: 103 us
  starting transfers between devices  51.5 us (50%)
  Pallas kernels  28.6 us (28%)
  waiting for transfers between devices  16.4 us (16%)
  local copies, waits for them, and re-layouts  5.33 us (5%)
    all_to_all x2, starting transfers between devices, across(): return lax.all_to_all(block, LON, split_axis=0, concat_axis=0, tiled=True)  18.7 us
    ppermute x7, starting transfers between devices, exchange_z(): lax.ppermute(pieces[m], 'z', [(z, (z + m) % 8) for z in range(8)])  15.7 us
    pallas_call x1, Pallas kernels, mlp(): pl.pallas_call(mlp_kernel, grid_spec=pltpu.PrefetchScalarGridSpec(num_sca...  12.4 us
    pallas_call x5, Pallas kernels, small(): pl.pallas_call(kernel, grid=(1,) if piped else (), in_specs=[pl.BlockSpec...  7.84 us
    ppermute x6, starting transfers between devices, permute(): return lax.ppermute(value, AXES, pairs)  7.77 us
    ppermute x5, starting transfers between devices, to_core(): return lax.ppermute(value, 'co', [(0, 1), (1, 0)])  6.65 us
    all_to_all x2, waiting for transfers between devices, across(): return lax.all_to_all(block, LON, split_axis=0, concat_axis=0, tiled=True)  6.07 us
    unnamed x32, local copies, waits for them, and re-layouts  4.72 us
  transfers between devices with their start and end apart: 21, of which 7 were waited for; matrix products, arithmetic and copies ran while one was open for 1% of the time, Pallas kernels for 10%

profile of v14, /device:TPU:1, one launch (start us, length us, event | category | flops | bytes accessed | tf_op | source)
XLA Modules:
  0.0 102.5 jit_solution(17922297120556659764)
XLA Ops:
  0.6 3.3 %collective-permute-start = (f32[192,640]{1,0:T(8,128)}, f32[192,640]{1,0:T(8,128)S(1)}, u32[]{:S(2)}, u32[]{:S(2)}) collective-permute-start(f32[192,640]{1,0:T(8,128)} %bitcast.25), channel_id=1, source_target_pairs={{0,64},{64,0},{1,65},{65,1},{2,66},{66,2},{3,67},{67,3},{4,68},{68... | collective-permute-start | bytes 1474568 | tf_op jit(solution)/shard_map/ppermute | solution.py:317
  4.0 0.1 collective-permute-start.1
  4.1 0.6 stack.28.place_ref
  4.7 1.0 collective-permute-done.act_other_ref
  5.7 0.7 collective-permute-done.1.cot_other_ref
  6.4 0.1 copy-done.14
  6.4 0.7 copy-done.15
  7.1 12.4 %mlp.1 = (f32[192,640]{1,0:T(8,128)}, f32[192,640]{1,0:T(8,128)}, f32[160,1280]{1,0:T(8,128)}, f32[160,1280]{1,0:T(8,128)}, f32[160,1280]{1,0:T(8,128)}, /*index=5*/f32[160,1280]{1,0:T(8,128)}) custom-call(s32[6]{0:T(128)} %stack.28.place_ref, f32[192,640]{1,0:T(8,128)} %bitcast.26, f32[192,640]{1,0:T(8,128)} %copy-done.14, f32[192,640]{1,0:T(8,128)} %bitcast.28, ...), custom_call_target="tpu_custom_call" | custom-call | flops 4718592000 | bytes 12000000 | tf_op jit(solution)/shard_map/mlp/pallas_call | solution.py:190
  19.5 1.2 %collective-permute-start.3 = (f32[160,1280]{1,0:T(8,128)}, f32[160,1280]{1,0:T(8,128)S(1)}, u32[]{:S(2)}, u32[]{:S(2)}) collective-permute-start(f32[160,1280]{1,0:T(8,128)} %get-tuple-element.34), channel_id=1, source_target_pairs={{0,16},{1,17},{2,18},{3,19},{4,20},{5,21},{6,22},{7,23},{8,24},{9,... | collective-permute-start | bytes 2457608 | tf_op jit(solution)/shard_map/ppermute | solution.py:295
  20.7 0.4 collective-permute-start.4
  21.1 1.7 %collective-permute-start.5 = (f32[160,1280]{1,0:T(8,128)}, f32[160,1280]{1,0:T(8,128)S(1)}, u32[]{:S(2)}, u32[]{:S(2)}) collective-permute-start(f32[160,1280]{1,0:T(8,128)} %get-tuple-element.36), channel_id=1, source_target_pairs={{0,48},{1,49},{2,50},{3,51},{4,52},{5,53},{6,54},{7,55},{8,56},{9,... | collective-permute-start | bytes 2457608 | tf_op jit(solution)/shard_map/ppermute | solution.py:295
  22.8 0.6 collective-permute-start.2
  23.4 1.7 %collective-permute-done.2.arrived_ref = f32[192,640]{1,0:T(8,128)S(1)} collective-permute-done((f32[192,640]{1,0:T(8,128)}, f32[192,640]{1,0:T(8,128)S(1)}, u32[]{:S(2)}, u32[]{:S(2)}) %collective-permute-start.2) | collective-permute-done | bytes 491552 | tf_op jit(solution)/shard_map/ppermute | solution.py:317
  25.1 0.8 copy-done.10
  25.9 2.6 %pack.1 = f32[64,16,128]{2,1,0:T(8,128)} custom-call(s32[6]{0:T(128)} %stack.28.place_ref, f32[3,10]{1,0:T(4,128)} %bitcast.22, f32[192,640]{1,0:T(8,128)} %get-tuple-element.31.unit_ref, f32[192,640]{1,0:T(8,128)} %copy-done.10), custom_call_target="tpu_custom_call" | custom-call | tf_op jit(solution)/shard_map/pack/pallas_call | solution.py:276
  28.5 12.5 %all-to-all-start = ((f32[64,16,128]{2,1,0:T(8,128)}), f32[64,16,128]{2,1,0:T(8,128)S(1)}, u32[]{:S(2)}, u32[]{:S(2)}) async-start(f32[64,16,128]{2,1,0:T(8,128)} %pack.1), calls=%async_computation | async-start | bytes 1048576 | tf_op jit(solution)/shard_map/all_to_all | solution.py:477
  41.0 0.0 collective-permute-done.3.refs_1_
  41.0 0.0 collective-permute-done.4.refs_2_
  41.0 0.0 copy-start.12
  41.0 0.5 collective-permute-done.5.refs_3_
  41.5 0.4 copy-done.11
  41.9 0.3 copy-done.12
  42.2 0.3 copy-done.13
  42.4 3.3 %swap.1 = (f32[80,640]{1,0:T(8,128)}, f32[80,640]{1,0:T(8,128)}, f32[80,640]{1,0:T(8,128)}, f32[80,640]{1,0:T(8,128)}) custom-call(s32[6]{0:T(128)} %stack.28.place_ref, f32[160,1280]{1,0:T(8,128)} %get-tuple-element.33.refs_0_, f32[160,1280]{1,0:T(8,128)} %copy-done.11, f32[160,1280]{1,0:T(8,128)} %copy-done.12, f32[160,1280]{1,0:T(8,128)} %copy-done.13), custom_call_target="tpu_custom_call" | custom-call | flops 10000000000 | bytes 4000000 | tf_op jit(solution)/shard_map/swap/pallas_call | solution.py:276
  45.7 0.8 collective-permute-start.8
  46.5 2.6 %collective-permute-start.9 = (f32[80,640]{1,0:T(8,128)}, f32[80,640]{1,0:T(8,128)S(1)}, u32[]{:S(2)}, u32[]{:S(2)}) collective-permute-start(f32[80,640]{1,0:T(8,128)} %get-tuple-element.43), channel_id=1, source_target_pairs={{0,128},{1,129},{2,130},{3,131},{4,132},{5,133},{6,134},{7,135},{8... | collective-permute-start | bytes 614408 | tf_op jit(solution)/shard_map/ppermute | solution.py:295
  49.1 1.1 %collective-permute-start.10 = (f32[80,640]{1,0:T(8,128)}, f32[80,640]{1,0:T(8,128)S(1)}, u32[]{:S(2)}, u32[]{:S(2)}) collective-permute-start(f32[80,640]{1,0:T(8,128)} %get-tuple-element.44), channel_id=1, source_target_pairs={{0,129},{1,128},{2,131},{3,130},{4,133},{5,132},{6,135},{7,134},{8... | collective-permute-start | bytes 614408 | tf_op jit(solution)/shard_map/ppermute | solution.py:295
  50.2 0.0 copy-done
  50.2 0.9 copy-done.7
  51.1 1.4 %kernel_spectrum.1._.kernel_ref = f32[336,768]{1,0:T(8,128)S(1)} custom-call(f32[336,768]{1,0:T(8,128)S(1)} %bitcast.21, bf16[768,768]{1,0:T(8,128)(2,1)S(1)} %copy-done.1, bf16[768,768]{1,0:T(8,128)(2,1)S(1)} %copy-done, f32[80,640]{1,0:T(8,128)S(1)} %copy-done.7), custom_call_target="tpu_custom_call" | custom-call | flops 1189085184 | bytes 5000000 | tf_op jit(solution)/shard_map/kernel_spectrum/pallas_call | solution.py:368
  52.5 6.1 %all-to-all-done.block_ref = f32[64,16,128]{2,1,0:T(8,128)S(1)} async-done(((f32[64,16,128]{2,1,0:T(8,128)}), f32[64,16,128]{2,1,0:T(8,128)S(1)}, u32[]{:S(2)}, u32[]{:S(2)}) %all-to-all-start) | async-done | bytes 524320 | tf_op jit(solution)/shard_map/all_to_all | solution.py:477
  58.6 1.3 %copy-done.5 = bf16[768,768]{1,0:T(8,128)(2,1)S(1)} copy-done((bf16[768,768]{1,0:T(8,128)(2,1)S(1)}, bf16[768,768]{1,0:T(8,128)(2,1)}, u32[]{:S(2)}) %copy-start.5) | copy-done | bytes 1179672
  59.9 1.6 %spectrum.1 = (f32[160,768]{1,0:T(8,128)S(1)}, f32[30,768]{1,0:T(8,128)S(1)}, f32[30,768]{1,0:T(8,128)S(1)}, f32[1,128]{1,0:T(1,128)S(1)}) custom-call(s32[6]{0:T(128)S(1)} %copy-done.9, f32[64,16,128]{2,1,0:T(8,128)S(1)} %all-to-all-done.block_ref, bf16[768,768]{1,0:T(8,128)(2,1)S(1)} %copy-done.5, bf16[768,768]{1,0:T(8,128)(2,1)S(1)} %copy-done.4, ...), custom_call_target="tpu_custom_call" | custom-call | flops 566231040 | bytes 4000000 | tf_op jit(solution)/shard_map/spectrum/pallas_call | solution.py:343
  61.4 0.0 copy-start.2
  61.5 0.0 collective-permute-done.8.refs_1_
  61.5 0.0 collective-permute-done.9.refs_2_
  61.5 0.0 collective-permute-done.10.refs_3_
  61.5 0.7 pair.1
  62.2 2.5 %collective-permute-start.11 = (f32[80,320]{1,0:T(8,128)S(1)}, f32[80,320]{1,0:T(8,128)S(1)}, u32[]{:S(2)}, u32[]{:S(2)}) collective-permute-start(f32[80,320]{1,0:T(8,128)S(1)} %get-tuple-element.45), channel_id=1, source_target_pairs={{0,64},{64,0},{1,65},{65,1},{2,66},{66,2},{3,67},{67,3},{4,68},{68... | collective-permute-start | bytes 307208 | tf_op jit(solution)/shard_map/ppermute | solution.py:317
  64.7 0.1 collective-permute-start.6
  64.8 2.6 %collective-permute-start.7 = (f32[30,768]{1,0:T(8,128)S(1)}, f32[30,768]{1,0:T(8,128)S(1)}, u32[]{:S(2)}, u32[]{:S(2)}) collective-permute-start(f32[30,768]{1,0:T(8,128)S(1)} %get-tuple-element.41), channel_id=1, source_target_pairs={{64,128},{128,64},{65,129},{129,65},{66,130},{130,66},{67,131},{13... | collective-permute-start | bytes 276488 | tf_op jit(solution)/shard_map/ppermute | solution.py:497
  67.4 0.0 collective-permute-done.6.near_ref
  67.4 3.3 %collective-permute-done.7.cross_ref = f32[30,768]{1,0:T(8,128)S(1)} collective-permute-done((f32[30,768]{1,0:T(8,128)S(1)}, f32[30,768]{1,0:T(8,128)S(1)}, u32[]{:S(2)}, u32[]{:S(2)}) %collective-permute-start.7) | collective-permute-done | bytes 92192 | tf_op jit(solution)/shard_map/ppermute | solution.py:497
  70.7 0.0 collective-permute-done.11.refs_0_.arrived_ref
  70.7 4.2 %filter.1._ = f32[64,16,128]{2,1,0:T(8,128)} custom-call(s32[6]{0:T(128)S(1)} %copy-done.9, f32[1,128]{1,0:T(1,128)S(1)} %get-tuple-element.38.mixing_ref, f32[160,768]{1,0:T(8,128)S(1)} %get-tuple-element.39._.data_ref, f32[30,768]{1,0:T(8,128)S(1)} %collective-permute-done.6.near_ref, f32[30,768]{1,0:T(8,128)S(1)} %collective-permute-done.7.cross_ref, ...), custom_call_target="tpu_custom_call" | custom-call | flops 566231040 | bytes 5000000 | tf_op jit(solution)/shard_map/filter/pallas_call | solution.py:428
  74.9 6.2 %all-to-all-start.1 = ((f32[64,16,128]{2,1,0:T(8,128)}), f32[64,16,128]{2,1,0:T(8,128)S(1)}, u32[]{:S(2)}, u32[]{:S(2)}) async-start(f32[64,16,128]{2,1,0:T(8,128)} %filter.1._), calls=%async_computation.1 | async-start | bytes 1048576 | tf_op jit(solution)/shard_map/all_to_all | solution.py:477
  81.1 0.6 stack.29
  81.7 5.0 %collective-permute-start.12 = (f32[20,320]{1,0:T(8,128)S(1)}, f32[20,320]{1,0:T(8,128)S(1)}, u32[]{:S(2)}, u32[]{:S(2)}) collective-permute-start(f32[20,320]{1,0:T(8,128)S(1)} %get-tuple-element.50), channel_id=1, source_target_pairs={{0,8},{2,10},{4,12},{6,14},{8,0},{10,2},{12,4},{14,6},{1,9},{3,11}... | collective-permute-start | bytes 76808 | tf_op jit(solution)/shard_map/ppermute | solution.py:312
  86.7 0.3 collective-permute-start.13
  87.0 4.2 %collective-permute-start.14 = (f32[20,320]{1,0:T(8,128)S(1)}, f32[20,320]{1,0:T(8,128)S(1)}, u32[]{:S(2)}, u32[]{:S(2)}) collective-permute-start(f32[20,320]{1,0:T(8,128)S(1)} %get-tuple-element.52), channel_id=1, source_target_pairs={{0,10},{2,12},{4,14},{6,0},{8,2},{10,4},{12,6},{14,8},{1,11},{3,13... | collective-permute-start | bytes 76808 | tf_op jit(solution)/shard_map/ppermute | solution.py:312
  91.2 0.3 collective-permute-start.15
  91.5 2.4 %collective-permute-start.16 = (f32[20,320]{1,0:T(8,128)S(1)}, f32[20,320]{1,0:T(8,128)S(1)}, u32[]{:S(2)}, u32[]{:S(2)}) collective-permute-start(f32[20,320]{1,0:T(8,128)S(1)} %get-tuple-element.54), channel_id=1, source_target_pairs={{0,14},{2,0},{4,2},{6,4},{8,6},{10,8},{12,10},{14,12},{1,15},{3,1}... | collective-permute-start | bytes 76808 | tf_op jit(solution)/shard_map/ppermute | solution.py:312
  93.9 3.0 %collective-permute-done.12.refs_1_ = f32[20,320]{1,0:T(8,128)S(1)} collective-permute-done((f32[20,320]{1,0:T(8,128)S(1)}, f32[20,320]{1,0:T(8,128)S(1)}, u32[]{:S(2)}, u32[]{:S(2)}) %collective-permute-start.12) | collective-permute-done | bytes 25632 | tf_op jit(solution)/shard_map/ppermute | solution.py:312
  96.9 0.4 collective-permute-start.17
  97.3 0.0 collective-permute-done.13.refs_2_
  97.3 3.2 %collective-permute-start.18 = (f32[20,320]{1,0:T(8,128)S(1)}, f32[20,320]{1,0:T(8,128)S(1)}, u32[]{:S(2)}, u32[]{:S(2)}) collective-permute-start(f32[20,320]{1,0:T(8,128)S(1)} %get-tuple-element.56), channel_id=1, source_target_pairs={{0,12},{2,14},{4,0},{6,2},{8,4},{10,6},{12,8},{14,10},{1,13},{3,15... | collective-permute-start | bytes 76808 | tf_op jit(solution)/shard_map/ppermute | solution.py:312
  100.5 0.0 all-to-all-done.1.block_ref
  100.5 1.3 %unpack.1 = (f32[192,640]{1,0:T(8,128)}, f32[8,128]{1,0:T(8,128)S(1)}) custom-call(f32[64,16,128]{2,1,0:T(8,128)S(1)} %all-to-all-done.1.block_ref), custom_call_target="tpu_custom_call" | custom-call | tf_op jit(solution)/shard_map/unpack/pallas_call | solution.py:463
  101.8 0.0 collective-permute-done.14.refs_3_
  101.8 0.0 collective-permute-done.15.refs_4_
  101.8 0.0 collective-permute-done.16.refs_5_
  101.8 0.0 collective-permute-done.17.refs_6_
  101.8 0.0 collective-permute-done.18.refs_7_
  101.9 0.7 last.1
  (21 shorter events, 0.0 us)
Async XLA Ops:
  0.6 5.0 %collective-permute-start = (f32[192,640]{1,0:T(8,128)}, f32[192,640]{1,0:T(8,128)S(1)}, u32[]{:S(2)}, u32[]{:S(2)}) collective-permute-start(f32[192,640]{1,0:T(8,128)} %bitcast.25), channel_id=1, source_target_pairs={{0,64},{64,0},{1,65},{65,1},{2,66},{66,2},{3,67},{67,3},{4,68},{68... | collective-permute-start | bytes 1474568 | tf_op jit(solution)/shard_map/ppermute | solution.py:317
  4.0 2.4 %collective-permute-start.1 = (f32[192,640]{1,0:T(8,128)}, f32[192,640]{1,0:T(8,128)S(1)}, u32[]{:S(2)}, u32[]{:S(2)}) collective-permute-start(f32[192,640]{1,0:T(8,128)} %bitcast.27), channel_id=1, source_target_pairs={{0,64},{64,0},{1,65},{65,1},{2,66},{66,2},{3,67},{67,3},{4,68},{68... | collective-permute-start | bytes 1474568 | tf_op jit(solution)/shard_map/ppermute | solution.py:317
  5.7 0.8 copy-start.14
  6.4 0.8 copy-start.15
  19.5 21.5 %collective-permute-start.3 = (f32[160,1280]{1,0:T(8,128)}, f32[160,1280]{1,0:T(8,128)S(1)}, u32[]{:S(2)}, u32[]{:S(2)}) collective-permute-start(f32[160,1280]{1,0:T(8,128)} %get-tuple-element.34), channel_id=1, source_target_pairs={{0,16},{1,17},{2,18},{3,19},{4,20},{5,21},{6,22},{7,23},{8,24},{9,... | collective-permute-start | bytes 2457608 | tf_op jit(solution)/shard_map/ppermute | solution.py:295
  20.7 20.3 %collective-permute-start.4 = (f32[160,1280]{1,0:T(8,128)}, f32[160,1280]{1,0:T(8,128)S(1)}, u32[]{:S(2)}, u32[]{:S(2)}) collective-permute-start(f32[160,1280]{1,0:T(8,128)} %get-tuple-element.35), channel_id=1, source_target_pairs={{0,32},{1,33},{2,34},{3,35},{4,36},{5,37},{6,38},{7,39},{8,40},{9,... | collective-permute-start | bytes 2457608 | tf_op jit(solution)/shard_map/ppermute | solution.py:295
  21.1 20.4 %collective-permute-start.5 = (f32[160,1280]{1,0:T(8,128)}, f32[160,1280]{1,0:T(8,128)S(1)}, u32[]{:S(2)}, u32[]{:S(2)}) collective-permute-start(f32[160,1280]{1,0:T(8,128)} %get-tuple-element.36), channel_id=1, source_target_pairs={{0,48},{1,49},{2,50},{3,51},{4,52},{5,53},{6,54},{7,55},{8,56},{9,... | collective-permute-start | bytes 2457608 | tf_op jit(solution)/shard_map/ppermute | solution.py:295
  22.8 2.3 %collective-permute-start.2 = (f32[192,640]{1,0:T(8,128)}, f32[192,640]{1,0:T(8,128)S(1)}, u32[]{:S(2)}, u32[]{:S(2)}) collective-permute-start(f32[192,640]{1,0:T(8,128)} %get-tuple-element.32), channel_id=1, source_target_pairs={{0,64},{64,0},{1,65},{65,1},{2,66},{66,2},{3,67},{67,3},{4,68},{68... | collective-permute-start | bytes 1474568 | tf_op jit(solution)/shard_map/ppermute | solution.py:317
  25.1 0.8 copy-start.10
  28.5 30.1 %all-to-all-start = ((f32[64,16,128]{2,1,0:T(8,128)}), f32[64,16,128]{2,1,0:T(8,128)S(1)}, u32[]{:S(2)}, u32[]{:S(2)}) async-start(f32[64,16,128]{2,1,0:T(8,128)} %pack.1), calls=%async_computation | async-start | bytes 1048576 | tf_op jit(solution)/shard_map/all_to_all | solution.py:477
  41.0 0.9 copy-start.11
  41.0 1.2 %copy-start.12 = (f32[160,1280]{1,0:T(8,128)}, f32[160,1280]{1,0:T(8,128)S(1)}, u32[]{:S(2)}) copy-start(f32[160,1280]{1,0:T(8,128)S(1)} %collective-permute-done.4.refs_2_) | copy-start | bytes 2457604
  41.5 0.9 copy-start.13
  42.4 7.8 %copy-start = (bf16[768,768]{1,0:T(8,128)(2,1)S(1)}, bf16[768,768]{1,0:T(8,128)(2,1)}, u32[]{:S(2)}) copy-start(bf16[768,768]{1,0:T(8,128)(2,1)} %constant.38.clone.low_ref) | copy-start | bytes 3538948
  42.4 7.8 %copy-start.1 = (bf16[768,768]{1,0:T(8,128)(2,1)S(1)}, bf16[768,768]{1,0:T(8,128)(2,1)}, u32[]{:S(2)}) copy-start(bf16[768,768]{1,0:T(8,128)(2,1)} %constant.37.clone.top_ref) | copy-start | bytes 3538948
  42.4 7.8 %copy-start.6 = (f32[3,16,7,768]{3,1,2,0:T(8,128)S(1)}, f32[3,16,7,768]{3,1,2,0:T(8,128)}, u32[]{:S(2)}) copy-start(f32[3,16,7,768]{3,1,2,0:T(8,128)} %param.16) | copy-start | bytes 3096580
  45.7 15.8 %collective-permute-start.8 = (f32[80,640]{1,0:T(8,128)}, f32[80,640]{1,0:T(8,128)S(1)}, u32[]{:S(2)}, u32[]{:S(2)}) collective-permute-start(f32[80,640]{1,0:T(8,128)} %get-tuple-element.42), channel_id=1, source_target_pairs={{0,1},{1,0},{2,3},{3,2},{4,5},{5,4},{6,7},{7,6},{8,9},{9,8},{10,11... | collective-permute-start | bytes 614408 | tf_op jit(solution)/shard_map/ppermute | solution.py:295
  46.5 14.9 %collective-permute-start.9 = (f32[80,640]{1,0:T(8,128)}, f32[80,640]{1,0:T(8,128)S(1)}, u32[]{:S(2)}, u32[]{:S(2)}) collective-permute-start(f32[80,640]{1,0:T(8,128)} %get-tuple-element.43), channel_id=1, source_target_pairs={{0,128},{1,129},{2,130},{3,131},{4,132},{5,133},{6,134},{7,135},{8... | collective-permute-start | bytes 614408 | tf_op jit(solution)/shard_map/ppermute | solution.py:295
  49.1 12.3 %collective-permute-start.10 = (f32[80,640]{1,0:T(8,128)}, f32[80,640]{1,0:T(8,128)S(1)}, u32[]{:S(2)}, u32[]{:S(2)}) collective-permute-start(f32[80,640]{1,0:T(8,128)} %get-tuple-element.44), channel_id=1, source_target_pairs={{0,129},{1,128},{2,131},{3,130},{4,133},{5,132},{6,135},{7,134},{8... | collective-permute-start | bytes 614408 | tf_op jit(solution)/shard_map/ppermute | solution.py:295
  50.2 0.9 copy-start.7
  51.1 7.4 %copy-start.4 = (bf16[768,768]{1,0:T(8,128)(2,1)S(1)}, bf16[768,768]{1,0:T(8,128)(2,1)}, u32[]{:S(2)}) copy-start(bf16[768,768]{1,0:T(8,128)(2,1)} %constant.40.clone.low_ref) | copy-start | bytes 3538948
  51.1 7.4 %copy-start.9 = (s32[6]{0:T(128)S(1)}, s32[6]{0:T(128)}, u32[]{:S(2)}) copy-start(s32[6]{0:T(128)} %stack.28.place_ref) | copy-start | bytes 76
  58.6 1.3 %copy-start.5 = (bf16[768,768]{1,0:T(8,128)(2,1)S(1)}, bf16[768,768]{1,0:T(8,128)(2,1)}, u32[]{:S(2)}) copy-start(bf16[768,768]{1,0:T(8,128)(2,1)} %constant.39.clone.top_ref) | copy-start | bytes 3538948
  59.9 1.6 %copy-start.8 = (f32[80,640]{1,0:T(8,128)S(1)}, f32[80,640]{1,0:T(8,128)}, u32[]{:S(2)}) copy-start(f32[80,640]{1,0:T(8,128)} %get-tuple-element.37._.refs_0_) | copy-start | bytes 614404
  59.9 10.8 %copy-start.3 = (bf16[768,768]{1,0:T(8,128)(2,1)S(1)}, bf16[768,768]{1,0:T(8,128)(2,1)}, u32[]{:S(2)}) copy-start(bf16[768,768]{1,0:T(8,128)(2,1)} %constant.41.clone.top_ref) | copy-start | bytes 3538948
  61.4 9.3 %copy-start.2 = (bf16[768,768]{1,0:T(8,128)(2,1)S(1)}, bf16[768,768]{1,0:T(8,128)(2,1)}, u32[]{:S(2)}) copy-start(bf16[768,768]{1,0:T(8,128)(2,1)} %constant.42.clone.low_ref) | copy-start | bytes 3538948
  62.2 8.5 %collective-permute-start.11 = (f32[80,320]{1,0:T(8,128)S(1)}, f32[80,320]{1,0:T(8,128)S(1)}, u32[]{:S(2)}, u32[]{:S(2)}) collective-permute-start(f32[80,320]{1,0:T(8,128)S(1)} %get-tuple-element.45), channel_id=1, source_target_pairs={{0,64},{64,0},{1,65},{65,1},{2,66},{66,2},{3,67},{67,3},{4,68},{68... | collective-permute-start | bytes 307208 | tf_op jit(solution)/shard_map/ppermute | solution.py:317
  64.7 2.7 %collective-permute-start.6 = (f32[30,768]{1,0:T(8,128)S(1)}, f32[30,768]{1,0:T(8,128)S(1)}, u32[]{:S(2)}, u32[]{:S(2)}) collective-permute-start(f32[30,768]{1,0:T(8,128)S(1)} %get-tuple-element.40), channel_id=1, source_target_pairs={{0,64},{64,0},{1,65},{65,1},{2,66},{66,2},{3,67},{67,3},{4,68},{68... | collective-permute-start | bytes 276488 | tf_op jit(solution)/shard_map/ppermute | solution.py:317
  64.8 5.9 %collective-permute-start.7 = (f32[30,768]{1,0:T(8,128)S(1)}, f32[30,768]{1,0:T(8,128)S(1)}, u32[]{:S(2)}, u32[]{:S(2)}) collective-permute-start(f32[30,768]{1,0:T(8,128)S(1)} %get-tuple-element.41), channel_id=1, source_target_pairs={{64,128},{128,64},{65,129},{129,65},{66,130},{130,66},{67,131},{13... | collective-permute-start | bytes 276488 | tf_op jit(solution)/shard_map/ppermute | solution.py:497
  74.9 25.6 %all-to-all-start.1 = ((f32[64,16,128]{2,1,0:T(8,128)}), f32[64,16,128]{2,1,0:T(8,128)S(1)}, u32[]{:S(2)}, u32[]{:S(2)}) async-start(f32[64,16,128]{2,1,0:T(8,128)} %filter.1._), calls=%async_computation.1 | async-start | bytes 1048576 | tf_op jit(solution)/shard_map/all_to_all | solution.py:477
  81.7 15.2 %collective-permute-start.12 = (f32[20,320]{1,0:T(8,128)S(1)}, f32[20,320]{1,0:T(8,128)S(1)}, u32[]{:S(2)}, u32[]{:S(2)}) collective-permute-start(f32[20,320]{1,0:T(8,128)S(1)} %get-tuple-element.50), channel_id=1, source_target_pairs={{0,8},{2,10},{4,12},{6,14},{8,0},{10,2},{12,4},{14,6},{1,9},{3,11}... | collective-permute-start | bytes 76808 | tf_op jit(solution)/shard_map/ppermute | solution.py:312
  86.7 10.6 %collective-permute-start.13 = (f32[20,320]{1,0:T(8,128)S(1)}, f32[20,320]{1,0:T(8,128)S(1)}, u32[]{:S(2)}, u32[]{:S(2)}) collective-permute-start(f32[20,320]{1,0:T(8,128)S(1)} %get-tuple-element.51), channel_id=1, source_target_pairs={{0,6},{2,8},{4,10},{6,12},{8,14},{10,0},{12,2},{14,4},{1,7},{3,9},... | collective-permute-start | bytes 76808 | tf_op jit(solution)/shard_map/ppermute | solution.py:312
  87.0 14.8 %collective-permute-start.14 = (f32[20,320]{1,0:T(8,128)S(1)}, f32[20,320]{1,0:T(8,128)S(1)}, u32[]{:S(2)}, u32[]{:S(2)}) collective-permute-start(f32[20,320]{1,0:T(8,128)S(1)} %get-tuple-element.52), channel_id=1, source_target_pairs={{0,10},{2,12},{4,14},{6,0},{8,2},{10,4},{12,6},{14,8},{1,11},{3,13... | collective-permute-start | bytes 76808 | tf_op jit(solution)/shard_map/ppermute | solution.py:312
  91.2 10.6 %collective-permute-start.15 = (f32[20,320]{1,0:T(8,128)S(1)}, f32[20,320]{1,0:T(8,128)S(1)}, u32[]{:S(2)}, u32[]{:S(2)}) collective-permute-start(f32[20,320]{1,0:T(8,128)S(1)} %get-tuple-element.53), channel_id=1, source_target_pairs={{0,2},{2,4},{4,6},{6,8},{8,10},{10,12},{12,14},{14,0},{1,3},{3,5},... | collective-permute-start | bytes 76808 | tf_op jit(solution)/shard_map/ppermute | solution.py:312
  91.5 10.3 %collective-permute-start.16 = (f32[20,320]{1,0:T(8,128)S(1)}, f32[20,320]{1,0:T(8,128)S(1)}, u32[]{:S(2)}, u32[]{:S(2)}) collective-permute-start(f32[20,320]{1,0:T(8,128)S(1)} %get-tuple-element.54), channel_id=1, source_target_pairs={{0,14},{2,0},{4,2},{6,4},{8,6},{10,8},{12,10},{14,12},{1,15},{3,1}... | collective-permute-start | bytes 76808 | tf_op jit(solution)/shard_map/ppermute | solution.py:312
  96.9 4.9 %collective-permute-start.17 = (f32[20,320]{1,0:T(8,128)S(1)}, f32[20,320]{1,0:T(8,128)S(1)}, u32[]{:S(2)}, u32[]{:S(2)}) collective-permute-start(f32[20,320]{1,0:T(8,128)S(1)} %get-tuple-element.55), channel_id=1, source_target_pairs={{0,4},{2,6},{4,8},{6,10},{8,12},{10,14},{12,0},{14,2},{1,5},{3,7},... | collective-permute-start | bytes 76808 | tf_op jit(solution)/shard_map/ppermute | solution.py:312
  97.3 4.5 %collective-permute-start.18 = (f32[20,320]{1,0:T(8,128)S(1)}, f32[20,320]{1,0:T(8,128)S(1)}, u32[]{:S(2)}, u32[]{:S(2)}) collective-permute-start(f32[20,320]{1,0:T(8,128)S(1)} %get-tuple-element.56), channel_id=1, source_target_pairs={{0,12},{2,14},{4,0},{6,2},{8,4},{10,6},{12,8},{14,10},{1,13},{3,15... | collective-permute-start | bytes 76808 | tf_op jit(solution)/shard_map/ppermute | solution.py:312

commit v15 on v13

--- a/solution.py
+++ b/solution.py
@@ -485,7 +485,7 @@
     place = jnp.stack([lax.axis_index(axis) for axis in (LON, "co", "yl", "yh", "x", "z")])
     unit, other, *pieces = mlp(place, act, to_core(act), cot, to_core(cot), weight_in, weight_out)
     operands = (place, mixing.T, unit, to_core(other))
-    (block,) = small(pack_kernel, operands, [(SHARDS, 16, 128)], 2, name="pack", piped=True)
+    (block,) = small(pack_kernel, operands, [(SHARDS, 16, 128)], 2, name="pack")
     moved = exchange(pieces, "xy")
     spread = across(block)
     kept = (pltpu.VMEM((4, 80, 640), F32),)

time: 102 us -> 102 us (level)
    unnamed x32 -> x36, local copies, waits for them, and re-layouts: 4.72 us -> 4.96 us
  transfers between devices with their start and end apart: 21 -> 21, of which waited for: 7 -> 7; matrix products, arithmetic and copies ran while one was open for 1% -> 1% of each run, Pallas kernels for 11% -> 10%
where the time goes in v15:
time: 102 us; the launch traced here: 101 us
  starting transfers between devices  51.4 us (50%)
  Pallas kernels  28.2 us (28%)
  waiting for transfers between devices  15.1 us (15%)
  local copies, waits for them, and re-layouts  5.57 us (5%)
    all_to_all x2, starting transfers between devices, across(): return lax.all_to_all(block, LON, split_axis=0, concat_axis=0, tiled=True)  19 us
    ppermute x7, starting transfers between devices, exchange_z(): lax.ppermute(pieces[m], 'z', [(z, (z + m) % 8) for z in range(8)])  15.7 us
    pallas_call x1, Pallas kernels, mlp(): pl.pallas_call(mlp_kernel, grid_spec=pltpu.PrefetchScalarGridSpec(num_sca...  12.5 us
    all_to_all x2, waiting for transfers between devices, across(): return lax.all_to_all(block, LON, split_axis=0, concat_axis=0, tiled=True)  7.55 us
    ppermute x6, starting transfers between devices, permute(): return lax.ppermute(value, AXES, pairs)  7.44 us
    pallas_call x5, Pallas kernels, small(): pl.pallas_call(kernel, grid=(1,) if piped else (), in_specs=[pl.BlockSpec...  7.24 us
    ppermute x5, starting transfers between devices, to_core(): return lax.ppermute(value, 'co', [(0, 1), (1, 0)])  6.65 us
    unnamed x36, local copies, waits for them, and re-layouts  4.96 us
  transfers between devices with their start and end apart: 21, of which 7 were waited for; matrix products, arithmetic and copies ran while one was open for 1% of the time, Pallas kernels for 10%

profile of v15, /device:TPU:1, one launch (start us, length us, event | category | flops | bytes accessed | tf_op | source)
XLA Modules:
  0.0 101.1 jit_solution(14606336684595034004)
XLA Ops:
  0.6 3.3 %collective-permute-start = (f32[192,640]{1,0:T(8,128)}, f32[192,640]{1,0:T(8,128)S(1)}, u32[]{:S(2)}, u32[]{:S(2)}) collective-permute-start(f32[192,640]{1,0:T(8,128)} %bitcast.25), channel_id=1, source_target_pairs={{0,64},{64,0},{1,65},{65,1},{2,66},{66,2},{3,67},{67,3},{4,68},{68... | collective-permute-start | bytes 1474568 | tf_op jit(solution)/shard_map/ppermute | solution.py:317
  4.0 0.1 collective-permute-start.1
  4.1 0.6 stack.28.place_ref
  4.7 1.0 collective-permute-done.act_other_ref
  5.7 0.7 collective-permute-done.1.cot_other_ref
  6.4 0.1 copy-done.16
  6.4 0.7 copy-done.17
  7.1 12.5 %mlp.1 = (f32[192,640]{1,0:T(8,128)}, f32[192,640]{1,0:T(8,128)}, f32[160,1280]{1,0:T(8,128)}, f32[160,1280]{1,0:T(8,128)}, f32[160,1280]{1,0:T(8,128)}, /*index=5*/f32[160,1280]{1,0:T(8,128)}) custom-call(s32[6]{0:T(128)} %stack.28.place_ref, f32[192,640]{1,0:T(8,128)} %bitcast.26, f32[192,640]{1,0:T(8,128)} %copy-done.16, f32[192,640]{1,0:T(8,128)} %bitcast.28, ...), custom_call_target="tpu_custom_call" | custom-call | flops 4718592000 | bytes 12000000 | tf_op jit(solution)/shard_map/mlp/pallas_call | solution.py:190
  19.6 1.2 %collective-permute-start.3 = (f32[160,1280]{1,0:T(8,128)}, f32[160,1280]{1,0:T(8,128)S(1)}, u32[]{:S(2)}, u32[]{:S(2)}) collective-permute-start(f32[160,1280]{1,0:T(8,128)} %get-tuple-element.34), channel_id=1, source_target_pairs={{0,16},{1,17},{2,18},{3,19},{4,20},{5,21},{6,22},{7,23},{8,24},{9,... | collective-permute-start | bytes 2457608 | tf_op jit(solution)/shard_map/ppermute | solution.py:295
  20.8 0.4 collective-permute-start.4
  21.2 1.7 %collective-permute-start.5 = (f32[160,1280]{1,0:T(8,128)}, f32[160,1280]{1,0:T(8,128)S(1)}, u32[]{:S(2)}, u32[]{:S(2)}) collective-permute-start(f32[160,1280]{1,0:T(8,128)} %get-tuple-element.36), channel_id=1, source_target_pairs={{0,48},{1,49},{2,50},{3,51},{4,52},{5,53},{6,54},{7,55},{8,56},{9,... | collective-permute-start | bytes 2457608 | tf_op jit(solution)/shard_map/ppermute | solution.py:295
  22.9 0.6 collective-permute-start.2
  23.5 1.7 %collective-permute-done.2.arrived_ref = f32[192,640]{1,0:T(8,128)S(1)} collective-permute-done((f32[192,640]{1,0:T(8,128)}, f32[192,640]{1,0:T(8,128)S(1)}, u32[]{:S(2)}, u32[]{:S(2)}) %collective-permute-start.2) | collective-permute-done | bytes 491552 | tf_op jit(solution)/shard_map/ppermute | solution.py:317
  25.2 1.0 %copy-done.9 = f32[192,640]{1,0:T(8,128)S(1)} copy-done((f32[192,640]{1,0:T(8,128)S(1)}, f32[192,640]{1,0:T(8,128)}, u32[]{:S(2)}) %copy-start.9) | copy-done | bytes 491544
  26.3 2.0 %pack.1 = f32[64,16,128]{2,1,0:T(8,128)} custom-call(s32[6]{0:T(128)S(1)} %copy-done.10, f32[3,10]{1,0:T(4,128)S(1)} %bitcast.22, f32[192,640]{1,0:T(8,128)S(1)} %copy-done.9, f32[192,640]{1,0:T(8,128)S(1)} %collective-permute-done.2.arrived_ref), custom_call_target="tpu_custom_call" | custom-call | tf_op jit(solution)/shard_map/pack/pallas_call | solution.py:276
  28.3 12.5 %all-to-all-start = ((f32[64,16,128]{2,1,0:T(8,128)}), f32[64,16,128]{2,1,0:T(8,128)S(1)}, u32[]{:S(2)}, u32[]{:S(2)}) async-start(f32[64,16,128]{2,1,0:T(8,128)} %pack.1), calls=%async_computation | async-start | bytes 1048576 | tf_op jit(solution)/shard_map/all_to_all | solution.py:477
  40.8 0.0 collective-permute-done.3.refs_1_
  40.8 0.0 collective-permute-done.4.refs_2_
  40.8 0.8 collective-permute-done.5.refs_3_
  41.6 0.0 copy-done.13
  41.7 0.3 copy-done.14
  41.9 0.6 copy-done.15
  42.5 3.3 %swap.1 = (f32[80,640]{1,0:T(8,128)}, f32[80,640]{1,0:T(8,128)}, f32[80,640]{1,0:T(8,128)}, f32[80,640]{1,0:T(8,128)}) custom-call(s32[6]{0:T(128)} %stack.28.place_ref, f32[160,1280]{1,0:T(8,128)} %get-tuple-element.33.refs_0_, f32[160,1280]{1,0:T(8,128)} %copy-done.13, f32[160,1280]{1,0:T(8,128)} %copy-done.14, f32[160,1280]{1,0:T(8,128)} %copy-done.15), custom_call_target="tpu_custom_call" | custom-call | flops 10000000000 | bytes 4000000 | tf_op jit(solution)/shard_map/swap/pallas_call | solution.py:276
  45.8 0.5 collective-permute-start.8
  46.3 2.6 %collective-permute-start.9 = (f32[80,640]{1,0:T(8,128)}, f32[80,640]{1,0:T(8,128)S(1)}, u32[]{:S(2)}, u32[]{:S(2)}) collective-permute-start(f32[80,640]{1,0:T(8,128)} %get-tuple-element.43), channel_id=1, source_target_pairs={{0,128},{1,129},{2,130},{3,131},{4,132},{5,133},{6,134},{7,135},{8... | collective-permute-start | bytes 614408 | tf_op jit(solution)/shard_map/ppermute | solution.py:295
  48.9 1.1 %collective-permute-start.10 = (f32[80,640]{1,0:T(8,128)}, f32[80,640]{1,0:T(8,128)S(1)}, u32[]{:S(2)}, u32[]{:S(2)}) collective-permute-start(f32[80,640]{1,0:T(8,128)} %get-tuple-element.44), channel_id=1, source_target_pairs={{0,129},{1,128},{2,131},{3,130},{4,133},{5,132},{6,135},{7,134},{8... | collective-permute-start | bytes 614408 | tf_op jit(solution)/shard_map/ppermute | solution.py:295
  50.0 0.0 copy-done
  50.0 0.0 copy-done.6
  50.0 0.9 copy-done.7
  50.9 1.4 %kernel_spectrum.1._.kernel_ref = f32[336,768]{1,0:T(8,128)S(1)} custom-call(f32[336,768]{1,0:T(8,128)S(1)} %bitcast.21, bf16[768,768]{1,0:T(8,128)(2,1)S(1)} %copy-done.1, bf16[768,768]{1,0:T(8,128)(2,1)S(1)} %copy-done, f32[80,640]{1,0:T(8,128)S(1)} %copy-done.7), custom_call_target="tpu_custom_call" | custom-call | flops 1189085184 | bytes 5000000 | tf_op jit(solution)/shard_map/kernel_spectrum/pallas_call | solution.py:368
  52.3 6.1 %all-to-all-done.block_ref = f32[64,16,128]{2,1,0:T(8,128)S(1)} async-done(((f32[64,16,128]{2,1,0:T(8,128)}), f32[64,16,128]{2,1,0:T(8,128)S(1)}, u32[]{:S(2)}, u32[]{:S(2)}) %all-to-all-start) | async-done | bytes 524320 | tf_op jit(solution)/shard_map/all_to_all | solution.py:477
  58.4 1.3 %copy-done.5 = bf16[768,768]{1,0:T(8,128)(2,1)S(1)} copy-done((bf16[768,768]{1,0:T(8,128)(2,1)S(1)}, bf16[768,768]{1,0:T(8,128)(2,1)}, u32[]{:S(2)}) %copy-start.5) | copy-done | bytes 1179672
  59.7 1.6 %spectrum.1 = (f32[160,768]{1,0:T(8,128)S(1)}, f32[30,768]{1,0:T(8,128)S(1)}, f32[30,768]{1,0:T(8,128)S(1)}, f32[1,128]{1,0:T(1,128)S(1)}) custom-call(s32[6]{0:T(128)S(1)} %copy-done.11, f32[64,16,128]{2,1,0:T(8,128)S(1)} %all-to-all-done.block_ref, bf16[768,768]{1,0:T(8,128)(2,1)S(1)} %copy-done.5, bf16[768,768]{1,0:T(8,128)(2,1)S(1)} %copy-done.4, ...), custom_call_target="tpu_custom_call" | custom-call | flops 566231040 | bytes 4000000 | tf_op jit(solution)/shard_map/spectrum/pallas_call | solution.py:343
  61.2 0.0 copy-start.2
  61.3 0.0 collective-permute-done.8.refs_1_
  61.3 0.0 collective-permute-done.9.refs_2_
  61.3 0.0 collective-permute-done.10.refs_3_
  61.3 0.7 pair.1
  62.0 2.5 %collective-permute-start.11 = (f32[80,320]{1,0:T(8,128)S(1)}, f32[80,320]{1,0:T(8,128)S(1)}, u32[]{:S(2)}, u32[]{:S(2)}) collective-permute-start(f32[80,320]{1,0:T(8,128)S(1)} %get-tuple-element.45), channel_id=1, source_target_pairs={{0,64},{64,0},{1,65},{65,1},{2,66},{66,2},{3,67},{67,3},{4,68},{68... | collective-permute-start | bytes 307208 | tf_op jit(solution)/shard_map/ppermute | solution.py:317
  64.5 0.1 collective-permute-start.6
  64.6 2.6 %collective-permute-start.7 = (f32[30,768]{1,0:T(8,128)S(1)}, f32[30,768]{1,0:T(8,128)S(1)}, u32[]{:S(2)}, u32[]{:S(2)}) collective-permute-start(f32[30,768]{1,0:T(8,128)S(1)} %get-tuple-element.41), channel_id=1, source_target_pairs={{64,128},{128,64},{65,129},{129,65},{66,130},{130,66},{67,131},{13... | collective-permute-start | bytes 276488 | tf_op jit(solution)/shard_map/ppermute | solution.py:497
  67.2 0.0 collective-permute-done.6.near_ref
  67.2 3.3 %collective-permute-done.7.cross_ref = f32[30,768]{1,0:T(8,128)S(1)} collective-permute-done((f32[30,768]{1,0:T(8,128)S(1)}, f32[30,768]{1,0:T(8,128)S(1)}, u32[]{:S(2)}, u32[]{:S(2)}) %collective-permute-start.7) | collective-permute-done | bytes 92192 | tf_op jit(solution)/shard_map/ppermute | solution.py:497
  70.5 0.0 collective-permute-done.11.refs_0_.arrived_ref
  70.5 4.2 %filter.1._ = f32[64,16,128]{2,1,0:T(8,128)} custom-call(s32[6]{0:T(128)S(1)} %copy-done.11, f32[1,128]{1,0:T(1,128)S(1)} %get-tuple-element.38.mixing_ref, f32[160,768]{1,0:T(8,128)S(1)} %get-tuple-element.39._.data_ref, f32[30,768]{1,0:T(8,128)S(1)} %collective-permute-done.6.near_ref, f32[30,768]{1,0:T(8,128)S(1)} %collective-permute-done.7.cross_ref, ...), custom_call_target="tpu_custom_call" | custom-call | flops 566231040 | bytes 5000000 | tf_op jit(solution)/shard_map/filter/pallas_call | solution.py:428
  74.7 6.6 %all-to-all-start.1 = ((f32[64,16,128]{2,1,0:T(8,128)}), f32[64,16,128]{2,1,0:T(8,128)S(1)}, u32[]{:S(2)}, u32[]{:S(2)}) async-start(f32[64,16,128]{2,1,0:T(8,128)} %filter.1._), calls=%async_computation.1 | async-start | bytes 1048576 | tf_op jit(solution)/shard_map/all_to_all | solution.py:477
  81.3 0.6 stack.29
  81.9 1.1 %collective-permute-start.12 = (f32[20,320]{1,0:T(8,128)S(1)}, f32[20,320]{1,0:T(8,128)S(1)}, u32[]{:S(2)}, u32[]{:S(2)}) collective-permute-start(f32[20,320]{1,0:T(8,128)S(1)} %get-tuple-element.50), channel_id=1, source_target_pairs={{0,2},{2,4},{4,6},{6,8},{8,10},{10,12},{12,14},{14,0},{1,3},{3,5},... | collective-permute-start | bytes 76808 | tf_op jit(solution)/shard_map/ppermute | solution.py:312
  83.0 1.7 %collective-permute-start.13 = (f32[20,320]{1,0:T(8,128)S(1)}, f32[20,320]{1,0:T(8,128)S(1)}, u32[]{:S(2)}, u32[]{:S(2)}) collective-permute-start(f32[20,320]{1,0:T(8,128)S(1)} %get-tuple-element.51), channel_id=1, source_target_pairs={{0,14},{2,0},{4,2},{6,4},{8,6},{10,8},{12,10},{14,12},{1,15},{3,1}... | collective-permute-start | bytes 76808 | tf_op jit(solution)/shard_map/ppermute | solution.py:312
  84.6 4.9 %collective-permute-start.14 = (f32[20,320]{1,0:T(8,128)S(1)}, f32[20,320]{1,0:T(8,128)S(1)}, u32[]{:S(2)}, u32[]{:S(2)}) collective-permute-start(f32[20,320]{1,0:T(8,128)S(1)} %get-tuple-element.52), channel_id=1, source_target_pairs={{0,8},{2,10},{4,12},{6,14},{8,0},{10,2},{12,4},{14,6},{1,9},{3,11}... | collective-permute-start | bytes 76808 | tf_op jit(solution)/shard_map/ppermute | solution.py:312
  89.5 0.0 collective-permute-start.15
  89.5 4.5 %collective-permute-start.16 = (f32[20,320]{1,0:T(8,128)S(1)}, f32[20,320]{1,0:T(8,128)S(1)}, u32[]{:S(2)}, u32[]{:S(2)}) collective-permute-start(f32[20,320]{1,0:T(8,128)S(1)} %get-tuple-element.54), channel_id=1, source_target_pairs={{0,10},{2,12},{4,14},{6,0},{8,2},{10,4},{12,6},{14,8},{1,11},{3,13... | collective-permute-start | bytes 76808 | tf_op jit(solution)/shard_map/ppermute | solution.py:312
  94.0 0.0 collective-permute-done.12.refs_1_
  94.0 1.1 %collective-permute-start.17 = (f32[20,320]{1,0:T(8,128)S(1)}, f32[20,320]{1,0:T(8,128)S(1)}, u32[]{:S(2)}, u32[]{:S(2)}) collective-permute-start(f32[20,320]{1,0:T(8,128)S(1)} %get-tuple-element.55), channel_id=1, source_target_pairs={{0,4},{2,6},{4,8},{6,10},{8,12},{10,14},{12,0},{14,2},{1,5},{3,7},... | collective-permute-start | bytes 76808 | tf_op jit(solution)/shard_map/ppermute | solution.py:312
  95.1 0.0 collective-permute-done.13.refs_2_
  95.1 2.5 %collective-permute-start.18 = (f32[20,320]{1,0:T(8,128)S(1)}, f32[20,320]{1,0:T(8,128)S(1)}, u32[]{:S(2)}, u32[]{:S(2)}) collective-permute-start(f32[20,320]{1,0:T(8,128)S(1)} %get-tuple-element.56), channel_id=1, source_target_pairs={{0,12},{2,14},{4,0},{6,2},{8,4},{10,6},{12,8},{14,10},{1,13},{3,15... | collective-permute-start | bytes 76808 | tf_op jit(solution)/shard_map/ppermute | solution.py:312
  97.6 1.5 %all-to-all-done.1.block_ref = f32[64,16,128]{2,1,0:T(8,128)S(1)} async-done(((f32[64,16,128]{2,1,0:T(8,128)}), f32[64,16,128]{2,1,0:T(8,128)S(1)}, u32[]{:S(2)}, u32[]{:S(2)}) %all-to-all-start.1) | async-done | bytes 524320 | tf_op jit(solution)/shard_map/all_to_all | solution.py:477
  99.1 1.3 %unpack.1 = (f32[192,640]{1,0:T(8,128)}, f32[8,128]{1,0:T(8,128)S(1)}) custom-call(f32[64,16,128]{2,1,0:T(8,128)S(1)} %all-to-all-done.1.block_ref), custom_call_target="tpu_custom_call" | custom-call | tf_op jit(solution)/shard_map/unpack/pallas_call | solution.py:463
  100.4 0.0 collective-permute-done.14.refs_3_
  100.4 0.0 collective-permute-done.15.refs_4_
  100.4 0.0 collective-permute-done.16.refs_5_
  100.4 0.0 collective-permute-done.17.refs_6_
  100.4 0.0 collective-permute-done.18.refs_7_
  100.4 0.7 last.1
  (25 shorter events, 0.0 us)
Async XLA Ops:
  0.6 5.0 %collective-permute-start = (f32[192,640]{1,0:T(8,128)}, f32[192,640]{1,0:T(8,128)S(1)}, u32[]{:S(2)}, u32[]{:S(2)}) collective-permute-start(f32[192,640]{1,0:T(8,128)} %bitcast.25), channel_id=1, source_target_pairs={{0,64},{64,0},{1,65},{65,1},{2,66},{66,2},{3,67},{67,3},{4,68},{68... | collective-permute-start | bytes 1474568 | tf_op jit(solution)/shard_map/ppermute | solution.py:317
  4.0 2.4 %collective-permute-start.1 = (f32[192,640]{1,0:T(8,128)}, f32[192,640]{1,0:T(8,128)S(1)}, u32[]{:S(2)}, u32[]{:S(2)}) collective-permute-start(f32[192,640]{1,0:T(8,128)} %bitcast.27), channel_id=1, source_target_pairs={{0,64},{64,0},{1,65},{65,1},{2,66},{66,2},{3,67},{67,3},{4,68},{68... | collective-permute-start | bytes 1474568 | tf_op jit(solution)/shard_map/ppermute | solution.py:317
  5.7 0.8 copy-start.16
  6.4 0.8 copy-start.17
  7.1 18.1 %copy-start.10 = (s32[6]{0:T(128)S(1)}, s32[6]{0:T(128)}, u32[]{:S(2)}) copy-start(s32[6]{0:T(128)} %stack.28.place_ref) | copy-start | bytes 76
  7.1 18.1 %copy-start.12 = (f32[10,3]{0,1:T(4,128)S(1)}, f32[10,3]{0,1:T(4,128)}, u32[]{:S(2)}) copy-start(f32[10,3]{0,1:T(4,128)} %param.17) | copy-start | bytes 364
  19.6 21.1 %collective-permute-start.3 = (f32[160,1280]{1,0:T(8,128)}, f32[160,1280]{1,0:T(8,128)S(1)}, u32[]{:S(2)}, u32[]{:S(2)}) collective-permute-start(f32[160,1280]{1,0:T(8,128)} %get-tuple-element.34), channel_id=1, source_target_pairs={{0,16},{1,17},{2,18},{3,19},{4,20},{5,21},{6,22},{7,23},{8,24},{9,... | collective-permute-start | bytes 2457608 | tf_op jit(solution)/shard_map/ppermute | solution.py:295
  20.8 20.0 %collective-permute-start.4 = (f32[160,1280]{1,0:T(8,128)}, f32[160,1280]{1,0:T(8,128)S(1)}, u32[]{:S(2)}, u32[]{:S(2)}) collective-permute-start(f32[160,1280]{1,0:T(8,128)} %get-tuple-element.35), channel_id=1, source_target_pairs={{0,32},{1,33},{2,34},{3,35},{4,36},{5,37},{6,38},{7,39},{8,40},{9,... | collective-permute-start | bytes 2457608 | tf_op jit(solution)/shard_map/ppermute | solution.py:295
  21.2 20.4 %collective-permute-start.5 = (f32[160,1280]{1,0:T(8,128)}, f32[160,1280]{1,0:T(8,128)S(1)}, u32[]{:S(2)}, u32[]{:S(2)}) collective-permute-start(f32[160,1280]{1,0:T(8,128)} %get-tuple-element.36), channel_id=1, source_target_pairs={{0,48},{1,49},{2,50},{3,51},{4,52},{5,53},{6,54},{7,55},{8,56},{9,... | collective-permute-start | bytes 2457608 | tf_op jit(solution)/shard_map/ppermute | solution.py:295
  22.9 2.3 %collective-permute-start.2 = (f32[192,640]{1,0:T(8,128)}, f32[192,640]{1,0:T(8,128)S(1)}, u32[]{:S(2)}, u32[]{:S(2)}) collective-permute-start(f32[192,640]{1,0:T(8,128)} %get-tuple-element.32), channel_id=1, source_target_pairs={{0,64},{64,0},{1,65},{65,1},{2,66},{66,2},{3,67},{67,3},{4,68},{68... | collective-permute-start | bytes 1474568 | tf_op jit(solution)/shard_map/ppermute | solution.py:317
  25.2 1.0 %copy-start.9 = (f32[192,640]{1,0:T(8,128)S(1)}, f32[192,640]{1,0:T(8,128)}, u32[]{:S(2)}) copy-start(f32[192,640]{1,0:T(8,128)} %get-tuple-element.31.unit_ref) | copy-start | bytes 1474564
  28.3 30.1 %all-to-all-start = ((f32[64,16,128]{2,1,0:T(8,128)}), f32[64,16,128]{2,1,0:T(8,128)S(1)}, u32[]{:S(2)}, u32[]{:S(2)}) async-start(f32[64,16,128]{2,1,0:T(8,128)} %pack.1), calls=%async_computation | async-start | bytes 1048576 | tf_op jit(solution)/shard_map/all_to_all | solution.py:477
  40.8 0.9 copy-start.13
  40.8 1.1 %copy-start.14 = (f32[160,1280]{1,0:T(8,128)}, f32[160,1280]{1,0:T(8,128)S(1)}, u32[]{:S(2)}) copy-start(f32[160,1280]{1,0:T(8,128)S(1)} %collective-permute-done.4.refs_2_) | copy-start | bytes 2457604
  41.6 0.9 copy-start.15
  42.5 7.5 %copy-start = (bf16[768,768]{1,0:T(8,128)(2,1)S(1)}, bf16[768,768]{1,0:T(8,128)(2,1)}, u32[]{:S(2)}) copy-start(bf16[768,768]{1,0:T(8,128)(2,1)} %constant.38.clone.low_ref) | copy-start | bytes 3538948
  42.5 7.5 %copy-start.1 = (bf16[768,768]{1,0:T(8,128)(2,1)S(1)}, bf16[768,768]{1,0:T(8,128)(2,1)}, u32[]{:S(2)}) copy-start(bf16[768,768]{1,0:T(8,128)(2,1)} %constant.37.clone.top_ref) | copy-start | bytes 3538948
  42.5 7.5 %copy-start.6 = (f32[3,16,7,768]{3,1,2,0:T(8,128)S(1)}, f32[3,16,7,768]{3,1,2,0:T(8,128)}, u32[]{:S(2)}) copy-start(f32[3,16,7,768]{3,1,2,0:T(8,128)} %param.16) | copy-start | bytes 3096580
  45.8 15.5 %collective-permute-start.8 = (f32[80,640]{1,0:T(8,128)}, f32[80,640]{1,0:T(8,128)S(1)}, u32[]{:S(2)}, u32[]{:S(2)}) collective-permute-start(f32[80,640]{1,0:T(8,128)} %get-tuple-element.42), channel_id=1, source_target_pairs={{0,1},{1,0},{2,3},{3,2},{4,5},{5,4},{6,7},{7,6},{8,9},{9,8},{10,11... | collective-permute-start | bytes 614408 | tf_op jit(solution)/shard_map/ppermute | solution.py:295
  46.3 14.9 %collective-permute-start.9 = (f32[80,640]{1,0:T(8,128)}, f32[80,640]{1,0:T(8,128)S(1)}, u32[]{:S(2)}, u32[]{:S(2)}) collective-permute-start(f32[80,640]{1,0:T(8,128)} %get-tuple-element.43), channel_id=1, source_target_pairs={{0,128},{1,129},{2,130},{3,131},{4,132},{5,133},{6,134},{7,135},{8... | collective-permute-start | bytes 614408 | tf_op jit(solution)/shard_map/ppermute | solution.py:295
  48.9 12.4 %collective-permute-start.10 = (f32[80,640]{1,0:T(8,128)}, f32[80,640]{1,0:T(8,128)S(1)}, u32[]{:S(2)}, u32[]{:S(2)}) collective-permute-start(f32[80,640]{1,0:T(8,128)} %get-tuple-element.44), channel_id=1, source_target_pairs={{0,129},{1,128},{2,131},{3,130},{4,133},{5,132},{6,135},{7,134},{8... | collective-permute-start | bytes 614408 | tf_op jit(solution)/shard_map/ppermute | solution.py:295
  50.0 0.9 copy-start.7
  50.9 7.4 %copy-start.4 = (bf16[768,768]{1,0:T(8,128)(2,1)S(1)}, bf16[768,768]{1,0:T(8,128)(2,1)}, u32[]{:S(2)}) copy-start(bf16[768,768]{1,0:T(8,128)(2,1)} %constant.40.clone.low_ref) | copy-start | bytes 3538948
  50.9 7.4 %copy-start.11 = (s32[6]{0:T(128)S(1)}, s32[6]{0:T(128)}, u32[]{:S(2)}) copy-start(s32[6]{0:T(128)} %stack.28.place_ref) | copy-start | bytes 76
  58.4 1.3 %copy-start.5 = (bf16[768,768]{1,0:T(8,128)(2,1)S(1)}, bf16[768,768]{1,0:T(8,128)(2,1)}, u32[]{:S(2)}) copy-start(bf16[768,768]{1,0:T(8,128)(2,1)} %constant.39.clone.top_ref) | copy-start | bytes 3538948
  59.7 1.6 %copy-start.8 = (f32[80,640]{1,0:T(8,128)S(1)}, f32[80,640]{1,0:T(8,128)}, u32[]{:S(2)}) copy-start(f32[80,640]{1,0:T(8,128)} %get-tuple-element.37._.refs_0_) | copy-start | bytes 614404
  59.7 10.8 %copy-start.3 = (bf16[768,768]{1,0:T(8,128)(2,1)S(1)}, bf16[768,768]{1,0:T(8,128)(2,1)}, u32[]{:S(2)}) copy-start(bf16[768,768]{1,0:T(8,128)(2,1)} %constant.41.clone.top_ref) | copy-start | bytes 3538948
  61.2 9.3 %copy-start.2 = (bf16[768,768]{1,0:T(8,128)(2,1)S(1)}, bf16[768,768]{1,0:T(8,128)(2,1)}, u32[]{:S(2)}) copy-start(bf16[768,768]{1,0:T(8,128)(2,1)} %constant.42.clone.low_ref) | copy-start | bytes 3538948
  62.0 8.5 %collective-permute-start.11 = (f32[80,320]{1,0:T(8,128)S(1)}, f32[80,320]{1,0:T(8,128)S(1)}, u32[]{:S(2)}, u32[]{:S(2)}) collective-permute-start(f32[80,320]{1,0:T(8,128)S(1)} %get-tuple-element.45), channel_id=1, source_target_pairs={{0,64},{64,0},{1,65},{65,1},{2,66},{66,2},{3,67},{67,3},{4,68},{68... | collective-permute-start | bytes 307208 | tf_op jit(solution)/shard_map/ppermute | solution.py:317
  64.5 2.7 %collective-permute-start.6 = (f32[30,768]{1,0:T(8,128)S(1)}, f32[30,768]{1,0:T(8,128)S(1)}, u32[]{:S(2)}, u32[]{:S(2)}) collective-permute-start(f32[30,768]{1,0:T(8,128)S(1)} %get-tuple-element.40), channel_id=1, source_target_pairs={{0,64},{64,0},{1,65},{65,1},{2,66},{66,2},{3,67},{67,3},{4,68},{68... | collective-permute-start | bytes 276488 | tf_op jit(solution)/shard_map/ppermute | solution.py:317
  64.6 5.9 %collective-permute-start.7 = (f32[30,768]{1,0:T(8,128)S(1)}, f32[30,768]{1,0:T(8,128)S(1)}, u32[]{:S(2)}, u32[]{:S(2)}) collective-permute-start(f32[30,768]{1,0:T(8,128)S(1)} %get-tuple-element.41), channel_id=1, source_target_pairs={{64,128},{128,64},{65,129},{129,65},{66,130},{130,66},{67,131},{13... | collective-permute-start | bytes 276488 | tf_op jit(solution)/shard_map/ppermute | solution.py:497
  74.7 24.4 %all-to-all-start.1 = ((f32[64,16,128]{2,1,0:T(8,128)}), f32[64,16,128]{2,1,0:T(8,128)S(1)}, u32[]{:S(2)}, u32[]{:S(2)}) async-start(f32[64,16,128]{2,1,0:T(8,128)} %filter.1._), calls=%async_computation.1 | async-start | bytes 1048576 | tf_op jit(solution)/shard_map/all_to_all | solution.py:477
  81.9 12.2 %collective-permute-start.12 = (f32[20,320]{1,0:T(8,128)S(1)}, f32[20,320]{1,0:T(8,128)S(1)}, u32[]{:S(2)}, u32[]{:S(2)}) collective-permute-start(f32[20,320]{1,0:T(8,128)S(1)} %get-tuple-element.50), channel_id=1, source_target_pairs={{0,2},{2,4},{4,6},{6,8},{8,10},{10,12},{12,14},{14,0},{1,3},{3,5},... | collective-permute-start | bytes 76808 | tf_op jit(solution)/shard_map/ppermute | solution.py:312
  83.0 12.2 %collective-permute-start.13 = (f32[20,320]{1,0:T(8,128)S(1)}, f32[20,320]{1,0:T(8,128)S(1)}, u32[]{:S(2)}, u32[]{:S(2)}) collective-permute-start(f32[20,320]{1,0:T(8,128)S(1)} %get-tuple-element.51), channel_id=1, source_target_pairs={{0,14},{2,0},{4,2},{6,4},{8,6},{10,8},{12,10},{14,12},{1,15},{3,1}... | collective-permute-start | bytes 76808 | tf_op jit(solution)/shard_map/ppermute | solution.py:312
  84.6 15.8 %collective-permute-start.14 = (f32[20,320]{1,0:T(8,128)S(1)}, f32[20,320]{1,0:T(8,128)S(1)}, u32[]{:S(2)}, u32[]{:S(2)}) collective-permute-start(f32[20,320]{1,0:T(8,128)S(1)} %get-tuple-element.52), channel_id=1, source_target_pairs={{0,8},{2,10},{4,12},{6,14},{8,0},{10,2},{12,4},{14,6},{1,9},{3,11}... | collective-permute-start | bytes 76808 | tf_op jit(solution)/shard_map/ppermute | solution.py:312
  89.5 10.8 %collective-permute-start.15 = (f32[20,320]{1,0:T(8,128)S(1)}, f32[20,320]{1,0:T(8,128)S(1)}, u32[]{:S(2)}, u32[]{:S(2)}) collective-permute-start(f32[20,320]{1,0:T(8,128)S(1)} %get-tuple-element.53), channel_id=1, source_target_pairs={{0,6},{2,8},{4,10},{6,12},{8,14},{10,0},{12,2},{14,4},{1,7},{3,9},... | collective-permute-start | bytes 76808 | tf_op jit(solution)/shard_map/ppermute | solution.py:312
  89.5 10.8 %collective-permute-start.16 = (f32[20,320]{1,0:T(8,128)S(1)}, f32[20,320]{1,0:T(8,128)S(1)}, u32[]{:S(2)}, u32[]{:S(2)}) collective-permute-start(f32[20,320]{1,0:T(8,128)S(1)} %get-tuple-element.54), channel_id=1, source_target_pairs={{0,10},{2,12},{4,14},{6,0},{8,2},{10,4},{12,6},{14,8},{1,11},{3,13... | collective-permute-start | bytes 76808 | tf_op jit(solution)/shard_map/ppermute | solution.py:312
  94.0 6.4 %collective-permute-start.17 = (f32[20,320]{1,0:T(8,128)S(1)}, f32[20,320]{1,0:T(8,128)S(1)}, u32[]{:S(2)}, u32[]{:S(2)}) collective-permute-start(f32[20,320]{1,0:T(8,128)S(1)} %get-tuple-element.55), channel_id=1, source_target_pairs={{0,4},{2,6},{4,8},{6,10},{8,12},{10,14},{12,0},{14,2},{1,5},{3,7},... | collective-permute-start | bytes 76808 | tf_op jit(solution)/shard_map/ppermute | solution.py:312
  95.1 5.3 %collective-permute-start.18 = (f32[20,320]{1,0:T(8,128)S(1)}, f32[20,320]{1,0:T(8,128)S(1)}, u32[]{:S(2)}, u32[]{:S(2)}) collective-permute-start(f32[20,320]{1,0:T(8,128)S(1)} %get-tuple-element.56), channel_id=1, source_target_pairs={{0,12},{2,14},{4,0},{6,2},{8,4},{10,6},{12,8},{14,10},{1,13},{3,15... | collective-permute-start | bytes 76808 | tf_op jit(solution)/shard_map/ppermute | solution.py:312
